TPU v7x, 128 devices: a whole 4x4x4 slice. The times are simulated.
128 devices in a mesh: dp: 16 (over y, z), mp: 8 (over x, core).
Axes of the slice: x: 4, y: 4, z: 4, core: 2. Of those that a mesh axis runs over, the one named last changes fastest.
Arguments:
- joined_rows: bfloat16 [4096, 24576], P('dp', 'mp'), may hold values from -6 to 6
- fc_weight: bfloat16 [24576, 8192], P('mp', 'dp'), may hold values from -0.0390625 to 0.0390625
- target_features: bfloat16 [4096, 8192], P('mp', 'dp'), may hold values from -6 to 6
- segment_ids: int32 [4096], P('mp'), may hold values from 0 to 63, never falling along the last dimension, each value on 1 to 512 neighbouring positions
- step_gains: float32 [3, 8192], P(None, 'dp'), may hold values from 0.25 to 1.75
Outputs:
- mean_loss: float32 [], replicated
- grad_weight: float32 [24576, 8192], P('mp', 'dp')
All inputs are finite; a program needn't handle non-finite values.
Results may differ from a plain program's by a relative error of at most 0.0029.
Values may be sent and summed in bfloat16 or wider, within the bound.
No kernel may reach another device: no remote copies, remote signals or barrier semaphores. Data moves between devices by JAX's collectives and lax.ppermute only.
A program may use at most 128 MiB of HBM per device.

v0:
```python
import math

import jax
import jax.numpy as jnp
from jax import lax
from jax.sharding import PartitionSpec as P

D = 8192
STEPS = 3


EPSILON = 1e-06


def shifted(block, axis, distance):
    devices = range(lax.axis_size(axis))
    route = [(i - distance, i) for i in devices if i - distance in devices]
    return lax.ppermute(block, axis, route)


def local(joined_rows, fc_weight, target_features, segment_ids, step_gains):
    gathered = lax.all_gather(joined_rows, "dp", axis=0, tiled=True)
    total_rows = gathered.shape[0]
    share_rows = total_rows // lax.axis_size("mp")
    first_state = lax.psum_scatter(
        jnp.dot(gathered, fc_weight, preferred_element_type=jnp.float32),
        "mp",
        scatter_dimension=0,
        tiled=True,
    )
    mp_index = lax.axis_index("mp")
    targets, segments = (target_features, segment_ids)
    offset = mp_index * share_rows
    next_targets, next_segments = shifted(
        (target_features[: STEPS - 1], segment_ids[: STEPS - 1]), "mp", -1
    )
    lead_mask = (lax.axis_index("dp") == 0).astype(jnp.float32)
    local_rows = first_state.shape[0]
    columns = first_state.shape[1]
    seg_ext = jnp.concatenate([segments, next_segments])
    position = offset + jnp.arange(local_rows + STEPS - 1, dtype=jnp.int32)
    inside = position < total_rows
    same_next = ((seg_ext[1 : local_rows + 1] == segments) & inside[1 : local_rows + 1]).astype(
        jnp.float32
    )
    prev_keep = jnp.concatenate([jnp.ones((1,), jnp.float32), same_next[:-1]])
    goal_ext = jnp.concatenate([targets, next_targets], axis=0)
    draft_state = first_state
    saved = []
    err_local = jnp.zeros((), jnp.float32)
    count_local = jnp.zeros((), jnp.float32)
    for step_index in range(STEPS):
        shift_incoming = shifted(draft_state[-1:] * same_next[-1], "mp", 1)
        mixed_rows = (
            first_state
            + jnp.concatenate([shift_incoming, draft_state[:-1]], axis=0) * prev_keep[:, None]
        )
        squares = lax.psum(jnp.sum(mixed_rows * mixed_rows, axis=1), "dp")
        scale_rows = lax.rsqrt(squares / D + EPSILON)[:, None]
        normed = mixed_rows * scale_rows
        draft_state = normed * step_gains[step_index]
        kept_mask = (
            (seg_ext[step_index : step_index + local_rows] == segments)
            & inside[step_index : step_index + local_rows]
        ).astype(jnp.float32)
        goal_rows = goal_ext[step_index : step_index + local_rows].astype(jnp.float32)
        error_rows = (draft_state - goal_rows) * kept_mask[:, None]
        err_local = err_local + jnp.sum(error_rows * error_rows)
        count_local = count_local + jnp.sum(kept_mask)
        saved.append((normed, scale_rows, error_rows))
    err_total, count_total = lax.psum((err_local, count_local * lead_mask), ("dp", "mp"))
    mean_loss = err_total / (2.0 * D * count_total)
    factor = 1.0 / math.sqrt(total_rows)
    carry_rows = jnp.zeros((local_rows, columns), jnp.float32)
    grad_state = jnp.zeros((local_rows, columns), jnp.float32)
    for step_index in reversed(range(STEPS)):
        normed, scale_rows, error_rows = saved[step_index]
        upstream = (error_rows * factor + carry_rows) * step_gains[step_index]
        products = lax.psum(jnp.sum(upstream * normed, axis=1), "dp")
        grad_mixed = scale_rows * (upstream - normed * (products / D)[:, None])
        grad_state = grad_state + grad_mixed
        incoming = shifted(grad_mixed[:1], "mp", -1)
        carry_rows = jnp.concatenate([grad_mixed[1:], incoming], axis=0) * same_next[:, None]
    grad_rows = (grad_state + carry_rows).astype(jnp.bfloat16)
    all_grads = lax.all_gather(grad_rows, "mp", axis=0, tiled=True)
    grad_weight = lax.dot_general(
        gathered, all_grads, (((0,), (0,)), ((), ())), preferred_element_type=jnp.float32
    )
    return (mean_loss, grad_weight)


def solution(mesh):
    in_specs = (P("dp", "mp"), P("mp", "dp"), P("mp", "dp"), P("mp"), P(None, "dp"))
    out_specs = (P(), P("mp", "dp"))
    return jax.shard_map(local, mesh=mesh, in_specs=in_specs, out_specs=out_specs, check_vma=False)
```

profile of v0, /device:TPU:1, one launch (start us, length us, event | category | flops | bytes accessed | tf_op | source)
XLA Modules:
  0.0 609.5 jit_solution(1412230000787661900)
XLA Ops:
  7.2 0.0 copy-start
  7.2 0.0 all-gather.3.cloned.1.call-start
  7.2 0.7 all-gather.3.cloned.1.call-update
  7.9 0.0 reduce-scatter.2.cloned.1.call-start
  8.0 159.8 %all-gather.3.cloned.1.call-done = bf16[4096,3072]{1,0:T(8,128)(2,1)} async-done(((bf16[256,3072]{1,0:T(8,128)(2,1)}), bf16[4096,3072]{1,0:T(8,128)(2,1)}) %all-gather.3.cloned.1.call-update) | async-done | bytes 25165840 | tf_op jit(solution)/shard_map/all_gather | solution.py:22
  167.8 19.9 %fusion.22 = f32[4096,512]{1,0:T(8,128)} fusion(bf16[4096,3072]{1,0:T(8,128)(2,1)} %all-gather.3.cloned.1.call-done, bf16[3072,512]{1,0:T(8,128)(2,1)S(1)} %copy-done), kind=kOutput, calls=%fused_computation.60 | convolution fusion | flops 12884901888 | bytes 36700160 | tf_op jit(solution)/shard_map/dot_general | solution.py:26
  187.7 0.0 reduce-scatter.2.cloned.1.call-update
  187.7 0.0 all-gather.5.cloned.1.call-start
  187.8 0.6 copy-done.11
  188.4 2.6 collective-permute-start
  191.0 1.9 collective-permute-start.3
  193.0 0.3 collective-permute-done
  193.3 0.8 fusion.14
  194.0 0.6 slice.89
  194.6 44.8 %reduce-scatter.2.cloned.1.call-done = f32[512,512]{1,0:T(8,128)} async-done(((f32[4096,512]{1,0:T(8,128)}), f32[512,512]{1,0:T(8,128)}) %reduce-scatter.2.cloned.1.call-update) | async-done | bytes 1048592 | tf_op jit(solution)/shard_map/reduce_scatter | solution.py:25
  239.4 1.5 slice_multiply_fusion.2
  240.8 1.9 collective-permute-start.1
  242.7 0.1 pad_maximum_fusion
  242.8 1.1 collective-permute-done.1
  243.9 1.9 multiply_reduce_fusion.8
  245.9 33.4 %psum.56 = f32[512]{0:T(512)S(1)} all-reduce(f32[512]{0:T(512)S(1)} %get-tuple-element.20), channel_id=1, replica_groups=mesh['dp'=16,'mp'=8] {'dp'}, use_global_device_ids=true, to_apply=%region_2.0 | all-reduce | flops 512 | bytes 4096 | tf_op jit(solution)/shard_map/psum | solution.py:58
  279.2 0.2 multiply_multiply_fusion.1
  279.4 0.7 slice_multiply_fusion.1
  280.1 11.0 %collective-permute-start.2 = (f32[1,512]{1,0:T(1,128)S(1)}, f32[1,512]{1,0:T(1,128)S(1)}, u32[]{:S(2)}, u32[]{:S(2)}) collective-permute-start(f32[1,512]{1,0:T(1,128)S(1)} %slice_multiply_fusion.1), channel_id=1, source_target_pairs={{0,1},{1,2},{2,3},{3,4},{4,5},{5,6},{6,7},{8,9},{9,10},{10,11},{11... | collective-permute-start | bytes 6152 | tf_op jit(solution)/shard_map/ppermute | solution.py:18
  291.1 0.8 constant_dynamic-update-slice_fusion.2
  291.9 0.0 collective-permute-done.2
  291.9 0.4 multiply_reduce_fusion.6
  292.3 28.5 %psum.57 = f32[512]{0:T(512)S(1)} all-reduce(f32[512]{0:T(512)S(1)} %get-tuple-element.18), channel_id=1, replica_groups=mesh['dp'=16,'mp'=8] {'dp'}, use_global_device_ids=true, to_apply=%region_5.0 | all-reduce | flops 512 | bytes 4096 | tf_op jit(solution)/shard_map/psum | solution.py:58
  320.9 0.2 multiply_multiply_fusion
  321.0 0.7 slice_multiply_fusion
  321.7 11.0 %collective-permute-start.4 = (f32[1,512]{1,0:T(1,128)S(1)}, f32[1,512]{1,0:T(1,128)S(1)}, u32[]{:S(2)}, u32[]{:S(2)}) collective-permute-start(f32[1,512]{1,0:T(1,128)S(1)} %slice_multiply_fusion), channel_id=1, source_target_pairs={{0,1},{1,2},{2,3},{3,4},{4,5},{5,6},{6,7},{8,9},{9,10},{10,11},{11... | collective-permute-start | bytes 6152 | tf_op jit(solution)/shard_map/ppermute | solution.py:18
  332.7 0.0 collective-permute-done.3
  332.7 0.6 constant_dynamic-update-slice_fusion.1
  333.3 0.1 collective-permute-done.4
  333.4 1.3 multiply_reduce_fusion.4
  334.7 30.4 %psum.58 = f32[512]{0:T(512)S(1)} all-reduce(f32[512]{0:T(512)S(1)} %get-tuple-element.16), channel_id=1, replica_groups=mesh['dp'=16,'mp'=8] {'dp'}, use_global_device_ids=true, to_apply=%region_8.0 | all-reduce | flops 512 | bytes 4096 | tf_op jit(solution)/shard_map/psum | solution.py:58
  365.1 2.6 multiply_reduce_fusion.2
  367.7 28.7 %psum.61 = f32[512]{0:T(512)S(1)} all-reduce(f32[512]{0:T(512)S(1)} %get-tuple-element.6), channel_id=1, replica_groups=mesh['dp'=16,'mp'=8] {'dp'}, use_global_device_ids=true, to_apply=%region_16.0 | all-reduce | flops 512 | bytes 4096 | tf_op jit(solution)/shard_map/psum | solution.py:79
  396.4 1.8 subtract_multiply_fusion.2
  398.3 10.8 %collective-permute-start.5 = (f32[1,512]{1,0:T(1,128)S(1)}, f32[1,512]{1,0:T(1,128)S(1)}, u32[]{:S(2)}, u32[]{:S(2)}) collective-permute-start(f32[1,512]{1,0:T(1,128)S(1)} %slice.120), channel_id=1, source_target_pairs={{1,0},{2,1},{3,2},{4,3},{5,4},{6,5},{7,6},{9,8},{10,9},{11,10},{12... | collective-permute-start | bytes 6152 | tf_op jit(solution)/shard_map/ppermute | solution.py:18
  409.1 0.1 slice.119
  409.2 0.0 copy-start.8
  409.2 8.7 %collective-permute-done.5 = f32[1,512]{1,0:T(1,128)S(1)} collective-permute-done((f32[1,512]{1,0:T(1,128)S(1)}, f32[1,512]{1,0:T(1,128)S(1)}, u32[]{:S(2)}, u32[]{:S(2)}) %collective-permute-start.5) | collective-permute-done | bytes 2080 | tf_op jit(solution)/shard_map/ppermute | solution.py:18
  417.9 0.0 copy-done.3
  417.9 1.5 multiply_reduce_fusion.1
  419.4 30.2 %psum.62 = f32[512]{0:T(512)S(1)} all-reduce(f32[512]{0:T(512)S(1)} %get-tuple-element.4), channel_id=1, replica_groups=mesh['dp'=16,'mp'=8] {'dp'}, use_global_device_ids=true, to_apply=%region_18.0 | all-reduce | flops 512 | bytes 4096 | tf_op jit(solution)/shard_map/psum | solution.py:79
  449.6 1.8 subtract_multiply_fusion.1
  451.4 2.2 collective-permute-start.6
  453.7 0.1 slice.121
  453.8 0.0 copy-start.9
  453.8 7.9 %collective-permute-done.6 = f32[1,512]{1,0:T(1,128)S(1)} collective-permute-done((f32[1,512]{1,0:T(1,128)S(1)}, f32[1,512]{1,0:T(1,128)S(1)}, u32[]{:S(2)}, u32[]{:S(2)}) %collective-permute-start.6) | collective-permute-done | bytes 2080 | tf_op jit(solution)/shard_map/ppermute | solution.py:18
  461.7 2.5 multiply_reduce_fusion
  464.2 28.8 %psum.63 = f32[512]{0:T(512)S(1)} all-reduce(f32[512]{0:T(512)S(1)} %get-tuple-element.8), channel_id=1, replica_groups=mesh['dp'=16,'mp'=8] {'dp'}, use_global_device_ids=true, to_apply=%region_20.0 | all-reduce | flops 512 | bytes 4096 | tf_op jit(solution)/shard_map/psum | solution.py:79
  493.0 1.8 subtract_multiply_fusion
  494.9 1.9 collective-permute-start.7
  496.8 0.1 slice.123
  496.9 7.8 %collective-permute-done.7 = f32[1,512]{1,0:T(1,128)S(1)} collective-permute-done((f32[1,512]{1,0:T(1,128)S(1)}, f32[1,512]{1,0:T(1,128)S(1)}, u32[]{:S(2)}, u32[]{:S(2)}) %collective-permute-start.7) | collective-permute-done | bytes 2080 | tf_op jit(solution)/shard_map/ppermute | solution.py:18
  504.7 1.1 fusion.8
  505.8 0.0 all-gather.5.cloned.1.call-update
  509.6 64.7 %all-reduce = (f32[]{:T(128)}, f32[]{:T(128)}) all-reduce(f32[]{:T(128)S(6)} %add.78, f32[]{:T(128)S(6)} %mul.272), channel_id=1, replica_groups=mesh['dp'=16,'mp'=8] {'dp','mp'}, use_global_device_ids=true, to_apply=%region_10.0 | all-reduce | flops 2 | bytes 16 | tf_op jit(solution)/shard_map/psum | solution.py:71
  575.6 0.0 all-gather.5.cloned.1.call-done
  575.6 0.0 copy-start.1
  575.6 19.6 %convolution_bitcast_fusion = f32[3072,512]{0,1:T(8,128)} fusion(bf16[4096,512]{1,0:T(8,128)(2,1)} %all-gather.5.cloned.1.call-done, bf16[4096,3072]{1,0:T(8,128)(2,1)} %all-gather.3.cloned.1.call-done), kind=kOutput, calls=%fused_computation | convolution fusion | flops 12884901888 | bytes 35651584 | tf_op jit(solution)/shard_map/dot_general | solution.py:86
  595.3 6.6 %copy.7 = f32[3072,512]{1,0:T(8,128)} copy(f32[3072,512]{0,1:T(8,128)} %convolution_bitcast_fusion) | data formatting | bytes 12582912
  (38 shorter events, 0.1 us)
Async XLA Ops:
  7.2 160.6 %copy-start = (bf16[3072,512]{1,0:T(8,128)(2,1)S(1)}, bf16[3072,512]{1,0:T(8,128)(2,1)}, u32[]{:S(2)}) copy-start(bf16[3072,512]{1,0:T(8,128)(2,1)} %param.6) | copy-start | bytes 9437188
  7.2 160.6 %all-gather.3.cloned.1.call-start = ((), (), s32[]{:S(2)}) async-start(), calls=%async_computation.1 | async-start | bytes 26738688 | tf_op jit(solution)/shard_map/all_gather | solution.py:22
  7.9 231.5 %reduce-scatter.2.cloned.1.call-start = ((), (), s32[]{:S(2)}) async-start(), calls=%async_computation.2 | async-start | bytes 9437184 | tf_op jit(solution)/shard_map/reduce_scatter | solution.py:25
  187.7 0.7 copy-start.11
  187.7 3.3 copy-start.10
  187.7 5.3 copy-start.12
  187.7 387.9 %all-gather.5.cloned.1.call-start = ((), (), s32[]{:S(2)}) async-start(), calls=%async_computation.3 | async-start | bytes 4718592 | tf_op jit(solution)/shard_map/all_gather | solution.py:85
  188.4 4.9 collective-permute-start
  191.0 141.7 %collective-permute-start.3 = (bf16[2,512]{1,0:T(2,128)(2,1)S(1)}, bf16[2,512]{1,0:T(2,128)(2,1)S(1)}, u32[]{:S(2)}, u32[]{:S(2)}) collective-permute-start(bf16[2,512]{1,0:T(2,128)(2,1)S(1)} %slice.97), channel_id=1, source_target_pairs={{1,0},{2,1},{3,2},{4,3},{5,4},{6,5},{7,6},{9,8},{10,9},{11,10},{12... | collective-permute-start | bytes 6152 | tf_op jit(solution)/shard_map/ppermute | solution.py:18
  239.4 52.6 %copy-start.2 = (f32[512,512]{1,0:T(8,128)S(1)}, f32[512,512]{1,0:T(8,128)}, u32[]{:S(2)}) copy-start(f32[512,512]{1,0:T(8,128)} %reduce-scatter.2.cloned.1.call-done) | copy-start | bytes 3145732
  240.8 3.1 collective-permute-start.1
  280.1 11.9 %collective-permute-start.2 = (f32[1,512]{1,0:T(1,128)S(1)}, f32[1,512]{1,0:T(1,128)S(1)}, u32[]{:S(2)}, u32[]{:S(2)}) collective-permute-start(f32[1,512]{1,0:T(1,128)S(1)} %slice_multiply_fusion.1), channel_id=1, source_target_pairs={{0,1},{1,2},{2,3},{3,4},{4,5},{5,6},{6,7},{8,9},{9,10},{10,11},{11... | collective-permute-start | bytes 6152 | tf_op jit(solution)/shard_map/ppermute | solution.py:18
  321.7 11.7 %collective-permute-start.4 = (f32[1,512]{1,0:T(1,128)S(1)}, f32[1,512]{1,0:T(1,128)S(1)}, u32[]{:S(2)}, u32[]{:S(2)}) collective-permute-start(f32[1,512]{1,0:T(1,128)S(1)} %slice_multiply_fusion), channel_id=1, source_target_pairs={{0,1},{1,2},{2,3},{3,4},{4,5},{5,6},{6,7},{8,9},{9,10},{10,11},{11... | collective-permute-start | bytes 6152 | tf_op jit(solution)/shard_map/ppermute | solution.py:18
  334.7 83.2 %copy-start.3 = (bf16[514,512]{1,0:T(8,128)(2,1)S(1)}, bf16[514,512]{1,0:T(8,128)(2,1)}, u32[]{:S(2)}) copy-start(bf16[514,512]{1,0:T(8,128)(2,1)} %constant_dynamic-update-slice_fusion.1) | copy-start | bytes 1579012
  398.2 10.8 %copy-start.6 = (f32[512,512]{1,0:T(8,128)}, f32[512,512]{1,0:T(8,128)S(1)}, u32[]{:S(2)}) copy-start(f32[512,512]{1,0:T(8,128)S(1)} %subtract_multiply_fusion.2) | copy-start | bytes 3145732
  398.3 19.7 %collective-permute-start.5 = (f32[1,512]{1,0:T(1,128)S(1)}, f32[1,512]{1,0:T(1,128)S(1)}, u32[]{:S(2)}, u32[]{:S(2)}) collective-permute-start(f32[1,512]{1,0:T(1,128)S(1)} %slice.120), channel_id=1, source_target_pairs={{1,0},{2,1},{3,2},{4,3},{5,4},{6,5},{7,6},{9,8},{10,9},{11,10},{12... | collective-permute-start | bytes 6152 | tf_op jit(solution)/shard_map/ppermute | solution.py:18
  409.2 8.7 %copy-start.8 = (f32[511,512]{1,0:T(8,128)}, f32[511,512]{1,0:T(8,128)S(1)}, u32[]{:S(2)}) copy-start(f32[511,512]{1,0:T(8,128)S(1)} %slice.119) | copy-start | bytes 3139588
  451.4 2.3 copy-start.4
  451.4 53.4 %copy-start.7 = (f32[512,512]{1,0:T(8,128)S(1)}, f32[512,512]{1,0:T(8,128)}, u32[]{:S(2)}) copy-start(f32[512,512]{1,0:T(8,128)} %copy-done.6) | copy-start | bytes 3145732
  451.4 10.3 %collective-permute-start.6 = (f32[1,512]{1,0:T(1,128)S(1)}, f32[1,512]{1,0:T(1,128)S(1)}, u32[]{:S(2)}, u32[]{:S(2)}) collective-permute-start(f32[1,512]{1,0:T(1,128)S(1)} %slice.122), channel_id=1, source_target_pairs={{1,0},{2,1},{3,2},{4,3},{5,4},{6,5},{7,6},{9,8},{10,9},{11,10},{12... | collective-permute-start | bytes 6152 | tf_op jit(solution)/shard_map/ppermute | solution.py:18
  453.8 7.9 %copy-start.9 = (f32[511,512]{1,0:T(8,128)}, f32[511,512]{1,0:T(8,128)S(1)}, u32[]{:S(2)}) copy-start(f32[511,512]{1,0:T(8,128)S(1)} %slice.121) | copy-start | bytes 3139588
  453.8 50.9 %copy-start.5 = (f32[512,512]{1,0:T(8,128)S(1)}, f32[512,512]{1,0:T(8,128)}, u32[]{:S(2)}) copy-start(f32[512,512]{1,0:T(8,128)} %copy-done.4) | copy-start | bytes 3145732
  494.9 9.9 %collective-permute-start.7 = (f32[1,512]{1,0:T(1,128)S(1)}, f32[1,512]{1,0:T(1,128)S(1)}, u32[]{:S(2)}, u32[]{:S(2)}) collective-permute-start(f32[1,512]{1,0:T(1,128)S(1)} %slice.124), channel_id=1, source_target_pairs={{1,0},{2,1},{3,2},{4,3},{5,4},{6,5},{7,6},{9,8},{10,9},{11,10},{12... | collective-permute-start | bytes 6152 | tf_op jit(solution)/shard_map/ppermute | solution.py:18
  575.6 26.2 %copy-start.1 = (bf16[3072,512]{1,0:T(8,128)(2,1)S(1)}, bf16[3072,512]{1,0:T(8,128)(2,1)}, u32[]{:S(2)}) copy-start(bf16[3072,512]{1,0:T(8,128)(2,1)} %param.6) | copy-start | bytes 9437188
Sparse Core Ops, SparseCore 0:
  10.2 157.5 all-gather.2
  187.9 51.4 reduce-scatter.1
  506.0 30.3 all-gather.4
where the time goes:
time: 610 us; the launch traced here: 609 us
  blocking collectives  245 us (40%)
  waiting for transfers between devices  231 us (38%)
  starting transfers between devices  43.5 us (7%)
  matrix products  39.6 us (6%)
  other arithmetic  20.6 us (3%)
  between operations  20.3 us (3%)
  local copies, waits for them, and re-layouts  9.6 us (2%)
    all_gather x1, waiting for transfers between devices, local(): gathered = lax.all_gather(joined_rows, 'dp', axis=0, tiled=True)  160 us
    psum x3, blocking collectives, local(): squares = lax.psum(jnp.sum(mixed_rows * mixed_rows, axis=1), 'dp')  92.3 us
    psum x3, blocking collectives, local(): products = lax.psum(jnp.sum(upstream * normed, axis=1), 'dp')  87.7 us
    psum x1, blocking collectives, local(): lax.psum((err_local, count_local * lead_mask), ('dp', 'mp'))  64.7 us
    reduce_scatter x1, waiting for transfers between devices, local(): lax.psum_scatter(jnp.dot(gathered, fc_weight, preferred_element_type=jnp....  44.8 us
    ppermute x8, starting transfers between devices, shifted(): return lax.ppermute(block, axis, route)  43.4 us
    ppermute x8, waiting for transfers between devices, shifted(): return lax.ppermute(block, axis, route)  25.9 us
    dot_general x1, matrix products, local(): jnp.dot(gathered, fc_weight, preferred_element_type=jnp.float32)  19.9 us
  transfers between devices with their start and end apart: 11, of which 8 were waited for; matrix products, arithmetic and copies ran while one was open for 1% of the time, Pallas kernels for 0%

commit v1 on v0

v1 whole, which is shorter than its diff:
```python
import math

import jax
import jax.numpy as jnp
from jax import lax
from jax.experimental import pallas as pl
from jax.experimental.pallas import tpu as pltpu
from jax.sharding import PartitionSpec as P

D = 8192
STEPS = 3
EPSILON = 1e-06

PAD = 16
LANES = 640
PRODUCTS = 24
VMEM = 48 * 1024 * 1024


def along_dp(block, dy, dz):
    route = [
        (y * 4 + z, (y + dy) % 4 * 4 + (z + dz) % 4) for y in range(4) for z in range(4)
    ]
    return lax.ppermute(block, "dp", route)


def along_mp(block, dx, dcore):
    route = [(x * 2 + c, (x + dx) % 4 * 2 + (c ^ dcore)) for x in range(4) for c in range(2)]
    return lax.ppermute(block, "mp", route)


def neighbour(block, distance):
    devices = range(lax.axis_size("mp"))
    route = [(i - distance, i) for i in devices if i - distance in devices]
    return lax.ppermute(block, "mp", route)


def down(block):
    return jnp.concatenate([block[-1:], block[:-1]], axis=0)


def up(block):
    return jnp.concatenate([block[1:], block[:1]], axis=0)


def before(row):
    return jnp.concatenate([row[:, -1:], row[:, :-1]], axis=1)


def after(row):
    return jnp.concatenate([row[:, 1:], row[:, :1]], axis=1)


def product_kernel(rows, state_ref, target_ref, keep_ref, gain_ref, out_ref, columns):
    gain0, gain1, gain2 = (gain_ref[k : k + 1, :] for k in range(STEPS))
    columns[...] = jnp.zeros_like(columns)
    lane = lax.broadcasted_iota(jnp.int32, (rows, 128), 1)

    def block(index, carry):
        start = pl.multiple_of(index * rows, 8)
        window = pl.ds(start, rows + 16)
        state, target, keep = state_ref[window, :], target_ref[window, :], keep_ref[window, :]
        previous = down(state)
        mixed0 = state + keep * previous
        scaled0 = gain0 * down(mixed0)
        second = gain1 * previous
        third = gain1 * down(scaled0)
        target1 = up(target)
        target2 = gain2 * up(target1)
        weight = gain2 * gain2
        weighted, weighted2, weighted3 = weight * state, weight * second, weight * third
        pairs = [
            (mixed0, mixed0),
            (state, state),
            (state, scaled0),
            (scaled0, scaled0),
            (state, second),
            (state, third),
            (second, second),
            (second, third),
            (third, third),
            (weighted, state),
            (weighted, second),
            (weighted, third),
            (weighted2, second),
            (weighted2, third),
            (weighted3, third),
            (target2, state),
            (target2, second),
            (target2, third),
            (gain1 * target1, state),
            (gain1 * target1, scaled0),
            (gain0 * target, mixed0),
        ]
        total = jnp.zeros((rows, 128), jnp.float32)
        for k, (left, right) in enumerate(pairs):
            value = jnp.sum((left * right)[8 : rows + 8], axis=1, keepdims=True)
            total = jnp.where(lane == k, value, total)
        columns[pl.ds(pl.multiple_of(start + 8, 8), rows), :] = total
        return carry

    lax.fori_loop(0, (state_ref.shape[0] - 16) // rows, block, 0)
    out_ref[...] = columns[...].T[:PRODUCTS, :]


def products(state, target, keep, gains):
    rows = 48
    return pl.pallas_call(
        lambda *refs: product_kernel(rows, *refs),
        out_shape=jax.ShapeDtypeStruct((PRODUCTS, LANES), jnp.float32),
        in_specs=[pl.BlockSpec(memory_space=pltpu.VMEM)] * 4,
        out_specs=pl.BlockSpec(memory_space=pltpu.VMEM),
        scratch_shapes=[pltpu.VMEM((LANES, 128), jnp.float32)],
        compiler_params=pltpu.CompilerParams(vmem_limit_bytes=VMEM),
    )(state, target, keep, gains)


def coefficients(product, keep, factor):
    p = [None] + [product[k : k + 1, :] for k in range(21)]

    def scale(squares):
        return lax.rsqrt(jnp.maximum(squares, 0.0) / D + EPSILON)

    scale0 = scale(p[1])
    r0 = keep * before(scale0)
    scale1 = scale(p[2] + 2.0 * r0 * p[3] + r0 * r0 * p[4])
    a = keep * before(scale1)
    b = a * before(r0)
    scale2 = scale(
        p[2] + a * a * p[7] + b * b * p[9] + 2.0 * a * p[5] + 2.0 * b * p[6] + 2.0 * a * b * p[8]
    )
    same_next = after(keep)
    same_second = same_next * after(same_next)
    x1 = p[10] + a * p[11] + b * p[12]
    x2 = p[11] + a * p[13] + b * p[14]
    x3 = p[12] + a * p[14] + b * p[15]
    product2 = (
        factor
        * same_second
        * scale2
        * (scale2 * (x1 + a * x2 + b * x3) - (p[16] + a * p[17] + b * p[18]))
    )
    alpha2 = factor * same_second * scale2 * scale2
    gamma2 = -factor * same_second * scale2
    beta2 = -scale2 * scale2 * product2 / D
    second = alpha2 * x2 + beta2 * (p[5] + a * p[7] + b * p[8]) + gamma2 * p[17]
    third = alpha2 * x3 + beta2 * (p[6] + a * p[8] + b * p[9]) + gamma2 * p[18]
    next7, next8, next9 = after(p[7]), after(p[8]), after(p[9])
    y1 = next7 + r0 * next8
    y2 = next8 + r0 * next9
    product1 = scale1 * (
        factor * same_next * (scale1 * (y1 + r0 * y2) - (p[19] + r0 * p[20]))
        + same_next * (after(second) + r0 * after(third))
    )
    alpha1 = factor * same_next * scale1 * scale1
    gamma1 = -factor * same_next * scale1
    eta1 = scale1 * same_next
    beta1 = -scale1 * scale1 * product1 / D
    carried = alpha1 * y2 + gamma1 * p[20] + eta1 * after(third) + beta1 * (p[3] + r0 * p[4])
    product0 = scale0 * (
        factor * (scale0 * after(p[4]) - p[21]) + same_next * after(carried)
    )
    alpha0 = factor * scale0 * scale0
    gamma0 = -factor * scale0
    eta0 = scale0 * same_next
    beta0 = -scale0 * scale0 * product0 / D
    return [
        r0, a, b, scale0, scale1, scale2, same_next, same_second,
        alpha2, beta2, gamma2, alpha1, beta1, gamma1, eta1, alpha0, beta0, gamma0, eta0,
    ]


def gradient_kernel(
    rows, factor, state_ref, target_ref, keep_ref, keep_row_ref, gain_ref, product_ref,
    grad_ref, error_ref, table, columns,
):
    gain0, gain1, gain2 = (gain_ref[k : k + 1, :] for k in range(STEPS))
    table[...] = jnp.zeros_like(table)
    found = coefficients(product_ref[...], keep_row_ref[...], factor)
    for k, row in enumerate(found):
        table[k : k + 1, :] = row
    columns[...] = table[...].T

    def block(index, carry):
        start = pl.multiple_of(index * rows + PAD - 8, 8)
        window = pl.ds(start, rows + 16)
        state, target, keep = state_ref[window, :], target_ref[window, :], keep_ref[window, :]
        values = columns[window, :]
        (
            r0, a, b, scale0, scale1, scale2, same_next, same_second,
            alpha2, beta2, gamma2, alpha1, beta1, gamma1, eta1, alpha0, beta0, gamma0, eta0,
        ) = (values[:, k : k + 1] for k in range(len(found)))
        previous = down(state)
        mixed0 = state + keep * previous
        scaled0 = gain0 * down(mixed0)
        mixed1 = state + r0 * scaled0
        mixed2 = state + gain1 * (a * previous + b * down(scaled0))
        target1 = up(target)
        target2 = up(target1)
        grad2 = (alpha2 * (gain2 * gain2) + beta2) * mixed2 + gamma2 * (gain2 * target2)
        grad1 = (alpha1 * (gain1 * gain1) + beta1) * mixed1 + gain1 * (
            gamma1 * target1 + eta1 * up(grad2)
        )
        grad0 = (alpha0 * (gain0 * gain0) + beta0) * mixed0 + gain0 * (
            gamma0 * target + eta0 * up(grad1)
        )
        grad = grad0 + grad1 + grad2 + same_next * up(grad0)
        grad_ref[pl.ds(pl.multiple_of(index * rows, 16), rows), :] = grad[8 : rows + 8].astype(
            jnp.bfloat16
        )
        error0 = scale0 * gain0 * mixed0 - target
        error1 = same_next * (scale1 * gain1 * mixed1 - target1)
        error2 = same_second * (scale2 * gain2 * mixed2 - target2)
        squares = (error0 * error0 + error1 * error1 + error2 * error2)[8 : rows + 8]
        count = (1.0 + same_next + same_second)[8 : rows + 8]
        return carry[0] + jnp.sum(squares, axis=0, keepdims=True), carry[1] + jnp.sum(
            count, axis=0, keepdims=True
        )

    zero = jnp.zeros((1, state_ref.shape[1]), jnp.float32)
    squares, count = lax.fori_loop(
        0, grad_ref.shape[0] // rows, block, (zero, jnp.zeros((1, 1), jnp.float32))
    )
    error = jnp.sum(squares, axis=1, keepdims=True)
    lane = lax.broadcasted_iota(jnp.int32, (1, 128), 1)
    error_ref[...] = jnp.where(lane == 0, error, jnp.where(lane == 1, count, 0.0))


def gradients(state, target, keep, keep_row, gains, product, factor):
    rows = 64
    own = state.shape[0] - 2 * PAD
    return pl.pallas_call(
        lambda *refs: gradient_kernel(rows, factor, *refs),
        out_shape=(
            jax.ShapeDtypeStruct((own, state.shape[1]), jnp.bfloat16),
            jax.ShapeDtypeStruct((1, 128), jnp.float32),
        ),
        in_specs=[pl.BlockSpec(memory_space=pltpu.VMEM)] * 6,
        out_specs=(pl.BlockSpec(memory_space=pltpu.VMEM),) * 2,
        scratch_shapes=[
            pltpu.VMEM((128, LANES), jnp.float32),
            pltpu.VMEM((LANES, 128), jnp.float32),
        ],
        compiler_params=pltpu.CompilerParams(vmem_limit_bytes=VMEM),
    )(state, target, keep, keep_row, gains, product)


def weight_kernel(place_ref, rows_ref, *refs):
    grads, out_ref = refs[:-1], refs[-1]
    total = None
    for k, grad_ref in enumerate(grads):
        size = grad_ref.shape[0]
        rows = rows_ref[pl.ds(pl.multiple_of(place_ref[k] * size, size), size), :]
        term = lax.dot_general(
            rows, grad_ref[...], (((0,), (0,)), ((), ())), preferred_element_type=jnp.float32
        )
        total = term if total is None else total + term
    out_ref[...] = total


def weight_gradient(rows, grads, places):
    tokens, features = rows.shape
    columns = grads[0].shape[1]
    width = 512
    return pl.pallas_call(
        weight_kernel,
        out_shape=jax.ShapeDtypeStruct((features, columns), jnp.float32),
        grid_spec=pltpu.PrefetchScalarGridSpec(
            num_scalar_prefetch=1,
            grid=(features // width,),
            in_specs=[pl.BlockSpec((tokens, width), lambda i, place: (0, i))]
            + [pl.BlockSpec(g.shape, lambda i, place: (0, 0)) for g in grads],
            out_specs=pl.BlockSpec((width, columns), lambda i, place: (i, 0)),
        ),
        compiler_params=pltpu.CompilerParams(vmem_limit_bytes=VMEM),
    )(places, rows, *grads)


def local(joined_rows, fc_weight, target_features, segment_ids, step_gains):
    mp_index = lax.axis_index("mp")
    x_index, core = mp_index // 2, mp_index % 2
    own = target_features.shape[0]
    columns = target_features.shape[1]
    gathered = lax.all_gather(joined_rows, "dp", axis=0, tiled=True)
    total_rows = gathered.shape[0]

    next_target = neighbour(target_features[:PAD], -1)
    segments = jnp.concatenate(
        [
            neighbour(segment_ids[-PAD - 1 :], 1),
            segment_ids,
            neighbour(segment_ids[:PAD], -1),
        ]
    )
    token = mp_index * own - PAD + jnp.arange(own + 2 * PAD, dtype=jnp.int32)
    keep = (
        (segments[1:] == segments[:-1]) & (token > 0) & (token < total_rows)
    ).astype(jnp.float32)
    keep_row = jnp.pad(keep, (0, LANES - keep.shape[0]))[None, :]
    keep = keep[:, None]
    target = jnp.concatenate(
        [jnp.zeros((PAD, columns), jnp.bfloat16), target_features, next_target]
    ).astype(jnp.float32)

    partial = jnp.dot(gathered, fc_weight, preferred_element_type=jnp.float32)
    partial = jnp.pad(partial, ((PAD, PAD), (0, 0)))

    def windows(which):
        return jnp.stack(
            [
                lax.dynamic_slice(
                    partial, ((2 * x + which) * own, 0), (own + 2 * PAD, columns)
                )
                for x in range(4)
            ]
        )

    summed = windows(core) + along_mp(windows(1 - core), 0, 1)
    state = lax.dynamic_index_in_dim(summed, x_index, 0, keepdims=False)
    for k in (1, 3, 2):
        block = lax.dynamic_index_in_dim(summed, (x_index + k) % 4, 0, keepdims=False)
        state = state + along_mp(block.astype(jnp.bfloat16), k, 0).astype(jnp.float32)

    product = products(state, target, keep, step_gains)
    product = product + sum(along_dp(product, 0, k) for k in (1, 2, 3))
    product = product + sum(along_dp(product, k, 0) for k in (1, 2, 3))
    factor = 1.0 / math.sqrt(total_rows)
    grad, error = gradients(state, target, keep, keep_row, step_gains, product, factor)

    sums = lax.all_gather(error, ("dp", "mp"), axis=0, tiled=True)
    grads = [grad] + [along_mp(grad, k, 0) for k in (1, 3, 2)]
    grads = grads + [along_mp(g, 0, 1) for g in grads]
    places = jnp.stack(
        [(x_index - k) % 4 * 2 + c for c in (core, 1 - core) for k in (0, 1, 3, 2)]
    ).astype(jnp.int32)
    grad_weight = weight_gradient(gathered, grads, places)
    error_total = jnp.sum(sums[:, 0])
    count_total = jnp.sum(sums[:, 1]) / lax.axis_size("dp")
    mean_loss = error_total / (2.0 * D * count_total)
    return (mean_loss, grad_weight)


def solution(mesh):
    in_specs = (P("dp", "mp"), P("mp", "dp"), P("mp", "dp"), P("mp"), P(None, "dp"))
    out_specs = (P(), P("mp", "dp"))
    return jax.shard_map(local, mesh=mesh, in_specs=in_specs, out_specs=out_specs, check_vma=False)
```

time: 610 us -> 350 us (0.57)
  blocking collectives: 245 us -> 30.3 us
  waiting for transfers between devices: 231 us -> 194 us
  Pallas kernels: 0 us -> 27.3 us
  matrix products: 39.6 us -> 16.4 us
  other arithmetic: 20.6 us -> 7.86 us
    psum x7 -> x0, blocking collectives: 245 us -> none  [the longest x3 92.3 us: local(): squares = lax.psum(jnp.sum(mixed_rows * mixed_rows, axis=1), 'dp')]
    reduce_scatter x1 -> x0, waiting for transfers between devices: 44.8 us -> none  [local(): lax.psum_scatter(jnp.dot(gathered, fc_weight, preferred_element_type=jnp....]
    all_gather x0 -> x1, blocking collectives: none -> 30.3 us  [local(): sums = lax.all_gather(error, ('dp', 'mp'), axis=0, tiled=True)]
    pallas_call x0 -> x3, Pallas kernels: none -> 27.3 us  [the longest x1 19 us: weight_gradient(): pl.pallas_call(weight_kernel, out_shape=jax.ShapeDtypeStruct((features, c...]
    dot_general x2 -> x1, matrix products: 39.6 us -> 16.4 us  [local(): partial = jnp.dot(gathered, fc_weight, preferred_element_type=jnp.float32)]
    reduce_sum x7 -> x1, other arithmetic: 10.9 us -> 0.69 us  [local(): count_total = jnp.sum(sums[:, 1]) / lax.axis_size('dp')]
    mul x9 -> x0, other arithmetic: 8.49 us -> none  [the longest x3 5.41 us: local(): grad_mixed = scale_rows * (upstream - normed * (products / D)[:, None])]
    ppermute x8 -> x20, waiting for transfers between devices: 25.9 us -> 33.6 us  [the longest x11 28.4 us: along_mp(): return lax.ppermute(block, 'mp', route)]
  transfers between devices with their start and end apart: 11 -> 21, of which waited for: 8 -> 10; matrix products, arithmetic and copies ran while one was open for 1% -> 2% of each run, Pallas kernels for 0% -> 0%
where the time goes in v1:
time: 350 us; the launch traced here: 349 us
  waiting for transfers between devices  194 us (55%)
  starting transfers between devices  42 us (12%)
  blocking collectives  30.3 us (9%)
  Pallas kernels  27.3 us (8%)
  between operations  16.7 us (5%)
  matrix products  16.4 us (5%)
  local copies, waits for them, and re-layouts  14.1 us (4%)
  other arithmetic  7.86 us (2%)
    all_gather x1, waiting for transfers between devices, local(): gathered = lax.all_gather(joined_rows, 'dp', axis=0, tiled=True)  160 us
    all_gather x1, blocking collectives, local(): sums = lax.all_gather(error, ('dp', 'mp'), axis=0, tiled=True)  30.3 us
    ppermute x11, waiting for transfers between devices, along_mp(): return lax.ppermute(block, 'mp', route)  28.4 us
    ppermute x11, starting transfers between devices, along_mp(): return lax.ppermute(block, 'mp', route)  27.2 us
    pallas_call x1, Pallas kernels, weight_gradient(): pl.pallas_call(weight_kernel, out_shape=jax.ShapeDtypeStruct((features, c...  19 us
    dot_general x1, matrix products, local(): partial = jnp.dot(gathered, fc_weight, preferred_element_type=jnp.float32)  16.4 us
    unnamed x34, local copies, waits for them, and re-layouts  11.1 us
    ppermute x6, starting transfers between devices, along_dp(): return lax.ppermute(block, 'dp', route)  7.98 us
  transfers between devices with their start and end apart: 21, of which 10 were waited for; matrix products, arithmetic and copies ran while one was open for 2% of the time, Pallas kernels for 0%

profile of v1, /device:TPU:1, one launch (start us, length us, event | category | flops | bytes accessed | tf_op | source)
XLA Modules:
  0.0 348.8 jit_solution(6173783215646977717)
XLA Ops:
  7.2 0.0 copy-start
  7.2 0.0 all-gather.3.cloned.1.call-start
  7.2 0.7 all-gather.3.cloned.1.call-update
  7.9 159.8 %all-gather.3.cloned.1.call-done.rows_ref = bf16[4096,3072]{1,0:T(8,128)(2,1)} async-done(((bf16[256,3072]{1,0:T(8,128)(2,1)}), bf16[4096,3072]{1,0:T(8,128)(2,1)}) %all-gather.3.cloned.1.call-update) | async-done | bytes 25165840 | tf_op jit(solution)/shard_map/all_gather | solution.py:284
  167.8 16.4 %fusion.18 = f32[4096,512]{1,0:T(8,128)S(1)} fusion(bf16[4096,3072]{1,0:T(8,128)(2,1)} %all-gather.3.cloned.1.call-done.rows_ref, bf16[3072,512]{1,0:T(8,128)(2,1)S(1)} %copy-done), kind=kOutput, calls=%fused_computation.40 | convolution fusion | flops 12884901888 | bytes 36700160 | tf_op jit(solution)/shard_map/dot_general | solution.py:305
  184.2 2.5 fusion
  186.7 2.6 pad_maximum_fusion
  189.3 0.7 collective-permute-start
  190.0 0.1 slice.22
  190.0 3.0 collective-permute-start.5
  193.0 1.9 collective-permute-start.6
  195.0 1.9 collective-permute-start.4
  197.0 0.5 collective-permute-done
  197.5 4.0 %maximum_add_fusion = f32[4,544,512]{2,1,0:T(8,128)S(1)} fusion(f32[4,544,512]{2,1,0:T(8,128)} %collective-permute-done, f32[1,544,512]{2,1,0:T(8,128)} %get-tuple-element.11, f32[1,544,512]{2,1,0:T(8,128)} %get-tuple-element.10, f32[1,544,512]{2,1,0:T(8,128)S(1)} %get-tuple-element.9, f32[1,544,512]{2,1,0:T(8,128)S(1)} %get-tuple-element.8), kind=kLoop, calls=%fused_computation.8 | loop fusion | flops 4456448 | bytes 13369344 | tf_op jit(solution)/shard_map/add | solution.py:318
  201.4 0.2 fusion.10
  201.7 0.0 copy-start.14
  201.7 1.5 collective-permute-start.1
  203.2 1.3 collective-permute-start.2
  204.5 0.0 collective-permute-done.6
  204.5 1.7 collective-permute-start.3
  206.2 0.1 pad_add_fusion
  206.2 0.1 fusion.17
  206.3 0.1 broadcast_in_dim.12.refs_2_
  206.4 0.0 collective-permute-done.4
  206.5 0.1 maximum_convert_fusion.refs_1_
  206.6 10.2 %collective-permute-done.1 = bf16[544,512]{1,0:T(8,128)(2,1)S(1)} collective-permute-done((bf16[544,512]{1,0:T(8,128)(2,1)S(1)}, bf16[544,512]{1,0:T(8,128)(2,1)S(1)}, u32[]{:S(2)}, u32[]{:S(2)}) %collective-permute-start.1) | collective-permute-done | bytes 557088 | tf_op jit(solution)/shard_map/ppermute | solution.py:29
  216.8 0.1 collective-permute-done.2
  216.9 13.2 %collective-permute-done.3 = bf16[544,512]{1,0:T(8,128)(2,1)S(1)} collective-permute-done((bf16[544,512]{1,0:T(8,128)(2,1)S(1)}, bf16[544,512]{1,0:T(8,128)(2,1)S(1)}, u32[]{:S(2)}, u32[]{:S(2)}) %collective-permute-start.3) | collective-permute-done | bytes 557088 | tf_op jit(solution)/shard_map/ppermute | solution.py:29
  230.1 0.3 fusion.9.refs_0_
  230.4 3.8 %shard_map.68 = f32[24,640]{1,0:T(8,128)S(1)} custom-call(f32[544,512]{1,0:T(8,128)S(1)} %fusion.9.refs_0_, f32[544,512]{1,0:T(8,128)S(1)} %maximum_convert_fusion.refs_1_, f32[544,1]{1,0:T(8,128)S(1)} %broadcast_in_dim.12.refs_2_, f32[3,512]{1,0:T(4,128)S(1)} %copy-done.14), custom_call_target="tpu_custom_call" | custom-call | tf_op jit(solution)/shard_map/pallas_call | solution.py:108
  234.2 1.2 collective-permute-start.7
  235.4 2.6 collective-permute-start.8
  238.0 1.1 collective-permute-start.9
  239.1 1.3 collective-permute-done.8
  240.4 1.5 collective-permute-done.9
  241.8 0.1 collective-permute-start.10
  241.9 1.9 collective-permute-start.11
  243.9 1.1 collective-permute-start.12
  245.0 1.8 collective-permute-done.10
  246.9 0.6 collective-permute-done.12
  247.4 4.5 %shard_map.69 = (bf16[512,512]{1,0:T(8,128)(2,1)S(1)}, f32[1,128]{1,0:T(1,128)S(1)}) custom-call(f32[544,512]{1,0:T(8,128)S(1)} %fusion.9.refs_0_, f32[544,512]{1,0:T(8,128)S(1)} %maximum_convert_fusion.refs_1_, f32[544,1]{1,0:T(8,128)S(1)} %broadcast_in_dim.12.refs_2_, f32[1,640]{1,0:T(1,128)S(1)} %broadcast_in_dim.11.refs_3_, f32[3,512]{1,0:T(4,128)S(1)} %copy-done.14, ...), custom_call_target="tpu_custom_call" | custom-call | tf_op jit(solution)/shard_map/pallas_call | solution.py:232
  252.0 0.6 collective-permute-start.13
  252.6 2.1 collective-permute-start.14
  254.7 4.0 %collective-permute-start.16 = (bf16[512,512]{1,0:T(8,128)(2,1)S(1)}, bf16[512,512]{1,0:T(8,128)(2,1)S(1)}, u32[]{:S(2)}, u32[]{:S(2)}) collective-permute-start(bf16[512,512]{1,0:T(8,128)(2,1)S(1)} %get-tuple-element.5.refs_0_), channel_id=1, source_target_pairs={{0,1},{1,0},{2,3},{3,2},{4,5},{5,4},{6,7},{7,6},{8,9},{9,8},{10,11... | collective-permute-start | bytes 1572872 | tf_op jit(solution)/shard_map/ppermute | solution.py:29
  258.7 0.8 copy-done.2
  259.5 4.4 %collective-permute-done.13.refs_1_ = bf16[512,512]{1,0:T(8,128)(2,1)S(1)} collective-permute-done((bf16[512,512]{1,0:T(8,128)(2,1)S(1)}, bf16[512,512]{1,0:T(8,128)(2,1)S(1)}, u32[]{:S(2)}, u32[]{:S(2)}) %collective-permute-start.13) | collective-permute-done | bytes 524320 | tf_op jit(solution)/shard_map/ppermute | solution.py:29
  263.9 14.9 %collective-permute-start.17 = (bf16[512,512]{1,0:T(8,128)(2,1)S(1)}, bf16[512,512]{1,0:T(8,128)(2,1)S(1)}, u32[]{:S(2)}, u32[]{:S(2)}) collective-permute-start(bf16[512,512]{1,0:T(8,128)(2,1)S(1)} %collective-permute-done.13.refs_1_), channel_id=1, source_target_pairs={{0,1},{1,0},{2,3},{3,2},{4,5},{5,4},{6,7},{7,6},{8,9},{9,8},{10,11... | collective-permute-start | bytes 1572872 | tf_op jit(solution)/shard_map/ppermute | solution.py:29
  278.8 0.8 copy-done.4
  279.6 0.0 collective-permute-start.18
  279.6 0.8 copy-done.6
  280.4 0.5 collective-permute-start.19
  280.9 0.8 copy-done.8
  281.7 0.1 stack.75.place_ref
  281.8 30.3 %all-gather = f32[128,1,128]{2,1,0:T(1,128)S(1)} all-gather(f32[1,1,128]{2,1,0:T(1,128)S(1)} %bitcast.40), channel_id=1, replica_groups=mesh['dp'=16,'mp'=8] {'dp','mp'}, dimensions={0}, use_global_device_ids=true | all-gather | bytes 66048 | tf_op jit(solution)/shard_map/all_gather | solution.py:330
  312.1 0.7 slice_reduce_fusion
  314.0 0.8 copy-done.10
  314.8 0.8 copy-done.12
  315.6 1.0 copy-done.3
  316.7 1.0 copy-done.5
  317.7 1.0 copy-done.7
  318.7 1.0 copy-done.9
  319.8 1.0 copy-done.11
  320.8 1.0 copy-done.13
  321.9 19.0 %shard_map.70 = f32[3072,512]{1,0:T(8,128)} custom-call(s32[8]{0:T(128)S(1)} %stack.75.place_ref, bf16[4096,3072]{1,0:T(8,128)(2,1)} %all-gather.3.cloned.1.call-done.rows_ref, bf16[512,512]{1,0:T(8,128)(2,1)S(1)} %copy-done.3, bf16[512,512]{1,0:T(8,128)(2,1)S(1)} %copy-done.5, bf16[512,512]{1,0:T(8,128)(2,1)S(1)} %copy-done.7, ...), custom_call_target="tpu_custom_call" | custom-call | tf_op jit(solution)/shard_map/pallas_call | solution.py:265
  (38 shorter events, 0.1 us)
Async XLA Ops:
  7.2 160.6 %copy-start = (bf16[3072,512]{1,0:T(8,128)(2,1)S(1)}, bf16[3072,512]{1,0:T(8,128)(2,1)}, u32[]{:S(2)}) copy-start(bf16[3072,512]{1,0:T(8,128)(2,1)} %param.6) | copy-start | bytes 9437188
  7.2 160.6 %all-gather.3.cloned.1.call-start = ((), (), s32[]{:S(2)}) async-start(), calls=%async_computation | async-start | bytes 26738688 | tf_op jit(solution)/shard_map/all_gather | solution.py:284
  186.7 3.3 copy-start.16
  186.7 8.2 %copy-start.15 = (bf16[512,512]{1,0:T(8,128)(2,1)S(1)}, bf16[512,512]{1,0:T(8,128)(2,1)}, u32[]{:S(2)}) copy-start(bf16[512,512]{1,0:T(8,128)(2,1)} %param.7) | copy-start | bytes 1572868
  189.3 8.2 %collective-permute-start = (f32[4,544,512]{2,1,0:T(8,128)}, f32[4,544,512]{2,1,0:T(8,128)}, u32[]{:S(2)}, u32[]{:S(2)}) collective-permute-start(f32[4,544,512]{2,1,0:T(8,128)} %pad_maximum_fusion), channel_id=1, source_target_pairs={{0,1},{1,0},{2,3},{3,2},{4,5},{5,4},{6,7},{7,6},{8,9},{9,8},{10,11... | collective-permute-start | bytes 13369352 | tf_op jit(solution)/shard_map/ppermute | solution.py:29
  190.0 16.1 %collective-permute-start.5 = (s32[17]{0:T(128)S(1)}, s32[17]{0:T(128)S(1)}, u32[]{:S(2)}, u32[]{:S(2)}) collective-permute-start(s32[17]{0:T(128)S(1)} %slice.22), channel_id=1, source_target_pairs={{0,1},{1,2},{2,3},{3,4},{4,5},{5,6},{6,7},{8,9},{9,10},{10,11},{11... | collective-permute-start | bytes 212 | tf_op jit(solution)/shard_map/ppermute | solution.py:35
  193.0 11.4 %collective-permute-start.6 = (s32[16]{0:T(128)S(1)}, s32[16]{0:T(128)S(1)}, u32[]{:S(2)}, u32[]{:S(2)}) collective-permute-start(s32[16]{0:T(128)S(1)} %slice.23), channel_id=1, source_target_pairs={{1,0},{2,1},{3,2},{4,3},{5,4},{6,5},{7,6},{9,8},{10,9},{11,10},{12... | collective-permute-start | bytes 200 | tf_op jit(solution)/shard_map/ppermute | solution.py:35
  195.0 11.5 %collective-permute-start.4 = (bf16[16,512]{1,0:T(8,128)(2,1)S(1)}, bf16[16,512]{1,0:T(8,128)(2,1)S(1)}, u32[]{:S(2)}, u32[]{:S(2)}) collective-permute-start(bf16[16,512]{1,0:T(8,128)(2,1)S(1)} %slice.21), channel_id=1, source_target_pairs={{1,0},{2,1},{3,2},{4,3},{5,4},{6,5},{7,6},{9,8},{10,9},{11,10},{12... | collective-permute-start | bytes 49160 | tf_op jit(solution)/shard_map/ppermute | solution.py:35
  201.7 28.7 %copy-start.14 = (f32[3,512]{1,0:T(4,128)S(1)}, f32[3,512]{1,0:T(4,128)}, u32[]{:S(2)}) copy-start(f32[3,512]{1,0:T(4,128)} %refs_4_.1) | copy-start | bytes 18436
  201.7 15.1 %collective-permute-start.1 = (bf16[544,512]{1,0:T(8,128)(2,1)S(1)}, bf16[544,512]{1,0:T(8,128)(2,1)S(1)}, u32[]{:S(2)}, u32[]{:S(2)}) collective-permute-start(bf16[544,512]{1,0:T(8,128)(2,1)S(1)} %get-tuple-element.16), channel_id=1, source_target_pairs={{0,2},{1,3},{2,4},{3,5},{4,6},{5,7},{6,0},{7,1},{8,10},{9,11},{10,... | collective-permute-start | bytes 1671176 | tf_op jit(solution)/shard_map/ppermute | solution.py:29
  203.2 13.8 %collective-permute-start.2 = (bf16[544,512]{1,0:T(8,128)(2,1)S(1)}, bf16[544,512]{1,0:T(8,128)(2,1)S(1)}, u32[]{:S(2)}, u32[]{:S(2)}) collective-permute-start(bf16[544,512]{1,0:T(8,128)(2,1)S(1)} %get-tuple-element.18), channel_id=1, source_target_pairs={{0,6},{1,7},{2,0},{3,1},{4,2},{5,3},{6,4},{7,5},{8,14},{9,15},{10,... | collective-permute-start | bytes 1671176 | tf_op jit(solution)/shard_map/ppermute | solution.py:29
  204.5 25.6 %collective-permute-start.3 = (bf16[544,512]{1,0:T(8,128)(2,1)S(1)}, bf16[544,512]{1,0:T(8,128)(2,1)S(1)}, u32[]{:S(2)}, u32[]{:S(2)}) collective-permute-start(bf16[544,512]{1,0:T(8,128)(2,1)S(1)} %get-tuple-element.17), channel_id=1, source_target_pairs={{0,4},{1,5},{2,6},{3,7},{4,0},{5,1},{6,2},{7,3},{8,12},{9,13},{10,... | collective-permute-start | bytes 1671176 | tf_op jit(solution)/shard_map/ppermute | solution.py:29
  234.2 4.8 %collective-permute-start.7 = (f32[24,640]{1,0:T(8,128)S(1)}, f32[24,640]{1,0:T(8,128)S(1)}, u32[]{:S(2)}, u32[]{:S(2)}) collective-permute-start(f32[24,640]{1,0:T(8,128)S(1)} %shard_map.68), channel_id=1, source_target_pairs={{0,8},{8,16},{16,24},{24,0},{32,40},{40,48},{48,56},{56,32},{64,72... | collective-permute-start | bytes 184328 | tf_op jit(solution)/shard_map/ppermute | solution.py:24
  235.4 5.0 %collective-permute-start.8 = (f32[24,640]{1,0:T(8,128)S(1)}, f32[24,640]{1,0:T(8,128)S(1)}, u32[]{:S(2)}, u32[]{:S(2)}) collective-permute-start(f32[24,640]{1,0:T(8,128)S(1)} %shard_map.68), channel_id=1, source_target_pairs={{0,16},{8,24},{16,0},{24,8},{32,48},{40,56},{48,32},{56,40},{64,80... | collective-permute-start | bytes 184328 | tf_op jit(solution)/shard_map/ppermute | solution.py:24
  238.0 3.8 %collective-permute-start.9 = (f32[24,640]{1,0:T(8,128)S(1)}, f32[24,640]{1,0:T(8,128)S(1)}, u32[]{:S(2)}, u32[]{:S(2)}) collective-permute-start(f32[24,640]{1,0:T(8,128)S(1)} %shard_map.68), channel_id=1, source_target_pairs={{0,24},{8,0},{16,8},{24,16},{32,56},{40,32},{48,40},{56,48},{64,88... | collective-permute-start | bytes 184328 | tf_op jit(solution)/shard_map/ppermute | solution.py:24
  241.8 5.0 %collective-permute-start.10 = (f32[24,640]{1,0:T(8,128)S(1)}, f32[24,640]{1,0:T(8,128)S(1)}, u32[]{:S(2)}, u32[]{:S(2)}) collective-permute-start(f32[24,640]{1,0:T(8,128)S(1)} %add_add_fusion.1), channel_id=1, source_target_pairs={{0,32},{8,40},{16,48},{24,56},{32,64},{40,72},{48,80},{56,88},{64,... | collective-permute-start | bytes 184328 | tf_op jit(solution)/shard_map/ppermute | solution.py:24
  241.9 4.9 %collective-permute-start.11 = (f32[24,640]{1,0:T(8,128)S(1)}, f32[24,640]{1,0:T(8,128)S(1)}, u32[]{:S(2)}, u32[]{:S(2)}) collective-permute-start(f32[24,640]{1,0:T(8,128)S(1)} %add_add_fusion.1), channel_id=1, source_target_pairs={{0,64},{8,72},{16,80},{24,88},{32,96},{40,104},{48,112},{56,120},{... | collective-permute-start | bytes 184328 | tf_op jit(solution)/shard_map/ppermute | solution.py:24
  243.9 3.6 %collective-permute-start.12 = (f32[24,640]{1,0:T(8,128)S(1)}, f32[24,640]{1,0:T(8,128)S(1)}, u32[]{:S(2)}, u32[]{:S(2)}) collective-permute-start(f32[24,640]{1,0:T(8,128)S(1)} %add_add_fusion.1), channel_id=1, source_target_pairs={{0,96},{8,104},{16,112},{24,120},{32,0},{40,8},{48,16},{56,24},{64... | collective-permute-start | bytes 184328 | tf_op jit(solution)/shard_map/ppermute | solution.py:24
  252.0 12.0 %collective-permute-start.13 = (bf16[512,512]{1,0:T(8,128)(2,1)S(1)}, bf16[512,512]{1,0:T(8,128)(2,1)S(1)}, u32[]{:S(2)}, u32[]{:S(2)}) collective-permute-start(bf16[512,512]{1,0:T(8,128)(2,1)S(1)} %get-tuple-element.5.refs_0_), channel_id=1, source_target_pairs={{0,2},{1,3},{2,4},{3,5},{4,6},{5,7},{6,0},{7,1},{8,10},{9,11},{10,... | collective-permute-start | bytes 1572872 | tf_op jit(solution)/shard_map/ppermute | solution.py:29
  252.6 26.9 %collective-permute-start.14 = (bf16[512,512]{1,0:T(8,128)(2,1)S(1)}, bf16[512,512]{1,0:T(8,128)(2,1)S(1)}, u32[]{:S(2)}, u32[]{:S(2)}) collective-permute-start(bf16[512,512]{1,0:T(8,128)(2,1)S(1)} %get-tuple-element.5.refs_0_), channel_id=1, source_target_pairs={{0,6},{1,7},{2,0},{3,1},{4,2},{5,3},{6,4},{7,5},{8,14},{9,15},{10,... | collective-permute-start | bytes 1572872 | tf_op jit(solution)/shard_map/ppermute | solution.py:29
  254.7 25.7 %collective-permute-start.15 = (bf16[512,512]{1,0:T(8,128)(2,1)S(1)}, bf16[512,512]{1,0:T(8,128)(2,1)S(1)}, u32[]{:S(2)}, u32[]{:S(2)}) collective-permute-start(bf16[512,512]{1,0:T(8,128)(2,1)S(1)} %get-tuple-element.5.refs_0_), channel_id=1, source_target_pairs={{0,4},{1,5},{2,6},{3,7},{4,0},{5,1},{6,2},{7,3},{8,12},{9,13},{10,... | collective-permute-start | bytes 1572872 | tf_op jit(solution)/shard_map/ppermute | solution.py:29
  254.7 59.3 %collective-permute-start.16 = (bf16[512,512]{1,0:T(8,128)(2,1)S(1)}, bf16[512,512]{1,0:T(8,128)(2,1)S(1)}, u32[]{:S(2)}, u32[]{:S(2)}) collective-permute-start(bf16[512,512]{1,0:T(8,128)(2,1)S(1)} %get-tuple-element.5.refs_0_), channel_id=1, source_target_pairs={{0,1},{1,0},{2,3},{3,2},{4,5},{5,4},{6,7},{7,6},{8,9},{9,8},{10,11... | collective-permute-start | bytes 1572872 | tf_op jit(solution)/shard_map/ppermute | solution.py:29
  258.7 0.8 copy-start.2
  263.9 50.9 %collective-permute-start.17 = (bf16[512,512]{1,0:T(8,128)(2,1)S(1)}, bf16[512,512]{1,0:T(8,128)(2,1)S(1)}, u32[]{:S(2)}, u32[]{:S(2)}) collective-permute-start(bf16[512,512]{1,0:T(8,128)(2,1)S(1)} %collective-permute-done.13.refs_1_), channel_id=1, source_target_pairs={{0,1},{1,0},{2,3},{3,2},{4,5},{5,4},{6,7},{7,6},{8,9},{9,8},{10,11... | collective-permute-start | bytes 1572872 | tf_op jit(solution)/shard_map/ppermute | solution.py:29
  278.8 0.8 copy-start.4
  279.6 36.0 %collective-permute-start.18 = (bf16[512,512]{1,0:T(8,128)(2,1)S(1)}, bf16[512,512]{1,0:T(8,128)(2,1)}, u32[]{:S(2)}, u32[]{:S(2)}) collective-permute-start(bf16[512,512]{1,0:T(8,128)(2,1)S(1)} %collective-permute-done.14.refs_2_), channel_id=1, source_target_pairs={{0,1},{1,0},{2,3},{3,2},{4,5},{5,4},{6,7},{7,6},{8,9},{9,8},{10,11... | collective-permute-start | bytes 1572872 | tf_op jit(solution)/shard_map/ppermute | solution.py:29
  279.6 0.8 copy-start.6
  280.4 35.2 %collective-permute-start.19 = (bf16[512,512]{1,0:T(8,128)(2,1)S(1)}, bf16[512,512]{1,0:T(8,128)(2,1)}, u32[]{:S(2)}, u32[]{:S(2)}) collective-permute-start(bf16[512,512]{1,0:T(8,128)(2,1)S(1)} %collective-permute-done.15.refs_3_), channel_id=1, source_target_pairs={{0,1},{1,0},{2,3},{3,2},{4,5},{5,4},{6,7},{7,6},{8,9},{9,8},{10,11... | collective-permute-start | bytes 1572872 | tf_op jit(solution)/shard_map/ppermute | solution.py:29
  280.9 0.8 copy-start.8
  314.0 0.8 copy-start.10
  314.8 0.8 copy-start.12
  315.6 1.0 copy-start.3
  316.6 1.0 copy-start.5
  317.7 1.0 copy-start.7
  318.7 1.0 copy-start.9
  319.8 1.0 copy-start.11
  320.8 1.0 copy-start.13
  321.9 19.0 %copy-start.1 = (bf16[3072,512]{1,0:T(8,128)(2,1)S(1)}, bf16[3072,512]{1,0:T(8,128)(2,1)}, u32[]{:S(2)}) copy-start(bf16[3072,512]{1,0:T(8,128)(2,1)} %param.6) | copy-start | bytes 9437188
Sparse Core Ops, SparseCore 0:
  10.2 157.5 all-gather.2

commit v2 on v1

v2 whole, which is shorter than its diff:
```python
import math

import jax
import jax.numpy as jnp
from jax import lax
from jax.experimental import pallas as pl
from jax.experimental.pallas import tpu as pltpu
from jax.sharding import PartitionSpec as P

D = 8192
STEPS = 3
EPSILON = 1e-06

SHARE = 32
PAD = 8
LENGTH = SHARE + 2 * PAD
BLOCKS = 16
PRODUCTS = 24
VMEM = 40 * 1024 * 1024


def from_dp(block, place):
    route = []
    for y in range(4):
        for z in range(4):
            sy, sz = place(y, z)
            route.append((sy % 4 * 4 + sz % 4, y * 4 + z))
    return lax.ppermute(block, "dp", route)


def along_mp(block, dx, dcore):
    route = [(x * 2 + c, (x + dx) % 4 * 2 + (c ^ dcore)) for x in range(4) for c in range(2)]
    return lax.ppermute(block, "mp", route)


def neighbour(block, distance):
    devices = range(lax.axis_size("mp"))
    route = [(i - distance, i) for i in devices if i - distance in devices]
    return lax.ppermute(block, "mp", route)


def down(block):
    return jnp.concatenate([block[-1:], block[:-1]], axis=0)


def up(block):
    return jnp.concatenate([block[1:], block[:1]], axis=0)


def before(row):
    return jnp.concatenate([row[:, -1:], row[:, :-1]], axis=1)


def after(row):
    return jnp.concatenate([row[:, 1:], row[:, :1]], axis=1)


def tie(value, *others):
    return lax.optimization_barrier((value, *others))[0]


FREE = pl.CostEstimate(flops=1, bytes_accessed=1, transcendentals=0)


def windows_kernel(block_rows, target_ref, out_ref):
    for owner in range(8):
        for block in range(2):
            start = block * block_rows + owner * SHARE + PAD
            out_ref[owner, block] = target_ref[start : start + LENGTH, :]


def windows(target, block_rows):
    return pl.pallas_call(
        lambda *refs: windows_kernel(block_rows, *refs),
        out_shape=jax.ShapeDtypeStruct((8, 2, LENGTH, target.shape[1]), target.dtype),
        in_specs=[pl.BlockSpec(memory_space=pltpu.VMEM)],
        out_specs=pl.BlockSpec(memory_space=pltpu.VMEM),
        compiler_params=pltpu.CompilerParams(vmem_limit_bytes=VMEM),
        cost_estimate=FREE,
        name="windows",
    )(target)


def product_kernel(state_ref, target_ref, keep_ref, gain_ref, out_ref, columns):
    gain0, gain1, gain2 = (gain_ref[k : k + 1, :] for k in range(STEPS))
    lane = lax.broadcasted_iota(jnp.int32, (LENGTH, 128), 1)

    def block(index, carry):
        state, target, keep = state_ref[index], target_ref[index], keep_ref[index]
        previous = down(state)
        mixed0 = state + keep * previous
        scaled0 = gain0 * down(mixed0)
        second = gain1 * previous
        third = gain1 * down(scaled0)
        target1 = up(target)
        target2 = gain2 * up(target1)
        weight = gain2 * gain2
        weighted, weighted2, weighted3 = weight * state, weight * second, weight * third
        pairs = [
            (mixed0, mixed0),
            (state, state),
            (state, scaled0),
            (scaled0, scaled0),
            (state, second),
            (state, third),
            (second, second),
            (second, third),
            (third, third),
            (weighted, state),
            (weighted, second),
            (weighted, third),
            (weighted2, second),
            (weighted2, third),
            (weighted3, third),
            (target2, state),
            (target2, second),
            (target2, third),
            (gain1 * target1, state),
            (gain1 * target1, scaled0),
            (gain0 * target, mixed0),
        ]
        total = jnp.zeros((LENGTH, 128), jnp.float32)
        for k, (left, right) in enumerate(pairs):
            value = jnp.sum(left * right, axis=1, keepdims=True)
            total = jnp.where(lane == k, value, total)
        columns[pl.ds(pl.multiple_of(index * LENGTH, 8), LENGTH), :] = total
        return carry

    lax.fori_loop(0, BLOCKS, block, 0)
    out_ref[...] = columns[...].T[:PRODUCTS, :]


def products(state, target, keep, gains):
    lanes = BLOCKS * LENGTH
    return pl.pallas_call(
        product_kernel,
        out_shape=jax.ShapeDtypeStruct((PRODUCTS, lanes), jnp.float32),
        in_specs=[pl.BlockSpec(memory_space=pltpu.VMEM)] * 4,
        out_specs=pl.BlockSpec(memory_space=pltpu.VMEM),
        scratch_shapes=[pltpu.VMEM((lanes, 128), jnp.float32)],
        compiler_params=pltpu.CompilerParams(vmem_limit_bytes=VMEM),
        cost_estimate=FREE,
        name="products",
    )(state, target, keep, gains)


def coefficients(product, keep, factor):
    p = [None] + [product[k : k + 1, :] for k in range(21)]

    def scale(squares):
        return lax.rsqrt(jnp.maximum(squares, 0.0) / D + EPSILON)

    scale0 = scale(p[1])
    r0 = keep * before(scale0)
    scale1 = scale(p[2] + 2.0 * r0 * p[3] + r0 * r0 * p[4])
    a = keep * before(scale1)
    b = a * before(r0)
    scale2 = scale(
        p[2] + a * a * p[7] + b * b * p[9] + 2.0 * a * p[5] + 2.0 * b * p[6] + 2.0 * a * b * p[8]
    )
    same_next = after(keep)
    same_second = same_next * after(same_next)
    x1 = p[10] + a * p[11] + b * p[12]
    x2 = p[11] + a * p[13] + b * p[14]
    x3 = p[12] + a * p[14] + b * p[15]
    product2 = (
        factor
        * same_second
        * scale2
        * (scale2 * (x1 + a * x2 + b * x3) - (p[16] + a * p[17] + b * p[18]))
    )
    alpha2 = factor * same_second * scale2 * scale2
    gamma2 = -factor * same_second * scale2
    beta2 = -scale2 * scale2 * product2 / D
    second = alpha2 * x2 + beta2 * (p[5] + a * p[7] + b * p[8]) + gamma2 * p[17]
    third = alpha2 * x3 + beta2 * (p[6] + a * p[8] + b * p[9]) + gamma2 * p[18]
    next7, next8, next9 = after(p[7]), after(p[8]), after(p[9])
    y1 = next7 + r0 * next8
    y2 = next8 + r0 * next9
    product1 = scale1 * (
        factor * same_next * (scale1 * (y1 + r0 * y2) - (p[19] + r0 * p[20]))
        + same_next * (after(second) + r0 * after(third))
    )
    alpha1 = factor * same_next * scale1 * scale1
    gamma1 = -factor * same_next * scale1
    eta1 = scale1 * same_next
    beta1 = -scale1 * scale1 * product1 / D
    carried = alpha1 * y2 + gamma1 * p[20] + eta1 * after(third) + beta1 * (p[3] + r0 * p[4])
    product0 = scale0 * (
        factor * (scale0 * after(p[4]) - p[21]) + same_next * after(carried)
    )
    alpha0 = factor * scale0 * scale0
    gamma0 = -factor * scale0
    eta0 = scale0 * same_next
    beta0 = -scale0 * scale0 * product0 / D
    return [
        r0, a, b, scale0, scale1, scale2, same_next, same_second,
        alpha2, beta2, gamma2, alpha1, beta1, gamma1, eta1, alpha0, beta0, gamma0, eta0,
    ]


def gradient_kernel(
    factor, state_ref, target_ref, keep_ref, keep_row_ref, gain_ref, product_ref,
    grad_ref, error_ref, table, columns,
):
    gain0, gain1, gain2 = (gain_ref[k : k + 1, :] for k in range(STEPS))
    table[...] = jnp.zeros_like(table)
    found = coefficients(product_ref[...], keep_row_ref[...], factor)
    for k, row in enumerate(found):
        table[k : k + 1, :] = row
    columns[...] = table[...].T

    def block(index, carry):
        state, target, keep = state_ref[index], target_ref[index], keep_ref[index]
        values = columns[pl.ds(pl.multiple_of(index * LENGTH, 8), LENGTH), :]
        (
            r0, a, b, scale0, scale1, scale2, same_next, same_second,
            alpha2, beta2, gamma2, alpha1, beta1, gamma1, eta1, alpha0, beta0, gamma0, eta0,
        ) = (values[:, k : k + 1] for k in range(len(found)))
        previous = down(state)
        mixed0 = state + keep * previous
        scaled0 = gain0 * down(mixed0)
        mixed1 = state + r0 * scaled0
        mixed2 = state + gain1 * (a * previous + b * down(scaled0))
        target1 = up(target)
        target2 = up(target1)
        grad2 = (alpha2 * (gain2 * gain2) + beta2) * mixed2 + gamma2 * (gain2 * target2)
        grad1 = (alpha1 * (gain1 * gain1) + beta1) * mixed1 + gain1 * (
            gamma1 * target1 + eta1 * up(grad2)
        )
        grad0 = (alpha0 * (gain0 * gain0) + beta0) * mixed0 + gain0 * (
            gamma0 * target + eta0 * up(grad1)
        )
        grad = grad0 + grad1 + grad2 + same_next * up(grad0)
        grad_ref[index] = grad[PAD : PAD + SHARE].astype(jnp.bfloat16)
        error0 = scale0 * gain0 * mixed0 - target
        error1 = same_next * (scale1 * gain1 * mixed1 - target1)
        error2 = same_second * (scale2 * gain2 * mixed2 - target2)
        squares = (error0 * error0 + error1 * error1 + error2 * error2)[PAD : PAD + SHARE]
        count = (1.0 + same_next + same_second)[PAD : PAD + SHARE]
        return carry[0] + jnp.sum(squares, axis=0, keepdims=True), carry[1] + jnp.sum(
            count, axis=0, keepdims=True
        )

    zero = jnp.zeros((1, state_ref.shape[2]), jnp.float32)
    squares, count = lax.fori_loop(
        0, BLOCKS, block, (zero, jnp.zeros((1, 1), jnp.float32))
    )
    error = jnp.sum(squares, axis=1, keepdims=True)
    lane = lax.broadcasted_iota(jnp.int32, (1, 128), 1)
    error_ref[...] = jnp.where(lane == 0, error, jnp.where(lane == 1, count, 0.0))


def gradients(state, target, keep, keep_row, gains, product, factor):
    lanes = product.shape[1]
    grad = jax.ShapeDtypeStruct((BLOCKS, SHARE, state.shape[2]), jnp.bfloat16)
    return pl.pallas_call(
        lambda *refs: gradient_kernel(factor, *refs),
        out_shape=(grad, jax.ShapeDtypeStruct((1, 128), jnp.float32)),
        in_specs=[pl.BlockSpec(memory_space=pltpu.VMEM)] * 6,
        out_specs=(pl.BlockSpec(memory_space=pltpu.VMEM),) * 2,
        scratch_shapes=[
            pltpu.VMEM((128, lanes), jnp.float32),
            pltpu.VMEM((lanes, 128), jnp.float32),
        ],
        compiler_params=pltpu.CompilerParams(vmem_limit_bytes=VMEM),
        cost_estimate=FREE,
        name="gradients",
    )(state, target, keep, keep_row, gains, product)


def project_kernel(pieces, blocks, core_ref, weight_ref, *refs):
    rows, (send_ref, keep_ref, total) = refs[:pieces], refs[pieces:]
    total[...] = jnp.dot(
        jnp.concatenate([r[...] for r in rows], axis=0),
        weight_ref[...],
        preferred_element_type=jnp.float32,
    )
    core = core_ref[0]
    for x in range(4):
        for block in range(blocks):
            start = (block * 4 + x) * 2 * SHARE
            keep = pl.ds(pl.multiple_of(start + core * SHARE, SHARE), SHARE)
            send = pl.ds(pl.multiple_of(start + (1 - core) * SHARE, SHARE), SHARE)
            keep_ref[x, block] = total[keep, :]
            send_ref[x, block] = total[send, :].astype(jnp.bfloat16)


def project(rows, weight, core):
    columns = weight.shape[1]
    tokens = sum(r.shape[0] for r in rows)
    blocks = tokens // (8 * SHARE)
    shape = (4, blocks, SHARE, columns)
    return pl.pallas_call(
        lambda *refs: project_kernel(len(rows), blocks, *refs),
        out_shape=(
            jax.ShapeDtypeStruct(shape, jnp.bfloat16),
            jax.ShapeDtypeStruct(shape, jnp.float32),
        ),
        in_specs=[pl.BlockSpec(memory_space=pltpu.SMEM)]
        + [pl.BlockSpec(memory_space=pltpu.VMEM)] * (len(rows) + 1),
        out_specs=(pl.BlockSpec(memory_space=pltpu.VMEM),) * 2,
        scratch_shapes=[pltpu.VMEM((tokens, columns), jnp.float32)],
        compiler_params=pltpu.CompilerParams(vmem_limit_bytes=VMEM),
        cost_estimate=FREE,
        name="project",
    )(jnp.stack([core]).astype(jnp.int32), weight, *rows)


def assemble_kernel(groups, place_ref, owner_ref, *refs):
    states, (before_ref, after_ref, window_ref) = refs[:groups], refs[groups:]
    first = (owner_ref[0] == 0).astype(jnp.int32)
    last = (owner_ref[0] == 7).astype(jnp.int32)
    edge = jnp.zeros((PAD, window_ref.shape[2]), jnp.float32)
    window_ref[0, :PAD] = edge
    window_ref[BLOCKS - 1, PAD + SHARE :] = edge
    k = 0
    for state_ref in states:
        for i in range(state_ref.shape[0]):
            block = place_ref[k]
            window_ref[block, PAD : PAD + SHARE] = state_ref[i]

            @pl.when(block + first < BLOCKS)
            def _():
                window_ref[jnp.minimum(block + first, BLOCKS - 1), :PAD] = before_ref[k]

            @pl.when(block >= last)
            def _():
                window_ref[jnp.maximum(block - last, 0), PAD + SHARE :] = after_ref[k]

            k += 1


def assemble(states, before, after, places, owner):
    return pl.pallas_call(
        lambda *refs: assemble_kernel(len(states), *refs),
        out_shape=jax.ShapeDtypeStruct((BLOCKS, LENGTH, before.shape[2]), jnp.float32),
        in_specs=[pl.BlockSpec(memory_space=pltpu.SMEM)] * 2
        + [pl.BlockSpec(memory_space=pltpu.VMEM)] * (len(states) + 2),
        out_specs=pl.BlockSpec(memory_space=pltpu.VMEM),
        compiler_params=pltpu.CompilerParams(vmem_limit_bytes=VMEM),
        cost_estimate=FREE,
        name="assemble",
    )(places, jnp.stack([owner]).astype(jnp.int32), *states, before, after)


def weight_kernel(pieces, block_ref, owner_ref, *refs):
    rows, grads, (out_ref, ordered) = refs[:pieces], refs[pieces : pieces + 2], refs[pieces + 2 :]

    @pl.when(pl.program_id(0) == 0)
    def _():
        for k in range(BLOCKS):
            for half in range(2):
                for i in range(4):
                    start = pl.multiple_of((k * 8 + owner_ref[half * 4 + i]) * SHARE, SHARE)
                    ordered[pl.ds(start, SHARE), :] = grads[half][i, block_ref[k]]

    out_ref[...] = lax.dot_general(
        jnp.concatenate([r[...] for r in rows], axis=0),
        ordered[...],
        (((0,), (0,)), ((), ())),
        preferred_element_type=jnp.float32,
    )


def weight_gradient(rows, blocks, mine, other, owners):
    features, columns = rows[0].shape[1], mine.shape[3]
    tokens = sum(r.shape[0] for r in rows)
    width = 512
    return pl.pallas_call(
        lambda *refs: weight_kernel(len(rows), *refs),
        out_shape=jax.ShapeDtypeStruct((features, columns), jnp.float32),
        grid_spec=pltpu.PrefetchScalarGridSpec(
            num_scalar_prefetch=2,
            grid=(features // width,),
            in_specs=[pl.BlockSpec((r.shape[0], width), lambda i, *_: (0, i)) for r in rows]
            + [pl.BlockSpec(mine.shape, lambda i, *_: (0, 0, 0, 0))] * 2,
            out_specs=pl.BlockSpec((width, columns), lambda i, *_: (i, 0)),
            scratch_shapes=[pltpu.VMEM((tokens, columns), jnp.bfloat16)],
        ),
        compiler_params=pltpu.CompilerParams(vmem_limit_bytes=VMEM),
        cost_estimate=FREE,
        name="weight_gradient",
    )(blocks, jnp.stack(owners).astype(jnp.int32), *rows, mine, other)


def sum_dp(value, places):
    return value + sum(from_dp(value, place) for place in places)


AROUND_Z = tuple(lambda y, z, k=k: (y, z + k) for k in (1, 3, 2))
AROUND_Y = tuple(lambda y, z, k=k: (y + k, z) for k in (1, 3, 2))


def step(block, dy, dz):
    return from_dp(block, lambda y, z: (y + dy, z + dz))


def ring(block, distance):
    return lax.ppermute(block, "mp", [((i - distance) % 8, i) for i in range(8)])


def local(joined_rows, fc_weight, target_features, segment_ids, step_gains):
    mp_index = lax.axis_index("mp")
    x_index, core = mp_index // 2, mp_index % 2
    dp_index = lax.axis_index("dp")
    y_index, z_index = dp_index // 4, dp_index % 4
    own, columns = target_features.shape
    block_rows = joined_rows.shape[0]
    total_rows = block_rows * lax.axis_size("dp")
    factor = 1.0 / math.sqrt(total_rows)
    barrier = lax.optimization_barrier

    def chip_sum(rows):
        send, kept = project(rows, fc_weight, core)
        return kept + along_mp(send, 0, 1).astype(jnp.float32)

    def first_state(summed):
        parts = [
            lax.dynamic_index_in_dim(summed, (x_index + k) % 4, 0, keepdims=False)
            for k in (0, 1, 3, 2)
        ]
        return parts[0] + sum(
            along_mp(part.astype(jnp.bfloat16), k, 0).astype(jnp.float32)
            for part, k in zip(parts[1:], (1, 3, 2))
        )

    own_block = joined_rows
    round1 = (
        step(own_block, 0, -1), step(own_block, 0, 1),
        step(own_block, -1, 0), step(own_block, 1, 0),
    )
    next_target = neighbour(target_features[: 2 * PAD], -1)
    next_segments = neighbour(segment_ids[: 2 * PAD], -1)
    last_segments = neighbour(segment_ids[-2 * PAD - 1 :], 1)
    round1, next_target, next_segments, last_segments = barrier(
        (round1, next_target, next_segments, last_segments)
    )
    b0m, b01, bm0, b10 = round1
    round2 = (step(b0m, -1, 0), step(bm0, 0, 1), step(b01, 1, 0), step(b10, 0, -1))

    segments = jnp.concatenate([last_segments, segment_ids, next_segments])
    token = mp_index * own - 2 * PAD + jnp.arange(own + 4 * PAD, dtype=jnp.int32)
    keep = (segments[1:] == segments[:-1]) & (token > 0) & (token < total_rows)
    target = jnp.concatenate(
        [jnp.zeros((2 * PAD, columns), jnp.bfloat16), target_features, next_target]
    )
    target = jnp.concatenate(
        [target, jnp.broadcast_to(keep.astype(jnp.bfloat16)[:, None], (target.shape[0], 128))],
        axis=1,
    )
    shares = lax.all_to_all(windows(target, block_rows), "mp", 0, 0, tiled=True)
    round2, shares = barrier((round2, shares))
    shares = shares.reshape(BLOCKS, LENGTH, columns + 128)
    target = shares[..., :columns].astype(jnp.float32)
    keep = shares[..., columns : columns + 1].astype(jnp.float32)
    keep_row = keep.reshape(1, BLOCKS * LENGTH)

    bmm, bm1, b11, b1m = round2
    round3 = (step(b0m, 0, -1), step(bm0, -1, 0), step(b11, 1, 0), step(b11, 0, 1))
    early = chip_sum([own_block, *round1, *round2])
    round3, early = barrier((round3, early))
    early = first_state(early)
    b02, b20, b21, b12 = round3
    half = block_rows // 2
    round4 = (
        step(bmm, 0, -1), step(bmm, -1, 0), step(b21[:half], 0, 1), step(b12[half:], 1, 0),
    )
    middle = chip_sum(round3)
    round4, early, middle = barrier((round4, early, middle))
    late = first_state(jnp.concatenate([middle, chip_sum(round4)], axis=1))

    names = [
        (0, 0), (0, -1), (0, 1), (-1, 0), (1, 0), (-1, -1), (-1, 1), (1, 1), (1, -1),
        (0, 2), (2, 0), (2, 1), (1, 2), (-1, 2), (2, -1), (2, 2),
    ]
    places = jnp.stack([(y_index + dy) % 4 * 4 + (z_index + dz) % 4 for dy, dz in names])
    places = places.astype(jnp.int32)
    states = [early, late]
    before = ring(jnp.concatenate([s[:, SHARE - PAD :] for s in states]), 1)
    after = ring(jnp.concatenate([s[:, :PAD] for s in states]), -1)
    window = assemble(states, before, after, places, mp_index)

    product = products(window, target, keep, step_gains)
    product = sum_dp(product, AROUND_Z)
    product = sum_dp(product, AROUND_Y)
    grad, error = gradients(window, target, keep, keep_row, step_gains, product, factor)

    arrived = [along_mp(grad, k, 0) for k in (1, 3, 2)]
    error = tie(error, arrived[0])
    error = sum_dp(sum_dp(error, AROUND_Z), AROUND_Y)
    error = error + sum(along_mp(error, k, 0) for k in (1, 3, 2))
    mine = tie(jnp.stack([grad] + arrived), error)
    other = along_mp(mine, 0, 1)
    owners = [(x_index - k) % 4 * 2 + c for c in (core, 1 - core) for k in (0, 1, 3, 2)]
    grad_weight = weight_gradient(
        [own_block, *round1, *round2, *round3, *round4], places, mine, other, owners
    )

    error = error + along_mp(error, 0, 1)
    mean_loss = error[0, 0] / (2.0 * D * (error[0, 1] / lax.axis_size("dp")))
    return (mean_loss, grad_weight)


def solution(mesh):
    in_specs = (P("dp", "mp"), P("mp", "dp"), P("mp", "dp"), P("mp"), P(None, "dp"))
    out_specs = (P(), P("mp", "dp"))
    return jax.shard_map(local, mesh=mesh, in_specs=in_specs, out_specs=out_specs, check_vma=False)
```

time: 350 us -> 295 us (0.84)
  waiting for transfers between devices: 194 us -> 106 us
  starting transfers between devices: 42 us -> 96.2 us
  Pallas kernels: 27.3 us -> 58.5 us
  blocking collectives: 30.3 us -> 0 us
  matrix products: 16.4 us -> 0 us
  between operations: 16.7 us -> 3.4 us
  other arithmetic: 7.86 us -> 19.4 us
    all_gather x1 -> x0, waiting for transfers between devices: 160 us -> none  [local(): gathered = lax.all_gather(joined_rows, 'dp', axis=0, tiled=True)]
    ppermute x6 -> x30, waiting for transfers between devices: 5.16 us -> 75 us  [the longest x28 70.2 us: from_dp(): return lax.ppermute(block, 'dp', route)]
    pallas_call x3 -> x8, Pallas kernels: 27.3 us -> 58.5 us  [the longest x3 27.4 us: project(): pl.pallas_call(lambda *refs: project_kernel(len(rows), blocks, *refs), ou...]
    all_gather x1 -> x0, blocking collectives: 30.3 us -> none  [local(): sums = lax.all_gather(error, ('dp', 'mp'), axis=0, tiled=True)]
    ppermute x6 -> x30, starting transfers between devices: 7.98 us -> 38.2 us  [the longest x28 36.5 us: from_dp(): return lax.ppermute(block, 'dp', route)]
    dot_general x1 -> x0, matrix products: 16.4 us -> none  [local(): partial = jnp.dot(gathered, fc_weight, preferred_element_type=jnp.float32)]
    ppermute x11 -> x17, starting transfers between devices: 27.2 us -> 43.3 us  [along_mp(): return lax.ppermute(block, 'mp', route)]
    unnamed x34 -> x24, local copies, waits for them, and re-layouts: 11.1 us -> 1.86 us
  transfers between devices with their start and end apart: 21 -> 51, of which waited for: 10 -> 28; matrix products, arithmetic and copies ran while one was open for 2% -> 9% of each run, Pallas kernels for 0% -> 7%
where the time goes in v2:
time: 295 us
  waiting for transfers between devices  106 us (36%)
  starting transfers between devices  96.2 us (33%)
  Pallas kernels  58.5 us (20%)
  other arithmetic  19.4 us (7%)
  local copies, waits for them, and re-layouts  11.5 us (4%)
  between operations  3.4 us (1%)
    ppermute x28, waiting for transfers between devices, from_dp(): return lax.ppermute(block, 'dp', route)  70.2 us
    ppermute x17, starting transfers between devices, along_mp(): return lax.ppermute(block, 'mp', route)  43.3 us
    ppermute x28, starting transfers between devices, from_dp(): return lax.ppermute(block, 'dp', route)  36.5 us
    pallas_call x3, Pallas kernels, project(): pl.pallas_call(lambda *refs: project_kernel(len(rows), blocks, *refs), ou...  27.4 us
    ppermute x17, waiting for transfers between devices, along_mp(): return lax.ppermute(block, 'mp', route)  24.9 us
    pallas_call x1, Pallas kernels, weight_gradient(): pl.pallas_call(lambda *refs: weight_kernel(len(rows), *refs), out_shape=j...  19.9 us
    all_to_all x1, starting transfers between devices, local(): shares = lax.all_to_all(windows(target, block_rows), 'mp', 0, 0, tiled=True)  7.58 us
    add x3, other arithmetic, chip_sum(): return kept + along_mp(send, 0, 1).astype(jnp.float32)  7.54 us
  transfers between devices with their start and end apart: 51, of which 28 were waited for; matrix products, arithmetic and copies ran while one was open for 9% of the time, Pallas kernels for 7%

profile of v2, /device:TPU:1, one launch (start us, length us, event | category | flops | bytes accessed | tf_op | source)
XLA Modules:
  0.0 294.6 jit_solution(7870601167193895172)
XLA Ops:
  0.6 3.6 %collective-permute-start.3 = (bf16[256,3072]{1,0:T(8,128)(2,1)}, bf16[256,3072]{1,0:T(8,128)(2,1)S(1)}, u32[]{:S(2)}, u32[]{:S(2)}) collective-permute-start(bf16[256,3072]{1,0:T(8,128)(2,1)} %refs_2_.3), channel_id=1, source_target_pairs={{32,0},{40,8},{48,16},{56,24},{64,32},{72,40},{80,48},{88,56},{96,... | collective-permute-start | bytes 4718600 | tf_op jit(solution)/shard_map/ppermute | solution.py:28
  4.3 3.8 %collective-permute-start.1 = (bf16[256,3072]{1,0:T(8,128)(2,1)}, bf16[256,3072]{1,0:T(8,128)(2,1)}, u32[]{:S(2)}, u32[]{:S(2)}) collective-permute-start(bf16[256,3072]{1,0:T(8,128)(2,1)} %refs_2_.3), channel_id=1, source_target_pairs={{8,0},{16,8},{24,16},{0,24},{40,32},{48,40},{56,48},{32,56},{72,64... | collective-permute-start | bytes 4718600 | tf_op jit(solution)/shard_map/ppermute | solution.py:28
  8.7 3.1 %collective-permute-start.5 = (s32[16]{0:T(128)S(1)}, s32[16]{0:T(128)S(1)}, u32[]{:S(2)}, u32[]{:S(2)}) collective-permute-start(s32[16]{0:T(128)S(1)} %slice.46), channel_id=1, source_target_pairs={{1,0},{2,1},{3,2},{4,3},{5,4},{6,5},{7,6},{9,8},{10,9},{11,10},{12... | collective-permute-start | bytes 200 | tf_op jit(solution)/shard_map/ppermute | solution.py:39
  12.6 1.9 collective-permute-done.5
  14.6 1.9 collective-permute-start.6
  17.6 2.1 collective-permute-start.4
  19.7 3.5 %collective-permute-done.4 = bf16[16,512]{1,0:T(8,128)(2,1)S(1)} collective-permute-done((bf16[16,512]{1,0:T(8,128)(2,1)S(1)}, bf16[16,512]{1,0:T(8,128)(2,1)S(1)}, u32[]{:S(2)}, u32[]{:S(2)}) %collective-permute-start.4) | collective-permute-done | bytes 16416 | tf_op jit(solution)/shard_map/ppermute | solution.py:39
  23.1 14.5 %collective-permute-done.3.refs_6_ = bf16[256,3072]{1,0:T(8,128)(2,1)S(1)} collective-permute-done((bf16[256,3072]{1,0:T(8,128)(2,1)}, bf16[256,3072]{1,0:T(8,128)(2,1)S(1)}, u32[]{:S(2)}, u32[]{:S(2)}) %collective-permute-start.3) | collective-permute-done | bytes 1572896 | tf_op jit(solution)/shard_map/ppermute | solution.py:28
  37.6 3.1 %collective-permute-done.2.refs_5_ = bf16[256,3072]{1,0:T(8,128)(2,1)} collective-permute-done((bf16[256,3072]{1,0:T(8,128)(2,1)}, bf16[256,3072]{1,0:T(8,128)(2,1)}, u32[]{:S(2)}, u32[]{:S(2)}) %collective-permute-start.2) | collective-permute-done | bytes 1572896 | tf_op jit(solution)/shard_map/ppermute | solution.py:28
  41.1 3.1 %collective-permute-done.refs_3_ = bf16[256,3072]{1,0:T(8,128)(2,1)} collective-permute-done((bf16[256,3072]{1,0:T(8,128)(2,1)}, bf16[256,3072]{1,0:T(8,128)(2,1)}, u32[]{:S(2)}, u32[]{:S(2)}) %collective-permute-start) | collective-permute-done | bytes 1572896 | tf_op jit(solution)/shard_map/ppermute | solution.py:28
  44.2 2.4 collective-permute-start.9
  46.6 2.7 collective-permute-start.8
  50.3 1.1 pad_maximum_fusion.1.refs_0_
  52.4 7.6 %all-to-all-start = ((bf16[8,2,48,640]{3,2,1,0:T(8,128)(2,1)}), bf16[8,2,48,640]{3,2,1,0:T(8,128)(2,1)}, u32[]{:S(2)}, u32[]{:S(2)}) async-start(bf16[8,2,48,640]{3,2,1,0:T(8,128)(2,1)} %copy-done.5), calls=%async_computation | async-start | bytes 1966080 | tf_op jit(solution)/shard_map/all_to_all | solution.py:452
  60.0 18.2 %collective-permute-done.9.refs_9_ = bf16[256,3072]{1,0:T(8,128)(2,1)} collective-permute-done((bf16[256,3072]{1,0:T(8,128)(2,1)}, bf16[256,3072]{1,0:T(8,128)(2,1)}, u32[]{:S(2)}, u32[]{:S(2)}) %collective-permute-start.9) | collective-permute-done | bytes 1572896 | tf_op jit(solution)/shard_map/ppermute | solution.py:28
  78.2 2.8 collective-permute-done.10.refs_10_
  81.3 2.4 collective-permute-start.16
  83.7 2.4 collective-permute-start.15
  86.1 14.5 %project.3 = (bf16[4,9,32,512]{3,2,1,0:T(8,128)(2,1)}, f32[4,9,32,512]{3,2,1,0:T(8,128)}) custom-call(s32[1]{0:T(128)} %bitcast.17.refs_0_, bf16[3072,512]{1,0:T(8,128)(2,1)} %refs_1_.5, bf16[256,3072]{1,0:T(8,128)(2,1)S(1)} %copy-done.1, bf16[256,3072]{1,0:T(8,128)(2,1)} %collective-permute-done.refs_3_, bf16[256,3072]{1,0:T(8,128)(2,1)} %collective-permute-done.1.refs_4_, ...), custom_call_target="tpu_custom_call" | custom-call | flops 1 | bytes 1 | tf_op jit(solution)/shard_map/project/pallas_call | solution.py:294
  100.6 5.3 %collective-permute-start.17 = (bf16[4,9,32,512]{3,2,1,0:T(8,128)(2,1)}, bf16[4,9,32,512]{3,2,1,0:T(8,128)(2,1)}, u32[]{:S(2)}, u32[]{:S(2)}) collective-permute-start(bf16[4,9,32,512]{3,2,1,0:T(8,128)(2,1)} %get-tuple-element.47), channel_id=1, source_target_pairs={{0,1},{1,0},{2,3},{3,2},{4,5},{5,4},{6,7},{7,6},{8,9},{9,8},{10,11... | collective-permute-start | bytes 3538952 | tf_op jit(solution)/shard_map/ppermute | solution.py:33
  105.9 8.9 %collective-permute-done.13.refs_2_.refs_11_ = bf16[256,3072]{1,0:T(8,128)(2,1)} collective-permute-done((bf16[256,3072]{1,0:T(8,128)(2,1)}, bf16[256,3072]{1,0:T(8,128)(2,1)}, u32[]{:S(2)}, u32[]{:S(2)}) %collective-permute-start.13) | collective-permute-done | bytes 1572896 | tf_op jit(solution)/shard_map/ppermute | solution.py:28
  114.8 4.1 %convert_add_fusion = f32[4,9,32,512]{3,2,1,0:T(8,128)} fusion(f32[4,9,32,512]{3,2,1,0:T(8,128)} %get-tuple-element.46, bf16[4,9,32,512]{3,2,1,0:T(8,128)(2,1)} %collective-permute-done.17), kind=kLoop, calls=%fused_computation.8 | loop fusion | flops 1179648 | bytes 5898240 | tf_op jit(solution)/shard_map/add | solution.py:416
  118.9 1.6 fusion.9
  120.5 1.3 collective-permute-start.20
  121.7 2.5 collective-permute-start.22
  124.2 1.2 collective-permute-start.21
  125.4 7.1 %project.4 = (bf16[4,4,32,512]{3,2,1,0:T(8,128)(2,1)}, f32[4,4,32,512]{3,2,1,0:T(8,128)S(1)}) custom-call(s32[1]{0:T(128)} %bitcast.17.refs_0_, bf16[3072,512]{1,0:T(8,128)(2,1)S(1)} %copy-done, bf16[256,3072]{1,0:T(8,128)(2,1)} %collective-permute-done.13.refs_2_.refs_11_, bf16[256,3072]{1,0:T(8,128)(2,1)} %collective-permute-done.14.refs_3_.refs_12_, ...), custom_call_target="tpu_custom_call" | custom-call | flops 1 | bytes 1 | tf_op jit(solution)/shard_map/project/pallas_call | solution.py:294
  132.5 4.5 %collective-permute-start.23 = (bf16[4,4,32,512]{3,2,1,0:T(8,128)(2,1)}, bf16[4,4,32,512]{3,2,1,0:T(8,128)(2,1)}, u32[]{:S(2)}, u32[]{:S(2)}) collective-permute-start(bf16[4,4,32,512]{3,2,1,0:T(8,128)(2,1)} %get-tuple-element.54), channel_id=1, source_target_pairs={{0,1},{1,0},{2,3},{3,2},{4,5},{5,4},{6,7},{7,6},{8,9},{9,8},{10,11... | collective-permute-start | bytes 1572872 | tf_op jit(solution)/shard_map/ppermute | solution.py:33
  137.0 2.1 slice.50
  139.0 2.1 slice.51
  141.2 2.9 collective-permute-start.19
  144.1 2.9 %collective-permute-start.18 = (bf16[128,3072]{1,0:T(8,128)(2,1)}, bf16[128,3072]{1,0:T(8,128)(2,1)}, u32[]{:S(2)}, u32[]{:S(2)}) collective-permute-start(bf16[128,3072]{1,0:T(8,128)(2,1)} %slice.50), channel_id=1, source_target_pairs={{8,0},{16,8},{24,16},{0,24},{40,32},{48,40},{56,48},{32,56},{72,64... | collective-permute-start | bytes 2359304 | tf_op jit(solution)/shard_map/ppermute | solution.py:28
  147.1 2.3 bitcast_add_fusion.refs_2_
  149.4 2.2 convert_add_fusion.1
  151.7 9.3 %collective-permute-done.19.refs_5_.refs_18_ = bf16[128,3072]{1,0:T(8,128)(2,1)} collective-permute-done((bf16[128,3072]{1,0:T(8,128)(2,1)}, bf16[128,3072]{1,0:T(8,128)(2,1)}, u32[]{:S(2)}, u32[]{:S(2)}) %collective-permute-start.19) | collective-permute-done | bytes 786464 | tf_op jit(solution)/shard_map/ppermute | solution.py:28
  161.0 2.6 collective-permute-done.18.refs_4_.refs_17_
  163.6 5.8 %project.5 = (bf16[4,3,32,512]{3,2,1,0:T(8,128)(2,1)}, f32[4,3,32,512]{3,2,1,0:T(8,128)S(1)}) custom-call(s32[1]{0:T(128)} %bitcast.17.refs_0_, bf16[3072,512]{1,0:T(8,128)(2,1)S(1)} %copy-done, bf16[256,3072]{1,0:T(8,128)(2,1)} %collective-permute-done.11.refs_2_.refs_15_, bf16[256,3072]{1,0:T(8,128)(2,1)} %collective-permute-done.12.refs_3_.refs_16_, ...), custom_call_target="tpu_custom_call" | custom-call | flops 1 | bytes 1 | tf_op jit(solution)/shard_map/project/pallas_call | solution.py:294
  170.3 1.5 collective-permute-start.24
  173.4 1.2 convert_add_fusion.2
  175.1 2.4 collective-permute-start.26
  177.5 10.2 %collective-permute-done.25 = bf16[7,32,512]{2,1,0:T(8,128)(2,1)S(1)} collective-permute-done((bf16[7,32,512]{2,1,0:T(8,128)(2,1)S(1)}, bf16[7,32,512]{2,1,0:T(8,128)(2,1)S(1)}, u32[]{:S(2)}, u32[]{:S(2)}) %collective-permute-start.25) | collective-permute-done | bytes 229408 | tf_op jit(solution)/shard_map/ppermute | solution.py:33
  187.9 1.7 collective-permute-start.28
  189.7 1.3 slice_convert_fusion.target_ref.refs_1_
  191.0 1.9 collective-permute-done.28.refs_4_
  192.9 2.8 collective-permute-done.29.refs_5_
  196.6 5.2 %products.1 = f32[24,768]{1,0:T(8,128)S(1)} custom-call(f32[16,48,512]{2,1,0:T(8,128)S(1)} %assemble.1.state_ref.refs_0_, f32[16,48,512]{2,1,0:T(8,128)S(1)} %slice_convert_fusion.target_ref.refs_1_, f32[16,48,1]{2,1,0:T(8,128)S(1)} %slice_convert_fusion.1.keep_ref.refs_2_, f32[3,512]{1,0:T(4,128)S(1)} %copy-done.10), custom_call_target="tpu_custom_call" | custom-call | flops 1 | bytes 1 | tf_op jit(solution)/shard_map/products/pallas_call | solution.py:135
  201.8 2.0 collective-permute-start.32
  203.8 2.1 collective-permute-start.31
  206.6 1.7 collective-permute-done.31
  208.2 1.3 collective-permute-done.30
  210.9 2.0 collective-permute-start.33
  212.9 1.7 fusion.15
  216.7 5.1 %gradients.1 = (bf16[16,32,512]{2,1,0:T(8,128)(2,1)S(1)}, f32[1,128]{1,0:T(1,128)S(1)}) custom-call(f32[16,48,512]{2,1,0:T(8,128)S(1)} %assemble.1.state_ref.refs_0_, f32[16,48,512]{2,1,0:T(8,128)S(1)} %slice_convert_fusion.target_ref.refs_1_, f32[16,48,1]{2,1,0:T(8,128)S(1)} %slice_convert_fusion.1.keep_ref.refs_2_, f32[1,768]{1,0:T(1,128)S(1)} %reshape.21.refs_3_, ...), custom_call_target="tpu_custom_call" | custom-call | flops 1 | bytes 1 | tf_op jit(solution)/shard_map/gradients/pallas_call | solution.py:257
  221.8 6.1 %collective-permute-start.48 = (bf16[16,32,512]{2,1,0:T(8,128)(2,1)S(1)}, bf16[16,32,512]{2,1,0:T(8,128)(2,1)S(1)}, u32[]{:S(2)}, u32[]{:S(2)}) collective-permute-start(bf16[16,32,512]{2,1,0:T(8,128)(2,1)S(1)} %get-tuple-element.65), channel_id=1, source_target_pairs={{0,4},{1,5},{2,6},{3,7},{4,0},{5,1},{6,2},{7,3},{8,12},{9,13},{10,... | collective-permute-start | bytes 1572872 | tf_op jit(solution)/shard_map/ppermute | solution.py:33
  227.9 10.3 %collective-permute-done.36 = bf16[16,32,512]{2,1,0:T(8,128)(2,1)S(1)} collective-permute-done((bf16[16,32,512]{2,1,0:T(8,128)(2,1)S(1)}, bf16[16,32,512]{2,1,0:T(8,128)(2,1)S(1)}, u32[]{:S(2)}, u32[]{:S(2)}) %collective-permute-start.36) | collective-permute-done | bytes 524320 | tf_op jit(solution)/shard_map/ppermute | solution.py:33
  238.8 2.1 collective-permute-start.38
  243.7 2.7 collective-permute-start.40
  246.4 1.4 collective-permute-done.42
  247.8 10.3 %collective-permute-start.45 = (f32[1,128]{1,0:T(1,128)S(1)}, f32[1,128]{1,0:T(1,128)S(1)}, u32[]{:S(2)}, u32[]{:S(2)}) collective-permute-start(f32[1,128]{1,0:T(1,128)S(1)} %add_add_fusion.3), channel_id=1, source_target_pairs={{0,4},{1,5},{2,6},{3,7},{4,0},{5,1},{6,2},{7,3},{8,12},{9,13},{10,... | collective-permute-start | bytes 1544 | tf_op jit(solution)/shard_map/ppermute | solution.py:33
  258.2 1.5 collective-permute-start.43
  259.6 1.7 pad_maximum_fusion.refs_19_
  261.8 6.3 %collective-permute-start.49 = (bf16[4,16,32,512]{3,2,1,0:T(8,128)(2,1)}, bf16[4,16,32,512]{3,2,1,0:T(8,128)(2,1)}, u32[]{:S(2)}, u32[]{:S(2)}) collective-permute-start(bf16[4,16,32,512]{3,2,1,0:T(8,128)(2,1)} %pad_maximum_fusion.refs_19_), channel_id=1, source_target_pairs={{0,1},{1,0},{2,3},{3,2},{4,5},{5,4},{6,7},{7,6},{8,9},{9,8},{10,11... | collective-permute-start | bytes 6291464 | tf_op jit(solution)/shard_map/ppermute | solution.py:33
  268.3 3.4 %collective-permute-done.46 = f32[1,128]{1,0:T(1,128)S(1)} collective-permute-done((f32[1,128]{1,0:T(1,128)S(1)}, f32[1,128]{1,0:T(1,128)S(1)}, u32[]{:S(2)}, u32[]{:S(2)}) %collective-permute-start.46) | collective-permute-done | bytes 544 | tf_op jit(solution)/shard_map/ppermute | solution.py:33
  273.6 19.9 %weight_gradient.1 = f32[3072,512]{1,0:T(8,128)} custom-call(s32[16]{0:T(128)S(1)} %stack.117.refs_0_, s32[8]{0:T(128)S(1)} %stack.128.refs_1_, bf16[256,3072]{1,0:T(8,128)(2,1)S(1)} %copy-done.2, bf16[256,3072]{1,0:T(8,128)(2,1)} %collective-permute-done.refs_3_, bf16[256,3072]{1,0:T(8,128)(2,1)} %collective-permute-done.1.refs_4_, ...), custom_call_target="tpu_custom_call" | custom-call | flops 1 | bytes 1 | tf_op jit(solution)/shard_map/weight_gradient/pallas_call | solution.py:370
  (105 shorter events, 18.0 us)
Async XLA Ops:
  0.6 37.0 %collective-permute-start.3 = (bf16[256,3072]{1,0:T(8,128)(2,1)}, bf16[256,3072]{1,0:T(8,128)(2,1)S(1)}, u32[]{:S(2)}, u32[]{:S(2)}) collective-permute-start(bf16[256,3072]{1,0:T(8,128)(2,1)} %refs_2_.3), channel_id=1, source_target_pairs={{32,0},{40,8},{48,16},{56,24},{64,32},{72,40},{80,48},{88,56},{96,... | collective-permute-start | bytes 4718600 | tf_op jit(solution)/shard_map/ppermute | solution.py:28
  4.3 36.5 %collective-permute-start.2 = (bf16[256,3072]{1,0:T(8,128)(2,1)}, bf16[256,3072]{1,0:T(8,128)(2,1)}, u32[]{:S(2)}, u32[]{:S(2)}) collective-permute-start(bf16[256,3072]{1,0:T(8,128)(2,1)} %refs_2_.3), channel_id=1, source_target_pairs={{96,0},{104,8},{112,16},{120,24},{0,32},{8,40},{16,48},{24,56},{32... | collective-permute-start | bytes 4718600 | tf_op jit(solution)/shard_map/ppermute | solution.py:28
  4.3 36.8 %collective-permute-start.1 = (bf16[256,3072]{1,0:T(8,128)(2,1)}, bf16[256,3072]{1,0:T(8,128)(2,1)}, u32[]{:S(2)}, u32[]{:S(2)}) collective-permute-start(bf16[256,3072]{1,0:T(8,128)(2,1)} %refs_2_.3), channel_id=1, source_target_pairs={{8,0},{16,8},{24,16},{0,24},{40,32},{48,40},{56,48},{32,56},{72,64... | collective-permute-start | bytes 4718600 | tf_op jit(solution)/shard_map/ppermute | solution.py:28
  8.0 36.2 %collective-permute-start = (bf16[256,3072]{1,0:T(8,128)(2,1)}, bf16[256,3072]{1,0:T(8,128)(2,1)}, u32[]{:S(2)}, u32[]{:S(2)}) collective-permute-start(bf16[256,3072]{1,0:T(8,128)(2,1)} %refs_2_.3), channel_id=1, source_target_pairs={{24,0},{0,8},{8,16},{16,24},{56,32},{32,40},{40,48},{48,56},{88,64... | collective-permute-start | bytes 4718600 | tf_op jit(solution)/shard_map/ppermute | solution.py:28
  8.7 5.8 %collective-permute-start.5 = (s32[16]{0:T(128)S(1)}, s32[16]{0:T(128)S(1)}, u32[]{:S(2)}, u32[]{:S(2)}) collective-permute-start(s32[16]{0:T(128)S(1)} %slice.46), channel_id=1, source_target_pairs={{1,0},{2,1},{3,2},{4,3},{5,4},{6,5},{7,6},{9,8},{10,9},{11,10},{12... | collective-permute-start | bytes 200 | tf_op jit(solution)/shard_map/ppermute | solution.py:39
  14.6 3.0 %collective-permute-start.6 = (s32[17]{0:T(128)S(1)}, s32[17]{0:T(128)S(1)}, u32[]{:S(2)}, u32[]{:S(2)}) collective-permute-start(s32[17]{0:T(128)S(1)} %slice.47), channel_id=1, source_target_pairs={{0,1},{1,2},{2,3},{3,4},{4,5},{5,6},{6,7},{8,9},{9,10},{10,11},{11... | collective-permute-start | bytes 212 | tf_op jit(solution)/shard_map/ppermute | solution.py:39
  17.6 5.6 %collective-permute-start.4 = (bf16[16,512]{1,0:T(8,128)(2,1)S(1)}, bf16[16,512]{1,0:T(8,128)(2,1)S(1)}, u32[]{:S(2)}, u32[]{:S(2)}) collective-permute-start(bf16[16,512]{1,0:T(8,128)(2,1)S(1)} %slice.45), channel_id=1, source_target_pairs={{1,0},{2,1},{3,2},{4,3},{5,4},{6,5},{7,6},{9,8},{10,9},{11,10},{12... | collective-permute-start | bytes 49160 | tf_op jit(solution)/shard_map/ppermute | solution.py:39
  37.6 48.4 %copy-start.3 = (bf16[256,3072]{1,0:T(8,128)(2,1)}, bf16[256,3072]{1,0:T(8,128)(2,1)S(1)}, u32[]{:S(2)}) copy-start(bf16[256,3072]{1,0:T(8,128)(2,1)S(1)} %collective-permute-done.3.refs_6_) | copy-start | bytes 4718596
  44.2 34.0 %collective-permute-start.9 = (bf16[256,3072]{1,0:T(8,128)(2,1)}, bf16[256,3072]{1,0:T(8,128)(2,1)}, u32[]{:S(2)}, u32[]{:S(2)}) collective-permute-start(bf16[256,3072]{1,0:T(8,128)(2,1)} %collective-permute-done.1.refs_4_), channel_id=1, source_target_pairs={{32,0},{40,8},{48,16},{56,24},{64,32},{72,40},{80,48},{88,56},{96,... | collective-permute-start | bytes 4718600 | tf_op jit(solution)/shard_map/ppermute | solution.py:28
  46.6 34.5 %collective-permute-start.10 = (bf16[256,3072]{1,0:T(8,128)(2,1)S(1)}, bf16[256,3072]{1,0:T(8,128)(2,1)}, u32[]{:S(2)}, u32[]{:S(2)}) collective-permute-start(bf16[256,3072]{1,0:T(8,128)(2,1)S(1)} %collective-permute-done.3.refs_6_), channel_id=1, source_target_pairs={{24,0},{0,8},{8,16},{16,24},{56,32},{32,40},{40,48},{48,56},{88,64... | collective-permute-start | bytes 4718600 | tf_op jit(solution)/shard_map/ppermute | solution.py:28
  46.6 34.7 %collective-permute-start.7 = (bf16[256,3072]{1,0:T(8,128)(2,1)}, bf16[256,3072]{1,0:T(8,128)(2,1)}, u32[]{:S(2)}, u32[]{:S(2)}) collective-permute-start(bf16[256,3072]{1,0:T(8,128)(2,1)} %collective-permute-done.refs_3_), channel_id=1, source_target_pairs={{96,0},{104,8},{112,16},{120,24},{0,32},{8,40},{16,48},{24,56},{32... | collective-permute-start | bytes 4718600 | tf_op jit(solution)/shard_map/ppermute | solution.py:28
  46.6 34.7 %collective-permute-start.8 = (bf16[256,3072]{1,0:T(8,128)(2,1)}, bf16[256,3072]{1,0:T(8,128)(2,1)}, u32[]{:S(2)}, u32[]{:S(2)}) collective-permute-start(bf16[256,3072]{1,0:T(8,128)(2,1)} %collective-permute-done.2.refs_5_), channel_id=1, source_target_pairs={{8,0},{16,8},{24,16},{0,24},{40,32},{48,40},{56,48},{32,56},{72,64... | collective-permute-start | bytes 4718600 | tf_op jit(solution)/shard_map/ppermute | solution.py:28
  51.4 34.7 %copy-start.1 = (bf16[256,3072]{1,0:T(8,128)(2,1)S(1)}, bf16[256,3072]{1,0:T(8,128)(2,1)}, u32[]{:S(2)}) copy-start(bf16[256,3072]{1,0:T(8,128)(2,1)} %refs_2_.3) | copy-start | bytes 4718596
  51.5 0.9 copy-start.5
  52.4 25.8 %all-to-all-start = ((bf16[8,2,48,640]{3,2,1,0:T(8,128)(2,1)}), bf16[8,2,48,640]{3,2,1,0:T(8,128)(2,1)}, u32[]{:S(2)}, u32[]{:S(2)}) async-start(bf16[8,2,48,640]{3,2,1,0:T(8,128)(2,1)} %copy-done.5), calls=%async_computation | async-start | bytes 1966080 | tf_op jit(solution)/shard_map/all_to_all | solution.py:452
  60.0 54.8 %collective-permute-start.13 = (bf16[256,3072]{1,0:T(8,128)(2,1)}, bf16[256,3072]{1,0:T(8,128)(2,1)}, u32[]{:S(2)}, u32[]{:S(2)}) collective-permute-start(bf16[256,3072]{1,0:T(8,128)(2,1)} %collective-permute-done.refs_3_), channel_id=1, source_target_pairs={{24,0},{0,8},{8,16},{16,24},{56,32},{32,40},{40,48},{48,56},{88,64... | collective-permute-start | bytes 4718600 | tf_op jit(solution)/shard_map/ppermute | solution.py:28
  78.2 40.7 %collective-permute-start.14 = (bf16[256,3072]{1,0:T(8,128)(2,1)}, bf16[256,3072]{1,0:T(8,128)(2,1)}, u32[]{:S(2)}, u32[]{:S(2)}) collective-permute-start(bf16[256,3072]{1,0:T(8,128)(2,1)} %collective-permute-done.2.refs_5_), channel_id=1, source_target_pairs={{96,0},{104,8},{112,16},{120,24},{0,32},{8,40},{16,48},{24,56},{32... | collective-permute-start | bytes 4718600 | tf_op jit(solution)/shard_map/ppermute | solution.py:28
  81.3 37.6 %collective-permute-start.16 = (bf16[256,3072]{1,0:T(8,128)(2,1)}, bf16[256,3072]{1,0:T(8,128)(2,1)}, u32[]{:S(2)}, u32[]{:S(2)}) collective-permute-start(bf16[256,3072]{1,0:T(8,128)(2,1)} %collective-permute-done.9.refs_9_), channel_id=1, source_target_pairs={{8,0},{16,8},{24,16},{0,24},{40,32},{48,40},{56,48},{32,56},{72,64... | collective-permute-start | bytes 4718600 | tf_op jit(solution)/shard_map/ppermute | solution.py:28
  83.7 35.2 %collective-permute-start.15 = (bf16[256,3072]{1,0:T(8,128)(2,1)}, bf16[256,3072]{1,0:T(8,128)(2,1)}, u32[]{:S(2)}, u32[]{:S(2)}) collective-permute-start(bf16[256,3072]{1,0:T(8,128)(2,1)} %collective-permute-done.9.refs_9_), channel_id=1, source_target_pairs={{32,0},{40,8},{48,16},{56,24},{64,32},{72,40},{80,48},{88,56},{96,... | collective-permute-start | bytes 4718600 | tf_op jit(solution)/shard_map/ppermute | solution.py:28
  100.6 14.2 %collective-permute-start.17 = (bf16[4,9,32,512]{3,2,1,0:T(8,128)(2,1)}, bf16[4,9,32,512]{3,2,1,0:T(8,128)(2,1)}, u32[]{:S(2)}, u32[]{:S(2)}) collective-permute-start(bf16[4,9,32,512]{3,2,1,0:T(8,128)(2,1)} %get-tuple-element.47), channel_id=1, source_target_pairs={{0,1},{1,0},{2,3},{3,2},{4,5},{5,4},{6,7},{7,6},{8,9},{9,8},{10,11... | collective-permute-start | bytes 3538952 | tf_op jit(solution)/shard_map/ppermute | solution.py:33
  114.8 36.9 %collective-permute-start.12 = (bf16[256,3072]{1,0:T(8,128)(2,1)}, bf16[256,3072]{1,0:T(8,128)(2,1)}, u32[]{:S(2)}, u32[]{:S(2)}) collective-permute-start(bf16[256,3072]{1,0:T(8,128)(2,1)} %collective-permute-done.7.refs_7_), channel_id=1, source_target_pairs={{96,0},{104,8},{112,16},{120,24},{0,32},{8,40},{16,48},{24,56},{32... | collective-permute-start | bytes 4718600 | tf_op jit(solution)/shard_map/ppermute | solution.py:28
  114.8 36.9 %collective-permute-start.11 = (bf16[256,3072]{1,0:T(8,128)(2,1)}, bf16[256,3072]{1,0:T(8,128)(2,1)}, u32[]{:S(2)}, u32[]{:S(2)}) collective-permute-start(bf16[256,3072]{1,0:T(8,128)(2,1)} %collective-permute-done.7.refs_7_), channel_id=1, source_target_pairs={{24,0},{0,8},{8,16},{16,24},{56,32},{32,40},{40,48},{48,56},{88,64... | collective-permute-start | bytes 4718600 | tf_op jit(solution)/shard_map/ppermute | solution.py:28
  114.8 10.6 %copy-start = (bf16[3072,512]{1,0:T(8,128)(2,1)S(1)}, bf16[3072,512]{1,0:T(8,128)(2,1)}, u32[]{:S(2)}) copy-start(bf16[3072,512]{1,0:T(8,128)(2,1)} %refs_1_.5) | copy-start | bytes 9437188
  120.5 12.0 %collective-permute-start.20 = (bf16[9,32,512]{2,1,0:T(8,128)(2,1)S(1)}, bf16[9,32,512]{2,1,0:T(8,128)(2,1)S(1)}, u32[]{:S(2)}, u32[]{:S(2)}) collective-permute-start(bf16[9,32,512]{2,1,0:T(8,128)(2,1)S(1)} %get-tuple-element.68), channel_id=1, source_target_pairs={{0,2},{1,3},{2,4},{3,5},{4,6},{5,7},{6,0},{7,1},{8,10},{9,11},{10,... | collective-permute-start | bytes 884744 | tf_op jit(solution)/shard_map/ppermute | solution.py:33
  121.7 19.5 %collective-permute-start.22 = (bf16[9,32,512]{2,1,0:T(8,128)(2,1)S(1)}, bf16[9,32,512]{2,1,0:T(8,128)(2,1)}, u32[]{:S(2)}, u32[]{:S(2)}) collective-permute-start(bf16[9,32,512]{2,1,0:T(8,128)(2,1)S(1)} %get-tuple-element.69), channel_id=1, source_target_pairs={{0,4},{1,5},{2,6},{3,7},{4,0},{5,1},{6,2},{7,3},{8,12},{9,13},{10,... | collective-permute-start | bytes 884744 | tf_op jit(solution)/shard_map/ppermute | solution.py:33
  124.2 19.9 %collective-permute-start.21 = (bf16[9,32,512]{2,1,0:T(8,128)(2,1)S(1)}, bf16[9,32,512]{2,1,0:T(8,128)(2,1)}, u32[]{:S(2)}, u32[]{:S(2)}) collective-permute-start(bf16[9,32,512]{2,1,0:T(8,128)(2,1)S(1)} %get-tuple-element.70), channel_id=1, source_target_pairs={{0,6},{1,7},{2,0},{3,1},{4,2},{5,3},{6,4},{7,5},{8,14},{9,15},{10,... | collective-permute-start | bytes 884744 | tf_op jit(solution)/shard_map/ppermute | solution.py:33
  132.5 8.7 %copy-start.7 = (f32[4,4,32,512]{3,2,1,0:T(8,128)}, f32[4,4,32,512]{3,2,1,0:T(8,128)S(1)}, u32[]{:S(2)}) copy-start(f32[4,4,32,512]{3,2,1,0:T(8,128)S(1)} %get-tuple-element.53) | copy-start | bytes 3145732
  132.5 16.9 %collective-permute-start.23 = (bf16[4,4,32,512]{3,2,1,0:T(8,128)(2,1)}, bf16[4,4,32,512]{3,2,1,0:T(8,128)(2,1)}, u32[]{:S(2)}, u32[]{:S(2)}) collective-permute-start(bf16[4,4,32,512]{3,2,1,0:T(8,128)(2,1)} %get-tuple-element.54), channel_id=1, source_target_pairs={{0,1},{1,0},{2,3},{3,2},{4,5},{5,4},{6,7},{7,6},{8,9},{9,8},{10,11... | collective-permute-start | bytes 1572872 | tf_op jit(solution)/shard_map/ppermute | solution.py:33
  141.2 19.8 %collective-permute-start.19 = (bf16[128,3072]{1,0:T(8,128)(2,1)}, bf16[128,3072]{1,0:T(8,128)(2,1)}, u32[]{:S(2)}, u32[]{:S(2)}) collective-permute-start(bf16[128,3072]{1,0:T(8,128)(2,1)} %slice.51), channel_id=1, source_target_pairs={{32,0},{40,8},{48,16},{56,24},{64,32},{72,40},{80,48},{88,56},{96,... | collective-permute-start | bytes 2359304 | tf_op jit(solution)/shard_map/ppermute | solution.py:28
  144.1 19.5 %collective-permute-start.18 = (bf16[128,3072]{1,0:T(8,128)(2,1)}, bf16[128,3072]{1,0:T(8,128)(2,1)}, u32[]{:S(2)}, u32[]{:S(2)}) collective-permute-start(bf16[128,3072]{1,0:T(8,128)(2,1)} %slice.50), channel_id=1, source_target_pairs={{8,0},{16,8},{24,16},{0,24},{40,32},{48,40},{56,48},{32,56},{72,64... | collective-permute-start | bytes 2359304 | tf_op jit(solution)/shard_map/ppermute | solution.py:28
  147.1 2.4 copy-start.8
  169.4 0.9 copy-start.9
  170.3 4.4 %copy-start.11 = (f32[4,4,32,512]{3,2,1,0:T(8,128)S(1)}, f32[4,4,32,512]{3,2,1,0:T(8,128)}, u32[]{:S(2)}) copy-start(f32[4,4,32,512]{3,2,1,0:T(8,128)} %convert_add_fusion.1) | copy-start | bytes 3145732
  170.3 3.1 %collective-permute-start.24 = (bf16[4,3,32,512]{3,2,1,0:T(8,128)(2,1)}, bf16[4,3,32,512]{3,2,1,0:T(8,128)(2,1)S(1)}, u32[]{:S(2)}, u32[]{:S(2)}) collective-permute-start(bf16[4,3,32,512]{3,2,1,0:T(8,128)(2,1)} %get-tuple-element.62), channel_id=1, source_target_pairs={{0,1},{1,0},{2,3},{3,2},{4,5},{5,4},{6,7},{7,6},{8,9},{9,8},{10,11... | collective-permute-start | bytes 1179656 | tf_op jit(solution)/shard_map/ppermute | solution.py:33
  174.6 2.9 copy-start.6
  174.8 13.0 %collective-permute-start.25 = (bf16[7,32,512]{2,1,0:T(8,128)(2,1)S(1)}, bf16[7,32,512]{2,1,0:T(8,128)(2,1)S(1)}, u32[]{:S(2)}, u32[]{:S(2)}) collective-permute-start(bf16[7,32,512]{2,1,0:T(8,128)(2,1)S(1)} %get-tuple-element.71), channel_id=1, source_target_pairs={{0,2},{1,3},{2,4},{3,5},{4,6},{5,7},{6,0},{7,1},{8,10},{9,11},{10,... | collective-permute-start | bytes 688136 | tf_op jit(solution)/shard_map/ppermute | solution.py:33
  175.1 12.6 %collective-permute-start.26 = (bf16[7,32,512]{2,1,0:T(8,128)(2,1)S(1)}, bf16[7,32,512]{2,1,0:T(8,128)(2,1)S(1)}, u32[]{:S(2)}, u32[]{:S(2)}) collective-permute-start(bf16[7,32,512]{2,1,0:T(8,128)(2,1)S(1)} %get-tuple-element.72), channel_id=1, source_target_pairs={{0,6},{1,7},{2,0},{3,1},{4,2},{5,3},{6,4},{7,5},{8,14},{9,15},{10,... | collective-permute-start | bytes 688136 | tf_op jit(solution)/shard_map/ppermute | solution.py:33
  177.5 10.3 %collective-permute-start.27 = (bf16[7,32,512]{2,1,0:T(8,128)(2,1)S(1)}, bf16[7,32,512]{2,1,0:T(8,128)(2,1)S(1)}, u32[]{:S(2)}, u32[]{:S(2)}) collective-permute-start(bf16[7,32,512]{2,1,0:T(8,128)(2,1)S(1)} %get-tuple-element.73), channel_id=1, source_target_pairs={{0,4},{1,5},{2,6},{3,7},{4,0},{5,1},{6,2},{7,3},{8,12},{9,13},{10,... | collective-permute-start | bytes 688136 | tf_op jit(solution)/shard_map/ppermute | solution.py:33
  187.9 5.0 %collective-permute-start.28 = (f32[16,8,512]{2,1,0:T(8,128)S(1)}, f32[16,8,512]{2,1,0:T(8,128)S(1)}, u32[]{:S(2)}, u32[]{:S(2)}) collective-permute-start(f32[16,8,512]{2,1,0:T(8,128)S(1)} %pad_maximum_fusion.2), channel_id=1, source_target_pairs={{7,0},{0,1},{1,2},{2,3},{3,4},{4,5},{5,6},{6,7},{15,8},{8,9},{9,10... | collective-permute-start | bytes 786440 | tf_op jit(solution)/shard_map/ppermute | solution.py:400
  189.6 6.1 %collective-permute-start.29 = (f32[16,8,512]{2,1,0:T(8,128)S(1)}, f32[16,8,512]{2,1,0:T(8,128)S(1)}, u32[]{:S(2)}, u32[]{:S(2)}) collective-permute-start(f32[16,8,512]{2,1,0:T(8,128)S(1)} %pad_maximum_fusion.3), channel_id=1, source_target_pairs={{1,0},{2,1},{3,2},{4,3},{5,4},{6,5},{7,6},{0,7},{9,8},{10,9},{11,1... | collective-permute-start | bytes 786440 | tf_op jit(solution)/shard_map/ppermute | solution.py:400
  195.7 0.8 copy-start.10
  201.8 4.8 %collective-permute-start.32 = (f32[24,768]{1,0:T(8,128)S(1)}, f32[24,768]{1,0:T(8,128)S(1)}, u32[]{:S(2)}, u32[]{:S(2)}) collective-permute-start(f32[24,768]{1,0:T(8,128)S(1)} %products.1), channel_id=1, source_target_pairs={{16,0},{24,8},{0,16},{8,24},{48,32},{56,40},{32,48},{40,56},{80,64... | collective-permute-start | bytes 221192 | tf_op jit(solution)/shard_map/ppermute | solution.py:28
  203.8 4.5 %collective-permute-start.31 = (f32[24,768]{1,0:T(8,128)S(1)}, f32[24,768]{1,0:T(8,128)S(1)}, u32[]{:S(2)}, u32[]{:S(2)}) collective-permute-start(f32[24,768]{1,0:T(8,128)S(1)} %products.1), channel_id=1, source_target_pairs={{24,0},{0,8},{8,16},{16,24},{56,32},{32,40},{40,48},{48,56},{88,64... | collective-permute-start | bytes 221192 | tf_op jit(solution)/shard_map/ppermute | solution.py:28
  205.8 3.7 %collective-permute-start.30 = (f32[24,768]{1,0:T(8,128)S(1)}, f32[24,768]{1,0:T(8,128)S(1)}, u32[]{:S(2)}, u32[]{:S(2)}) collective-permute-start(f32[24,768]{1,0:T(8,128)S(1)} %products.1), channel_id=1, source_target_pairs={{8,0},{16,8},{24,16},{0,24},{40,32},{48,40},{56,48},{32,56},{72,64... | collective-permute-start | bytes 221192 | tf_op jit(solution)/shard_map/ppermute | solution.py:28
  210.2 5.2 %collective-permute-start.35 = (f32[24,768]{1,0:T(8,128)}, f32[24,768]{1,0:T(8,128)}, u32[]{:S(2)}, u32[]{:S(2)}) collective-permute-start(f32[24,768]{1,0:T(8,128)} %add_add_fusion.1), channel_id=1, source_target_pairs={{64,0},{72,8},{80,16},{88,24},{96,32},{104,40},{112,48},{120,56},{... | collective-permute-start | bytes 221192 | tf_op jit(solution)/shard_map/ppermute | solution.py:28
  210.2 5.5 %collective-permute-start.34 = (f32[24,768]{1,0:T(8,128)}, f32[24,768]{1,0:T(8,128)}, u32[]{:S(2)}, u32[]{:S(2)}) collective-permute-start(f32[24,768]{1,0:T(8,128)} %add_add_fusion.1), channel_id=1, source_target_pairs={{96,0},{104,8},{112,16},{120,24},{0,32},{8,40},{16,48},{24,56},{32... | collective-permute-start | bytes 221192 | tf_op jit(solution)/shard_map/ppermute | solution.py:28
  210.9 4.9 %collective-permute-start.33 = (f32[24,768]{1,0:T(8,128)}, f32[24,768]{1,0:T(8,128)}, u32[]{:S(2)}, u32[]{:S(2)}) collective-permute-start(f32[24,768]{1,0:T(8,128)} %add_add_fusion.1), channel_id=1, source_target_pairs={{32,0},{40,8},{48,16},{56,24},{64,32},{72,40},{80,48},{88,56},{96,... | collective-permute-start | bytes 221192 | tf_op jit(solution)/shard_map/ppermute | solution.py:28
  221.8 16.4 %collective-permute-start.36 = (bf16[16,32,512]{2,1,0:T(8,128)(2,1)S(1)}, bf16[16,32,512]{2,1,0:T(8,128)(2,1)S(1)}, u32[]{:S(2)}, u32[]{:S(2)}) collective-permute-start(bf16[16,32,512]{2,1,0:T(8,128)(2,1)S(1)} %get-tuple-element.65), channel_id=1, source_target_pairs={{0,2},{1,3},{2,4},{3,5},{4,6},{5,7},{6,0},{7,1},{8,10},{9,11},{10,... | collective-permute-start | bytes 1572872 | tf_op jit(solution)/shard_map/ppermute | solution.py:33
  221.8 37.8 %collective-permute-start.48 = (bf16[16,32,512]{2,1,0:T(8,128)(2,1)S(1)}, bf16[16,32,512]{2,1,0:T(8,128)(2,1)S(1)}, u32[]{:S(2)}, u32[]{:S(2)}) collective-permute-start(bf16[16,32,512]{2,1,0:T(8,128)(2,1)S(1)} %get-tuple-element.65), channel_id=1, source_target_pairs={{0,4},{1,5},{2,6},{3,7},{4,0},{5,1},{6,2},{7,3},{8,12},{9,13},{10,... | collective-permute-start | bytes 1572872 | tf_op jit(solution)/shard_map/ppermute | solution.py:33
  227.9 31.7 %collective-permute-start.47 = (bf16[16,32,512]{2,1,0:T(8,128)(2,1)S(1)}, bf16[16,32,512]{2,1,0:T(8,128)(2,1)S(1)}, u32[]{:S(2)}, u32[]{:S(2)}) collective-permute-start(bf16[16,32,512]{2,1,0:T(8,128)(2,1)S(1)} %get-tuple-element.65), channel_id=1, source_target_pairs={{0,6},{1,7},{2,0},{3,1},{4,2},{5,3},{6,4},{7,5},{8,14},{9,15},{10,... | collective-permute-start | bytes 1572872 | tf_op jit(solution)/shard_map/ppermute | solution.py:33
  238.2 4.2 %collective-permute-start.39 = (f32[1,128]{1,0:T(1,128)S(1)}, f32[1,128]{1,0:T(1,128)S(1)}, u32[]{:S(2)}, u32[]{:S(2)}) collective-permute-start(f32[1,128]{1,0:T(1,128)S(1)} %get-tuple-element.66), channel_id=1, source_target_pairs={{16,0},{24,8},{0,16},{8,24},{48,32},{56,40},{32,48},{40,56},{80,64... | collective-permute-start | bytes 1544 | tf_op jit(solution)/shard_map/ppermute | solution.py:28
  238.8 3.9 %collective-permute-start.38 = (f32[1,128]{1,0:T(1,128)S(1)}, f32[1,128]{1,0:T(1,128)S(1)}, u32[]{:S(2)}, u32[]{:S(2)}) collective-permute-start(f32[1,128]{1,0:T(1,128)S(1)} %get-tuple-element.66), channel_id=1, source_target_pairs={{24,0},{0,8},{8,16},{16,24},{56,32},{32,40},{40,48},{48,56},{88,64... | collective-permute-start | bytes 1544 | tf_op jit(solution)/shard_map/ppermute | solution.py:28
  240.9 2.7 collective-permute-start.37
  243.6 4.2 %collective-permute-start.42 = (f32[1,128]{1,0:T(1,128)S(1)}, f32[1,128]{1,0:T(1,128)S(1)}, u32[]{:S(2)}, u32[]{:S(2)}) collective-permute-start(f32[1,128]{1,0:T(1,128)S(1)} %add_add_fusion.4), channel_id=1, source_target_pairs={{64,0},{72,8},{80,16},{88,24},{96,32},{104,40},{112,48},{120,56},{... | collective-permute-start | bytes 1544 | tf_op jit(solution)/shard_map/ppermute | solution.py:28
  243.6 4.2 %collective-permute-start.41 = (f32[1,128]{1,0:T(1,128)S(1)}, f32[1,128]{1,0:T(1,128)S(1)}, u32[]{:S(2)}, u32[]{:S(2)}) collective-permute-start(f32[1,128]{1,0:T(1,128)S(1)} %add_add_fusion.4), channel_id=1, source_target_pairs={{96,0},{104,8},{112,16},{120,24},{0,32},{8,40},{16,48},{24,56},{32... | collective-permute-start | bytes 1544 | tf_op jit(solution)/shard_map/ppermute | solution.py:28
  243.7 4.1 %collective-permute-start.40 = (f32[1,128]{1,0:T(1,128)S(1)}, f32[1,128]{1,0:T(1,128)S(1)}, u32[]{:S(2)}, u32[]{:S(2)}) collective-permute-start(f32[1,128]{1,0:T(1,128)S(1)} %add_add_fusion.4), channel_id=1, source_target_pairs={{32,0},{40,8},{48,16},{56,24},{64,32},{72,40},{80,48},{88,56},{96,... | collective-permute-start | bytes 1544 | tf_op jit(solution)/shard_map/ppermute | solution.py:28
  247.8 13.5 %collective-permute-start.45 = (f32[1,128]{1,0:T(1,128)S(1)}, f32[1,128]{1,0:T(1,128)S(1)}, u32[]{:S(2)}, u32[]{:S(2)}) collective-permute-start(f32[1,128]{1,0:T(1,128)S(1)} %add_add_fusion.3), channel_id=1, source_target_pairs={{0,4},{1,5},{2,6},{3,7},{4,0},{5,1},{6,2},{7,3},{8,12},{9,13},{10,... | collective-permute-start | bytes 1544 | tf_op jit(solution)/shard_map/ppermute | solution.py:33
  258.2 3.1 %collective-permute-start.44 = (f32[1,128]{1,0:T(1,128)S(1)}, f32[1,128]{1,0:T(1,128)S(1)}, u32[]{:S(2)}, u32[]{:S(2)}) collective-permute-start(f32[1,128]{1,0:T(1,128)S(1)} %add_add_fusion.3), channel_id=1, source_target_pairs={{0,6},{1,7},{2,0},{3,1},{4,2},{5,3},{6,4},{7,5},{8,14},{9,15},{10,... | collective-permute-start | bytes 1544 | tf_op jit(solution)/shard_map/ppermute | solution.py:33
  258.2 3.6 %collective-permute-start.43 = (f32[1,128]{1,0:T(1,128)S(1)}, f32[1,128]{1,0:T(1,128)S(1)}, u32[]{:S(2)}, u32[]{:S(2)}) collective-permute-start(f32[1,128]{1,0:T(1,128)S(1)} %add_add_fusion.3), channel_id=1, source_target_pairs={{0,2},{1,3},{2,4},{3,5},{4,6},{5,7},{6,0},{7,1},{8,10},{9,11},{10,... | collective-permute-start | bytes 1544 | tf_op jit(solution)/shard_map/ppermute | solution.py:33
  259.6 14.0 %copy-start.2 = (bf16[256,3072]{1,0:T(8,128)(2,1)S(1)}, bf16[256,3072]{1,0:T(8,128)(2,1)}, u32[]{:S(2)}) copy-start(bf16[256,3072]{1,0:T(8,128)(2,1)} %refs_2_.3) | copy-start | bytes 4718596
  259.6 14.0 %copy-start.4 = (bf16[256,3072]{1,0:T(8,128)(2,1)S(1)}, bf16[256,3072]{1,0:T(8,128)(2,1)}, u32[]{:S(2)}) copy-start(bf16[256,3072]{1,0:T(8,128)(2,1)} %copy-done.3) | copy-start | bytes 4718596
  261.8 11.8 %collective-permute-start.49 = (bf16[4,16,32,512]{3,2,1,0:T(8,128)(2,1)}, bf16[4,16,32,512]{3,2,1,0:T(8,128)(2,1)}, u32[]{:S(2)}, u32[]{:S(2)}) collective-permute-start(bf16[4,16,32,512]{3,2,1,0:T(8,128)(2,1)} %pad_maximum_fusion.refs_19_), channel_id=1, source_target_pairs={{0,1},{1,0},{2,3},{3,2},{4,5},{5,4},{6,7},{7,6},{8,9},{9,8},{10,11... | collective-permute-start | bytes 6291464 | tf_op jit(solution)/shard_map/ppermute | solution.py:33
  268.1 3.6 %collective-permute-start.46 = (f32[1,128]{1,0:T(1,128)S(1)}, f32[1,128]{1,0:T(1,128)S(1)}, u32[]{:S(2)}, u32[]{:S(2)}) collective-permute-start(f32[1,128]{1,0:T(1,128)S(1)} %add_add_fusion.2), channel_id=1, source_target_pairs={{0,1},{1,0},{2,3},{3,2},{4,5},{5,4},{6,7},{7,6},{8,9},{9,8},{10,11... | collective-permute-start | bytes 1544 | tf_op jit(solution)/shard_map/ppermute | solution.py:33

commit v3 on v2

--- a/solution.py
+++ b/solution.py
@@ -118,6 +118,7 @@
             (gain1 * target1, state),
             (gain1 * target1, scaled0),
             (gain0 * target, mixed0),
+            (target, target),
         ]
         total = jnp.zeros((LENGTH, 128), jnp.float32)
         for k, (left, right) in enumerate(pairs):
@@ -145,7 +146,7 @@
 
 
 def coefficients(product, keep, factor):
-    p = [None] + [product[k : k + 1, :] for k in range(21)]
+    p = [None] + [product[k : k + 1, :] for k in range(22)]
 
     def scale(squares):
         return lax.rsqrt(jnp.maximum(squares, 0.0) / D + EPSILON)
@@ -193,19 +194,34 @@
     gamma0 = -factor * scale0
     eta0 = scale0 * same_next
     beta0 = -scale0 * scale0 * product0 / D
-    return [
-        r0, a, b, scale0, scale1, scale2, same_next, same_second,
+    goal0 = p[22]
+    goal1, goal2 = after(goal0), after(after(goal0))
+    squares = (
+        scale0 * (scale0 * after(p[4]) - 2.0 * p[21])
+        + goal0
+        + same_next * (scale1 * (scale1 * (y1 + r0 * y2) - 2.0 * (p[19] + r0 * p[20])) + goal1)
+        + same_second
+        * (
+            scale2 * (scale2 * (x1 + a * x2 + b * x3) - 2.0 * (p[16] + a * p[17] + b * p[18]))
+            + goal2
+        )
+    )
+    count = 1.0 + same_next + same_second
+    table = [
+        r0, a, b, same_next,
         alpha2, beta2, gamma2, alpha1, beta1, gamma1, eta1, alpha0, beta0, gamma0, eta0,
     ]
-
-
-def gradient_kernel(
-    factor, state_ref, target_ref, keep_ref, keep_row_ref, gain_ref, product_ref,
-    grad_ref, error_ref, table, columns,
-):
+    return table, squares, count
+
+
+def gradient_kernel(factor, state_ref, target_ref, keep_ref, keep_row_ref, gain_ref, *refs):
+    product_refs, (grad_ref, table, columns) = refs[:4], refs[4:]
+    product = product_refs[0][...]
+    for ref in product_refs[1:]:
+        product = product + ref[...]
     gain0, gain1, gain2 = (gain_ref[k : k + 1, :] for k in range(STEPS))
     table[...] = jnp.zeros_like(table)
-    found = coefficients(product_ref[...], keep_row_ref[...], factor)
+    found, squares, count = coefficients(product, keep_row_ref[...], factor)
     for k, row in enumerate(found):
         table[k : k + 1, :] = row
     columns[...] = table[...].T
@@ -214,7 +230,7 @@
         state, target, keep = state_ref[index], target_ref[index], keep_ref[index]
         values = columns[pl.ds(pl.multiple_of(index * LENGTH, 8), LENGTH), :]
         (
-            r0, a, b, scale0, scale1, scale2, same_next, same_second,
+            r0, a, b, same_next,
             alpha2, beta2, gamma2, alpha1, beta1, gamma1, eta1, alpha0, beta0, gamma0, eta0,
         ) = (values[:, k : k + 1] for k in range(len(found)))
         previous = down(state)
@@ -233,32 +249,32 @@
         )
         grad = grad0 + grad1 + grad2 + same_next * up(grad0)
         grad_ref[index] = grad[PAD : PAD + SHARE].astype(jnp.bfloat16)
-        error0 = scale0 * gain0 * mixed0 - target
-        error1 = same_next * (scale1 * gain1 * mixed1 - target1)
-        error2 = same_second * (scale2 * gain2 * mixed2 - target2)
-        squares = (error0 * error0 + error1 * error1 + error2 * error2)[PAD : PAD + SHARE]
-        count = (1.0 + same_next + same_second)[PAD : PAD + SHARE]
-        return carry[0] + jnp.sum(squares, axis=0, keepdims=True), carry[1] + jnp.sum(
-            count, axis=0, keepdims=True
-        )
-
-    zero = jnp.zeros((1, state_ref.shape[2]), jnp.float32)
-    squares, count = lax.fori_loop(
-        0, BLOCKS, block, (zero, jnp.zeros((1, 1), jnp.float32))
-    )
-    error = jnp.sum(squares, axis=1, keepdims=True)
-    lane = lax.broadcasted_iota(jnp.int32, (1, 128), 1)
-    error_ref[...] = jnp.where(lane == 0, error, jnp.where(lane == 1, count, 0.0))
+        return carry
+
+    lax.fori_loop(0, BLOCKS, block, 0)
+    place = lax.broadcasted_iota(jnp.int32, squares.shape, 1) % LENGTH
+    own_rows = (place >= PAD) & (place < PAD + SHARE)
+    parts = []
+    for value in (squares, count):
+        value = jnp.sum(jnp.where(own_rows, value, 0.0), axis=1, keepdims=True)
+        for _ in range(3):
+            part = value.astype(jnp.bfloat16).astype(jnp.float32)
+            parts.append(part)
+            value = value - part
+    lane = lax.broadcasted_iota(jnp.int32, grad_ref.shape[1:], 1)
+    sums = jnp.zeros(lane.shape, jnp.float32)
+    for i, part in enumerate(parts):
+        sums = jnp.where(lane == i, part, sums)
+    grad_ref[BLOCKS] = sums.astype(jnp.bfloat16)
 
 
 def gradients(state, target, keep, keep_row, gains, product, factor):
-    lanes = product.shape[1]
-    grad = jax.ShapeDtypeStruct((BLOCKS, SHARE, state.shape[2]), jnp.bfloat16)
+    lanes = product[0].shape[1]
     return pl.pallas_call(
         lambda *refs: gradient_kernel(factor, *refs),
-        out_shape=(grad, jax.ShapeDtypeStruct((1, 128), jnp.float32)),
-        in_specs=[pl.BlockSpec(memory_space=pltpu.VMEM)] * 6,
-        out_specs=(pl.BlockSpec(memory_space=pltpu.VMEM),) * 2,
+        out_shape=jax.ShapeDtypeStruct((BLOCKS + 1, SHARE, state.shape[2]), jnp.bfloat16),
+        in_specs=[pl.BlockSpec(memory_space=pltpu.VMEM)] * 9,
+        out_specs=pl.BlockSpec(memory_space=pltpu.VMEM),
         scratch_shapes=[
             pltpu.VMEM((128, lanes), jnp.float32),
             pltpu.VMEM((lanes, 128), jnp.float32),
@@ -266,7 +282,7 @@
         compiler_params=pltpu.CompilerParams(vmem_limit_bytes=VMEM),
         cost_estimate=FREE,
         name="gradients",
-    )(state, target, keep, keep_row, gains, product)
+    )(state, target, keep, keep_row, gains, *product)
 
 
 def project_kernel(pieces, blocks, core_ref, weight_ref, *refs):
@@ -345,15 +361,21 @@
 
 
 def weight_kernel(pieces, block_ref, owner_ref, *refs):
-    rows, grads, (out_ref, ordered) = refs[:pieces], refs[pieces : pieces + 2], refs[pieces + 2 :]
+    rows, grads = refs[:pieces], refs[pieces : pieces + 8]
+    out_ref, loss_ref, ordered = refs[pieces + 8 :]
 
     @pl.when(pl.program_id(0) == 0)
     def _():
-        for k in range(BLOCKS):
-            for half in range(2):
-                for i in range(4):
-                    start = pl.multiple_of((k * 8 + owner_ref[half * 4 + i]) * SHARE, SHARE)
-                    ordered[pl.ds(start, SHARE), :] = grads[half][i, block_ref[k]]
+        for i, grad_ref in enumerate(grads):
+            for k in range(BLOCKS):
+                start = pl.multiple_of((k * 8 + owner_ref[i]) * SHARE, SHARE)
+                ordered[pl.ds(start, SHARE), :] = grad_ref[block_ref[k]]
+        sums = sum(grad_ref[BLOCKS].astype(jnp.float32) for grad_ref in grads)
+        row = lax.broadcasted_iota(jnp.int32, sums.shape, 0)
+        lane = lax.broadcasted_iota(jnp.int32, sums.shape, 1)
+        error = jnp.sum(jnp.where((row == 0) & (lane < 3), sums, 0.0))
+        count = jnp.sum(jnp.where((row == 0) & (lane >= 3) & (lane < 6), sums, 0.0))
+        loss_ref[...] = jnp.full(loss_ref.shape, error / (2.0 * D * count), jnp.float32)
 
     out_ref[...] = lax.dot_general(
         jnp.concatenate([r[...] for r in rows], axis=0),
@@ -363,25 +385,31 @@
     )
 
 
-def weight_gradient(rows, blocks, mine, other, owners):
-    features, columns = rows[0].shape[1], mine.shape[3]
+def weight_gradient(rows, blocks, grads, owners):
+    features, columns = rows[0].shape[1], grads[0].shape[2]
     tokens = sum(r.shape[0] for r in rows)
     width = 512
     return pl.pallas_call(
         lambda *refs: weight_kernel(len(rows), *refs),
-        out_shape=jax.ShapeDtypeStruct((features, columns), jnp.float32),
+        out_shape=(
+            jax.ShapeDtypeStruct((features, columns), jnp.float32),
+            jax.ShapeDtypeStruct((1, 128), jnp.float32),
+        ),
         grid_spec=pltpu.PrefetchScalarGridSpec(
             num_scalar_prefetch=2,
             grid=(features // width,),
             in_specs=[pl.BlockSpec((r.shape[0], width), lambda i, *_: (0, i)) for r in rows]
-            + [pl.BlockSpec(mine.shape, lambda i, *_: (0, 0, 0, 0))] * 2,
-            out_specs=pl.BlockSpec((width, columns), lambda i, *_: (i, 0)),
+            + [pl.BlockSpec(g.shape, lambda i, *_: (0, 0, 0)) for g in grads],
+            out_specs=(
+                pl.BlockSpec((width, columns), lambda i, *_: (i, 0)),
+                pl.BlockSpec((1, 128), lambda i, *_: (0, 0)),
+            ),
             scratch_shapes=[pltpu.VMEM((tokens, columns), jnp.bfloat16)],
         ),
         compiler_params=pltpu.CompilerParams(vmem_limit_bytes=VMEM),
         cost_estimate=FREE,
         name="weight_gradient",
-    )(blocks, jnp.stack(owners).astype(jnp.int32), *rows, mine, other)
+    )(blocks, jnp.stack(owners).astype(jnp.int32), *rows, *grads)
 
 
 def sum_dp(value, places):
@@ -462,12 +490,11 @@
     round3, early = barrier((round3, early))
     early = first_state(early)
     b02, b20, b21, b12 = round3
-    half = block_rows // 2
-    round4 = (
-        step(bmm, 0, -1), step(bmm, -1, 0), step(b21[:half], 0, 1), step(b12[half:], 1, 0),
-    )
+    round4 = (step(bmm, 0, -1), step(bmm, -1, 0), step(b21, 0, 1))
     middle = chip_sum(round3)
-    round4, early, middle = barrier((round4, early, middle))
+    round4, early, middle, target, keep, keep_row = barrier(
+        (round4, early, middle, target, keep, keep_row)
+    )
     late = first_state(jnp.concatenate([middle, chip_sum(round4)], axis=1))
 
     names = [
@@ -483,22 +510,16 @@
 
     product = products(window, target, keep, step_gains)
     product = sum_dp(product, AROUND_Z)
-    product = sum_dp(product, AROUND_Y)
-    grad, error = gradients(window, target, keep, keep_row, step_gains, product, factor)
-
-    arrived = [along_mp(grad, k, 0) for k in (1, 3, 2)]
-    error = tie(error, arrived[0])
-    error = sum_dp(sum_dp(error, AROUND_Z), AROUND_Y)
-    error = error + sum(along_mp(error, k, 0) for k in (1, 3, 2))
-    mine = tie(jnp.stack([grad] + arrived), error)
-    other = along_mp(mine, 0, 1)
+    product = [product] + [from_dp(product, place) for place in AROUND_Y]
+    grad = gradients(window, target, keep, keep_row, step_gains, product, factor)
+
+    grads = [grad] + [along_mp(grad, k, 0) for k in (1, 3, 2)]
+    grads = grads + [along_mp(g, 0, 1) for g in grads]
     owners = [(x_index - k) % 4 * 2 + c for c in (core, 1 - core) for k in (0, 1, 3, 2)]
-    grad_weight = weight_gradient(
-        [own_block, *round1, *round2, *round3, *round4], places, mine, other, owners
-    )
-
-    error = error + along_mp(error, 0, 1)
-    mean_loss = error[0, 0] / (2.0 * D * (error[0, 1] / lax.axis_size("dp")))
+    grad_weight, mean_loss = weight_gradient(
+        [own_block, *round1, *round2, *round3, *round4], places, grads, owners
+    )
+    mean_loss = mean_loss[0, 0]
     return (mean_loss, grad_weight)
 
 

time: 295 us -> 261 us (0.88)
  starting transfers between devices: 96.2 us -> 84.7 us
  waiting for transfers between devices: 106 us -> 98.3 us
  other arithmetic: 19.4 us -> 12.3 us
  local copies, waits for them, and re-layouts: 11.5 us -> 6.51 us
    ppermute x28 -> x21, waiting for transfers between devices: 70.2 us -> 51 us  [from_dp(): return lax.ppermute(block, 'dp', route)]
    ppermute x17 -> x16, waiting for transfers between devices: 24.9 us -> 35.9 us  [along_mp(): return lax.ppermute(block, 'mp', route)]
    ppermute x28 -> x21, starting transfers between devices: 36.5 us -> 29.1 us  [from_dp(): return lax.ppermute(block, 'dp', route)]
    slice x3 -> x0, local copies, waits for them, and re-layouts: 4.79 us -> none  [the longest x1 2.15 us: local(): b12[half:]]
    ppermute x17 -> x16, starting transfers between devices: 43.3 us -> 38.9 us  [along_mp(): return lax.ppermute(block, 'mp', route)]
    add x3, other arithmetic: 7.54 us -> 4.05 us  [chip_sum(): return kept + along_mp(send, 0, 1).astype(jnp.float32)]
  transfers between devices with their start and end apart: 51 -> 43, of which waited for: 28 -> 29; matrix products, arithmetic and copies ran while one was open for 9% -> 7% of each run, Pallas kernels for 7% -> 8%
where the time goes in v3:
time: 261 us; the launch traced here: 260 us
  waiting for transfers between devices  98.3 us (38%)
  starting transfers between devices  84.7 us (32%)
  Pallas kernels  57 us (22%)
  other arithmetic  12.3 us (5%)
  local copies, waits for them, and re-layouts  6.51 us (2%)
    ppermute x21, waiting for transfers between devices, from_dp(): return lax.ppermute(block, 'dp', route)  51 us
    ppermute x16, starting transfers between devices, along_mp(): return lax.ppermute(block, 'mp', route)  38.9 us
    ppermute x16, waiting for transfers between devices, along_mp(): return lax.ppermute(block, 'mp', route)  35.9 us
    ppermute x21, starting transfers between devices, from_dp(): return lax.ppermute(block, 'dp', route)  29.1 us
    pallas_call x3, Pallas kernels, project(): pl.pallas_call(lambda *refs: project_kernel(len(rows), blocks, *refs), ou...  25.7 us
    pallas_call x1, Pallas kernels, weight_gradient(): pl.pallas_call(lambda *refs: weight_kernel(len(rows), *refs), out_shape=(...  19.9 us
    all_to_all x1, starting transfers between devices, local(): shares = lax.all_to_all(windows(target, block_rows), 'mp', 0, 0, tiled=True)  7.58 us
    ppermute x3, starting transfers between devices, neighbour(): return lax.ppermute(block, 'mp', route)  7.14 us
  transfers between devices with their start and end apart: 43, of which 29 were waited for; matrix products, arithmetic and copies ran while one was open for 7% of the time, Pallas kernels for 8%

profile of v3, /device:TPU:1, one launch (start us, length us, event | category | flops | bytes accessed | tf_op | source)
XLA Modules:
  0.0 260.0 jit_solution(1973990441111446297)
XLA Ops:
  0.6 3.6 %collective-permute-start.3 = (bf16[256,3072]{1,0:T(8,128)(2,1)}, bf16[256,3072]{1,0:T(8,128)(2,1)S(1)}, u32[]{:S(2)}, u32[]{:S(2)}) collective-permute-start(bf16[256,3072]{1,0:T(8,128)(2,1)} %refs_2_.3), channel_id=1, source_target_pairs={{32,0},{40,8},{48,16},{56,24},{64,32},{72,40},{80,48},{88,56},{96,... | collective-permute-start | bytes 4718600 | tf_op jit(solution)/shard_map/ppermute | solution.py:28
  4.3 3.8 %collective-permute-start.1 = (bf16[256,3072]{1,0:T(8,128)(2,1)}, bf16[256,3072]{1,0:T(8,128)(2,1)}, u32[]{:S(2)}, u32[]{:S(2)}) collective-permute-start(bf16[256,3072]{1,0:T(8,128)(2,1)} %refs_2_.3), channel_id=1, source_target_pairs={{8,0},{16,8},{24,16},{0,24},{40,32},{48,40},{56,48},{32,56},{72,64... | collective-permute-start | bytes 4718600 | tf_op jit(solution)/shard_map/ppermute | solution.py:28
  8.7 3.1 %collective-permute-start.5 = (s32[16]{0:T(128)S(1)}, s32[16]{0:T(128)S(1)}, u32[]{:S(2)}, u32[]{:S(2)}) collective-permute-start(s32[16]{0:T(128)S(1)} %slice.37), channel_id=1, source_target_pairs={{1,0},{2,1},{3,2},{4,3},{5,4},{6,5},{7,6},{9,8},{10,9},{11,10},{12... | collective-permute-start | bytes 200 | tf_op jit(solution)/shard_map/ppermute | solution.py:39
  12.6 1.9 collective-permute-done.5
  14.6 1.9 collective-permute-start.6
  17.6 2.1 collective-permute-start.4
  19.7 3.5 %collective-permute-done.4 = bf16[16,512]{1,0:T(8,128)(2,1)S(1)} collective-permute-done((bf16[16,512]{1,0:T(8,128)(2,1)S(1)}, bf16[16,512]{1,0:T(8,128)(2,1)S(1)}, u32[]{:S(2)}, u32[]{:S(2)}) %collective-permute-start.4) | collective-permute-done | bytes 16416 | tf_op jit(solution)/shard_map/ppermute | solution.py:39
  23.1 14.5 %collective-permute-done.3.refs_6_ = bf16[256,3072]{1,0:T(8,128)(2,1)S(1)} collective-permute-done((bf16[256,3072]{1,0:T(8,128)(2,1)}, bf16[256,3072]{1,0:T(8,128)(2,1)S(1)}, u32[]{:S(2)}, u32[]{:S(2)}) %collective-permute-start.3) | collective-permute-done | bytes 1572896 | tf_op jit(solution)/shard_map/ppermute | solution.py:28
  37.6 3.1 %collective-permute-done.2.refs_5_ = bf16[256,3072]{1,0:T(8,128)(2,1)} collective-permute-done((bf16[256,3072]{1,0:T(8,128)(2,1)}, bf16[256,3072]{1,0:T(8,128)(2,1)}, u32[]{:S(2)}, u32[]{:S(2)}) %collective-permute-start.2) | collective-permute-done | bytes 1572896 | tf_op jit(solution)/shard_map/ppermute | solution.py:28
  41.1 3.1 %collective-permute-done.refs_3_ = bf16[256,3072]{1,0:T(8,128)(2,1)} collective-permute-done((bf16[256,3072]{1,0:T(8,128)(2,1)}, bf16[256,3072]{1,0:T(8,128)(2,1)}, u32[]{:S(2)}, u32[]{:S(2)}) %collective-permute-start) | collective-permute-done | bytes 1572896 | tf_op jit(solution)/shard_map/ppermute | solution.py:28
  44.2 2.4 collective-permute-start.9
  46.6 2.7 %collective-permute-start.8 = (bf16[256,3072]{1,0:T(8,128)(2,1)}, bf16[256,3072]{1,0:T(8,128)(2,1)}, u32[]{:S(2)}, u32[]{:S(2)}) collective-permute-start(bf16[256,3072]{1,0:T(8,128)(2,1)} %collective-permute-done.2.refs_5_), channel_id=1, source_target_pairs={{8,0},{16,8},{24,16},{0,24},{40,32},{48,40},{56,48},{32,56},{72,64... | collective-permute-start | bytes 4718600 | tf_op jit(solution)/shard_map/ppermute | solution.py:28
  50.3 1.1 pad_maximum_fusion.refs_0_
  52.4 7.6 %all-to-all-start = ((bf16[8,2,48,640]{3,2,1,0:T(8,128)(2,1)}), bf16[8,2,48,640]{3,2,1,0:T(8,128)(2,1)}, u32[]{:S(2)}, u32[]{:S(2)}) async-start(bf16[8,2,48,640]{3,2,1,0:T(8,128)(2,1)} %copy-done.6), calls=%async_computation | async-start | bytes 1966080 | tf_op jit(solution)/shard_map/all_to_all | solution.py:480
  60.0 18.2 %collective-permute-done.9.refs_9_ = bf16[256,3072]{1,0:T(8,128)(2,1)} collective-permute-done((bf16[256,3072]{1,0:T(8,128)(2,1)}, bf16[256,3072]{1,0:T(8,128)(2,1)}, u32[]{:S(2)}, u32[]{:S(2)}) %collective-permute-start.9) | collective-permute-done | bytes 1572896 | tf_op jit(solution)/shard_map/ppermute | solution.py:28
  78.2 2.8 %collective-permute-done.10.refs_10_ = bf16[256,3072]{1,0:T(8,128)(2,1)} collective-permute-done((bf16[256,3072]{1,0:T(8,128)(2,1)S(1)}, bf16[256,3072]{1,0:T(8,128)(2,1)}, u32[]{:S(2)}, u32[]{:S(2)}) %collective-permute-start.10) | collective-permute-done | bytes 1572896 | tf_op jit(solution)/shard_map/ppermute | solution.py:28
  81.3 2.4 collective-permute-start.14
  83.7 2.4 collective-permute-start.13
  86.1 14.3 %project.3 = (bf16[4,9,32,512]{3,2,1,0:T(8,128)(2,1)S(1)}, f32[4,9,32,512]{3,2,1,0:T(8,128)}) custom-call(s32[1]{0:T(128)} %bitcast.24.refs_0_, bf16[3072,512]{1,0:T(8,128)(2,1)} %refs_1_.5, bf16[256,3072]{1,0:T(8,128)(2,1)S(1)} %copy-done.2, bf16[256,3072]{1,0:T(8,128)(2,1)} %collective-permute-done.refs_3_, ...), custom_call_target="tpu_custom_call" | custom-call | flops 1 | bytes 1 | tf_op jit(solution)/shard_map/project/pallas_call | solution.py:310
  100.3 5.3 %collective-permute-start.15 = (bf16[4,9,32,512]{3,2,1,0:T(8,128)(2,1)S(1)}, bf16[4,9,32,512]{3,2,1,0:T(8,128)(2,1)S(1)}, u32[]{:S(2)}, u32[]{:S(2)}) collective-permute-start(bf16[4,9,32,512]{3,2,1,0:T(8,128)(2,1)S(1)} %get-tuple-element.47), channel_id=1, source_target_pairs={{0,1},{1,0},{2,3},{3,2},{4,5},{5,4},{6,7},{7,6},{8,9},{9,8},{10,11... | collective-permute-start | bytes 3538952 | tf_op jit(solution)/shard_map/ppermute | solution.py:33
  105.6 2.5 collective-permute-done.15
  108.1 1.7 collective-permute-start.17
  109.8 3.8 %convert_add_fusion = f32[4,9,32,512]{3,2,1,0:T(8,128)} fusion(f32[4,9,32,512]{3,2,1,0:T(8,128)} %get-tuple-element.46, bf16[4,9,32,512]{3,2,1,0:T(8,128)(2,1)S(1)} %collective-permute-done.15), kind=kLoop, calls=%fused_computation.8 | loop fusion | flops 1179648 | bytes 5898240 | tf_op jit(solution)/shard_map/add | solution.py:444
  113.6 1.2 collective-permute-done.11.refs_2_.refs_11_
  114.8 1.3 collective-permute-done.12.refs_3_.refs_12_
  116.0 1.5 collective-permute-start.18
  117.5 2.4 fusion.9
  119.9 1.2 collective-permute-start.19
  121.1 2.5 collective-permute-start.21
  124.5 2.8 %collective-permute-done.19 = bf16[9,32,512]{2,1,0:T(8,128)(2,1)} collective-permute-done((bf16[9,32,512]{2,1,0:T(8,128)(2,1)}, bf16[9,32,512]{2,1,0:T(8,128)(2,1)}, u32[]{:S(2)}, u32[]{:S(2)}) %collective-permute-start.19) | collective-permute-done | bytes 294944 | tf_op jit(solution)/shard_map/ppermute | solution.py:33
  127.3 1.3 collective-permute-start.20
  128.6 1.1 fusion.15
  129.8 6.4 %project.4 = (bf16[4,4,32,512]{3,2,1,0:T(8,128)(2,1)S(1)}, f32[4,4,32,512]{3,2,1,0:T(8,128)S(1)}) custom-call(s32[1]{0:T(128)} %bitcast.24.refs_0_, bf16[3072,512]{1,0:T(8,128)(2,1)S(1)} %copy-done, bf16[256,3072]{1,0:T(8,128)(2,1)} %collective-permute-done.11.refs_2_.refs_11_, bf16[256,3072]{1,0:T(8,128)(2,1)} %collective-permute-done.12.refs_3_.refs_12_, ...), custom_call_target="tpu_custom_call" | custom-call | flops 1 | bytes 1 | tf_op jit(solution)/shard_map/project/pallas_call | solution.py:310
  136.2 8.7 %collective-permute-start.22 = (bf16[4,4,32,512]{3,2,1,0:T(8,128)(2,1)S(1)}, bf16[4,4,32,512]{3,2,1,0:T(8,128)(2,1)S(1)}, u32[]{:S(2)}, u32[]{:S(2)}) collective-permute-start(bf16[4,4,32,512]{3,2,1,0:T(8,128)(2,1)S(1)} %get-tuple-element.54), channel_id=1, source_target_pairs={{0,1},{1,0},{2,3},{3,2},{4,5},{5,4},{6,7},{7,6},{8,9},{9,8},{10,11... | collective-permute-start | bytes 1572872 | tf_op jit(solution)/shard_map/ppermute | solution.py:33
  144.9 2.6 slice_convert_fusion.target_ref.refs_1_
  147.5 1.5 bitcast_add_fusion.refs_2_
  149.8 5.1 %project.5 = (bf16[4,3,32,512]{3,2,1,0:T(8,128)(2,1)S(1)}, f32[4,3,32,512]{3,2,1,0:T(8,128)S(1)}) custom-call(s32[1]{0:T(128)} %bitcast.24.refs_0_, bf16[3072,512]{1,0:T(8,128)(2,1)S(1)} %copy-done, bf16[256,3072]{1,0:T(8,128)(2,1)} %collective-permute-done.16.refs_2_.refs_15_, bf16[256,3072]{1,0:T(8,128)(2,1)} %collective-permute-done.17.refs_3_.refs_16_, ...), custom_call_target="tpu_custom_call" | custom-call | flops 1 | bytes 1 | tf_op jit(solution)/shard_map/project/pallas_call | solution.py:310
  154.8 3.5 %collective-permute-start.23 = (bf16[4,3,32,512]{3,2,1,0:T(8,128)(2,1)S(1)}, bf16[4,3,32,512]{3,2,1,0:T(8,128)(2,1)S(1)}, u32[]{:S(2)}, u32[]{:S(2)}) collective-permute-start(bf16[4,3,32,512]{3,2,1,0:T(8,128)(2,1)S(1)} %get-tuple-element.62), channel_id=1, source_target_pairs={{0,1},{1,0},{2,3},{3,2},{4,5},{5,4},{6,7},{7,6},{8,9},{9,8},{10,11... | collective-permute-start | bytes 1179656 | tf_op jit(solution)/shard_map/ppermute | solution.py:33
  158.3 1.3 collective-permute-done.23
  159.9 1.3 collective-permute-start.24
  161.2 1.5 collective-permute-start.25
  162.6 1.5 collective-permute-start.26
  164.2 3.8 %collective-permute-done.24 = bf16[7,32,512]{2,1,0:T(8,128)(2,1)S(1)} collective-permute-done((bf16[7,32,512]{2,1,0:T(8,128)(2,1)S(1)}, bf16[7,32,512]{2,1,0:T(8,128)(2,1)S(1)}, u32[]{:S(2)}, u32[]{:S(2)}) %collective-permute-start.24) | collective-permute-done | bytes 229408 | tf_op jit(solution)/shard_map/ppermute | solution.py:33
  168.0 5.9 %collective-permute-done.26 = bf16[7,32,512]{2,1,0:T(8,128)(2,1)S(1)} collective-permute-done((bf16[7,32,512]{2,1,0:T(8,128)(2,1)S(1)}, bf16[7,32,512]{2,1,0:T(8,128)(2,1)S(1)}, u32[]{:S(2)}, u32[]{:S(2)}) %collective-permute-start.26) | collective-permute-done | bytes 229408 | tf_op jit(solution)/shard_map/ppermute | solution.py:33
  174.1 2.0 collective-permute-start.27
  176.3 3.0 %collective-permute-done.27.refs_4_ = f32[16,8,512]{2,1,0:T(8,128)S(1)} collective-permute-done((f32[16,8,512]{2,1,0:T(8,128)S(1)}, f32[16,8,512]{2,1,0:T(8,128)S(1)}, u32[]{:S(2)}, u32[]{:S(2)}) %collective-permute-start.27) | collective-permute-done | bytes 262176 | tf_op jit(solution)/shard_map/ppermute | solution.py:428
  179.3 2.5 collective-permute-done.28.refs_5_
  183.3 5.3 %products.1 = f32[24,768]{1,0:T(8,128)S(1)} custom-call(f32[16,48,512]{2,1,0:T(8,128)S(1)} %assemble.1.state_ref.refs_0_, f32[16,48,512]{2,1,0:T(8,128)S(1)} %copy-done.1, f32[16,48,1]{2,1,0:T(8,128)S(1)} %slice_convert_fusion.1.keep_ref.refs_2_, f32[3,512]{1,0:T(4,128)S(1)} %copy-done.9), custom_call_target="tpu_custom_call" | custom-call | flops 1 | bytes 1 | tf_op jit(solution)/shard_map/products/pallas_call | solution.py:136
  188.6 1.3 collective-permute-start.31
  189.9 2.1 collective-permute-start.30
  193.4 2.2 collective-permute-done.30
  195.7 1.9 collective-permute-start.34
  198.6 1.7 collective-permute-start.32
  200.4 2.4 collective-permute-done.33.refs_7_
  202.8 5.2 %gradients.1.refs_18_ = bf16[17,32,512]{2,1,0:T(8,128)(2,1)} custom-call(f32[16,48,512]{2,1,0:T(8,128)S(1)} %assemble.1.state_ref.refs_0_, f32[16,48,512]{2,1,0:T(8,128)S(1)} %copy-done.1, f32[16,48,1]{2,1,0:T(8,128)S(1)} %slice_convert_fusion.1.keep_ref.refs_2_, f32[1,768]{1,0:T(1,128)S(1)} %reshape.18.refs_3_, f32[3,512]{1,0:T(4,128)S(1)} %copy-done.9, ...), custom_call_target="tpu_custom_call" | custom-call | flops 1 | bytes 1 | tf_op jit(solution)/shard_map/gradients/pallas_call | solution.py:273
  208.0 1.8 collective-permute-start.37
  209.8 1.0 collective-permute-start.36
  211.4 1.5 collective-permute-start.38
  212.9 8.8 %collective-permute-done.37.refs_21_ = bf16[17,32,512]{2,1,0:T(8,128)(2,1)} collective-permute-done((bf16[17,32,512]{2,1,0:T(8,128)(2,1)}, bf16[17,32,512]{2,1,0:T(8,128)(2,1)}, u32[]{:S(2)}, u32[]{:S(2)}) %collective-permute-start.37) | collective-permute-done | bytes 557088 | tf_op jit(solution)/shard_map/ppermute | solution.py:33
  221.7 6.0 %collective-permute-start.41 = (bf16[17,32,512]{2,1,0:T(8,128)(2,1)}, bf16[17,32,512]{2,1,0:T(8,128)(2,1)}, u32[]{:S(2)}, u32[]{:S(2)}) collective-permute-start(bf16[17,32,512]{2,1,0:T(8,128)(2,1)} %collective-permute-done.37.refs_21_), channel_id=1, source_target_pairs={{0,1},{1,0},{2,3},{3,2},{4,5},{5,4},{6,7},{7,6},{8,9},{9,8},{10,11... | collective-permute-start | bytes 1671176 | tf_op jit(solution)/shard_map/ppermute | solution.py:33
  227.7 8.2 %collective-permute-done.36.refs_20_ = bf16[17,32,512]{2,1,0:T(8,128)(2,1)} collective-permute-done((bf16[17,32,512]{2,1,0:T(8,128)(2,1)}, bf16[17,32,512]{2,1,0:T(8,128)(2,1)}, u32[]{:S(2)}, u32[]{:S(2)}) %collective-permute-start.36) | collective-permute-done | bytes 557088 | tf_op jit(solution)/shard_map/ppermute | solution.py:33
  235.9 1.4 collective-permute-start.40
  237.3 1.8 collective-permute-done.40.refs_24_
  240.0 19.9 %weight_gradient.1 = (f32[3072,512]{1,0:T(8,128)}, f32[1,128]{1,0:T(1,128)}) custom-call(s32[16]{0:T(128)S(1)} %stack.102.refs_0_, s32[8]{0:T(128)S(1)} %stack.111.refs_1_, bf16[256,3072]{1,0:T(8,128)(2,1)S(1)} %copy-done.3, bf16[256,3072]{1,0:T(8,128)(2,1)} %collective-permute-done.refs_3_, bf16[256,3072]{1,0:T(8,128)(2,1)} %collective-permute-done.1.refs_4_, ...), custom_call_target="tpu_custom_call" | custom-call | flops 1 | bytes 1 | tf_op jit(solution)/shard_map/weight_gradient/pallas_call | solution.py:392
  (76 shorter events, 13.0 us)
Async XLA Ops:
  0.6 37.0 %collective-permute-start.3 = (bf16[256,3072]{1,0:T(8,128)(2,1)}, bf16[256,3072]{1,0:T(8,128)(2,1)S(1)}, u32[]{:S(2)}, u32[]{:S(2)}) collective-permute-start(bf16[256,3072]{1,0:T(8,128)(2,1)} %refs_2_.3), channel_id=1, source_target_pairs={{32,0},{40,8},{48,16},{56,24},{64,32},{72,40},{80,48},{88,56},{96,... | collective-permute-start | bytes 4718600 | tf_op jit(solution)/shard_map/ppermute | solution.py:28
  4.3 36.5 %collective-permute-start.2 = (bf16[256,3072]{1,0:T(8,128)(2,1)}, bf16[256,3072]{1,0:T(8,128)(2,1)}, u32[]{:S(2)}, u32[]{:S(2)}) collective-permute-start(bf16[256,3072]{1,0:T(8,128)(2,1)} %refs_2_.3), channel_id=1, source_target_pairs={{96,0},{104,8},{112,16},{120,24},{0,32},{8,40},{16,48},{24,56},{32... | collective-permute-start | bytes 4718600 | tf_op jit(solution)/shard_map/ppermute | solution.py:28
  4.3 36.8 %collective-permute-start.1 = (bf16[256,3072]{1,0:T(8,128)(2,1)}, bf16[256,3072]{1,0:T(8,128)(2,1)}, u32[]{:S(2)}, u32[]{:S(2)}) collective-permute-start(bf16[256,3072]{1,0:T(8,128)(2,1)} %refs_2_.3), channel_id=1, source_target_pairs={{8,0},{16,8},{24,16},{0,24},{40,32},{48,40},{56,48},{32,56},{72,64... | collective-permute-start | bytes 4718600 | tf_op jit(solution)/shard_map/ppermute | solution.py:28
  8.0 36.2 %collective-permute-start = (bf16[256,3072]{1,0:T(8,128)(2,1)}, bf16[256,3072]{1,0:T(8,128)(2,1)}, u32[]{:S(2)}, u32[]{:S(2)}) collective-permute-start(bf16[256,3072]{1,0:T(8,128)(2,1)} %refs_2_.3), channel_id=1, source_target_pairs={{24,0},{0,8},{8,16},{16,24},{56,32},{32,40},{40,48},{48,56},{88,64... | collective-permute-start | bytes 4718600 | tf_op jit(solution)/shard_map/ppermute | solution.py:28
  8.7 5.8 %collective-permute-start.5 = (s32[16]{0:T(128)S(1)}, s32[16]{0:T(128)S(1)}, u32[]{:S(2)}, u32[]{:S(2)}) collective-permute-start(s32[16]{0:T(128)S(1)} %slice.37), channel_id=1, source_target_pairs={{1,0},{2,1},{3,2},{4,3},{5,4},{6,5},{7,6},{9,8},{10,9},{11,10},{12... | collective-permute-start | bytes 200 | tf_op jit(solution)/shard_map/ppermute | solution.py:39
  14.6 3.0 %collective-permute-start.6 = (s32[17]{0:T(128)S(1)}, s32[17]{0:T(128)S(1)}, u32[]{:S(2)}, u32[]{:S(2)}) collective-permute-start(s32[17]{0:T(128)S(1)} %slice.38), channel_id=1, source_target_pairs={{0,1},{1,2},{2,3},{3,4},{4,5},{5,6},{6,7},{8,9},{9,10},{10,11},{11... | collective-permute-start | bytes 212 | tf_op jit(solution)/shard_map/ppermute | solution.py:39
  17.6 5.6 %collective-permute-start.4 = (bf16[16,512]{1,0:T(8,128)(2,1)S(1)}, bf16[16,512]{1,0:T(8,128)(2,1)S(1)}, u32[]{:S(2)}, u32[]{:S(2)}) collective-permute-start(bf16[16,512]{1,0:T(8,128)(2,1)S(1)} %slice.36), channel_id=1, source_target_pairs={{1,0},{2,1},{3,2},{4,3},{5,4},{6,5},{7,6},{9,8},{10,9},{11,10},{12... | collective-permute-start | bytes 49160 | tf_op jit(solution)/shard_map/ppermute | solution.py:39
  37.6 48.4 %copy-start.4 = (bf16[256,3072]{1,0:T(8,128)(2,1)}, bf16[256,3072]{1,0:T(8,128)(2,1)S(1)}, u32[]{:S(2)}) copy-start(bf16[256,3072]{1,0:T(8,128)(2,1)S(1)} %collective-permute-done.3.refs_6_) | copy-start | bytes 4718596
  44.2 34.0 %collective-permute-start.9 = (bf16[256,3072]{1,0:T(8,128)(2,1)}, bf16[256,3072]{1,0:T(8,128)(2,1)}, u32[]{:S(2)}, u32[]{:S(2)}) collective-permute-start(bf16[256,3072]{1,0:T(8,128)(2,1)} %collective-permute-done.1.refs_4_), channel_id=1, source_target_pairs={{32,0},{40,8},{48,16},{56,24},{64,32},{72,40},{80,48},{88,56},{96,... | collective-permute-start | bytes 4718600 | tf_op jit(solution)/shard_map/ppermute | solution.py:28
  46.6 34.5 %collective-permute-start.10 = (bf16[256,3072]{1,0:T(8,128)(2,1)S(1)}, bf16[256,3072]{1,0:T(8,128)(2,1)}, u32[]{:S(2)}, u32[]{:S(2)}) collective-permute-start(bf16[256,3072]{1,0:T(8,128)(2,1)S(1)} %collective-permute-done.3.refs_6_), channel_id=1, source_target_pairs={{24,0},{0,8},{8,16},{16,24},{56,32},{32,40},{40,48},{48,56},{88,64... | collective-permute-start | bytes 4718600 | tf_op jit(solution)/shard_map/ppermute | solution.py:28
  46.6 34.7 %collective-permute-start.7 = (bf16[256,3072]{1,0:T(8,128)(2,1)}, bf16[256,3072]{1,0:T(8,128)(2,1)}, u32[]{:S(2)}, u32[]{:S(2)}) collective-permute-start(bf16[256,3072]{1,0:T(8,128)(2,1)} %collective-permute-done.refs_3_), channel_id=1, source_target_pairs={{96,0},{104,8},{112,16},{120,24},{0,32},{8,40},{16,48},{24,56},{32... | collective-permute-start | bytes 4718600 | tf_op jit(solution)/shard_map/ppermute | solution.py:28
  46.6 34.7 %collective-permute-start.8 = (bf16[256,3072]{1,0:T(8,128)(2,1)}, bf16[256,3072]{1,0:T(8,128)(2,1)}, u32[]{:S(2)}, u32[]{:S(2)}) collective-permute-start(bf16[256,3072]{1,0:T(8,128)(2,1)} %collective-permute-done.2.refs_5_), channel_id=1, source_target_pairs={{8,0},{16,8},{24,16},{0,24},{40,32},{48,40},{56,48},{32,56},{72,64... | collective-permute-start | bytes 4718600 | tf_op jit(solution)/shard_map/ppermute | solution.py:28
  51.4 34.7 %copy-start.2 = (bf16[256,3072]{1,0:T(8,128)(2,1)S(1)}, bf16[256,3072]{1,0:T(8,128)(2,1)}, u32[]{:S(2)}) copy-start(bf16[256,3072]{1,0:T(8,128)(2,1)} %refs_2_.3) | copy-start | bytes 4718596
  51.5 0.9 copy-start.6
  52.4 25.8 %all-to-all-start = ((bf16[8,2,48,640]{3,2,1,0:T(8,128)(2,1)}), bf16[8,2,48,640]{3,2,1,0:T(8,128)(2,1)}, u32[]{:S(2)}, u32[]{:S(2)}) async-start(bf16[8,2,48,640]{3,2,1,0:T(8,128)(2,1)} %copy-done.6), calls=%async_computation | async-start | bytes 1966080 | tf_op jit(solution)/shard_map/all_to_all | solution.py:480
  60.0 54.8 %collective-permute-start.11 = (bf16[256,3072]{1,0:T(8,128)(2,1)}, bf16[256,3072]{1,0:T(8,128)(2,1)}, u32[]{:S(2)}, u32[]{:S(2)}) collective-permute-start(bf16[256,3072]{1,0:T(8,128)(2,1)} %collective-permute-done.refs_3_), channel_id=1, source_target_pairs={{24,0},{0,8},{8,16},{16,24},{56,32},{32,40},{40,48},{48,56},{88,64... | collective-permute-start | bytes 4718600 | tf_op jit(solution)/shard_map/ppermute | solution.py:28
  78.2 37.8 %collective-permute-start.12 = (bf16[256,3072]{1,0:T(8,128)(2,1)}, bf16[256,3072]{1,0:T(8,128)(2,1)}, u32[]{:S(2)}, u32[]{:S(2)}) collective-permute-start(bf16[256,3072]{1,0:T(8,128)(2,1)} %collective-permute-done.2.refs_5_), channel_id=1, source_target_pairs={{96,0},{104,8},{112,16},{120,24},{0,32},{8,40},{16,48},{24,56},{32... | collective-permute-start | bytes 4718600 | tf_op jit(solution)/shard_map/ppermute | solution.py:28
  81.3 34.8 %collective-permute-start.14 = (bf16[256,3072]{1,0:T(8,128)(2,1)}, bf16[256,3072]{1,0:T(8,128)(2,1)}, u32[]{:S(2)}, u32[]{:S(2)}) collective-permute-start(bf16[256,3072]{1,0:T(8,128)(2,1)} %collective-permute-done.9.refs_9_), channel_id=1, source_target_pairs={{8,0},{16,8},{24,16},{0,24},{40,32},{48,40},{56,48},{32,56},{72,64... | collective-permute-start | bytes 4718600 | tf_op jit(solution)/shard_map/ppermute | solution.py:28
  83.7 32.4 %collective-permute-start.13 = (bf16[256,3072]{1,0:T(8,128)(2,1)}, bf16[256,3072]{1,0:T(8,128)(2,1)}, u32[]{:S(2)}, u32[]{:S(2)}) collective-permute-start(bf16[256,3072]{1,0:T(8,128)(2,1)} %collective-permute-done.9.refs_9_), channel_id=1, source_target_pairs={{32,0},{40,8},{48,16},{56,24},{64,32},{72,40},{80,48},{88,56},{96,... | collective-permute-start | bytes 4718600 | tf_op jit(solution)/shard_map/ppermute | solution.py:28
  100.3 7.7 %collective-permute-start.15 = (bf16[4,9,32,512]{3,2,1,0:T(8,128)(2,1)S(1)}, bf16[4,9,32,512]{3,2,1,0:T(8,128)(2,1)S(1)}, u32[]{:S(2)}, u32[]{:S(2)}) collective-permute-start(bf16[4,9,32,512]{3,2,1,0:T(8,128)(2,1)S(1)} %get-tuple-element.47), channel_id=1, source_target_pairs={{0,1},{1,0},{2,3},{3,2},{4,5},{5,4},{6,7},{7,6},{8,9},{9,8},{10,11... | collective-permute-start | bytes 3538952 | tf_op jit(solution)/shard_map/ppermute | solution.py:33
  108.1 41.7 %collective-permute-start.17 = (bf16[256,3072]{1,0:T(8,128)(2,1)}, bf16[256,3072]{1,0:T(8,128)(2,1)}, u32[]{:S(2)}, u32[]{:S(2)}) collective-permute-start(bf16[256,3072]{1,0:T(8,128)(2,1)} %collective-permute-done.7.refs_7_), channel_id=1, source_target_pairs={{96,0},{104,8},{112,16},{120,24},{0,32},{8,40},{16,48},{24,56},{32... | collective-permute-start | bytes 4718600 | tf_op jit(solution)/shard_map/ppermute | solution.py:28
  109.8 19.9 %copy-start = (bf16[3072,512]{1,0:T(8,128)(2,1)S(1)}, bf16[3072,512]{1,0:T(8,128)(2,1)}, u32[]{:S(2)}) copy-start(bf16[3072,512]{1,0:T(8,128)(2,1)} %refs_1_.5) | copy-start | bytes 9437188
  114.8 35.0 %collective-permute-start.16 = (bf16[256,3072]{1,0:T(8,128)(2,1)}, bf16[256,3072]{1,0:T(8,128)(2,1)}, u32[]{:S(2)}, u32[]{:S(2)}) collective-permute-start(bf16[256,3072]{1,0:T(8,128)(2,1)} %collective-permute-done.7.refs_7_), channel_id=1, source_target_pairs={{24,0},{0,8},{8,16},{16,24},{56,32},{32,40},{40,48},{48,56},{88,64... | collective-permute-start | bytes 4718600 | tf_op jit(solution)/shard_map/ppermute | solution.py:28
  116.0 33.7 %collective-permute-start.18 = (bf16[256,3072]{1,0:T(8,128)(2,1)}, bf16[256,3072]{1,0:T(8,128)(2,1)}, u32[]{:S(2)}, u32[]{:S(2)}) collective-permute-start(bf16[256,3072]{1,0:T(8,128)(2,1)} %collective-permute-done.13.refs_4_.refs_13_), channel_id=1, source_target_pairs={{8,0},{16,8},{24,16},{0,24},{40,32},{48,40},{56,48},{32,56},{72,64... | collective-permute-start | bytes 4718600 | tf_op jit(solution)/shard_map/ppermute | solution.py:28
  119.9 7.4 %collective-permute-start.19 = (bf16[9,32,512]{2,1,0:T(8,128)(2,1)}, bf16[9,32,512]{2,1,0:T(8,128)(2,1)}, u32[]{:S(2)}, u32[]{:S(2)}) collective-permute-start(bf16[9,32,512]{2,1,0:T(8,128)(2,1)} %get-tuple-element.68), channel_id=1, source_target_pairs={{0,2},{1,3},{2,4},{3,5},{4,6},{5,7},{6,0},{7,1},{8,10},{9,11},{10,... | collective-permute-start | bytes 884744 | tf_op jit(solution)/shard_map/ppermute | solution.py:33
  121.1 15.0 %collective-permute-start.21 = (bf16[9,32,512]{2,1,0:T(8,128)(2,1)}, bf16[9,32,512]{2,1,0:T(8,128)(2,1)}, u32[]{:S(2)}, u32[]{:S(2)}) collective-permute-start(bf16[9,32,512]{2,1,0:T(8,128)(2,1)} %get-tuple-element.69), channel_id=1, source_target_pairs={{0,4},{1,5},{2,6},{3,7},{4,0},{5,1},{6,2},{7,3},{8,12},{9,13},{10,... | collective-permute-start | bytes 884744 | tf_op jit(solution)/shard_map/ppermute | solution.py:33
  127.3 20.2 %collective-permute-start.20 = (bf16[9,32,512]{2,1,0:T(8,128)(2,1)}, bf16[9,32,512]{2,1,0:T(8,128)(2,1)}, u32[]{:S(2)}, u32[]{:S(2)}) collective-permute-start(bf16[9,32,512]{2,1,0:T(8,128)(2,1)} %get-tuple-element.70), channel_id=1, source_target_pairs={{0,6},{1,7},{2,0},{3,1},{4,2},{5,3},{6,4},{7,5},{8,14},{9,15},{10,... | collective-permute-start | bytes 884744 | tf_op jit(solution)/shard_map/ppermute | solution.py:33
  136.2 12.8 %collective-permute-start.22 = (bf16[4,4,32,512]{3,2,1,0:T(8,128)(2,1)S(1)}, bf16[4,4,32,512]{3,2,1,0:T(8,128)(2,1)S(1)}, u32[]{:S(2)}, u32[]{:S(2)}) collective-permute-start(bf16[4,4,32,512]{3,2,1,0:T(8,128)(2,1)S(1)} %get-tuple-element.54), channel_id=1, source_target_pairs={{0,1},{1,0},{2,3},{3,2},{4,5},{5,4},{6,7},{7,6},{8,9},{9,8},{10,11... | collective-permute-start | bytes 1572872 | tf_op jit(solution)/shard_map/ppermute | solution.py:33
  149.0 15.2 %copy-start.7 = (f32[9,32,512]{2,1,0:T(8,128)}, f32[9,32,512]{2,1,0:T(8,128)S(1)}, u32[]{:S(2)}) copy-start(f32[9,32,512]{2,1,0:T(8,128)S(1)} %bitcast_add_fusion.refs_2_) | copy-start | bytes 1769476
  154.8 4.8 %collective-permute-start.23 = (bf16[4,3,32,512]{3,2,1,0:T(8,128)(2,1)S(1)}, bf16[4,3,32,512]{3,2,1,0:T(8,128)(2,1)S(1)}, u32[]{:S(2)}, u32[]{:S(2)}) collective-permute-start(bf16[4,3,32,512]{3,2,1,0:T(8,128)(2,1)S(1)} %get-tuple-element.62), channel_id=1, source_target_pairs={{0,1},{1,0},{2,3},{3,2},{4,5},{5,4},{6,7},{7,6},{8,9},{9,8},{10,11... | collective-permute-start | bytes 1179656 | tf_op jit(solution)/shard_map/ppermute | solution.py:33
  159.9 8.1 %collective-permute-start.24 = (bf16[7,32,512]{2,1,0:T(8,128)(2,1)S(1)}, bf16[7,32,512]{2,1,0:T(8,128)(2,1)S(1)}, u32[]{:S(2)}, u32[]{:S(2)}) collective-permute-start(bf16[7,32,512]{2,1,0:T(8,128)(2,1)S(1)} %get-tuple-element.71), channel_id=1, source_target_pairs={{0,2},{1,3},{2,4},{3,5},{4,6},{5,7},{6,0},{7,1},{8,10},{9,11},{10,... | collective-permute-start | bytes 688136 | tf_op jit(solution)/shard_map/ppermute | solution.py:33
  161.2 6.8 %collective-permute-start.25 = (bf16[7,32,512]{2,1,0:T(8,128)(2,1)S(1)}, bf16[7,32,512]{2,1,0:T(8,128)(2,1)S(1)}, u32[]{:S(2)}, u32[]{:S(2)}) collective-permute-start(bf16[7,32,512]{2,1,0:T(8,128)(2,1)S(1)} %get-tuple-element.72), channel_id=1, source_target_pairs={{0,6},{1,7},{2,0},{3,1},{4,2},{5,3},{6,4},{7,5},{8,14},{9,15},{10,... | collective-permute-start | bytes 688136 | tf_op jit(solution)/shard_map/ppermute | solution.py:33
  162.6 11.3 %collective-permute-start.26 = (bf16[7,32,512]{2,1,0:T(8,128)(2,1)S(1)}, bf16[7,32,512]{2,1,0:T(8,128)(2,1)S(1)}, u32[]{:S(2)}, u32[]{:S(2)}) collective-permute-start(bf16[7,32,512]{2,1,0:T(8,128)(2,1)S(1)} %get-tuple-element.73), channel_id=1, source_target_pairs={{0,4},{1,5},{2,6},{3,7},{4,0},{5,1},{6,2},{7,3},{8,12},{9,13},{10,... | collective-permute-start | bytes 688136 | tf_op jit(solution)/shard_map/ppermute | solution.py:33
  174.0 7.9 %copy-start.8 = (f32[9,32,512]{2,1,0:T(8,128)S(1)}, f32[9,32,512]{2,1,0:T(8,128)}, u32[]{:S(2)}) copy-start(f32[9,32,512]{2,1,0:T(8,128)} %copy-done.7) | copy-start | bytes 1769476
  174.1 5.3 %collective-permute-start.27 = (f32[16,8,512]{2,1,0:T(8,128)S(1)}, f32[16,8,512]{2,1,0:T(8,128)S(1)}, u32[]{:S(2)}, u32[]{:S(2)}) collective-permute-start(f32[16,8,512]{2,1,0:T(8,128)S(1)} %pad_maximum_fusion.1), channel_id=1, source_target_pairs={{7,0},{0,1},{1,2},{2,3},{3,4},{4,5},{5,6},{6,7},{15,8},{8,9},{9,10... | collective-permute-start | bytes 786440 | tf_op jit(solution)/shard_map/ppermute | solution.py:428
  176.0 5.8 %collective-permute-start.28 = (f32[16,8,512]{2,1,0:T(8,128)S(1)}, f32[16,8,512]{2,1,0:T(8,128)S(1)}, u32[]{:S(2)}, u32[]{:S(2)}) collective-permute-start(f32[16,8,512]{2,1,0:T(8,128)S(1)} %pad_maximum_fusion.2), channel_id=1, source_target_pairs={{1,0},{2,1},{3,2},{4,3},{5,4},{6,5},{7,6},{0,7},{9,8},{10,9},{11,1... | collective-permute-start | bytes 786440 | tf_op jit(solution)/shard_map/ppermute | solution.py:428
  181.9 1.4 copy-start.1
  181.9 1.4 copy-start.9
  188.6 4.8 %collective-permute-start.31 = (f32[24,768]{1,0:T(8,128)S(1)}, f32[24,768]{1,0:T(8,128)S(1)}, u32[]{:S(2)}, u32[]{:S(2)}) collective-permute-start(f32[24,768]{1,0:T(8,128)S(1)} %products.1), channel_id=1, source_target_pairs={{16,0},{24,8},{0,16},{8,24},{48,32},{56,40},{32,48},{40,56},{80,64... | collective-permute-start | bytes 221192 | tf_op jit(solution)/shard_map/ppermute | solution.py:28
  189.9 5.7 %collective-permute-start.30 = (f32[24,768]{1,0:T(8,128)S(1)}, f32[24,768]{1,0:T(8,128)S(1)}, u32[]{:S(2)}, u32[]{:S(2)}) collective-permute-start(f32[24,768]{1,0:T(8,128)S(1)} %products.1), channel_id=1, source_target_pairs={{24,0},{0,8},{8,16},{16,24},{56,32},{32,40},{40,48},{48,56},{88,64... | collective-permute-start | bytes 221192 | tf_op jit(solution)/shard_map/ppermute | solution.py:28
  191.9 3.7 %collective-permute-start.29 = (f32[24,768]{1,0:T(8,128)S(1)}, f32[24,768]{1,0:T(8,128)S(1)}, u32[]{:S(2)}, u32[]{:S(2)}) collective-permute-start(f32[24,768]{1,0:T(8,128)S(1)} %products.1), channel_id=1, source_target_pairs={{8,0},{16,8},{24,16},{0,24},{40,32},{48,40},{56,48},{32,56},{72,64... | collective-permute-start | bytes 221192 | tf_op jit(solution)/shard_map/ppermute | solution.py:28
  195.6 44.3 %copy-start.3 = (bf16[256,3072]{1,0:T(8,128)(2,1)S(1)}, bf16[256,3072]{1,0:T(8,128)(2,1)}, u32[]{:S(2)}) copy-start(bf16[256,3072]{1,0:T(8,128)(2,1)} %refs_2_.3) | copy-start | bytes 4718596
  195.6 44.3 %copy-start.5 = (bf16[256,3072]{1,0:T(8,128)(2,1)S(1)}, bf16[256,3072]{1,0:T(8,128)(2,1)}, u32[]{:S(2)}) copy-start(bf16[256,3072]{1,0:T(8,128)(2,1)} %copy-done.4) | copy-start | bytes 4718596
  195.7 4.8 %collective-permute-start.34 = (f32[24,768]{1,0:T(8,128)S(1)}, f32[24,768]{1,0:T(8,128)S(1)}, u32[]{:S(2)}, u32[]{:S(2)}) collective-permute-start(f32[24,768]{1,0:T(8,128)S(1)} %add_add_fusion.refs_5_), channel_id=1, source_target_pairs={{64,0},{72,8},{80,16},{88,24},{96,32},{104,40},{112,48},{120,56},{... | collective-permute-start | bytes 221192 | tf_op jit(solution)/shard_map/ppermute | solution.py:28
  197.6 5.2 %collective-permute-start.33 = (f32[24,768]{1,0:T(8,128)S(1)}, f32[24,768]{1,0:T(8,128)S(1)}, u32[]{:S(2)}, u32[]{:S(2)}) collective-permute-start(f32[24,768]{1,0:T(8,128)S(1)} %add_add_fusion.refs_5_), channel_id=1, source_target_pairs={{96,0},{104,8},{112,16},{120,24},{0,32},{8,40},{16,48},{24,56},{32... | collective-permute-start | bytes 221192 | tf_op jit(solution)/shard_map/ppermute | solution.py:28
  198.6 4.3 %collective-permute-start.32 = (f32[24,768]{1,0:T(8,128)S(1)}, f32[24,768]{1,0:T(8,128)S(1)}, u32[]{:S(2)}, u32[]{:S(2)}) collective-permute-start(f32[24,768]{1,0:T(8,128)S(1)} %add_add_fusion.refs_5_), channel_id=1, source_target_pairs={{32,0},{40,8},{48,16},{56,24},{64,32},{72,40},{80,48},{88,56},{96,... | collective-permute-start | bytes 221192 | tf_op jit(solution)/shard_map/ppermute | solution.py:28
  208.0 13.7 %collective-permute-start.37 = (bf16[17,32,512]{2,1,0:T(8,128)(2,1)}, bf16[17,32,512]{2,1,0:T(8,128)(2,1)}, u32[]{:S(2)}, u32[]{:S(2)}) collective-permute-start(bf16[17,32,512]{2,1,0:T(8,128)(2,1)} %gradients.1.refs_18_), channel_id=1, source_target_pairs={{0,4},{1,5},{2,6},{3,7},{4,0},{5,1},{6,2},{7,3},{8,12},{9,13},{10,... | collective-permute-start | bytes 1671176 | tf_op jit(solution)/shard_map/ppermute | solution.py:33
  209.8 26.1 %collective-permute-start.36 = (bf16[17,32,512]{2,1,0:T(8,128)(2,1)}, bf16[17,32,512]{2,1,0:T(8,128)(2,1)}, u32[]{:S(2)}, u32[]{:S(2)}) collective-permute-start(bf16[17,32,512]{2,1,0:T(8,128)(2,1)} %gradients.1.refs_18_), channel_id=1, source_target_pairs={{0,6},{1,7},{2,0},{3,1},{4,2},{5,3},{6,4},{7,5},{8,14},{9,15},{10,... | collective-permute-start | bytes 1671176 | tf_op jit(solution)/shard_map/ppermute | solution.py:33
  210.8 26.4 %collective-permute-start.35 = (bf16[17,32,512]{2,1,0:T(8,128)(2,1)}, bf16[17,32,512]{2,1,0:T(8,128)(2,1)}, u32[]{:S(2)}, u32[]{:S(2)}) collective-permute-start(bf16[17,32,512]{2,1,0:T(8,128)(2,1)} %gradients.1.refs_18_), channel_id=1, source_target_pairs={{0,2},{1,3},{2,4},{3,5},{4,6},{5,7},{6,0},{7,1},{8,10},{9,11},{10,... | collective-permute-start | bytes 1671176 | tf_op jit(solution)/shard_map/ppermute | solution.py:33
  211.4 26.0 %collective-permute-start.38 = (bf16[17,32,512]{2,1,0:T(8,128)(2,1)}, bf16[17,32,512]{2,1,0:T(8,128)(2,1)}, u32[]{:S(2)}, u32[]{:S(2)}) collective-permute-start(bf16[17,32,512]{2,1,0:T(8,128)(2,1)} %gradients.1.refs_18_), channel_id=1, source_target_pairs={{0,1},{1,0},{2,3},{3,2},{4,5},{5,4},{6,7},{7,6},{8,9},{9,8},{10,11... | collective-permute-start | bytes 1671176 | tf_op jit(solution)/shard_map/ppermute | solution.py:33
  221.7 15.6 %collective-permute-start.41 = (bf16[17,32,512]{2,1,0:T(8,128)(2,1)}, bf16[17,32,512]{2,1,0:T(8,128)(2,1)}, u32[]{:S(2)}, u32[]{:S(2)}) collective-permute-start(bf16[17,32,512]{2,1,0:T(8,128)(2,1)} %collective-permute-done.37.refs_21_), channel_id=1, source_target_pairs={{0,1},{1,0},{2,3},{3,2},{4,5},{5,4},{6,7},{7,6},{8,9},{9,8},{10,11... | collective-permute-start | bytes 1671176 | tf_op jit(solution)/shard_map/ppermute | solution.py:33
  235.9 3.3 %collective-permute-start.40 = (bf16[17,32,512]{2,1,0:T(8,128)(2,1)}, bf16[17,32,512]{2,1,0:T(8,128)(2,1)}, u32[]{:S(2)}, u32[]{:S(2)}) collective-permute-start(bf16[17,32,512]{2,1,0:T(8,128)(2,1)} %collective-permute-done.36.refs_20_), channel_id=1, source_target_pairs={{0,1},{1,0},{2,3},{3,2},{4,5},{5,4},{6,7},{7,6},{8,9},{9,8},{10,11... | collective-permute-start | bytes 1671176 | tf_op jit(solution)/shard_map/ppermute | solution.py:33
  237.2 2.7 %collective-permute-start.39 = (bf16[17,32,512]{2,1,0:T(8,128)(2,1)}, bf16[17,32,512]{2,1,0:T(8,128)(2,1)}, u32[]{:S(2)}, u32[]{:S(2)}) collective-permute-start(bf16[17,32,512]{2,1,0:T(8,128)(2,1)} %collective-permute-done.35.refs_19_), channel_id=1, source_target_pairs={{0,1},{1,0},{2,3},{3,2},{4,5},{5,4},{6,7},{7,6},{8,9},{9,8},{10,11... | collective-permute-start | bytes 1671176 | tf_op jit(solution)/shard_map/ppermute | solution.py:33

commit v4 on v3

--- a/solution.py
+++ b/solution.py
@@ -16,7 +16,7 @@
 LENGTH = SHARE + 2 * PAD
 BLOCKS = 16
 PRODUCTS = 24
-VMEM = 40 * 1024 * 1024
+MIB = 1024 * 1024
 
 
 def from_dp(block, place):
@@ -75,7 +75,7 @@
         out_shape=jax.ShapeDtypeStruct((8, 2, LENGTH, target.shape[1]), target.dtype),
         in_specs=[pl.BlockSpec(memory_space=pltpu.VMEM)],
         out_specs=pl.BlockSpec(memory_space=pltpu.VMEM),
-        compiler_params=pltpu.CompilerParams(vmem_limit_bytes=VMEM),
+        compiler_params=pltpu.CompilerParams(vmem_limit_bytes=8 * MIB),
         cost_estimate=FREE,
         name="windows",
     )(target)
@@ -139,7 +139,7 @@
         in_specs=[pl.BlockSpec(memory_space=pltpu.VMEM)] * 4,
         out_specs=pl.BlockSpec(memory_space=pltpu.VMEM),
         scratch_shapes=[pltpu.VMEM((lanes, 128), jnp.float32)],
-        compiler_params=pltpu.CompilerParams(vmem_limit_bytes=VMEM),
+        compiler_params=pltpu.CompilerParams(vmem_limit_bytes=12 * MIB),
         cost_estimate=FREE,
         name="products",
     )(state, target, keep, gains)
@@ -215,7 +215,7 @@
 
 
 def gradient_kernel(factor, state_ref, target_ref, keep_ref, keep_row_ref, gain_ref, *refs):
-    product_refs, (grad_ref, table, columns) = refs[:4], refs[4:]
+    product_refs, (low_ref, high_ref, table, columns) = refs[:4], refs[4:]
     product = product_refs[0][...]
     for ref in product_refs[1:]:
         product = product + ref[...]
@@ -226,7 +226,7 @@
         table[k : k + 1, :] = row
     columns[...] = table[...].T
 
-    def block(index, carry):
+    def block(index, grad_ref, first):
         state, target, keep = state_ref[index], target_ref[index], keep_ref[index]
         values = columns[pl.ds(pl.multiple_of(index * LENGTH, 8), LENGTH), :]
         (
@@ -248,10 +248,11 @@
             gamma0 * target + eta0 * up(grad1)
         )
         grad = grad0 + grad1 + grad2 + same_next * up(grad0)
-        grad_ref[index] = grad[PAD : PAD + SHARE].astype(jnp.bfloat16)
-        return carry
-
-    lax.fori_loop(0, BLOCKS, block, 0)
+        grad_ref[index - first] = grad[PAD : PAD + SHARE].astype(jnp.bfloat16)
+
+    half = BLOCKS // 2
+    pl.loop(0, half)(lambda index: block(index, low_ref, 0))
+    pl.loop(half, BLOCKS)(lambda index: block(index, high_ref, half))
     place = lax.broadcasted_iota(jnp.int32, squares.shape, 1) % LENGTH
     own_rows = (place >= PAD) & (place < PAD + SHARE)
     parts = []
@@ -261,25 +262,28 @@
             part = value.astype(jnp.bfloat16).astype(jnp.float32)
             parts.append(part)
             value = value - part
-    lane = lax.broadcasted_iota(jnp.int32, grad_ref.shape[1:], 1)
+    lane = lax.broadcasted_iota(jnp.int32, high_ref.shape[1:], 1)
     sums = jnp.zeros(lane.shape, jnp.float32)
     for i, part in enumerate(parts):
         sums = jnp.where(lane == i, part, sums)
-    grad_ref[BLOCKS] = sums.astype(jnp.bfloat16)
+    high_ref[half] = sums.astype(jnp.bfloat16)
 
 
 def gradients(state, target, keep, keep_row, gains, product, factor):
     lanes = product[0].shape[1]
     return pl.pallas_call(
         lambda *refs: gradient_kernel(factor, *refs),
-        out_shape=jax.ShapeDtypeStruct((BLOCKS + 1, SHARE, state.shape[2]), jnp.bfloat16),
+        out_shape=tuple(
+            jax.ShapeDtypeStruct((BLOCKS // 2 + more, SHARE, state.shape[2]), jnp.bfloat16)
+            for more in (0, 1)
+        ),
         in_specs=[pl.BlockSpec(memory_space=pltpu.VMEM)] * 9,
-        out_specs=pl.BlockSpec(memory_space=pltpu.VMEM),
+        out_specs=(pl.BlockSpec(memory_space=pltpu.VMEM),) * 2,
         scratch_shapes=[
             pltpu.VMEM((128, lanes), jnp.float32),
             pltpu.VMEM((lanes, 128), jnp.float32),
         ],
-        compiler_params=pltpu.CompilerParams(vmem_limit_bytes=VMEM),
+        compiler_params=pltpu.CompilerParams(vmem_limit_bytes=12 * MIB),
         cost_estimate=FREE,
         name="gradients",
     )(state, target, keep, keep_row, gains, *product)
@@ -317,7 +321,7 @@
         + [pl.BlockSpec(memory_space=pltpu.VMEM)] * (len(rows) + 1),
         out_specs=(pl.BlockSpec(memory_space=pltpu.VMEM),) * 2,
         scratch_shapes=[pltpu.VMEM((tokens, columns), jnp.float32)],
-        compiler_params=pltpu.CompilerParams(vmem_limit_bytes=VMEM),
+        compiler_params=pltpu.CompilerParams(vmem_limit_bytes=32 * MIB),
         cost_estimate=FREE,
         name="project",
     )(jnp.stack([core]).astype(jnp.int32), weight, *rows)
@@ -354,23 +358,25 @@
         in_specs=[pl.BlockSpec(memory_space=pltpu.SMEM)] * 2
         + [pl.BlockSpec(memory_space=pltpu.VMEM)] * (len(states) + 2),
         out_specs=pl.BlockSpec(memory_space=pltpu.VMEM),
-        compiler_params=pltpu.CompilerParams(vmem_limit_bytes=VMEM),
+        compiler_params=pltpu.CompilerParams(vmem_limit_bytes=12 * MIB),
         cost_estimate=FREE,
         name="assemble",
     )(places, jnp.stack([owner]).astype(jnp.int32), *states, before, after)
 
 
-def weight_kernel(pieces, block_ref, owner_ref, *refs):
-    rows, grads = refs[:pieces], refs[pieces : pieces + 8]
-    out_ref, loss_ref, ordered = refs[pieces + 8 :]
+def weight_kernel(pieces, position_ref, owner_ref, *refs):
+    rows, grads = refs[:pieces], refs[pieces : pieces + 16]
+    out_ref, loss_ref, ordered = refs[pieces + 16 :]
+    half = BLOCKS // 2
 
     @pl.when(pl.program_id(0) == 0)
     def _():
-        for i, grad_ref in enumerate(grads):
-            for k in range(BLOCKS):
-                start = pl.multiple_of((k * 8 + owner_ref[i]) * SHARE, SHARE)
-                ordered[pl.ds(start, SHARE), :] = grad_ref[block_ref[k]]
-        sums = sum(grad_ref[BLOCKS].astype(jnp.float32) for grad_ref in grads)
+        for i in range(8):
+            for block in range(BLOCKS):
+                start = (position_ref[block] * 8 + owner_ref[i]) * SHARE
+                grad = grads[2 * i + block // half][block % half]
+                ordered[pl.ds(pl.multiple_of(start, SHARE), SHARE), :] = grad
+        sums = sum(grad_ref[half].astype(jnp.float32) for grad_ref in grads[1::2])
         row = lax.broadcasted_iota(jnp.int32, sums.shape, 0)
         lane = lax.broadcasted_iota(jnp.int32, sums.shape, 1)
         error = jnp.sum(jnp.where((row == 0) & (lane < 3), sums, 0.0))
@@ -385,7 +391,7 @@
     )
 
 
-def weight_gradient(rows, blocks, grads, owners):
+def weight_gradient(rows, positions, grads, owners):
     features, columns = rows[0].shape[1], grads[0].shape[2]
     tokens = sum(r.shape[0] for r in rows)
     width = 512
@@ -406,10 +412,10 @@
             ),
             scratch_shapes=[pltpu.VMEM((tokens, columns), jnp.bfloat16)],
         ),
-        compiler_params=pltpu.CompilerParams(vmem_limit_bytes=VMEM),
+        compiler_params=pltpu.CompilerParams(vmem_limit_bytes=58 * MIB),
         cost_estimate=FREE,
         name="weight_gradient",
-    )(blocks, jnp.stack(owners).astype(jnp.int32), *rows, *grads)
+    )(positions, jnp.stack(owners).astype(jnp.int32), *rows, *grads)
 
 
 def sum_dp(value, places):
@@ -454,18 +460,20 @@
         )
 
     own_block = joined_rows
-    round1 = (
-        step(own_block, 0, -1), step(own_block, 0, 1),
-        step(own_block, -1, 0), step(own_block, 1, 0),
-    )
+    b01, b10 = step(own_block, 0, 1), step(own_block, 1, 0)
+    bm0, b0m = step(own_block, -1, 0), step(own_block, 0, -1)
+    round1 = (b0m, b01, bm0, b10)
     next_target = neighbour(target_features[: 2 * PAD], -1)
     next_segments = neighbour(segment_ids[: 2 * PAD], -1)
     last_segments = neighbour(segment_ids[-2 * PAD - 1 :], 1)
-    round1, next_target, next_segments, last_segments = barrier(
-        (round1, next_target, next_segments, last_segments)
-    )
+    b01, next_target, next_segments, last_segments = barrier(
+        (round1[1], next_target, next_segments, last_segments)
+    )
+    round1 = (round1[0], b01, *round1[2:])
     b0m, b01, bm0, b10 = round1
-    round2 = (step(b0m, -1, 0), step(bm0, 0, 1), step(b01, 1, 0), step(b10, 0, -1))
+    bm1, b11 = step(bm0, 0, 1), step(b01, 1, 0)
+    bmm, b1m = step(b0m, -1, 0), step(b10, 0, -1)
+    round2 = (bmm, bm1, b11, b1m)
 
     segments = jnp.concatenate([last_segments, segment_ids, next_segments])
     token = mp_index * own - 2 * PAD + jnp.arange(own + 4 * PAD, dtype=jnp.int32)
@@ -484,7 +492,6 @@
     keep = shares[..., columns : columns + 1].astype(jnp.float32)
     keep_row = keep.reshape(1, BLOCKS * LENGTH)
 
-    bmm, bm1, b11, b1m = round2
     round3 = (step(b0m, 0, -1), step(bm0, -1, 0), step(b11, 1, 0), step(b11, 0, 1))
     early = chip_sum([own_block, *round1, *round2])
     round3, early = barrier((round3, early))
@@ -503,21 +510,29 @@
     ]
     places = jnp.stack([(y_index + dy) % 4 * 4 + (z_index + dz) % 4 for dy, dz in names])
     places = places.astype(jnp.int32)
+    positions = jnp.sum(
+        jnp.where(places[None, :] == jnp.arange(BLOCKS)[:, None], jnp.arange(BLOCKS)[None, :], 0),
+        axis=1,
+    ).astype(jnp.int32)
     states = [early, late]
     before = ring(jnp.concatenate([s[:, SHARE - PAD :] for s in states]), 1)
     after = ring(jnp.concatenate([s[:, :PAD] for s in states]), -1)
     window = assemble(states, before, after, places, mp_index)
 
+    window, positions = barrier((window, positions))
     product = products(window, target, keep, step_gains)
     product = sum_dp(product, AROUND_Z)
     product = [product] + [from_dp(product, place) for place in AROUND_Y]
-    grad = gradients(window, target, keep, keep_row, step_gains, product, factor)
-
-    grads = [grad] + [along_mp(grad, k, 0) for k in (1, 3, 2)]
+    low, high = gradients(window, target, keep, keep_row, step_gains, product, factor)
+
+    low1, high3 = along_mp(low, 1, 0), along_mp(high, 3, 0)
+    high1, low3 = along_mp(high, 1, 0), along_mp(low, 3, 0)
+    low2, high2 = along_mp(low1, 1, 0), along_mp(high3, 3, 0)
+    grads = [low, high, low1, high1, low3, high3, low2, high2]
     grads = grads + [along_mp(g, 0, 1) for g in grads]
     owners = [(x_index - k) % 4 * 2 + c for c in (core, 1 - core) for k in (0, 1, 3, 2)]
     grad_weight, mean_loss = weight_gradient(
-        [own_block, *round1, *round2, *round3, *round4], places, grads, owners
+        [own_block, *round1, *round2, *round3, *round4], positions, grads, owners
     )
     mean_loss = mean_loss[0, 0]
     return (mean_loss, grad_weight)

time: 261 us -> 259 us (level)
  waiting for transfers between devices: 98.3 us -> 92.5 us
  starting transfers between devices: 84.7 us -> 89.2 us
  local copies, waits for them, and re-layouts: 6.51 us -> 9.24 us
    ppermute x16 -> x23, waiting for transfers between devices: 35.9 us -> 29.3 us  [along_mp(): return lax.ppermute(block, 'mp', route)]
    ppermute x16 -> x23, starting transfers between devices: 38.9 us -> 45.1 us  [along_mp(): return lax.ppermute(block, 'mp', route)]
  transfers between devices with their start and end apart: 43 -> 50, of which waited for: 29 -> 25; matrix products, arithmetic and copies ran while one was open for 7% -> 6% of each run, Pallas kernels for 8% -> 7%
where the time goes in v4:
time: 259 us; the launch traced here: 258 us
  waiting for transfers between devices  92.5 us (36%)
  starting transfers between devices  89.2 us (34%)
  Pallas kernels  54.5 us (21%)
  other arithmetic  11.3 us (4%)
  local copies, waits for them, and re-layouts  9.24 us (4%)
    ppermute x21, waiting for transfers between devices, from_dp(): return lax.ppermute(block, 'dp', route)  52.5 us
    ppermute x23, starting transfers between devices, along_mp(): return lax.ppermute(block, 'mp', route)  45.1 us
    ppermute x23, waiting for transfers between devices, along_mp(): return lax.ppermute(block, 'mp', route)  29.3 us
    ppermute x21, starting transfers between devices, from_dp(): return lax.ppermute(block, 'dp', route)  27.9 us
    pallas_call x3, Pallas kernels, project(): pl.pallas_call(lambda *refs: project_kernel(len(rows), blocks, *refs), ou...  23.9 us
    pallas_call x1, Pallas kernels, weight_gradient(): pl.pallas_call(lambda *refs: weight_kernel(len(rows), *refs), out_shape=(...  20.1 us
    ppermute x3, starting transfers between devices, neighbour(): return lax.ppermute(block, 'mp', route)  7.14 us
    all_to_all x1, starting transfers between devices, local(): shares = lax.all_to_all(windows(target, block_rows), 'mp', 0, 0, tiled=True)  7.13 us
  transfers between devices with their start and end apart: 50, of which 25 were waited for; matrix products, arithmetic and copies ran while one was open for 6% of the time, Pallas kernels for 7%

profile of v4, /device:TPU:1, one launch (start us, length us, event | category | flops | bytes accessed | tf_op | source)
XLA Modules:
  0.0 258.1 jit_solution(16338775653079834935)
XLA Ops:
  0.6 4.7 %collective-permute-start.7 = (bf16[256,3072]{1,0:T(8,128)(2,1)}, bf16[256,3072]{1,0:T(8,128)(2,1)}, u32[]{:S(2)}, u32[]{:S(2)}) collective-permute-start(bf16[256,3072]{1,0:T(8,128)(2,1)} %refs_2_.3), channel_id=1, source_target_pairs={{8,0},{16,8},{24,16},{0,24},{40,32},{48,40},{56,48},{32,56},{72,64... | collective-permute-start | bytes 4718600 | tf_op jit(solution)/shard_map/ppermute | solution.py:28
  5.3 2.7 %collective-permute-start.14 = (bf16[256,3072]{1,0:T(8,128)(2,1)}, bf16[256,3072]{1,0:T(8,128)(2,1)}, u32[]{:S(2)}, u32[]{:S(2)}) collective-permute-start(bf16[256,3072]{1,0:T(8,128)(2,1)} %refs_2_.3), channel_id=1, source_target_pairs={{32,0},{40,8},{48,16},{56,24},{64,32},{72,40},{80,48},{88,56},{96,... | collective-permute-start | bytes 4718600 | tf_op jit(solution)/shard_map/ppermute | solution.py:28
  8.7 3.1 %collective-permute-start.9 = (s32[16]{0:T(128)S(1)}, s32[16]{0:T(128)S(1)}, u32[]{:S(2)}, u32[]{:S(2)}) collective-permute-start(s32[16]{0:T(128)S(1)} %slice.37), channel_id=1, source_target_pairs={{1,0},{2,1},{3,2},{4,3},{5,4},{6,5},{7,6},{9,8},{10,9},{11,10},{12... | collective-permute-start | bytes 200 | tf_op jit(solution)/shard_map/ppermute | solution.py:39
  12.6 1.9 collective-permute-done.9
  14.6 1.9 collective-permute-start.10
  17.6 2.1 collective-permute-start.8
  19.7 3.5 %collective-permute-done.8 = bf16[16,512]{1,0:T(8,128)(2,1)S(1)} collective-permute-done((bf16[16,512]{1,0:T(8,128)(2,1)S(1)}, bf16[16,512]{1,0:T(8,128)(2,1)S(1)}, u32[]{:S(2)}, u32[]{:S(2)}) %collective-permute-start.8) | collective-permute-done | bytes 16416 | tf_op jit(solution)/shard_map/ppermute | solution.py:39
  23.1 15.5 %collective-permute-done.7.refs_4_ = bf16[256,3072]{1,0:T(8,128)(2,1)} collective-permute-done((bf16[256,3072]{1,0:T(8,128)(2,1)}, bf16[256,3072]{1,0:T(8,128)(2,1)}, u32[]{:S(2)}, u32[]{:S(2)}) %collective-permute-start.7) | collective-permute-done | bytes 1572896 | tf_op jit(solution)/shard_map/ppermute | solution.py:28
  38.7 2.4 collective-permute-done.14.refs_6_
  41.1 3.4 %collective-permute-start.11 = (bf16[256,3072]{1,0:T(8,128)(2,1)}, bf16[256,3072]{1,0:T(8,128)(2,1)}, u32[]{:S(2)}, u32[]{:S(2)}) collective-permute-start(bf16[256,3072]{1,0:T(8,128)(2,1)} %collective-permute-done.7.refs_4_), channel_id=1, source_target_pairs={{32,0},{40,8},{48,16},{56,24},{64,32},{72,40},{80,48},{88,56},{96,... | collective-permute-start | bytes 4718600 | tf_op jit(solution)/shard_map/ppermute | solution.py:28
  44.5 2.7 %collective-permute-start.15 = (bf16[256,3072]{1,0:T(8,128)(2,1)}, bf16[256,3072]{1,0:T(8,128)(2,1)}, u32[]{:S(2)}, u32[]{:S(2)}) collective-permute-start(bf16[256,3072]{1,0:T(8,128)(2,1)} %collective-permute-done.5.refs_5_), channel_id=1, source_target_pairs={{8,0},{16,8},{24,16},{0,24},{40,32},{48,40},{56,48},{32,56},{72,64... | collective-permute-start | bytes 4718600 | tf_op jit(solution)/shard_map/ppermute | solution.py:28
  48.2 1.1 pad_maximum_fusion.refs_0_
  50.3 7.1 %all-to-all-start = ((bf16[8,2,48,640]{3,2,1,0:T(8,128)(2,1)}), bf16[8,2,48,640]{3,2,1,0:T(8,128)(2,1)}, u32[]{:S(2)}, u32[]{:S(2)}) async-start(bf16[8,2,48,640]{3,2,1,0:T(8,128)(2,1)} %copy-done.3), calls=%async_computation | async-start | bytes 1966080 | tf_op jit(solution)/shard_map/all_to_all | solution.py:488
  57.5 20.5 %collective-permute-done.16.refs_10_ = bf16[256,3072]{1,0:T(8,128)(2,1)} collective-permute-done((bf16[256,3072]{1,0:T(8,128)(2,1)}, bf16[256,3072]{1,0:T(8,128)(2,1)}, u32[]{:S(2)}, u32[]{:S(2)}) %collective-permute-start.16) | collective-permute-done | bytes 1572896 | tf_op jit(solution)/shard_map/ppermute | solution.py:28
  77.9 2.7 %collective-permute-start.13 = (bf16[256,3072]{1,0:T(8,128)(2,1)}, bf16[256,3072]{1,0:T(8,128)(2,1)}, u32[]{:S(2)}, u32[]{:S(2)}) collective-permute-start(bf16[256,3072]{1,0:T(8,128)(2,1)} %collective-permute-done.11.refs_9_), channel_id=1, source_target_pairs={{8,0},{16,8},{24,16},{0,24},{40,32},{48,40},{56,48},{32,56},{72,64... | collective-permute-start | bytes 4718600 | tf_op jit(solution)/shard_map/ppermute | solution.py:28
  80.6 2.1 collective-permute-start.12
  82.7 1.4 copy-done.2
  84.1 12.5 %project.3 = (bf16[4,9,32,512]{3,2,1,0:T(8,128)(2,1)S(1)}, f32[4,9,32,512]{3,2,1,0:T(8,128)S(1)}) custom-call(s32[1]{0:T(128)} %bitcast.17.refs_0_, bf16[3072,512]{1,0:T(8,128)(2,1)S(1)} %copy-done, bf16[256,3072]{1,0:T(8,128)(2,1)S(1)} %copy-done.2, bf16[256,3072]{1,0:T(8,128)(2,1)} %collective-permute-done.refs_3_, ...), custom_call_target="tpu_custom_call" | custom-call | flops 1 | bytes 1 | tf_op jit(solution)/shard_map/project/pallas_call | solution.py:314
  96.6 6.1 %collective-permute-start.17 = (bf16[4,9,32,512]{3,2,1,0:T(8,128)(2,1)S(1)}, bf16[4,9,32,512]{3,2,1,0:T(8,128)(2,1)S(1)}, u32[]{:S(2)}, u32[]{:S(2)}) collective-permute-start(bf16[4,9,32,512]{3,2,1,0:T(8,128)(2,1)S(1)} %get-tuple-element.45), channel_id=1, source_target_pairs={{0,1},{1,0},{2,3},{3,2},{4,5},{5,4},{6,7},{7,6},{8,9},{9,8},{10,11... | collective-permute-start | bytes 3538952 | tf_op jit(solution)/shard_map/ppermute | solution.py:33
  102.7 2.5 collective-permute-done.17
  105.2 1.9 convert_add_fusion
  107.1 8.5 %collective-permute-done.6.refs_3_.refs_12_ = bf16[256,3072]{1,0:T(8,128)(2,1)} collective-permute-done((bf16[256,3072]{1,0:T(8,128)(2,1)}, bf16[256,3072]{1,0:T(8,128)(2,1)}, u32[]{:S(2)}, u32[]{:S(2)}) %collective-permute-start.6) | collective-permute-done | bytes 1572896 | tf_op jit(solution)/shard_map/ppermute | solution.py:28
  115.6 2.7 %collective-permute-start.18 = (bf16[256,3072]{1,0:T(8,128)(2,1)}, bf16[256,3072]{1,0:T(8,128)(2,1)}, u32[]{:S(2)}, u32[]{:S(2)}) collective-permute-start(bf16[256,3072]{1,0:T(8,128)(2,1)} %collective-permute-done.12.refs_4_.refs_13_), channel_id=1, source_target_pairs={{8,0},{16,8},{24,16},{0,24},{40,32},{48,40},{56,48},{32,56},{72,64... | collective-permute-start | bytes 4718600 | tf_op jit(solution)/shard_map/ppermute | solution.py:28
  118.3 2.4 fusion.9
  120.8 1.2 collective-permute-start.19
  122.0 2.5 collective-permute-start.21
  124.5 1.0 slice_convert_fusion.1.keep_ref.refs_2_
  125.4 2.8 %collective-permute-done.19 = bf16[9,32,512]{2,1,0:T(8,128)(2,1)} collective-permute-done((bf16[9,32,512]{2,1,0:T(8,128)(2,1)}, bf16[9,32,512]{2,1,0:T(8,128)(2,1)}, u32[]{:S(2)}, u32[]{:S(2)}) %collective-permute-start.19) | collective-permute-done | bytes 294944 | tf_op jit(solution)/shard_map/ppermute | solution.py:33
  128.2 1.3 collective-permute-start.20
  129.5 1.1 fusion.15
  130.7 6.4 %project.4 = (bf16[4,4,32,512]{3,2,1,0:T(8,128)(2,1)S(1)}, f32[4,4,32,512]{3,2,1,0:T(8,128)S(1)}) custom-call(s32[1]{0:T(128)} %bitcast.17.refs_0_, bf16[3072,512]{1,0:T(8,128)(2,1)S(1)} %copy-done, bf16[256,3072]{1,0:T(8,128)(2,1)} %collective-permute-done.4.refs_2_.refs_11_, bf16[256,3072]{1,0:T(8,128)(2,1)} %collective-permute-done.6.refs_3_.refs_12_, ...), custom_call_target="tpu_custom_call" | custom-call | flops 1 | bytes 1 | tf_op jit(solution)/shard_map/project/pallas_call | solution.py:314
  137.0 8.6 %collective-permute-start.22 = (bf16[4,4,32,512]{3,2,1,0:T(8,128)(2,1)S(1)}, bf16[4,4,32,512]{3,2,1,0:T(8,128)(2,1)S(1)}, u32[]{:S(2)}, u32[]{:S(2)}) collective-permute-start(bf16[4,4,32,512]{3,2,1,0:T(8,128)(2,1)S(1)} %get-tuple-element.52), channel_id=1, source_target_pairs={{0,1},{1,0},{2,3},{3,2},{4,5},{5,4},{6,7},{7,6},{8,9},{9,8},{10,11... | collective-permute-start | bytes 1572872 | tf_op jit(solution)/shard_map/ppermute | solution.py:33
  145.7 2.6 %slice_convert_fusion.target_ref.refs_1_ = f32[16,48,512]{2,1,0:T(8,128)} fusion(bf16[16,48,640]{2,1,0:T(8,128)(2,1)} %bitcast.22), kind=kLoop, calls=%fused_computation.10 | loop fusion | flops 393216 | bytes 2359296 | tf_op jit(solution)/shard_map/convert_element_type | solution.py:491
  148.3 1.5 bitcast_add_fusion.refs_2_
  150.0 5.1 %project.5 = (bf16[4,3,32,512]{3,2,1,0:T(8,128)(2,1)S(1)}, f32[4,3,32,512]{3,2,1,0:T(8,128)S(1)}) custom-call(s32[1]{0:T(128)} %bitcast.17.refs_0_, bf16[3072,512]{1,0:T(8,128)(2,1)S(1)} %copy-done, bf16[256,3072]{1,0:T(8,128)(2,1)} %collective-permute-done.2.refs_2_.refs_15_, bf16[256,3072]{1,0:T(8,128)(2,1)} %collective-permute-done.3.refs_3_.refs_16_, ...), custom_call_target="tpu_custom_call" | custom-call | flops 1 | bytes 1 | tf_op jit(solution)/shard_map/project/pallas_call | solution.py:314
  155.1 4.0 %collective-permute-start.23 = (bf16[4,3,32,512]{3,2,1,0:T(8,128)(2,1)S(1)}, bf16[4,3,32,512]{3,2,1,0:T(8,128)(2,1)S(1)}, u32[]{:S(2)}, u32[]{:S(2)}) collective-permute-start(bf16[4,3,32,512]{3,2,1,0:T(8,128)(2,1)S(1)} %get-tuple-element.60), channel_id=1, source_target_pairs={{0,1},{1,0},{2,3},{3,2},{4,5},{5,4},{6,7},{7,6},{8,9},{9,8},{10,11... | collective-permute-start | bytes 1179656 | tf_op jit(solution)/shard_map/ppermute | solution.py:33
  159.1 1.3 collective-permute-done.23
  160.7 1.3 collective-permute-start.24
  161.9 1.5 collective-permute-start.25
  163.4 1.5 collective-permute-start.26
  165.0 3.8 %collective-permute-done.24 = bf16[7,32,512]{2,1,0:T(8,128)(2,1)S(1)} collective-permute-done((bf16[7,32,512]{2,1,0:T(8,128)(2,1)S(1)}, bf16[7,32,512]{2,1,0:T(8,128)(2,1)S(1)}, u32[]{:S(2)}, u32[]{:S(2)}) %collective-permute-start.24) | collective-permute-done | bytes 229408 | tf_op jit(solution)/shard_map/ppermute | solution.py:33
  168.8 5.9 %collective-permute-done.26 = bf16[7,32,512]{2,1,0:T(8,128)(2,1)S(1)} collective-permute-done((bf16[7,32,512]{2,1,0:T(8,128)(2,1)S(1)}, bf16[7,32,512]{2,1,0:T(8,128)(2,1)S(1)}, u32[]{:S(2)}, u32[]{:S(2)}) %collective-permute-start.26) | collective-permute-done | bytes 229408 | tf_op jit(solution)/shard_map/ppermute | solution.py:33
  174.9 2.0 collective-permute-start.27
  177.8 2.4 collective-permute-done.27.refs_4_
  180.1 2.5 collective-permute-done.28.refs_5_
  184.1 5.3 %products.1 = f32[24,768]{1,0:T(8,128)S(1)} custom-call(f32[16,48,512]{2,1,0:T(8,128)S(1)} %assemble.1.state_ref.refs_0_, f32[16,48,512]{2,1,0:T(8,128)S(1)} %copy-done.1, f32[16,48,1]{2,1,0:T(8,128)S(1)} %slice_convert_fusion.1.keep_ref.refs_2_, f32[3,512]{1,0:T(4,128)S(1)} %copy-done.8), custom_call_target="tpu_custom_call" | custom-call | flops 1 | bytes 1 | tf_op jit(solution)/shard_map/products/pallas_call | solution.py:136
  189.4 1.3 collective-permute-start.31
  190.7 2.1 collective-permute-start.30
  194.2 2.2 collective-permute-done.30
  197.2 2.2 collective-permute-start.32
  199.3 2.1 collective-permute-done.34.refs_8_
  201.8 4.3 %gradients.1 = (bf16[8,32,512]{2,1,0:T(8,128)(2,1)S(1)}, bf16[9,32,512]{2,1,0:T(8,128)(2,1)S(1)}) custom-call(f32[16,48,512]{2,1,0:T(8,128)S(1)} %assemble.1.state_ref.refs_0_, f32[16,48,512]{2,1,0:T(8,128)S(1)} %copy-done.1, f32[16,48,1]{2,1,0:T(8,128)S(1)} %slice_convert_fusion.1.keep_ref.refs_2_, f32[1,768]{1,0:T(1,128)S(1)} %reshape.19.refs_3_, ...), custom_call_target="tpu_custom_call" | custom-call | flops 1 | bytes 1 | tf_op jit(solution)/shard_map/gradients/pallas_call | solution.py:274
  206.2 4.5 %collective-permute-start.38 = (bf16[9,32,512]{2,1,0:T(8,128)(2,1)S(1)}, bf16[9,32,512]{2,1,0:T(8,128)(2,1)S(1)}, u32[]{:S(2)}, u32[]{:S(2)}) collective-permute-start(bf16[9,32,512]{2,1,0:T(8,128)(2,1)S(1)} %get-tuple-element.67.refs_19_), channel_id=1, source_target_pairs={{0,6},{1,7},{2,0},{3,1},{4,2},{5,3},{6,4},{7,5},{8,14},{9,15},{10,... | collective-permute-start | bytes 884744 | tf_op jit(solution)/shard_map/ppermute | solution.py:33
  210.7 1.0 collective-permute-start.41
  211.7 1.5 collective-permute-start.35
  213.7 2.6 %collective-permute-done.38.refs_23_ = bf16[9,32,512]{2,1,0:T(8,128)(2,1)S(1)} collective-permute-done((bf16[9,32,512]{2,1,0:T(8,128)(2,1)S(1)}, bf16[9,32,512]{2,1,0:T(8,128)(2,1)S(1)}, u32[]{:S(2)}, u32[]{:S(2)}) %collective-permute-start.38) | collective-permute-done | bytes 294944 | tf_op jit(solution)/shard_map/ppermute | solution.py:33
  216.3 3.4 %collective-permute-start.40 = (bf16[9,32,512]{2,1,0:T(8,128)(2,1)S(1)}, bf16[9,32,512]{2,1,0:T(8,128)(2,1)S(1)}, u32[]{:S(2)}, u32[]{:S(2)}) collective-permute-start(bf16[9,32,512]{2,1,0:T(8,128)(2,1)S(1)} %collective-permute-done.38.refs_23_), channel_id=1, source_target_pairs={{0,6},{1,7},{2,0},{3,1},{4,2},{5,3},{6,4},{7,5},{8,14},{9,15},{10,... | collective-permute-start | bytes 884744 | tf_op jit(solution)/shard_map/ppermute | solution.py:33
  219.7 2.2 collective-permute-done.37.refs_22_
  221.9 2.8 %collective-permute-start.45 = (bf16[8,32,512]{2,1,0:T(8,128)(2,1)S(1)}, bf16[8,32,512]{2,1,0:T(8,128)(2,1)S(1)}, u32[]{:S(2)}, u32[]{:S(2)}) collective-permute-start(bf16[8,32,512]{2,1,0:T(8,128)(2,1)S(1)} %collective-permute-done.37.refs_22_), channel_id=1, source_target_pairs={{0,1},{1,0},{2,3},{3,2},{4,5},{5,4},{6,7},{7,6},{8,9},{9,8},{10,11... | collective-permute-start | bytes 786440 | tf_op jit(solution)/shard_map/ppermute | solution.py:33
  224.9 2.0 collective-permute-done.36.refs_21_
  226.9 1.0 collective-permute-start.44
  228.3 1.6 collective-permute-start.48
  229.9 4.9 %collective-permute-done.39.refs_24_ = bf16[8,32,512]{2,1,0:T(8,128)(2,1)} collective-permute-done((bf16[8,32,512]{2,1,0:T(8,128)(2,1)S(1)}, bf16[8,32,512]{2,1,0:T(8,128)(2,1)}, u32[]{:S(2)}, u32[]{:S(2)}) %collective-permute-start.39) | collective-permute-done | bytes 262176 | tf_op jit(solution)/shard_map/ppermute | solution.py:33
  237.8 20.1 %weight_gradient.1 = (f32[3072,512]{1,0:T(8,128)}, f32[1,128]{1,0:T(1,128)}) custom-call(s32[16]{0:T(128)} %select_reduce_fusion.refs_0_, s32[8]{0:T(128)} %stack.113.refs_1_, bf16[256,3072]{1,0:T(8,128)(2,1)} %refs_2_.3, bf16[256,3072]{1,0:T(8,128)(2,1)} %collective-permute-done.refs_3_, bf16[256,3072]{1,0:T(8,128)(2,1)} %collective-permute-done.7.refs_4_, ...), custom_call_target="tpu_custom_call" | custom-call | flops 1 | bytes 1 | tf_op jit(solution)/shard_map/weight_gradient/pallas_call | solution.py:398
  (111 shorter events, 14.2 us)
Async XLA Ops:
  0.6 38.0 %collective-permute-start.7 = (bf16[256,3072]{1,0:T(8,128)(2,1)}, bf16[256,3072]{1,0:T(8,128)(2,1)}, u32[]{:S(2)}, u32[]{:S(2)}) collective-permute-start(bf16[256,3072]{1,0:T(8,128)(2,1)} %refs_2_.3), channel_id=1, source_target_pairs={{8,0},{16,8},{24,16},{0,24},{40,32},{48,40},{56,48},{32,56},{72,64... | collective-permute-start | bytes 4718600 | tf_op jit(solution)/shard_map/ppermute | solution.py:28
  5.3 35.8 %collective-permute-start.14 = (bf16[256,3072]{1,0:T(8,128)(2,1)}, bf16[256,3072]{1,0:T(8,128)(2,1)}, u32[]{:S(2)}, u32[]{:S(2)}) collective-permute-start(bf16[256,3072]{1,0:T(8,128)(2,1)} %refs_2_.3), channel_id=1, source_target_pairs={{32,0},{40,8},{48,16},{56,24},{64,32},{72,40},{80,48},{88,56},{96,... | collective-permute-start | bytes 4718600 | tf_op jit(solution)/shard_map/ppermute | solution.py:28
  8.0 36.5 %collective-permute-start.5 = (bf16[256,3072]{1,0:T(8,128)(2,1)}, bf16[256,3072]{1,0:T(8,128)(2,1)}, u32[]{:S(2)}, u32[]{:S(2)}) collective-permute-start(bf16[256,3072]{1,0:T(8,128)(2,1)} %refs_2_.3), channel_id=1, source_target_pairs={{96,0},{104,8},{112,16},{120,24},{0,32},{8,40},{16,48},{24,56},{32... | collective-permute-start | bytes 4718600 | tf_op jit(solution)/shard_map/ppermute | solution.py:28
  8.0 39.2 %collective-permute-start = (bf16[256,3072]{1,0:T(8,128)(2,1)}, bf16[256,3072]{1,0:T(8,128)(2,1)}, u32[]{:S(2)}, u32[]{:S(2)}) collective-permute-start(bf16[256,3072]{1,0:T(8,128)(2,1)} %refs_2_.3), channel_id=1, source_target_pairs={{24,0},{0,8},{8,16},{16,24},{56,32},{32,40},{40,48},{48,56},{88,64... | collective-permute-start | bytes 4718600 | tf_op jit(solution)/shard_map/ppermute | solution.py:28
  8.7 5.8 %collective-permute-start.9 = (s32[16]{0:T(128)S(1)}, s32[16]{0:T(128)S(1)}, u32[]{:S(2)}, u32[]{:S(2)}) collective-permute-start(s32[16]{0:T(128)S(1)} %slice.37), channel_id=1, source_target_pairs={{1,0},{2,1},{3,2},{4,3},{5,4},{6,5},{7,6},{9,8},{10,9},{11,10},{12... | collective-permute-start | bytes 200 | tf_op jit(solution)/shard_map/ppermute | solution.py:39
  14.6 3.0 %collective-permute-start.10 = (s32[17]{0:T(128)S(1)}, s32[17]{0:T(128)S(1)}, u32[]{:S(2)}, u32[]{:S(2)}) collective-permute-start(s32[17]{0:T(128)S(1)} %slice.38), channel_id=1, source_target_pairs={{0,1},{1,2},{2,3},{3,4},{4,5},{5,6},{6,7},{8,9},{9,10},{10,11},{11... | collective-permute-start | bytes 212 | tf_op jit(solution)/shard_map/ppermute | solution.py:39
  17.6 5.6 %collective-permute-start.8 = (bf16[16,512]{1,0:T(8,128)(2,1)S(1)}, bf16[16,512]{1,0:T(8,128)(2,1)S(1)}, u32[]{:S(2)}, u32[]{:S(2)}) collective-permute-start(bf16[16,512]{1,0:T(8,128)(2,1)S(1)} %slice.36), channel_id=1, source_target_pairs={{1,0},{2,1},{3,2},{4,3},{5,4},{6,5},{7,6},{9,8},{10,9},{11,10},{12... | collective-permute-start | bytes 49160 | tf_op jit(solution)/shard_map/ppermute | solution.py:39
  41.1 36.8 %collective-permute-start.16 = (bf16[256,3072]{1,0:T(8,128)(2,1)}, bf16[256,3072]{1,0:T(8,128)(2,1)}, u32[]{:S(2)}, u32[]{:S(2)}) collective-permute-start(bf16[256,3072]{1,0:T(8,128)(2,1)} %collective-permute-done.14.refs_6_), channel_id=1, source_target_pairs={{24,0},{0,8},{8,16},{16,24},{56,32},{32,40},{40,48},{48,56},{88,64... | collective-permute-start | bytes 4718600 | tf_op jit(solution)/shard_map/ppermute | solution.py:28
  41.1 36.8 %collective-permute-start.11 = (bf16[256,3072]{1,0:T(8,128)(2,1)}, bf16[256,3072]{1,0:T(8,128)(2,1)}, u32[]{:S(2)}, u32[]{:S(2)}) collective-permute-start(bf16[256,3072]{1,0:T(8,128)(2,1)} %collective-permute-done.7.refs_4_), channel_id=1, source_target_pairs={{32,0},{40,8},{48,16},{56,24},{64,32},{72,40},{80,48},{88,56},{96,... | collective-permute-start | bytes 4718600 | tf_op jit(solution)/shard_map/ppermute | solution.py:28
  44.5 36.1 %collective-permute-start.15 = (bf16[256,3072]{1,0:T(8,128)(2,1)}, bf16[256,3072]{1,0:T(8,128)(2,1)}, u32[]{:S(2)}, u32[]{:S(2)}) collective-permute-start(bf16[256,3072]{1,0:T(8,128)(2,1)} %collective-permute-done.5.refs_5_), channel_id=1, source_target_pairs={{8,0},{16,8},{24,16},{0,24},{40,32},{48,40},{56,48},{32,56},{72,64... | collective-permute-start | bytes 4718600 | tf_op jit(solution)/shard_map/ppermute | solution.py:28
  47.2 35.6 %collective-permute-start.1 = (bf16[256,3072]{1,0:T(8,128)(2,1)}, bf16[256,3072]{1,0:T(8,128)(2,1)}, u32[]{:S(2)}, u32[]{:S(2)}) collective-permute-start(bf16[256,3072]{1,0:T(8,128)(2,1)} %collective-permute-done.refs_3_), channel_id=1, source_target_pairs={{96,0},{104,8},{112,16},{120,24},{0,32},{8,40},{16,48},{24,56},{32... | collective-permute-start | bytes 4718600 | tf_op jit(solution)/shard_map/ppermute | solution.py:28
  49.3 33.5 %copy-start = (bf16[3072,512]{1,0:T(8,128)(2,1)S(1)}, bf16[3072,512]{1,0:T(8,128)(2,1)}, u32[]{:S(2)}) copy-start(bf16[3072,512]{1,0:T(8,128)(2,1)} %refs_1_.5) | copy-start | bytes 9437188
  50.3 32.4 %all-to-all-start = ((bf16[8,2,48,640]{3,2,1,0:T(8,128)(2,1)}), bf16[8,2,48,640]{3,2,1,0:T(8,128)(2,1)}, u32[]{:S(2)}, u32[]{:S(2)}) async-start(bf16[8,2,48,640]{3,2,1,0:T(8,128)(2,1)} %copy-done.3), calls=%async_computation | async-start | bytes 1966080 | tf_op jit(solution)/shard_map/all_to_all | solution.py:488
  57.5 58.1 %collective-permute-start.6 = (bf16[256,3072]{1,0:T(8,128)(2,1)}, bf16[256,3072]{1,0:T(8,128)(2,1)}, u32[]{:S(2)}, u32[]{:S(2)}) collective-permute-start(bf16[256,3072]{1,0:T(8,128)(2,1)} %collective-permute-done.5.refs_5_), channel_id=1, source_target_pairs={{96,0},{104,8},{112,16},{120,24},{0,32},{8,40},{16,48},{24,56},{32... | collective-permute-start | bytes 4718600 | tf_op jit(solution)/shard_map/ppermute | solution.py:28
  77.9 37.7 %collective-permute-start.4 = (bf16[256,3072]{1,0:T(8,128)(2,1)}, bf16[256,3072]{1,0:T(8,128)(2,1)}, u32[]{:S(2)}, u32[]{:S(2)}) collective-permute-start(bf16[256,3072]{1,0:T(8,128)(2,1)} %collective-permute-done.refs_3_), channel_id=1, source_target_pairs={{24,0},{0,8},{8,16},{16,24},{56,32},{32,40},{40,48},{48,56},{88,64... | collective-permute-start | bytes 4718600 | tf_op jit(solution)/shard_map/ppermute | solution.py:28
  77.9 37.7 %collective-permute-start.13 = (bf16[256,3072]{1,0:T(8,128)(2,1)}, bf16[256,3072]{1,0:T(8,128)(2,1)}, u32[]{:S(2)}, u32[]{:S(2)}) collective-permute-start(bf16[256,3072]{1,0:T(8,128)(2,1)} %collective-permute-done.11.refs_9_), channel_id=1, source_target_pairs={{8,0},{16,8},{24,16},{0,24},{40,32},{48,40},{56,48},{32,56},{72,64... | collective-permute-start | bytes 4718600 | tf_op jit(solution)/shard_map/ppermute | solution.py:28
  80.6 35.0 %collective-permute-start.12 = (bf16[256,3072]{1,0:T(8,128)(2,1)}, bf16[256,3072]{1,0:T(8,128)(2,1)}, u32[]{:S(2)}, u32[]{:S(2)}) collective-permute-start(bf16[256,3072]{1,0:T(8,128)(2,1)} %collective-permute-done.11.refs_9_), channel_id=1, source_target_pairs={{32,0},{40,8},{48,16},{56,24},{64,32},{72,40},{80,48},{88,56},{96,... | collective-permute-start | bytes 4718600 | tf_op jit(solution)/shard_map/ppermute | solution.py:28
  82.7 1.4 copy-start.2
  96.6 8.6 %collective-permute-start.17 = (bf16[4,9,32,512]{3,2,1,0:T(8,128)(2,1)S(1)}, bf16[4,9,32,512]{3,2,1,0:T(8,128)(2,1)S(1)}, u32[]{:S(2)}, u32[]{:S(2)}) collective-permute-start(bf16[4,9,32,512]{3,2,1,0:T(8,128)(2,1)S(1)} %get-tuple-element.45), channel_id=1, source_target_pairs={{0,1},{1,0},{2,3},{3,2},{4,5},{5,4},{6,7},{7,6},{8,9},{9,8},{10,11... | collective-permute-start | bytes 3538952 | tf_op jit(solution)/shard_map/ppermute | solution.py:33
  105.2 44.8 %collective-permute-start.3 = (bf16[256,3072]{1,0:T(8,128)(2,1)}, bf16[256,3072]{1,0:T(8,128)(2,1)}, u32[]{:S(2)}, u32[]{:S(2)}) collective-permute-start(bf16[256,3072]{1,0:T(8,128)(2,1)} %collective-permute-done.1.refs_7_), channel_id=1, source_target_pairs={{96,0},{104,8},{112,16},{120,24},{0,32},{8,40},{16,48},{24,56},{32... | collective-permute-start | bytes 4718600 | tf_op jit(solution)/shard_map/ppermute | solution.py:28
  115.6 34.4 %collective-permute-start.2 = (bf16[256,3072]{1,0:T(8,128)(2,1)}, bf16[256,3072]{1,0:T(8,128)(2,1)}, u32[]{:S(2)}, u32[]{:S(2)}) collective-permute-start(bf16[256,3072]{1,0:T(8,128)(2,1)} %collective-permute-done.1.refs_7_), channel_id=1, source_target_pairs={{24,0},{0,8},{8,16},{16,24},{56,32},{32,40},{40,48},{48,56},{88,64... | collective-permute-start | bytes 4718600 | tf_op jit(solution)/shard_map/ppermute | solution.py:28
  115.6 34.4 %collective-permute-start.18 = (bf16[256,3072]{1,0:T(8,128)(2,1)}, bf16[256,3072]{1,0:T(8,128)(2,1)}, u32[]{:S(2)}, u32[]{:S(2)}) collective-permute-start(bf16[256,3072]{1,0:T(8,128)(2,1)} %collective-permute-done.12.refs_4_.refs_13_), channel_id=1, source_target_pairs={{8,0},{16,8},{24,16},{0,24},{40,32},{48,40},{56,48},{32,56},{72,64... | collective-permute-start | bytes 4718600 | tf_op jit(solution)/shard_map/ppermute | solution.py:28
  120.8 7.4 %collective-permute-start.19 = (bf16[9,32,512]{2,1,0:T(8,128)(2,1)}, bf16[9,32,512]{2,1,0:T(8,128)(2,1)}, u32[]{:S(2)}, u32[]{:S(2)}) collective-permute-start(bf16[9,32,512]{2,1,0:T(8,128)(2,1)} %get-tuple-element.70), channel_id=1, source_target_pairs={{0,2},{1,3},{2,4},{3,5},{4,6},{5,7},{6,0},{7,1},{8,10},{9,11},{10,... | collective-permute-start | bytes 884744 | tf_op jit(solution)/shard_map/ppermute | solution.py:33
  122.0 15.0 %collective-permute-start.21 = (bf16[9,32,512]{2,1,0:T(8,128)(2,1)}, bf16[9,32,512]{2,1,0:T(8,128)(2,1)}, u32[]{:S(2)}, u32[]{:S(2)}) collective-permute-start(bf16[9,32,512]{2,1,0:T(8,128)(2,1)} %get-tuple-element.71), channel_id=1, source_target_pairs={{0,4},{1,5},{2,6},{3,7},{4,0},{5,1},{6,2},{7,3},{8,12},{9,13},{10,... | collective-permute-start | bytes 884744 | tf_op jit(solution)/shard_map/ppermute | solution.py:33
  128.2 20.1 %collective-permute-start.20 = (bf16[9,32,512]{2,1,0:T(8,128)(2,1)}, bf16[9,32,512]{2,1,0:T(8,128)(2,1)}, u32[]{:S(2)}, u32[]{:S(2)}) collective-permute-start(bf16[9,32,512]{2,1,0:T(8,128)(2,1)} %get-tuple-element.72), channel_id=1, source_target_pairs={{0,6},{1,7},{2,0},{3,1},{4,2},{5,3},{6,4},{7,5},{8,14},{9,15},{10,... | collective-permute-start | bytes 884744 | tf_op jit(solution)/shard_map/ppermute | solution.py:33
  137.0 12.7 %collective-permute-start.22 = (bf16[4,4,32,512]{3,2,1,0:T(8,128)(2,1)S(1)}, bf16[4,4,32,512]{3,2,1,0:T(8,128)(2,1)S(1)}, u32[]{:S(2)}, u32[]{:S(2)}) collective-permute-start(bf16[4,4,32,512]{3,2,1,0:T(8,128)(2,1)S(1)} %get-tuple-element.52), channel_id=1, source_target_pairs={{0,1},{1,0},{2,3},{3,2},{4,5},{5,4},{6,7},{7,6},{8,9},{9,8},{10,11... | collective-permute-start | bytes 1572872 | tf_op jit(solution)/shard_map/ppermute | solution.py:33
  149.8 15.2 %copy-start.4 = (f32[9,32,512]{2,1,0:T(8,128)}, f32[9,32,512]{2,1,0:T(8,128)S(1)}, u32[]{:S(2)}) copy-start(f32[9,32,512]{2,1,0:T(8,128)S(1)} %bitcast_add_fusion.refs_2_) | copy-start | bytes 1769476
  155.1 5.4 %collective-permute-start.23 = (bf16[4,3,32,512]{3,2,1,0:T(8,128)(2,1)S(1)}, bf16[4,3,32,512]{3,2,1,0:T(8,128)(2,1)S(1)}, u32[]{:S(2)}, u32[]{:S(2)}) collective-permute-start(bf16[4,3,32,512]{3,2,1,0:T(8,128)(2,1)S(1)} %get-tuple-element.60), channel_id=1, source_target_pairs={{0,1},{1,0},{2,3},{3,2},{4,5},{5,4},{6,7},{7,6},{8,9},{9,8},{10,11... | collective-permute-start | bytes 1179656 | tf_op jit(solution)/shard_map/ppermute | solution.py:33
  160.7 8.1 %collective-permute-start.24 = (bf16[7,32,512]{2,1,0:T(8,128)(2,1)S(1)}, bf16[7,32,512]{2,1,0:T(8,128)(2,1)S(1)}, u32[]{:S(2)}, u32[]{:S(2)}) collective-permute-start(bf16[7,32,512]{2,1,0:T(8,128)(2,1)S(1)} %get-tuple-element.73), channel_id=1, source_target_pairs={{0,2},{1,3},{2,4},{3,5},{4,6},{5,7},{6,0},{7,1},{8,10},{9,11},{10,... | collective-permute-start | bytes 688136 | tf_op jit(solution)/shard_map/ppermute | solution.py:33
  161.9 6.8 %collective-permute-start.25 = (bf16[7,32,512]{2,1,0:T(8,128)(2,1)S(1)}, bf16[7,32,512]{2,1,0:T(8,128)(2,1)S(1)}, u32[]{:S(2)}, u32[]{:S(2)}) collective-permute-start(bf16[7,32,512]{2,1,0:T(8,128)(2,1)S(1)} %get-tuple-element.74), channel_id=1, source_target_pairs={{0,6},{1,7},{2,0},{3,1},{4,2},{5,3},{6,4},{7,5},{8,14},{9,15},{10,... | collective-permute-start | bytes 688136 | tf_op jit(solution)/shard_map/ppermute | solution.py:33
  163.4 11.3 %collective-permute-start.26 = (bf16[7,32,512]{2,1,0:T(8,128)(2,1)S(1)}, bf16[7,32,512]{2,1,0:T(8,128)(2,1)S(1)}, u32[]{:S(2)}, u32[]{:S(2)}) collective-permute-start(bf16[7,32,512]{2,1,0:T(8,128)(2,1)S(1)} %get-tuple-element.75), channel_id=1, source_target_pairs={{0,4},{1,5},{2,6},{3,7},{4,0},{5,1},{6,2},{7,3},{8,12},{9,13},{10,... | collective-permute-start | bytes 688136 | tf_op jit(solution)/shard_map/ppermute | solution.py:33
  174.8 7.9 %copy-start.5 = (f32[9,32,512]{2,1,0:T(8,128)S(1)}, f32[9,32,512]{2,1,0:T(8,128)}, u32[]{:S(2)}) copy-start(f32[9,32,512]{2,1,0:T(8,128)} %copy-done.4) | copy-start | bytes 1769476
  174.9 5.3 %collective-permute-start.27 = (f32[16,8,512]{2,1,0:T(8,128)S(1)}, f32[16,8,512]{2,1,0:T(8,128)S(1)}, u32[]{:S(2)}, u32[]{:S(2)}) collective-permute-start(f32[16,8,512]{2,1,0:T(8,128)S(1)} %pad_maximum_fusion.1), channel_id=1, source_target_pairs={{7,0},{0,1},{1,2},{2,3},{3,4},{4,5},{5,6},{6,7},{15,8},{8,9},{9,10... | collective-permute-start | bytes 786440 | tf_op jit(solution)/shard_map/ppermute | solution.py:434
  176.8 5.8 %collective-permute-start.28 = (f32[16,8,512]{2,1,0:T(8,128)S(1)}, f32[16,8,512]{2,1,0:T(8,128)S(1)}, u32[]{:S(2)}, u32[]{:S(2)}) collective-permute-start(f32[16,8,512]{2,1,0:T(8,128)S(1)} %pad_maximum_fusion.2), channel_id=1, source_target_pairs={{1,0},{2,1},{3,2},{4,3},{5,4},{6,5},{7,6},{0,7},{9,8},{10,9},{11,1... | collective-permute-start | bytes 786440 | tf_op jit(solution)/shard_map/ppermute | solution.py:434
  189.4 4.8 %collective-permute-start.31 = (f32[24,768]{1,0:T(8,128)S(1)}, f32[24,768]{1,0:T(8,128)S(1)}, u32[]{:S(2)}, u32[]{:S(2)}) collective-permute-start(f32[24,768]{1,0:T(8,128)S(1)} %products.1), channel_id=1, source_target_pairs={{16,0},{24,8},{0,16},{8,24},{48,32},{56,40},{32,48},{40,56},{80,64... | collective-permute-start | bytes 221192 | tf_op jit(solution)/shard_map/ppermute | solution.py:28
  190.7 5.6 %collective-permute-start.30 = (f32[24,768]{1,0:T(8,128)S(1)}, f32[24,768]{1,0:T(8,128)S(1)}, u32[]{:S(2)}, u32[]{:S(2)}) collective-permute-start(f32[24,768]{1,0:T(8,128)S(1)} %products.1), channel_id=1, source_target_pairs={{24,0},{0,8},{8,16},{16,24},{56,32},{32,40},{40,48},{48,56},{88,64... | collective-permute-start | bytes 221192 | tf_op jit(solution)/shard_map/ppermute | solution.py:28
  192.8 3.7 %collective-permute-start.29 = (f32[24,768]{1,0:T(8,128)S(1)}, f32[24,768]{1,0:T(8,128)S(1)}, u32[]{:S(2)}, u32[]{:S(2)}) collective-permute-start(f32[24,768]{1,0:T(8,128)S(1)} %products.1), channel_id=1, source_target_pairs={{8,0},{16,8},{24,16},{0,24},{40,32},{48,40},{56,48},{32,56},{72,64... | collective-permute-start | bytes 221192 | tf_op jit(solution)/shard_map/ppermute | solution.py:28
  196.5 4.9 %collective-permute-start.34 = (f32[24,768]{1,0:T(8,128)S(1)}, f32[24,768]{1,0:T(8,128)S(1)}, u32[]{:S(2)}, u32[]{:S(2)}) collective-permute-start(f32[24,768]{1,0:T(8,128)S(1)} %add_add_fusion.refs_5_), channel_id=1, source_target_pairs={{64,0},{72,8},{80,16},{88,24},{96,32},{104,40},{112,48},{120,56},{... | collective-permute-start | bytes 221192 | tf_op jit(solution)/shard_map/ppermute | solution.py:28
  196.6 5.3 %collective-permute-start.33 = (f32[24,768]{1,0:T(8,128)S(1)}, f32[24,768]{1,0:T(8,128)S(1)}, u32[]{:S(2)}, u32[]{:S(2)}) collective-permute-start(f32[24,768]{1,0:T(8,128)S(1)} %add_add_fusion.refs_5_), channel_id=1, source_target_pairs={{96,0},{104,8},{112,16},{120,24},{0,32},{8,40},{16,48},{24,56},{32... | collective-permute-start | bytes 221192 | tf_op jit(solution)/shard_map/ppermute | solution.py:28
  197.2 4.7 %collective-permute-start.32 = (f32[24,768]{1,0:T(8,128)S(1)}, f32[24,768]{1,0:T(8,128)S(1)}, u32[]{:S(2)}, u32[]{:S(2)}) collective-permute-start(f32[24,768]{1,0:T(8,128)S(1)} %add_add_fusion.refs_5_), channel_id=1, source_target_pairs={{32,0},{40,8},{48,16},{56,24},{64,32},{72,40},{80,48},{88,56},{96,... | collective-permute-start | bytes 221192 | tf_op jit(solution)/shard_map/ppermute | solution.py:28
  206.2 30.8 %copy-start.6 = (bf16[9,32,512]{2,1,0:T(8,128)(2,1)}, bf16[9,32,512]{2,1,0:T(8,128)(2,1)S(1)}, u32[]{:S(2)}) copy-start(bf16[9,32,512]{2,1,0:T(8,128)(2,1)S(1)} %get-tuple-element.67.refs_19_) | copy-start | bytes 884740
  206.2 30.8 %copy-start.7 = (bf16[8,32,512]{2,1,0:T(8,128)(2,1)}, bf16[8,32,512]{2,1,0:T(8,128)(2,1)S(1)}, u32[]{:S(2)}) copy-start(bf16[8,32,512]{2,1,0:T(8,128)(2,1)S(1)} %get-tuple-element.66.refs_18_) | copy-start | bytes 786436
  206.2 10.1 %collective-permute-start.38 = (bf16[9,32,512]{2,1,0:T(8,128)(2,1)S(1)}, bf16[9,32,512]{2,1,0:T(8,128)(2,1)S(1)}, u32[]{:S(2)}, u32[]{:S(2)}) collective-permute-start(bf16[9,32,512]{2,1,0:T(8,128)(2,1)S(1)} %get-tuple-element.67.refs_19_), channel_id=1, source_target_pairs={{0,6},{1,7},{2,0},{3,1},{4,2},{5,3},{6,4},{7,5},{8,14},{9,15},{10,... | collective-permute-start | bytes 884744 | tf_op jit(solution)/shard_map/ppermute | solution.py:33
  210.7 3.0 %collective-permute-start.41 = (bf16[8,32,512]{2,1,0:T(8,128)(2,1)S(1)}, bf16[8,32,512]{2,1,0:T(8,128)(2,1)S(1)}, u32[]{:S(2)}, u32[]{:S(2)}) collective-permute-start(bf16[8,32,512]{2,1,0:T(8,128)(2,1)S(1)} %get-tuple-element.66.refs_18_), channel_id=1, source_target_pairs={{0,1},{1,0},{2,3},{3,2},{4,5},{5,4},{6,7},{7,6},{8,9},{9,8},{10,11... | collective-permute-start | bytes 786440 | tf_op jit(solution)/shard_map/ppermute | solution.py:33
  211.7 10.3 %collective-permute-start.37 = (bf16[8,32,512]{2,1,0:T(8,128)(2,1)S(1)}, bf16[8,32,512]{2,1,0:T(8,128)(2,1)S(1)}, u32[]{:S(2)}, u32[]{:S(2)}) collective-permute-start(bf16[8,32,512]{2,1,0:T(8,128)(2,1)S(1)} %get-tuple-element.66.refs_18_), channel_id=1, source_target_pairs={{0,6},{1,7},{2,0},{3,1},{4,2},{5,3},{6,4},{7,5},{8,14},{9,15},{10,... | collective-permute-start | bytes 786440 | tf_op jit(solution)/shard_map/ppermute | solution.py:33
  211.7 13.0 %collective-permute-start.35 = (bf16[8,32,512]{2,1,0:T(8,128)(2,1)S(1)}, bf16[8,32,512]{2,1,0:T(8,128)(2,1)S(1)}, u32[]{:S(2)}, u32[]{:S(2)}) collective-permute-start(bf16[8,32,512]{2,1,0:T(8,128)(2,1)S(1)} %get-tuple-element.66.refs_18_), channel_id=1, source_target_pairs={{0,2},{1,3},{2,4},{3,5},{4,6},{5,7},{6,0},{7,1},{8,10},{9,11},{10,... | collective-permute-start | bytes 786440 | tf_op jit(solution)/shard_map/ppermute | solution.py:33
  213.1 11.6 %collective-permute-start.42 = (bf16[9,32,512]{2,1,0:T(8,128)(2,1)S(1)}, bf16[9,32,512]{2,1,0:T(8,128)(2,1)S(1)}, u32[]{:S(2)}, u32[]{:S(2)}) collective-permute-start(bf16[9,32,512]{2,1,0:T(8,128)(2,1)S(1)} %get-tuple-element.67.refs_19_), channel_id=1, source_target_pairs={{0,1},{1,0},{2,3},{3,2},{4,5},{5,4},{6,7},{7,6},{8,9},{9,8},{10,11... | collective-permute-start | bytes 884744 | tf_op jit(solution)/shard_map/ppermute | solution.py:33
  213.7 23.3 %copy-start.16 = (bf16[8,32,512]{2,1,0:T(8,128)(2,1)}, bf16[8,32,512]{2,1,0:T(8,128)(2,1)S(1)}, u32[]{:S(2)}) copy-start(bf16[8,32,512]{2,1,0:T(8,128)(2,1)S(1)} %collective-permute-done.41.refs_26_) | copy-start | bytes 786436
  213.7 13.2 %collective-permute-start.36 = (bf16[9,32,512]{2,1,0:T(8,128)(2,1)S(1)}, bf16[9,32,512]{2,1,0:T(8,128)(2,1)S(1)}, u32[]{:S(2)}, u32[]{:S(2)}) collective-permute-start(bf16[9,32,512]{2,1,0:T(8,128)(2,1)S(1)} %get-tuple-element.67.refs_19_), channel_id=1, source_target_pairs={{0,2},{1,3},{2,4},{3,5},{4,6},{5,7},{6,0},{7,1},{8,10},{9,11},{10,... | collective-permute-start | bytes 884744 | tf_op jit(solution)/shard_map/ppermute | solution.py:33
  216.3 20.7 %copy-start.9 = (bf16[9,32,512]{2,1,0:T(8,128)(2,1)}, bf16[9,32,512]{2,1,0:T(8,128)(2,1)S(1)}, u32[]{:S(2)}) copy-start(bf16[9,32,512]{2,1,0:T(8,128)(2,1)S(1)} %collective-permute-done.38.refs_23_) | copy-start | bytes 884740
  216.3 11.9 %collective-permute-start.40 = (bf16[9,32,512]{2,1,0:T(8,128)(2,1)S(1)}, bf16[9,32,512]{2,1,0:T(8,128)(2,1)S(1)}, u32[]{:S(2)}, u32[]{:S(2)}) collective-permute-start(bf16[9,32,512]{2,1,0:T(8,128)(2,1)S(1)} %collective-permute-done.38.refs_23_), channel_id=1, source_target_pairs={{0,6},{1,7},{2,0},{3,1},{4,2},{5,3},{6,4},{7,5},{8,14},{9,15},{10,... | collective-permute-start | bytes 884744 | tf_op jit(solution)/shard_map/ppermute | solution.py:33
  221.9 15.1 %copy-start.17 = (bf16[8,32,512]{2,1,0:T(8,128)(2,1)}, bf16[8,32,512]{2,1,0:T(8,128)(2,1)S(1)}, u32[]{:S(2)}) copy-start(bf16[8,32,512]{2,1,0:T(8,128)(2,1)S(1)} %collective-permute-done.37.refs_22_) | copy-start | bytes 786436
  221.9 7.9 %collective-permute-start.45 = (bf16[8,32,512]{2,1,0:T(8,128)(2,1)S(1)}, bf16[8,32,512]{2,1,0:T(8,128)(2,1)S(1)}, u32[]{:S(2)}, u32[]{:S(2)}) collective-permute-start(bf16[8,32,512]{2,1,0:T(8,128)(2,1)S(1)} %collective-permute-done.37.refs_22_), channel_id=1, source_target_pairs={{0,1},{1,0},{2,3},{3,2},{4,5},{5,4},{6,7},{7,6},{8,9},{9,8},{10,11... | collective-permute-start | bytes 786440 | tf_op jit(solution)/shard_map/ppermute | solution.py:33
  224.7 12.3 %copy-start.18 = (bf16[8,32,512]{2,1,0:T(8,128)(2,1)}, bf16[8,32,512]{2,1,0:T(8,128)(2,1)S(1)}, u32[]{:S(2)}) copy-start(bf16[8,32,512]{2,1,0:T(8,128)(2,1)S(1)} %collective-permute-done.35.refs_20_) | copy-start | bytes 786436
  224.7 10.1 %collective-permute-start.39 = (bf16[8,32,512]{2,1,0:T(8,128)(2,1)S(1)}, bf16[8,32,512]{2,1,0:T(8,128)(2,1)}, u32[]{:S(2)}, u32[]{:S(2)}) collective-permute-start(bf16[8,32,512]{2,1,0:T(8,128)(2,1)S(1)} %collective-permute-done.35.refs_20_), channel_id=1, source_target_pairs={{0,2},{1,3},{2,4},{3,5},{4,6},{5,7},{6,0},{7,1},{8,10},{9,11},{10,... | collective-permute-start | bytes 786440 | tf_op jit(solution)/shard_map/ppermute | solution.py:33
  224.7 12.3 %copy-start.10 = (bf16[9,32,512]{2,1,0:T(8,128)(2,1)}, bf16[9,32,512]{2,1,0:T(8,128)(2,1)S(1)}, u32[]{:S(2)}) copy-start(bf16[9,32,512]{2,1,0:T(8,128)(2,1)S(1)} %collective-permute-done.42.refs_27_) | copy-start | bytes 884740
  224.7 11.4 %collective-permute-start.46 = (bf16[9,32,512]{2,1,0:T(8,128)(2,1)S(1)}, bf16[9,32,512]{2,1,0:T(8,128)(2,1)S(1)}, u32[]{:S(2)}, u32[]{:S(2)}) collective-permute-start(bf16[9,32,512]{2,1,0:T(8,128)(2,1)S(1)} %collective-permute-done.38.refs_23_), channel_id=1, source_target_pairs={{0,1},{1,0},{2,3},{3,2},{4,5},{5,4},{6,7},{7,6},{8,9},{9,8},{10,11... | collective-permute-start | bytes 884744 | tf_op jit(solution)/shard_map/ppermute | solution.py:33
  226.9 10.1 %copy-start.11 = (bf16[9,32,512]{2,1,0:T(8,128)(2,1)}, bf16[9,32,512]{2,1,0:T(8,128)(2,1)S(1)}, u32[]{:S(2)}) copy-start(bf16[9,32,512]{2,1,0:T(8,128)(2,1)S(1)} %collective-permute-done.36.refs_21_) | copy-start | bytes 884740
  226.9 9.2 %collective-permute-start.44 = (bf16[9,32,512]{2,1,0:T(8,128)(2,1)S(1)}, bf16[9,32,512]{2,1,0:T(8,128)(2,1)S(1)}, u32[]{:S(2)}, u32[]{:S(2)}) collective-permute-start(bf16[9,32,512]{2,1,0:T(8,128)(2,1)S(1)} %collective-permute-done.36.refs_21_), channel_id=1, source_target_pairs={{0,1},{1,0},{2,3},{3,2},{4,5},{5,4},{6,7},{7,6},{8,9},{9,8},{10,11... | collective-permute-start | bytes 884744 | tf_op jit(solution)/shard_map/ppermute | solution.py:33
  228.3 8.8 %copy-start.12 = (bf16[9,32,512]{2,1,0:T(8,128)(2,1)}, bf16[9,32,512]{2,1,0:T(8,128)(2,1)S(1)}, u32[]{:S(2)}) copy-start(bf16[9,32,512]{2,1,0:T(8,128)(2,1)S(1)} %collective-permute-done.40.refs_25_) | copy-start | bytes 884740
  228.3 8.7 %collective-permute-start.48 = (bf16[9,32,512]{2,1,0:T(8,128)(2,1)S(1)}, bf16[9,32,512]{2,1,0:T(8,128)(2,1)S(1)}, u32[]{:S(2)}, u32[]{:S(2)}) collective-permute-start(bf16[9,32,512]{2,1,0:T(8,128)(2,1)S(1)} %collective-permute-done.40.refs_25_), channel_id=1, source_target_pairs={{0,1},{1,0},{2,3},{3,2},{4,5},{5,4},{6,7},{7,6},{8,9},{9,8},{10,11... | collective-permute-start | bytes 884744 | tf_op jit(solution)/shard_map/ppermute | solution.py:33
  229.8 5.0 %copy-start.19 = (bf16[8,32,512]{2,1,0:T(8,128)(2,1)}, bf16[8,32,512]{2,1,0:T(8,128)(2,1)S(1)}, u32[]{:S(2)}) copy-start(bf16[8,32,512]{2,1,0:T(8,128)(2,1)S(1)} %collective-permute-done.45.refs_30_) | copy-start | bytes 786436
  229.8 6.3 %collective-permute-start.43 = (bf16[8,32,512]{2,1,0:T(8,128)(2,1)S(1)}, bf16[8,32,512]{2,1,0:T(8,128)(2,1)}, u32[]{:S(2)}, u32[]{:S(2)}) collective-permute-start(bf16[8,32,512]{2,1,0:T(8,128)(2,1)S(1)} %collective-permute-done.35.refs_20_), channel_id=1, source_target_pairs={{0,1},{1,0},{2,3},{3,2},{4,5},{5,4},{6,7},{7,6},{8,9},{9,8},{10,11... | collective-permute-start | bytes 786440 | tf_op jit(solution)/shard_map/ppermute | solution.py:33
  234.8 2.2 collective-permute-start.47
  (6 other events, 6.4 us)

commit v5 on v4

--- a/solution.py
+++ b/solution.py
@@ -291,12 +291,23 @@
 
 def project_kernel(pieces, blocks, core_ref, weight_ref, *refs):
     rows, (send_ref, keep_ref, total) = refs[:pieces], refs[pieces:]
-    total[...] = jnp.dot(
+    found = jnp.dot(
         jnp.concatenate([r[...] for r in rows], axis=0),
         weight_ref[...],
         preferred_element_type=jnp.float32,
     )
-    core = core_ref[0]
+
+    @pl.when(pl.program_id(0) == 0)
+    def _():
+        total[...] = found
+
+    @pl.when(pl.program_id(0) == 1)
+    def _():
+        total[...] += found
+        share(blocks, core_ref[0], send_ref, keep_ref, total)
+
+
+def share(blocks, core, send_ref, keep_ref, total):
     for x in range(4):
         for block in range(blocks):
             start = (block * 4 + x) * 2 * SHARE
@@ -317,8 +328,12 @@
             jax.ShapeDtypeStruct(shape, jnp.bfloat16),
             jax.ShapeDtypeStruct(shape, jnp.float32),
         ),
-        in_specs=[pl.BlockSpec(memory_space=pltpu.SMEM)]
-        + [pl.BlockSpec(memory_space=pltpu.VMEM)] * (len(rows) + 1),
+        grid=(2,),
+        in_specs=[
+            pl.BlockSpec(memory_space=pltpu.SMEM),
+            pl.BlockSpec((weight.shape[0] // 2, columns), lambda i: (i, 0)),
+        ]
+        + [pl.BlockSpec((r.shape[0], r.shape[1] // 2), lambda i: (0, i)) for r in rows],
         out_specs=(pl.BlockSpec(memory_space=pltpu.VMEM),) * 2,
         scratch_shapes=[pltpu.VMEM((tokens, columns), jnp.float32)],
         compiler_params=pltpu.CompilerParams(vmem_limit_bytes=32 * MIB),
@@ -412,10 +427,10 @@
             ),
             scratch_shapes=[pltpu.VMEM((tokens, columns), jnp.bfloat16)],
         ),
-        compiler_params=pltpu.CompilerParams(vmem_limit_bytes=58 * MIB),
+        compiler_params=pltpu.CompilerParams(vmem_limit_bytes=40 * MIB),
         cost_estimate=FREE,
         name="weight_gradient",
-    )(positions, jnp.stack(owners).astype(jnp.int32), *rows, *grads)
+    )(positions, owners, *rows, *grads)
 
 
 def sum_dp(value, places):
@@ -499,11 +514,6 @@
     b02, b20, b21, b12 = round3
     round4 = (step(bmm, 0, -1), step(bmm, -1, 0), step(b21, 0, 1))
     middle = chip_sum(round3)
-    round4, early, middle, target, keep, keep_row = barrier(
-        (round4, early, middle, target, keep, keep_row)
-    )
-    late = first_state(jnp.concatenate([middle, chip_sum(round4)], axis=1))
-
     names = [
         (0, 0), (0, -1), (0, 1), (-1, 0), (1, 0), (-1, -1), (-1, 1), (1, 1), (1, -1),
         (0, 2), (2, 0), (2, 1), (1, 2), (-1, 2), (2, -1), (2, 2),
@@ -514,12 +524,18 @@
         jnp.where(places[None, :] == jnp.arange(BLOCKS)[:, None], jnp.arange(BLOCKS)[None, :], 0),
         axis=1,
     ).astype(jnp.int32)
+    owners = [(x_index - k) % 4 * 2 + c for c in (core, 1 - core) for k in (0, 1, 3, 2)]
+    owners = jnp.stack(owners).astype(jnp.int32)
+    round4, early, middle, target, keep, keep_row, places, positions, owners = barrier(
+        (round4, early, middle, target, keep, keep_row, places, positions, owners)
+    )
+    late = first_state(jnp.concatenate([middle, chip_sum(round4)], axis=1))
+
     states = [early, late]
     before = ring(jnp.concatenate([s[:, SHARE - PAD :] for s in states]), 1)
     after = ring(jnp.concatenate([s[:, :PAD] for s in states]), -1)
     window = assemble(states, before, after, places, mp_index)
 
-    window, positions = barrier((window, positions))
     product = products(window, target, keep, step_gains)
     product = sum_dp(product, AROUND_Z)
     product = [product] + [from_dp(product, place) for place in AROUND_Y]
@@ -530,7 +546,6 @@
     low2, high2 = along_mp(low1, 1, 0), along_mp(high3, 3, 0)
     grads = [low, high, low1, high1, low3, high3, low2, high2]
     grads = grads + [along_mp(g, 0, 1) for g in grads]
-    owners = [(x_index - k) % 4 * 2 + c for c in (core, 1 - core) for k in (0, 1, 3, 2)]
     grad_weight, mean_loss = weight_gradient(
         [own_block, *round1, *round2, *round3, *round4], positions, grads, owners
     )

time: 259 us -> 255 us (0.985)
  Pallas kernels: 54.5 us -> 51.2 us
where the time goes in v5:
time: 255 us; the launch traced here: 254 us
  waiting for transfers between devices  94.4 us (37%)
  starting transfers between devices  89.1 us (35%)
  Pallas kernels  51.2 us (20%)
  other arithmetic  10 us (4%)
  local copies, waits for them, and re-layouts  8.04 us (3%)
    ppermute x21, waiting for transfers between devices, from_dp(): return lax.ppermute(block, 'dp', route)  53.4 us
    ppermute x23, starting transfers between devices, along_mp(): return lax.ppermute(block, 'mp', route)  45 us
    ppermute x23, waiting for transfers between devices, along_mp(): return lax.ppermute(block, 'mp', route)  29.4 us
    ppermute x21, starting transfers between devices, from_dp(): return lax.ppermute(block, 'dp', route)  27.9 us
    pallas_call x3, Pallas kernels, project(): pl.pallas_call(lambda *refs: project_kernel(len(rows), blocks, *refs), ou...  22.2 us
    pallas_call x1, Pallas kernels, weight_gradient(): pl.pallas_call(lambda *refs: weight_kernel(len(rows), *refs), out_shape=(...  18.5 us
    ppermute x3, starting transfers between devices, neighbour(): return lax.ppermute(block, 'mp', route)  7.14 us
    all_to_all x1, starting transfers between devices, local(): shares = lax.all_to_all(windows(target, block_rows), 'mp', 0, 0, tiled=True)  7.13 us
  transfers between devices with their start and end apart: 50, of which 25 were waited for; matrix products, arithmetic and copies ran while one was open for 6% of the time, Pallas kernels for 7%

profile of v5, /device:TPU:1, one launch (start us, length us, event | category | flops | bytes accessed | tf_op | source)
XLA Modules:
  0.0 254.0 jit_solution(10080629920712141208)
XLA Ops:
  0.6 4.7 %collective-permute-start.7 = (bf16[256,3072]{1,0:T(8,128)(2,1)}, bf16[256,3072]{1,0:T(8,128)(2,1)}, u32[]{:S(2)}, u32[]{:S(2)}) collective-permute-start(bf16[256,3072]{1,0:T(8,128)(2,1)} %refs_2_.3), channel_id=1, source_target_pairs={{8,0},{16,8},{24,16},{0,24},{40,32},{48,40},{56,48},{32,56},{72,64... | collective-permute-start | bytes 4718600 | tf_op jit(solution)/shard_map/ppermute | solution.py:28
  5.3 2.7 %collective-permute-start.14 = (bf16[256,3072]{1,0:T(8,128)(2,1)}, bf16[256,3072]{1,0:T(8,128)(2,1)}, u32[]{:S(2)}, u32[]{:S(2)}) collective-permute-start(bf16[256,3072]{1,0:T(8,128)(2,1)} %refs_2_.3), channel_id=1, source_target_pairs={{32,0},{40,8},{48,16},{56,24},{64,32},{72,40},{80,48},{88,56},{96,... | collective-permute-start | bytes 4718600 | tf_op jit(solution)/shard_map/ppermute | solution.py:28
  8.7 3.1 %collective-permute-start.9 = (s32[16]{0:T(128)S(1)}, s32[16]{0:T(128)S(1)}, u32[]{:S(2)}, u32[]{:S(2)}) collective-permute-start(s32[16]{0:T(128)S(1)} %slice.37), channel_id=1, source_target_pairs={{1,0},{2,1},{3,2},{4,3},{5,4},{6,5},{7,6},{9,8},{10,9},{11,10},{12... | collective-permute-start | bytes 200 | tf_op jit(solution)/shard_map/ppermute | solution.py:39
  12.6 1.9 collective-permute-done.9
  14.6 1.9 collective-permute-start.10
  17.6 2.1 collective-permute-start.8
  19.7 3.5 %collective-permute-done.8 = bf16[16,512]{1,0:T(8,128)(2,1)S(1)} collective-permute-done((bf16[16,512]{1,0:T(8,128)(2,1)S(1)}, bf16[16,512]{1,0:T(8,128)(2,1)S(1)}, u32[]{:S(2)}, u32[]{:S(2)}) %collective-permute-start.8) | collective-permute-done | bytes 16416 | tf_op jit(solution)/shard_map/ppermute | solution.py:39
  23.1 15.5 %collective-permute-done.7.refs_4_ = bf16[256,3072]{1,0:T(8,128)(2,1)} collective-permute-done((bf16[256,3072]{1,0:T(8,128)(2,1)}, bf16[256,3072]{1,0:T(8,128)(2,1)}, u32[]{:S(2)}, u32[]{:S(2)}) %collective-permute-start.7) | collective-permute-done | bytes 1572896 | tf_op jit(solution)/shard_map/ppermute | solution.py:28
  38.7 2.4 collective-permute-done.14.refs_6_
  41.1 3.4 %collective-permute-start.11 = (bf16[256,3072]{1,0:T(8,128)(2,1)}, bf16[256,3072]{1,0:T(8,128)(2,1)}, u32[]{:S(2)}, u32[]{:S(2)}) collective-permute-start(bf16[256,3072]{1,0:T(8,128)(2,1)} %collective-permute-done.7.refs_4_), channel_id=1, source_target_pairs={{32,0},{40,8},{48,16},{56,24},{64,32},{72,40},{80,48},{88,56},{96,... | collective-permute-start | bytes 4718600 | tf_op jit(solution)/shard_map/ppermute | solution.py:28
  44.5 2.7 %collective-permute-start.15 = (bf16[256,3072]{1,0:T(8,128)(2,1)}, bf16[256,3072]{1,0:T(8,128)(2,1)}, u32[]{:S(2)}, u32[]{:S(2)}) collective-permute-start(bf16[256,3072]{1,0:T(8,128)(2,1)} %collective-permute-done.5.refs_5_), channel_id=1, source_target_pairs={{8,0},{16,8},{24,16},{0,24},{40,32},{48,40},{56,48},{32,56},{72,64... | collective-permute-start | bytes 4718600 | tf_op jit(solution)/shard_map/ppermute | solution.py:28
  48.2 1.1 pad_maximum_fusion.refs_0_
  50.3 7.1 %all-to-all-start = ((bf16[8,2,48,640]{3,2,1,0:T(8,128)(2,1)}), bf16[8,2,48,640]{3,2,1,0:T(8,128)(2,1)}, u32[]{:S(2)}, u32[]{:S(2)}) async-start(bf16[8,2,48,640]{3,2,1,0:T(8,128)(2,1)} %copy-done.3), calls=%async_computation | async-start | bytes 1966080 | tf_op jit(solution)/shard_map/all_to_all | solution.py:503
  57.5 20.5 %collective-permute-done.16.refs_10_ = bf16[256,3072]{1,0:T(8,128)(2,1)} collective-permute-done((bf16[256,3072]{1,0:T(8,128)(2,1)}, bf16[256,3072]{1,0:T(8,128)(2,1)}, u32[]{:S(2)}, u32[]{:S(2)}) %collective-permute-start.16) | collective-permute-done | bytes 1572896 | tf_op jit(solution)/shard_map/ppermute | solution.py:28
  77.9 2.7 %collective-permute-start.13 = (bf16[256,3072]{1,0:T(8,128)(2,1)}, bf16[256,3072]{1,0:T(8,128)(2,1)}, u32[]{:S(2)}, u32[]{:S(2)}) collective-permute-start(bf16[256,3072]{1,0:T(8,128)(2,1)} %collective-permute-done.11.refs_9_), channel_id=1, source_target_pairs={{8,0},{16,8},{24,16},{0,24},{40,32},{48,40},{56,48},{32,56},{72,64... | collective-permute-start | bytes 4718600 | tf_op jit(solution)/shard_map/ppermute | solution.py:28
  80.6 2.1 collective-permute-start.12
  82.7 1.4 copy-done.1
  84.1 11.6 %project.3 = (bf16[4,9,32,512]{3,2,1,0:T(8,128)(2,1)S(1)}, f32[4,9,32,512]{3,2,1,0:T(8,128)S(1)}) custom-call(s32[1]{0:T(128)} %bitcast.refs_0_, bf16[3072,512]{1,0:T(8,128)(2,1)S(1)} %copy-done, bf16[256,3072]{1,0:T(8,128)(2,1)S(1)} %copy-done.1, bf16[256,3072]{1,0:T(8,128)(2,1)} %collective-permute-done.refs_3_, ...), custom_call_target="tpu_custom_call" | custom-call | flops 1 | bytes 1 | tf_op jit(solution)/shard_map/project/pallas_call | solution.py:325
  95.7 6.1 %collective-permute-start.17 = (bf16[4,9,32,512]{3,2,1,0:T(8,128)(2,1)S(1)}, bf16[4,9,32,512]{3,2,1,0:T(8,128)(2,1)S(1)}, u32[]{:S(2)}, u32[]{:S(2)}) collective-permute-start(bf16[4,9,32,512]{3,2,1,0:T(8,128)(2,1)S(1)} %get-tuple-element.46), channel_id=1, source_target_pairs={{0,1},{1,0},{2,3},{3,2},{4,5},{5,4},{6,7},{7,6},{8,9},{9,8},{10,11... | collective-permute-start | bytes 3538952 | tf_op jit(solution)/shard_map/ppermute | solution.py:33
  101.8 2.5 collective-permute-done.17
  104.3 1.9 convert_add_fusion
  106.3 9.3 %collective-permute-done.6.refs_3_.refs_12_ = bf16[256,3072]{1,0:T(8,128)(2,1)} collective-permute-done((bf16[256,3072]{1,0:T(8,128)(2,1)}, bf16[256,3072]{1,0:T(8,128)(2,1)}, u32[]{:S(2)}, u32[]{:S(2)}) %collective-permute-start.6) | collective-permute-done | bytes 1572896 | tf_op jit(solution)/shard_map/ppermute | solution.py:28
  115.6 2.7 %collective-permute-start.18 = (bf16[256,3072]{1,0:T(8,128)(2,1)}, bf16[256,3072]{1,0:T(8,128)(2,1)}, u32[]{:S(2)}, u32[]{:S(2)}) collective-permute-start(bf16[256,3072]{1,0:T(8,128)(2,1)} %collective-permute-done.12.refs_4_.refs_13_), channel_id=1, source_target_pairs={{8,0},{16,8},{24,16},{0,24},{40,32},{48,40},{56,48},{32,56},{72,64... | collective-permute-start | bytes 4718600 | tf_op jit(solution)/shard_map/ppermute | solution.py:28
  118.4 2.4 fusion.9
  120.8 1.2 collective-permute-start.19
  122.3 2.5 collective-permute-start.21
  125.7 2.5 collective-permute-done.19
  128.2 1.3 collective-permute-start.20
  129.5 1.7 fusion.15
  132.0 5.9 %project.4 = (bf16[4,4,32,512]{3,2,1,0:T(8,128)(2,1)S(1)}, f32[4,4,32,512]{3,2,1,0:T(8,128)S(1)}) custom-call(s32[1]{0:T(128)} %bitcast.refs_0_, bf16[3072,512]{1,0:T(8,128)(2,1)S(1)} %copy-done, bf16[256,3072]{1,0:T(8,128)(2,1)} %collective-permute-done.4.refs_2_.refs_11_, bf16[256,3072]{1,0:T(8,128)(2,1)} %collective-permute-done.6.refs_3_.refs_12_, ...), custom_call_target="tpu_custom_call" | custom-call | flops 1 | bytes 1 | tf_op jit(solution)/shard_map/project/pallas_call | solution.py:325
  137.9 8.6 %collective-permute-start.22 = (bf16[4,4,32,512]{3,2,1,0:T(8,128)(2,1)S(1)}, bf16[4,4,32,512]{3,2,1,0:T(8,128)(2,1)S(1)}, u32[]{:S(2)}, u32[]{:S(2)}) collective-permute-start(bf16[4,4,32,512]{3,2,1,0:T(8,128)(2,1)S(1)} %get-tuple-element.53), channel_id=1, source_target_pairs={{0,1},{1,0},{2,3},{3,2},{4,5},{5,4},{6,7},{7,6},{8,9},{9,8},{10,11... | collective-permute-start | bytes 1572872 | tf_op jit(solution)/shard_map/ppermute | solution.py:33
  146.5 1.3 slice_convert_fusion.target_ref.refs_1_
  147.9 1.5 bitcast_add_fusion.refs_2_
  149.6 4.7 %project.5 = (bf16[4,3,32,512]{3,2,1,0:T(8,128)(2,1)S(1)}, f32[4,3,32,512]{3,2,1,0:T(8,128)S(1)}) custom-call(s32[1]{0:T(128)} %bitcast.refs_0_, bf16[3072,512]{1,0:T(8,128)(2,1)S(1)} %copy-done, bf16[256,3072]{1,0:T(8,128)(2,1)} %collective-permute-done.2.refs_2_.refs_15_, bf16[256,3072]{1,0:T(8,128)(2,1)} %collective-permute-done.3.refs_3_.refs_16_, ...), custom_call_target="tpu_custom_call" | custom-call | flops 1 | bytes 1 | tf_op jit(solution)/shard_map/project/pallas_call | solution.py:325
  154.3 4.4 %collective-permute-start.23 = (bf16[4,3,32,512]{3,2,1,0:T(8,128)(2,1)S(1)}, bf16[4,3,32,512]{3,2,1,0:T(8,128)(2,1)S(1)}, u32[]{:S(2)}, u32[]{:S(2)}) collective-permute-start(bf16[4,3,32,512]{3,2,1,0:T(8,128)(2,1)S(1)} %get-tuple-element.64), channel_id=1, source_target_pairs={{0,1},{1,0},{2,3},{3,2},{4,5},{5,4},{6,7},{7,6},{8,9},{9,8},{10,11... | collective-permute-start | bytes 1179656 | tf_op jit(solution)/shard_map/ppermute | solution.py:33
  158.7 1.3 collective-permute-done.23
  160.3 1.3 collective-permute-start.24
  161.6 1.5 collective-permute-start.25
  163.0 1.5 collective-permute-start.26
  164.6 3.8 %collective-permute-done.24 = bf16[7,32,512]{2,1,0:T(8,128)(2,1)S(1)} collective-permute-done((bf16[7,32,512]{2,1,0:T(8,128)(2,1)S(1)}, bf16[7,32,512]{2,1,0:T(8,128)(2,1)S(1)}, u32[]{:S(2)}, u32[]{:S(2)}) %collective-permute-start.24) | collective-permute-done | bytes 229408 | tf_op jit(solution)/shard_map/ppermute | solution.py:33
  168.4 5.9 %collective-permute-done.26 = bf16[7,32,512]{2,1,0:T(8,128)(2,1)S(1)} collective-permute-done((bf16[7,32,512]{2,1,0:T(8,128)(2,1)S(1)}, bf16[7,32,512]{2,1,0:T(8,128)(2,1)S(1)}, u32[]{:S(2)}, u32[]{:S(2)}) %collective-permute-start.26) | collective-permute-done | bytes 229408 | tf_op jit(solution)/shard_map/ppermute | solution.py:33
  174.5 2.0 collective-permute-start.27
  176.5 3.3 %collective-permute-done.27.refs_4_ = f32[16,8,512]{2,1,0:T(8,128)S(1)} collective-permute-done((f32[16,8,512]{2,1,0:T(8,128)S(1)}, f32[16,8,512]{2,1,0:T(8,128)S(1)}, u32[]{:S(2)}, u32[]{:S(2)}) %collective-permute-start.27) | collective-permute-done | bytes 262176 | tf_op jit(solution)/shard_map/ppermute | solution.py:449
  179.7 2.5 %collective-permute-done.28.refs_5_ = f32[16,8,512]{2,1,0:T(8,128)S(1)} collective-permute-done((f32[16,8,512]{2,1,0:T(8,128)S(1)}, f32[16,8,512]{2,1,0:T(8,128)S(1)}, u32[]{:S(2)}, u32[]{:S(2)}) %collective-permute-start.28) | collective-permute-done | bytes 262176 | tf_op jit(solution)/shard_map/ppermute | solution.py:449
  183.1 5.3 %products.1 = f32[24,768]{1,0:T(8,128)S(1)} custom-call(f32[16,48,512]{2,1,0:T(8,128)S(1)} %assemble.1.state_ref.refs_0_, f32[16,48,512]{2,1,0:T(8,128)S(1)} %slice_convert_fusion.target_ref.refs_1_, f32[16,48,1]{2,1,0:T(8,128)S(1)} %slice_convert_fusion.1.keep_ref.refs_2_, f32[3,512]{1,0:T(4,128)S(1)} %copy-done.4), custom_call_target="tpu_custom_call" | custom-call | flops 1 | bytes 1 | tf_op jit(solution)/shard_map/products/pallas_call | solution.py:136
  188.4 1.3 collective-permute-start.31
  189.8 2.1 collective-permute-start.30
  193.2 2.2 collective-permute-done.30
  196.3 2.1 collective-permute-start.32
  198.4 2.1 collective-permute-done.34.refs_8_
  200.9 4.3 %gradients.1 = (bf16[8,32,512]{2,1,0:T(8,128)(2,1)S(1)}, bf16[9,32,512]{2,1,0:T(8,128)(2,1)S(1)}) custom-call(f32[16,48,512]{2,1,0:T(8,128)S(1)} %assemble.1.state_ref.refs_0_, f32[16,48,512]{2,1,0:T(8,128)S(1)} %slice_convert_fusion.target_ref.refs_1_, f32[16,48,1]{2,1,0:T(8,128)S(1)} %slice_convert_fusion.1.keep_ref.refs_2_, ...), custom_call_target="tpu_custom_call" | custom-call | flops 1 | bytes 1 | tf_op jit(solution)/shard_map/gradients/pallas_call | solution.py:274
  205.3 4.3 %collective-permute-start.38 = (bf16[9,32,512]{2,1,0:T(8,128)(2,1)S(1)}, bf16[9,32,512]{2,1,0:T(8,128)(2,1)S(1)}, u32[]{:S(2)}, u32[]{:S(2)}) collective-permute-start(bf16[9,32,512]{2,1,0:T(8,128)(2,1)S(1)} %get-tuple-element.69.refs_19_), channel_id=1, source_target_pairs={{0,6},{1,7},{2,0},{3,1},{4,2},{5,3},{6,4},{7,5},{8,14},{9,15},{10,... | collective-permute-start | bytes 884744 | tf_op jit(solution)/shard_map/ppermute | solution.py:33
  209.5 1.0 collective-permute-start.41
  210.5 1.5 collective-permute-start.35
  212.5 2.6 %collective-permute-done.38.refs_23_ = bf16[9,32,512]{2,1,0:T(8,128)(2,1)S(1)} collective-permute-done((bf16[9,32,512]{2,1,0:T(8,128)(2,1)S(1)}, bf16[9,32,512]{2,1,0:T(8,128)(2,1)S(1)}, u32[]{:S(2)}, u32[]{:S(2)}) %collective-permute-start.38) | collective-permute-done | bytes 294944 | tf_op jit(solution)/shard_map/ppermute | solution.py:33
  215.2 3.4 %collective-permute-start.40 = (bf16[9,32,512]{2,1,0:T(8,128)(2,1)S(1)}, bf16[9,32,512]{2,1,0:T(8,128)(2,1)S(1)}, u32[]{:S(2)}, u32[]{:S(2)}) collective-permute-start(bf16[9,32,512]{2,1,0:T(8,128)(2,1)S(1)} %collective-permute-done.38.refs_23_), channel_id=1, source_target_pairs={{0,6},{1,7},{2,0},{3,1},{4,2},{5,3},{6,4},{7,5},{8,14},{9,15},{10,... | collective-permute-start | bytes 884744 | tf_op jit(solution)/shard_map/ppermute | solution.py:33
  218.6 2.2 collective-permute-done.37.refs_22_
  220.8 2.8 %collective-permute-start.45 = (bf16[8,32,512]{2,1,0:T(8,128)(2,1)S(1)}, bf16[8,32,512]{2,1,0:T(8,128)(2,1)S(1)}, u32[]{:S(2)}, u32[]{:S(2)}) collective-permute-start(bf16[8,32,512]{2,1,0:T(8,128)(2,1)S(1)} %collective-permute-done.37.refs_22_), channel_id=1, source_target_pairs={{0,1},{1,0},{2,3},{3,2},{4,5},{5,4},{6,7},{7,6},{8,9},{9,8},{10,11... | collective-permute-start | bytes 786440 | tf_op jit(solution)/shard_map/ppermute | solution.py:33
  223.7 2.1 collective-permute-done.36.refs_21_
  225.8 1.0 collective-permute-start.44
  227.1 1.6 collective-permute-start.48
  228.7 5.0 %collective-permute-done.39.refs_24_ = bf16[8,32,512]{2,1,0:T(8,128)(2,1)S(1)} collective-permute-done((bf16[8,32,512]{2,1,0:T(8,128)(2,1)S(1)}, bf16[8,32,512]{2,1,0:T(8,128)(2,1)S(1)}, u32[]{:S(2)}, u32[]{:S(2)}) %collective-permute-start.39) | collective-permute-done | bytes 262176 | tf_op jit(solution)/shard_map/ppermute | solution.py:33
  234.2 1.1 collective-permute-done.47.refs_32_
  235.4 18.5 %weight_gradient.1 = (f32[3072,512]{1,0:T(8,128)}, f32[1,128]{1,0:T(1,128)}) custom-call(s32[16]{0:T(128)S(1)} %select_reduce_fusion.refs_0_, s32[8]{0:T(128)S(1)} %stack.112.refs_1_, bf16[256,3072]{1,0:T(8,128)(2,1)S(1)} %copy-done.2, bf16[256,3072]{1,0:T(8,128)(2,1)} %collective-permute-done.refs_3_, bf16[256,3072]{1,0:T(8,128)(2,1)} %collective-permute-done.7.refs_4_, ...), custom_call_target="tpu_custom_call" | custom-call | flops 1 | bytes 1 | tf_op jit(solution)/shard_map/weight_gradient/pallas_call | solution.py:413
  (81 shorter events, 12.3 us)
Async XLA Ops:
  0.6 38.0 %collective-permute-start.7 = (bf16[256,3072]{1,0:T(8,128)(2,1)}, bf16[256,3072]{1,0:T(8,128)(2,1)}, u32[]{:S(2)}, u32[]{:S(2)}) collective-permute-start(bf16[256,3072]{1,0:T(8,128)(2,1)} %refs_2_.3), channel_id=1, source_target_pairs={{8,0},{16,8},{24,16},{0,24},{40,32},{48,40},{56,48},{32,56},{72,64... | collective-permute-start | bytes 4718600 | tf_op jit(solution)/shard_map/ppermute | solution.py:28
  5.3 35.8 %collective-permute-start.14 = (bf16[256,3072]{1,0:T(8,128)(2,1)}, bf16[256,3072]{1,0:T(8,128)(2,1)}, u32[]{:S(2)}, u32[]{:S(2)}) collective-permute-start(bf16[256,3072]{1,0:T(8,128)(2,1)} %refs_2_.3), channel_id=1, source_target_pairs={{32,0},{40,8},{48,16},{56,24},{64,32},{72,40},{80,48},{88,56},{96,... | collective-permute-start | bytes 4718600 | tf_op jit(solution)/shard_map/ppermute | solution.py:28
  8.0 36.5 %collective-permute-start.5 = (bf16[256,3072]{1,0:T(8,128)(2,1)}, bf16[256,3072]{1,0:T(8,128)(2,1)}, u32[]{:S(2)}, u32[]{:S(2)}) collective-permute-start(bf16[256,3072]{1,0:T(8,128)(2,1)} %refs_2_.3), channel_id=1, source_target_pairs={{96,0},{104,8},{112,16},{120,24},{0,32},{8,40},{16,48},{24,56},{32... | collective-permute-start | bytes 4718600 | tf_op jit(solution)/shard_map/ppermute | solution.py:28
  8.0 39.2 %collective-permute-start = (bf16[256,3072]{1,0:T(8,128)(2,1)}, bf16[256,3072]{1,0:T(8,128)(2,1)}, u32[]{:S(2)}, u32[]{:S(2)}) collective-permute-start(bf16[256,3072]{1,0:T(8,128)(2,1)} %refs_2_.3), channel_id=1, source_target_pairs={{24,0},{0,8},{8,16},{16,24},{56,32},{32,40},{40,48},{48,56},{88,64... | collective-permute-start | bytes 4718600 | tf_op jit(solution)/shard_map/ppermute | solution.py:28
  8.7 5.8 %collective-permute-start.9 = (s32[16]{0:T(128)S(1)}, s32[16]{0:T(128)S(1)}, u32[]{:S(2)}, u32[]{:S(2)}) collective-permute-start(s32[16]{0:T(128)S(1)} %slice.37), channel_id=1, source_target_pairs={{1,0},{2,1},{3,2},{4,3},{5,4},{6,5},{7,6},{9,8},{10,9},{11,10},{12... | collective-permute-start | bytes 200 | tf_op jit(solution)/shard_map/ppermute | solution.py:39
  14.6 3.0 %collective-permute-start.10 = (s32[17]{0:T(128)S(1)}, s32[17]{0:T(128)S(1)}, u32[]{:S(2)}, u32[]{:S(2)}) collective-permute-start(s32[17]{0:T(128)S(1)} %slice.38), channel_id=1, source_target_pairs={{0,1},{1,2},{2,3},{3,4},{4,5},{5,6},{6,7},{8,9},{9,10},{10,11},{11... | collective-permute-start | bytes 212 | tf_op jit(solution)/shard_map/ppermute | solution.py:39
  17.6 5.6 %collective-permute-start.8 = (bf16[16,512]{1,0:T(8,128)(2,1)S(1)}, bf16[16,512]{1,0:T(8,128)(2,1)S(1)}, u32[]{:S(2)}, u32[]{:S(2)}) collective-permute-start(bf16[16,512]{1,0:T(8,128)(2,1)S(1)} %slice.36), channel_id=1, source_target_pairs={{1,0},{2,1},{3,2},{4,3},{5,4},{6,5},{7,6},{9,8},{10,9},{11,10},{12... | collective-permute-start | bytes 49160 | tf_op jit(solution)/shard_map/ppermute | solution.py:39
  41.1 36.8 %collective-permute-start.16 = (bf16[256,3072]{1,0:T(8,128)(2,1)}, bf16[256,3072]{1,0:T(8,128)(2,1)}, u32[]{:S(2)}, u32[]{:S(2)}) collective-permute-start(bf16[256,3072]{1,0:T(8,128)(2,1)} %collective-permute-done.14.refs_6_), channel_id=1, source_target_pairs={{24,0},{0,8},{8,16},{16,24},{56,32},{32,40},{40,48},{48,56},{88,64... | collective-permute-start | bytes 4718600 | tf_op jit(solution)/shard_map/ppermute | solution.py:28
  41.1 36.8 %collective-permute-start.11 = (bf16[256,3072]{1,0:T(8,128)(2,1)}, bf16[256,3072]{1,0:T(8,128)(2,1)}, u32[]{:S(2)}, u32[]{:S(2)}) collective-permute-start(bf16[256,3072]{1,0:T(8,128)(2,1)} %collective-permute-done.7.refs_4_), channel_id=1, source_target_pairs={{32,0},{40,8},{48,16},{56,24},{64,32},{72,40},{80,48},{88,56},{96,... | collective-permute-start | bytes 4718600 | tf_op jit(solution)/shard_map/ppermute | solution.py:28
  44.5 36.1 %collective-permute-start.15 = (bf16[256,3072]{1,0:T(8,128)(2,1)}, bf16[256,3072]{1,0:T(8,128)(2,1)}, u32[]{:S(2)}, u32[]{:S(2)}) collective-permute-start(bf16[256,3072]{1,0:T(8,128)(2,1)} %collective-permute-done.5.refs_5_), channel_id=1, source_target_pairs={{8,0},{16,8},{24,16},{0,24},{40,32},{48,40},{56,48},{32,56},{72,64... | collective-permute-start | bytes 4718600 | tf_op jit(solution)/shard_map/ppermute | solution.py:28
  47.2 35.6 %collective-permute-start.1 = (bf16[256,3072]{1,0:T(8,128)(2,1)}, bf16[256,3072]{1,0:T(8,128)(2,1)}, u32[]{:S(2)}, u32[]{:S(2)}) collective-permute-start(bf16[256,3072]{1,0:T(8,128)(2,1)} %collective-permute-done.refs_3_), channel_id=1, source_target_pairs={{96,0},{104,8},{112,16},{120,24},{0,32},{8,40},{16,48},{24,56},{32... | collective-permute-start | bytes 4718600 | tf_op jit(solution)/shard_map/ppermute | solution.py:28
  49.3 33.5 %copy-start = (bf16[3072,512]{1,0:T(8,128)(2,1)S(1)}, bf16[3072,512]{1,0:T(8,128)(2,1)}, u32[]{:S(2)}) copy-start(bf16[3072,512]{1,0:T(8,128)(2,1)} %refs_1_.5) | copy-start | bytes 9437188
  49.4 0.9 copy-start.3
  50.3 32.4 %all-to-all-start = ((bf16[8,2,48,640]{3,2,1,0:T(8,128)(2,1)}), bf16[8,2,48,640]{3,2,1,0:T(8,128)(2,1)}, u32[]{:S(2)}, u32[]{:S(2)}) async-start(bf16[8,2,48,640]{3,2,1,0:T(8,128)(2,1)} %copy-done.3), calls=%async_computation | async-start | bytes 1966080 | tf_op jit(solution)/shard_map/all_to_all | solution.py:503
  57.5 58.1 %collective-permute-start.6 = (bf16[256,3072]{1,0:T(8,128)(2,1)}, bf16[256,3072]{1,0:T(8,128)(2,1)}, u32[]{:S(2)}, u32[]{:S(2)}) collective-permute-start(bf16[256,3072]{1,0:T(8,128)(2,1)} %collective-permute-done.5.refs_5_), channel_id=1, source_target_pairs={{96,0},{104,8},{112,16},{120,24},{0,32},{8,40},{16,48},{24,56},{32... | collective-permute-start | bytes 4718600 | tf_op jit(solution)/shard_map/ppermute | solution.py:28
  77.9 37.7 %collective-permute-start.4 = (bf16[256,3072]{1,0:T(8,128)(2,1)}, bf16[256,3072]{1,0:T(8,128)(2,1)}, u32[]{:S(2)}, u32[]{:S(2)}) collective-permute-start(bf16[256,3072]{1,0:T(8,128)(2,1)} %collective-permute-done.refs_3_), channel_id=1, source_target_pairs={{24,0},{0,8},{8,16},{16,24},{56,32},{32,40},{40,48},{48,56},{88,64... | collective-permute-start | bytes 4718600 | tf_op jit(solution)/shard_map/ppermute | solution.py:28
  77.9 37.7 %collective-permute-start.13 = (bf16[256,3072]{1,0:T(8,128)(2,1)}, bf16[256,3072]{1,0:T(8,128)(2,1)}, u32[]{:S(2)}, u32[]{:S(2)}) collective-permute-start(bf16[256,3072]{1,0:T(8,128)(2,1)} %collective-permute-done.11.refs_9_), channel_id=1, source_target_pairs={{8,0},{16,8},{24,16},{0,24},{40,32},{48,40},{56,48},{32,56},{72,64... | collective-permute-start | bytes 4718600 | tf_op jit(solution)/shard_map/ppermute | solution.py:28
  80.6 35.0 %collective-permute-start.12 = (bf16[256,3072]{1,0:T(8,128)(2,1)}, bf16[256,3072]{1,0:T(8,128)(2,1)}, u32[]{:S(2)}, u32[]{:S(2)}) collective-permute-start(bf16[256,3072]{1,0:T(8,128)(2,1)} %collective-permute-done.11.refs_9_), channel_id=1, source_target_pairs={{32,0},{40,8},{48,16},{56,24},{64,32},{72,40},{80,48},{88,56},{96,... | collective-permute-start | bytes 4718600 | tf_op jit(solution)/shard_map/ppermute | solution.py:28
  82.7 1.4 copy-start.1
  95.7 8.6 %collective-permute-start.17 = (bf16[4,9,32,512]{3,2,1,0:T(8,128)(2,1)S(1)}, bf16[4,9,32,512]{3,2,1,0:T(8,128)(2,1)S(1)}, u32[]{:S(2)}, u32[]{:S(2)}) collective-permute-start(bf16[4,9,32,512]{3,2,1,0:T(8,128)(2,1)S(1)} %get-tuple-element.46), channel_id=1, source_target_pairs={{0,1},{1,0},{2,3},{3,2},{4,5},{5,4},{6,7},{7,6},{8,9},{9,8},{10,11... | collective-permute-start | bytes 3538952 | tf_op jit(solution)/shard_map/ppermute | solution.py:33
  104.3 45.3 %collective-permute-start.3 = (bf16[256,3072]{1,0:T(8,128)(2,1)}, bf16[256,3072]{1,0:T(8,128)(2,1)}, u32[]{:S(2)}, u32[]{:S(2)}) collective-permute-start(bf16[256,3072]{1,0:T(8,128)(2,1)} %collective-permute-done.1.refs_7_), channel_id=1, source_target_pairs={{96,0},{104,8},{112,16},{120,24},{0,32},{8,40},{16,48},{24,56},{32... | collective-permute-start | bytes 4718600 | tf_op jit(solution)/shard_map/ppermute | solution.py:28
  115.6 34.0 %collective-permute-start.2 = (bf16[256,3072]{1,0:T(8,128)(2,1)}, bf16[256,3072]{1,0:T(8,128)(2,1)}, u32[]{:S(2)}, u32[]{:S(2)}) collective-permute-start(bf16[256,3072]{1,0:T(8,128)(2,1)} %collective-permute-done.1.refs_7_), channel_id=1, source_target_pairs={{24,0},{0,8},{8,16},{16,24},{56,32},{32,40},{40,48},{48,56},{88,64... | collective-permute-start | bytes 4718600 | tf_op jit(solution)/shard_map/ppermute | solution.py:28
  115.6 34.0 %collective-permute-start.18 = (bf16[256,3072]{1,0:T(8,128)(2,1)}, bf16[256,3072]{1,0:T(8,128)(2,1)}, u32[]{:S(2)}, u32[]{:S(2)}) collective-permute-start(bf16[256,3072]{1,0:T(8,128)(2,1)} %collective-permute-done.12.refs_4_.refs_13_), channel_id=1, source_target_pairs={{8,0},{16,8},{24,16},{0,24},{40,32},{48,40},{56,48},{32,56},{72,64... | collective-permute-start | bytes 4718600 | tf_op jit(solution)/shard_map/ppermute | solution.py:28
  120.8 7.4 %collective-permute-start.19 = (bf16[9,32,512]{2,1,0:T(8,128)(2,1)}, bf16[9,32,512]{2,1,0:T(8,128)(2,1)}, u32[]{:S(2)}, u32[]{:S(2)}) collective-permute-start(bf16[9,32,512]{2,1,0:T(8,128)(2,1)} %get-tuple-element.72), channel_id=1, source_target_pairs={{0,2},{1,3},{2,4},{3,5},{4,6},{5,7},{6,0},{7,1},{8,10},{9,11},{10,... | collective-permute-start | bytes 884744 | tf_op jit(solution)/shard_map/ppermute | solution.py:33
  122.3 15.6 %collective-permute-start.21 = (bf16[9,32,512]{2,1,0:T(8,128)(2,1)}, bf16[9,32,512]{2,1,0:T(8,128)(2,1)}, u32[]{:S(2)}, u32[]{:S(2)}) collective-permute-start(bf16[9,32,512]{2,1,0:T(8,128)(2,1)} %get-tuple-element.73), channel_id=1, source_target_pairs={{0,4},{1,5},{2,6},{3,7},{4,0},{5,1},{6,2},{7,3},{8,12},{9,13},{10,... | collective-permute-start | bytes 884744 | tf_op jit(solution)/shard_map/ppermute | solution.py:33
  128.2 19.6 %collective-permute-start.20 = (bf16[9,32,512]{2,1,0:T(8,128)(2,1)}, bf16[9,32,512]{2,1,0:T(8,128)(2,1)}, u32[]{:S(2)}, u32[]{:S(2)}) collective-permute-start(bf16[9,32,512]{2,1,0:T(8,128)(2,1)} %get-tuple-element.74), channel_id=1, source_target_pairs={{0,6},{1,7},{2,0},{3,1},{4,2},{5,3},{6,4},{7,5},{8,14},{9,15},{10,... | collective-permute-start | bytes 884744 | tf_op jit(solution)/shard_map/ppermute | solution.py:33
  137.9 11.5 %collective-permute-start.22 = (bf16[4,4,32,512]{3,2,1,0:T(8,128)(2,1)S(1)}, bf16[4,4,32,512]{3,2,1,0:T(8,128)(2,1)S(1)}, u32[]{:S(2)}, u32[]{:S(2)}) collective-permute-start(bf16[4,4,32,512]{3,2,1,0:T(8,128)(2,1)S(1)} %get-tuple-element.53), channel_id=1, source_target_pairs={{0,1},{1,0},{2,3},{3,2},{4,5},{5,4},{6,7},{7,6},{8,9},{9,8},{10,11... | collective-permute-start | bytes 1572872 | tf_op jit(solution)/shard_map/ppermute | solution.py:33
  154.3 5.7 %collective-permute-start.23 = (bf16[4,3,32,512]{3,2,1,0:T(8,128)(2,1)S(1)}, bf16[4,3,32,512]{3,2,1,0:T(8,128)(2,1)S(1)}, u32[]{:S(2)}, u32[]{:S(2)}) collective-permute-start(bf16[4,3,32,512]{3,2,1,0:T(8,128)(2,1)S(1)} %get-tuple-element.64), channel_id=1, source_target_pairs={{0,1},{1,0},{2,3},{3,2},{4,5},{5,4},{6,7},{7,6},{8,9},{9,8},{10,11... | collective-permute-start | bytes 1179656 | tf_op jit(solution)/shard_map/ppermute | solution.py:33
  160.3 8.1 %collective-permute-start.24 = (bf16[7,32,512]{2,1,0:T(8,128)(2,1)S(1)}, bf16[7,32,512]{2,1,0:T(8,128)(2,1)S(1)}, u32[]{:S(2)}, u32[]{:S(2)}) collective-permute-start(bf16[7,32,512]{2,1,0:T(8,128)(2,1)S(1)} %get-tuple-element.75), channel_id=1, source_target_pairs={{0,2},{1,3},{2,4},{3,5},{4,6},{5,7},{6,0},{7,1},{8,10},{9,11},{10,... | collective-permute-start | bytes 688136 | tf_op jit(solution)/shard_map/ppermute | solution.py:33
  161.6 6.8 %collective-permute-start.25 = (bf16[7,32,512]{2,1,0:T(8,128)(2,1)S(1)}, bf16[7,32,512]{2,1,0:T(8,128)(2,1)S(1)}, u32[]{:S(2)}, u32[]{:S(2)}) collective-permute-start(bf16[7,32,512]{2,1,0:T(8,128)(2,1)S(1)} %get-tuple-element.76), channel_id=1, source_target_pairs={{0,6},{1,7},{2,0},{3,1},{4,2},{5,3},{6,4},{7,5},{8,14},{9,15},{10,... | collective-permute-start | bytes 688136 | tf_op jit(solution)/shard_map/ppermute | solution.py:33
  163.0 11.2 %collective-permute-start.26 = (bf16[7,32,512]{2,1,0:T(8,128)(2,1)S(1)}, bf16[7,32,512]{2,1,0:T(8,128)(2,1)S(1)}, u32[]{:S(2)}, u32[]{:S(2)}) collective-permute-start(bf16[7,32,512]{2,1,0:T(8,128)(2,1)S(1)} %get-tuple-element.77), channel_id=1, source_target_pairs={{0,4},{1,5},{2,6},{3,7},{4,0},{5,1},{6,2},{7,3},{8,12},{9,13},{10,... | collective-permute-start | bytes 688136 | tf_op jit(solution)/shard_map/ppermute | solution.py:33
  174.5 5.3 %collective-permute-start.27 = (f32[16,8,512]{2,1,0:T(8,128)S(1)}, f32[16,8,512]{2,1,0:T(8,128)S(1)}, u32[]{:S(2)}, u32[]{:S(2)}) collective-permute-start(f32[16,8,512]{2,1,0:T(8,128)S(1)} %pad_maximum_fusion.1), channel_id=1, source_target_pairs={{7,0},{0,1},{1,2},{2,3},{3,4},{4,5},{5,6},{6,7},{15,8},{8,9},{9,10... | collective-permute-start | bytes 786440 | tf_op jit(solution)/shard_map/ppermute | solution.py:449
  176.4 5.8 %collective-permute-start.28 = (f32[16,8,512]{2,1,0:T(8,128)S(1)}, f32[16,8,512]{2,1,0:T(8,128)S(1)}, u32[]{:S(2)}, u32[]{:S(2)}) collective-permute-start(f32[16,8,512]{2,1,0:T(8,128)S(1)} %pad_maximum_fusion.2), channel_id=1, source_target_pairs={{1,0},{2,1},{3,2},{4,3},{5,4},{6,5},{7,6},{0,7},{9,8},{10,9},{11,1... | collective-permute-start | bytes 786440 | tf_op jit(solution)/shard_map/ppermute | solution.py:449
  182.3 0.8 copy-start.4
  188.4 4.8 %collective-permute-start.31 = (f32[24,768]{1,0:T(8,128)S(1)}, f32[24,768]{1,0:T(8,128)S(1)}, u32[]{:S(2)}, u32[]{:S(2)}) collective-permute-start(f32[24,768]{1,0:T(8,128)S(1)} %products.1), channel_id=1, source_target_pairs={{16,0},{24,8},{0,16},{8,24},{48,32},{56,40},{32,48},{40,56},{80,64... | collective-permute-start | bytes 221192 | tf_op jit(solution)/shard_map/ppermute | solution.py:28
  189.8 5.6 %collective-permute-start.30 = (f32[24,768]{1,0:T(8,128)S(1)}, f32[24,768]{1,0:T(8,128)S(1)}, u32[]{:S(2)}, u32[]{:S(2)}) collective-permute-start(f32[24,768]{1,0:T(8,128)S(1)} %products.1), channel_id=1, source_target_pairs={{24,0},{0,8},{8,16},{16,24},{56,32},{32,40},{40,48},{48,56},{88,64... | collective-permute-start | bytes 221192 | tf_op jit(solution)/shard_map/ppermute | solution.py:28
  191.8 3.7 %collective-permute-start.29 = (f32[24,768]{1,0:T(8,128)S(1)}, f32[24,768]{1,0:T(8,128)S(1)}, u32[]{:S(2)}, u32[]{:S(2)}) collective-permute-start(f32[24,768]{1,0:T(8,128)S(1)} %products.1), channel_id=1, source_target_pairs={{8,0},{16,8},{24,16},{0,24},{40,32},{48,40},{56,48},{32,56},{72,64... | collective-permute-start | bytes 221192 | tf_op jit(solution)/shard_map/ppermute | solution.py:28
  195.5 39.9 %copy-start.2 = (bf16[256,3072]{1,0:T(8,128)(2,1)S(1)}, bf16[256,3072]{1,0:T(8,128)(2,1)}, u32[]{:S(2)}) copy-start(bf16[256,3072]{1,0:T(8,128)(2,1)} %refs_2_.3) | copy-start | bytes 4718596
  195.5 4.9 %collective-permute-start.34 = (f32[24,768]{1,0:T(8,128)S(1)}, f32[24,768]{1,0:T(8,128)S(1)}, u32[]{:S(2)}, u32[]{:S(2)}) collective-permute-start(f32[24,768]{1,0:T(8,128)S(1)} %add_add_fusion.refs_5_), channel_id=1, source_target_pairs={{64,0},{72,8},{80,16},{88,24},{96,32},{104,40},{112,48},{120,56},{... | collective-permute-start | bytes 221192 | tf_op jit(solution)/shard_map/ppermute | solution.py:28
  195.6 5.3 %collective-permute-start.33 = (f32[24,768]{1,0:T(8,128)S(1)}, f32[24,768]{1,0:T(8,128)S(1)}, u32[]{:S(2)}, u32[]{:S(2)}) collective-permute-start(f32[24,768]{1,0:T(8,128)S(1)} %add_add_fusion.refs_5_), channel_id=1, source_target_pairs={{96,0},{104,8},{112,16},{120,24},{0,32},{8,40},{16,48},{24,56},{32... | collective-permute-start | bytes 221192 | tf_op jit(solution)/shard_map/ppermute | solution.py:28
  196.3 4.7 %collective-permute-start.32 = (f32[24,768]{1,0:T(8,128)S(1)}, f32[24,768]{1,0:T(8,128)S(1)}, u32[]{:S(2)}, u32[]{:S(2)}) collective-permute-start(f32[24,768]{1,0:T(8,128)S(1)} %add_add_fusion.refs_5_), channel_id=1, source_target_pairs={{32,0},{40,8},{48,16},{56,24},{64,32},{72,40},{80,48},{88,56},{96,... | collective-permute-start | bytes 221192 | tf_op jit(solution)/shard_map/ppermute | solution.py:28
  205.3 9.9 %collective-permute-start.38 = (bf16[9,32,512]{2,1,0:T(8,128)(2,1)S(1)}, bf16[9,32,512]{2,1,0:T(8,128)(2,1)S(1)}, u32[]{:S(2)}, u32[]{:S(2)}) collective-permute-start(bf16[9,32,512]{2,1,0:T(8,128)(2,1)S(1)} %get-tuple-element.69.refs_19_), channel_id=1, source_target_pairs={{0,6},{1,7},{2,0},{3,1},{4,2},{5,3},{6,4},{7,5},{8,14},{9,15},{10,... | collective-permute-start | bytes 884744 | tf_op jit(solution)/shard_map/ppermute | solution.py:33
  209.5 3.0 %collective-permute-start.41 = (bf16[8,32,512]{2,1,0:T(8,128)(2,1)S(1)}, bf16[8,32,512]{2,1,0:T(8,128)(2,1)S(1)}, u32[]{:S(2)}, u32[]{:S(2)}) collective-permute-start(bf16[8,32,512]{2,1,0:T(8,128)(2,1)S(1)} %get-tuple-element.68.refs_18_), channel_id=1, source_target_pairs={{0,1},{1,0},{2,3},{3,2},{4,5},{5,4},{6,7},{7,6},{8,9},{9,8},{10,11... | collective-permute-start | bytes 786440 | tf_op jit(solution)/shard_map/ppermute | solution.py:33
  210.5 10.3 %collective-permute-start.37 = (bf16[8,32,512]{2,1,0:T(8,128)(2,1)S(1)}, bf16[8,32,512]{2,1,0:T(8,128)(2,1)S(1)}, u32[]{:S(2)}, u32[]{:S(2)}) collective-permute-start(bf16[8,32,512]{2,1,0:T(8,128)(2,1)S(1)} %get-tuple-element.68.refs_18_), channel_id=1, source_target_pairs={{0,6},{1,7},{2,0},{3,1},{4,2},{5,3},{6,4},{7,5},{8,14},{9,15},{10,... | collective-permute-start | bytes 786440 | tf_op jit(solution)/shard_map/ppermute | solution.py:33
  210.5 13.0 %collective-permute-start.35 = (bf16[8,32,512]{2,1,0:T(8,128)(2,1)S(1)}, bf16[8,32,512]{2,1,0:T(8,128)(2,1)S(1)}, u32[]{:S(2)}, u32[]{:S(2)}) collective-permute-start(bf16[8,32,512]{2,1,0:T(8,128)(2,1)S(1)} %get-tuple-element.68.refs_18_), channel_id=1, source_target_pairs={{0,2},{1,3},{2,4},{3,5},{4,6},{5,7},{6,0},{7,1},{8,10},{9,11},{10,... | collective-permute-start | bytes 786440 | tf_op jit(solution)/shard_map/ppermute | solution.py:33
  212.0 11.6 %collective-permute-start.42 = (bf16[9,32,512]{2,1,0:T(8,128)(2,1)S(1)}, bf16[9,32,512]{2,1,0:T(8,128)(2,1)S(1)}, u32[]{:S(2)}, u32[]{:S(2)}) collective-permute-start(bf16[9,32,512]{2,1,0:T(8,128)(2,1)S(1)} %get-tuple-element.69.refs_19_), channel_id=1, source_target_pairs={{0,1},{1,0},{2,3},{3,2},{4,5},{5,4},{6,7},{7,6},{8,9},{9,8},{10,11... | collective-permute-start | bytes 884744 | tf_op jit(solution)/shard_map/ppermute | solution.py:33
  212.5 13.2 %collective-permute-start.36 = (bf16[9,32,512]{2,1,0:T(8,128)(2,1)S(1)}, bf16[9,32,512]{2,1,0:T(8,128)(2,1)S(1)}, u32[]{:S(2)}, u32[]{:S(2)}) collective-permute-start(bf16[9,32,512]{2,1,0:T(8,128)(2,1)S(1)} %get-tuple-element.69.refs_19_), channel_id=1, source_target_pairs={{0,2},{1,3},{2,4},{3,5},{4,6},{5,7},{6,0},{7,1},{8,10},{9,11},{10,... | collective-permute-start | bytes 884744 | tf_op jit(solution)/shard_map/ppermute | solution.py:33
  215.2 11.9 %collective-permute-start.40 = (bf16[9,32,512]{2,1,0:T(8,128)(2,1)S(1)}, bf16[9,32,512]{2,1,0:T(8,128)(2,1)S(1)}, u32[]{:S(2)}, u32[]{:S(2)}) collective-permute-start(bf16[9,32,512]{2,1,0:T(8,128)(2,1)S(1)} %collective-permute-done.38.refs_23_), channel_id=1, source_target_pairs={{0,6},{1,7},{2,0},{3,1},{4,2},{5,3},{6,4},{7,5},{8,14},{9,15},{10,... | collective-permute-start | bytes 884744 | tf_op jit(solution)/shard_map/ppermute | solution.py:33
  220.8 7.9 %collective-permute-start.45 = (bf16[8,32,512]{2,1,0:T(8,128)(2,1)S(1)}, bf16[8,32,512]{2,1,0:T(8,128)(2,1)S(1)}, u32[]{:S(2)}, u32[]{:S(2)}) collective-permute-start(bf16[8,32,512]{2,1,0:T(8,128)(2,1)S(1)} %collective-permute-done.37.refs_22_), channel_id=1, source_target_pairs={{0,1},{1,0},{2,3},{3,2},{4,5},{5,4},{6,7},{7,6},{8,9},{9,8},{10,11... | collective-permute-start | bytes 786440 | tf_op jit(solution)/shard_map/ppermute | solution.py:33
  223.5 10.1 %collective-permute-start.39 = (bf16[8,32,512]{2,1,0:T(8,128)(2,1)S(1)}, bf16[8,32,512]{2,1,0:T(8,128)(2,1)S(1)}, u32[]{:S(2)}, u32[]{:S(2)}) collective-permute-start(bf16[8,32,512]{2,1,0:T(8,128)(2,1)S(1)} %collective-permute-done.35.refs_20_), channel_id=1, source_target_pairs={{0,2},{1,3},{2,4},{3,5},{4,6},{5,7},{6,0},{7,1},{8,10},{9,11},{10,... | collective-permute-start | bytes 786440 | tf_op jit(solution)/shard_map/ppermute | solution.py:33
  223.6 10.7 %collective-permute-start.46 = (bf16[9,32,512]{2,1,0:T(8,128)(2,1)S(1)}, bf16[9,32,512]{2,1,0:T(8,128)(2,1)S(1)}, u32[]{:S(2)}, u32[]{:S(2)}) collective-permute-start(bf16[9,32,512]{2,1,0:T(8,128)(2,1)S(1)} %collective-permute-done.38.refs_23_), channel_id=1, source_target_pairs={{0,1},{1,0},{2,3},{3,2},{4,5},{5,4},{6,7},{7,6},{8,9},{9,8},{10,11... | collective-permute-start | bytes 884744 | tf_op jit(solution)/shard_map/ppermute | solution.py:33
  225.8 8.4 %collective-permute-start.44 = (bf16[9,32,512]{2,1,0:T(8,128)(2,1)S(1)}, bf16[9,32,512]{2,1,0:T(8,128)(2,1)S(1)}, u32[]{:S(2)}, u32[]{:S(2)}) collective-permute-start(bf16[9,32,512]{2,1,0:T(8,128)(2,1)S(1)} %collective-permute-done.36.refs_21_), channel_id=1, source_target_pairs={{0,1},{1,0},{2,3},{3,2},{4,5},{5,4},{6,7},{7,6},{8,9},{9,8},{10,11... | collective-permute-start | bytes 884744 | tf_op jit(solution)/shard_map/ppermute | solution.py:33
  227.1 8.3 %collective-permute-start.48 = (bf16[9,32,512]{2,1,0:T(8,128)(2,1)S(1)}, bf16[9,32,512]{2,1,0:T(8,128)(2,1)S(1)}, u32[]{:S(2)}, u32[]{:S(2)}) collective-permute-start(bf16[9,32,512]{2,1,0:T(8,128)(2,1)S(1)} %collective-permute-done.40.refs_25_), channel_id=1, source_target_pairs={{0,1},{1,0},{2,3},{3,2},{4,5},{5,4},{6,7},{7,6},{8,9},{9,8},{10,11... | collective-permute-start | bytes 884744 | tf_op jit(solution)/shard_map/ppermute | solution.py:33
  228.7 5.5 %collective-permute-start.43 = (bf16[8,32,512]{2,1,0:T(8,128)(2,1)S(1)}, bf16[8,32,512]{2,1,0:T(8,128)(2,1)S(1)}, u32[]{:S(2)}, u32[]{:S(2)}) collective-permute-start(bf16[8,32,512]{2,1,0:T(8,128)(2,1)S(1)} %collective-permute-done.35.refs_20_), channel_id=1, source_target_pairs={{0,1},{1,0},{2,3},{3,2},{4,5},{5,4},{6,7},{7,6},{8,9},{9,8},{10,11... | collective-permute-start | bytes 786440 | tf_op jit(solution)/shard_map/ppermute | solution.py:33
  233.6 1.7 collective-permute-start.47

commit v6 on v5

--- a/solution.py
+++ b/solution.py
@@ -127,7 +127,7 @@
         columns[pl.ds(pl.multiple_of(index * LENGTH, 8), LENGTH), :] = total
         return carry
 
-    lax.fori_loop(0, BLOCKS, block, 0)
+    lax.fori_loop(0, BLOCKS, block, 0, unroll=2)
     out_ref[...] = columns[...].T[:PRODUCTS, :]
 
 
@@ -251,8 +251,8 @@
         grad_ref[index - first] = grad[PAD : PAD + SHARE].astype(jnp.bfloat16)
 
     half = BLOCKS // 2
-    pl.loop(0, half)(lambda index: block(index, low_ref, 0))
-    pl.loop(half, BLOCKS)(lambda index: block(index, high_ref, half))
+    pl.loop(0, half, unroll=2)(lambda index: block(index, low_ref, 0))
+    pl.loop(half, BLOCKS, unroll=2)(lambda index: block(index, high_ref, half))
     place = lax.broadcasted_iota(jnp.int32, squares.shape, 1) % LENGTH
     own_rows = (place >= PAD) & (place < PAD + SHARE)
     parts = []

time: 255 us -> 254 us (level)
  no operation moved by 1% of the time
where the time goes in v6:
time: 254 us; the launch traced here: 253 us
  waiting for transfers between devices  94.4 us (37%)
  starting transfers between devices  89.1 us (35%)
  Pallas kernels  50.6 us (20%)
  other arithmetic  10 us (4%)
  local copies, waits for them, and re-layouts  8.04 us (3%)
    ppermute x21, waiting for transfers between devices, from_dp(): return lax.ppermute(block, 'dp', route)  53.4 us
    ppermute x23, starting transfers between devices, along_mp(): return lax.ppermute(block, 'mp', route)  45 us
    ppermute x23, waiting for transfers between devices, along_mp(): return lax.ppermute(block, 'mp', route)  29.4 us
    ppermute x21, starting transfers between devices, from_dp(): return lax.ppermute(block, 'dp', route)  27.9 us
    pallas_call x3, Pallas kernels, project(): pl.pallas_call(lambda *refs: project_kernel(len(rows), blocks, *refs), ou...  22.2 us
    pallas_call x1, Pallas kernels, weight_gradient(): pl.pallas_call(lambda *refs: weight_kernel(len(rows), *refs), out_shape=(...  18.5 us
    ppermute x3, starting transfers between devices, neighbour(): return lax.ppermute(block, 'mp', route)  7.14 us
    all_to_all x1, starting transfers between devices, local(): shares = lax.all_to_all(windows(target, block_rows), 'mp', 0, 0, tiled=True)  7.13 us
  transfers between devices with their start and end apart: 50, of which 25 were waited for; matrix products, arithmetic and copies ran while one was open for 6% of the time, Pallas kernels for 7%

profile of v6, /device:TPU:1, one launch (start us, length us, event | category | flops | bytes accessed | tf_op | source)
XLA Modules:
  0.0 253.4 jit_solution(3530229052645876829)
XLA Ops:
  0.6 4.7 %collective-permute-start.7 = (bf16[256,3072]{1,0:T(8,128)(2,1)}, bf16[256,3072]{1,0:T(8,128)(2,1)}, u32[]{:S(2)}, u32[]{:S(2)}) collective-permute-start(bf16[256,3072]{1,0:T(8,128)(2,1)} %refs_2_.3), channel_id=1, source_target_pairs={{8,0},{16,8},{24,16},{0,24},{40,32},{48,40},{56,48},{32,56},{72,64... | collective-permute-start | bytes 4718600 | tf_op jit(solution)/shard_map/ppermute | solution.py:28
  5.3 2.7 %collective-permute-start.14 = (bf16[256,3072]{1,0:T(8,128)(2,1)}, bf16[256,3072]{1,0:T(8,128)(2,1)}, u32[]{:S(2)}, u32[]{:S(2)}) collective-permute-start(bf16[256,3072]{1,0:T(8,128)(2,1)} %refs_2_.3), channel_id=1, source_target_pairs={{32,0},{40,8},{48,16},{56,24},{64,32},{72,40},{80,48},{88,56},{96,... | collective-permute-start | bytes 4718600 | tf_op jit(solution)/shard_map/ppermute | solution.py:28
  8.7 3.1 %collective-permute-start.9 = (s32[16]{0:T(128)S(1)}, s32[16]{0:T(128)S(1)}, u32[]{:S(2)}, u32[]{:S(2)}) collective-permute-start(s32[16]{0:T(128)S(1)} %slice.37), channel_id=1, source_target_pairs={{1,0},{2,1},{3,2},{4,3},{5,4},{6,5},{7,6},{9,8},{10,9},{11,10},{12... | collective-permute-start | bytes 200 | tf_op jit(solution)/shard_map/ppermute | solution.py:39
  12.6 1.9 collective-permute-done.9
  14.6 1.9 collective-permute-start.10
  17.6 2.1 collective-permute-start.8
  19.7 3.5 %collective-permute-done.8 = bf16[16,512]{1,0:T(8,128)(2,1)S(1)} collective-permute-done((bf16[16,512]{1,0:T(8,128)(2,1)S(1)}, bf16[16,512]{1,0:T(8,128)(2,1)S(1)}, u32[]{:S(2)}, u32[]{:S(2)}) %collective-permute-start.8) | collective-permute-done | bytes 16416 | tf_op jit(solution)/shard_map/ppermute | solution.py:39
  23.1 15.5 %collective-permute-done.7.refs_4_ = bf16[256,3072]{1,0:T(8,128)(2,1)} collective-permute-done((bf16[256,3072]{1,0:T(8,128)(2,1)}, bf16[256,3072]{1,0:T(8,128)(2,1)}, u32[]{:S(2)}, u32[]{:S(2)}) %collective-permute-start.7) | collective-permute-done | bytes 1572896 | tf_op jit(solution)/shard_map/ppermute | solution.py:28
  38.7 2.4 collective-permute-done.14.refs_6_
  41.1 3.4 %collective-permute-start.11 = (bf16[256,3072]{1,0:T(8,128)(2,1)}, bf16[256,3072]{1,0:T(8,128)(2,1)}, u32[]{:S(2)}, u32[]{:S(2)}) collective-permute-start(bf16[256,3072]{1,0:T(8,128)(2,1)} %collective-permute-done.7.refs_4_), channel_id=1, source_target_pairs={{32,0},{40,8},{48,16},{56,24},{64,32},{72,40},{80,48},{88,56},{96,... | collective-permute-start | bytes 4718600 | tf_op jit(solution)/shard_map/ppermute | solution.py:28
  44.5 2.7 %collective-permute-start.15 = (bf16[256,3072]{1,0:T(8,128)(2,1)}, bf16[256,3072]{1,0:T(8,128)(2,1)}, u32[]{:S(2)}, u32[]{:S(2)}) collective-permute-start(bf16[256,3072]{1,0:T(8,128)(2,1)} %collective-permute-done.5.refs_5_), channel_id=1, source_target_pairs={{8,0},{16,8},{24,16},{0,24},{40,32},{48,40},{56,48},{32,56},{72,64... | collective-permute-start | bytes 4718600 | tf_op jit(solution)/shard_map/ppermute | solution.py:28
  48.2 1.1 pad_maximum_fusion.refs_0_
  50.3 7.1 %all-to-all-start = ((bf16[8,2,48,640]{3,2,1,0:T(8,128)(2,1)}), bf16[8,2,48,640]{3,2,1,0:T(8,128)(2,1)}, u32[]{:S(2)}, u32[]{:S(2)}) async-start(bf16[8,2,48,640]{3,2,1,0:T(8,128)(2,1)} %copy-done.3), calls=%async_computation | async-start | bytes 1966080 | tf_op jit(solution)/shard_map/all_to_all | solution.py:503
  57.5 20.5 %collective-permute-done.16.refs_10_ = bf16[256,3072]{1,0:T(8,128)(2,1)} collective-permute-done((bf16[256,3072]{1,0:T(8,128)(2,1)}, bf16[256,3072]{1,0:T(8,128)(2,1)}, u32[]{:S(2)}, u32[]{:S(2)}) %collective-permute-start.16) | collective-permute-done | bytes 1572896 | tf_op jit(solution)/shard_map/ppermute | solution.py:28
  77.9 2.7 %collective-permute-start.13 = (bf16[256,3072]{1,0:T(8,128)(2,1)}, bf16[256,3072]{1,0:T(8,128)(2,1)}, u32[]{:S(2)}, u32[]{:S(2)}) collective-permute-start(bf16[256,3072]{1,0:T(8,128)(2,1)} %collective-permute-done.11.refs_9_), channel_id=1, source_target_pairs={{8,0},{16,8},{24,16},{0,24},{40,32},{48,40},{56,48},{32,56},{72,64... | collective-permute-start | bytes 4718600 | tf_op jit(solution)/shard_map/ppermute | solution.py:28
  80.6 2.1 collective-permute-start.12
  82.7 1.4 copy-done.1
  84.1 11.6 %project.3 = (bf16[4,9,32,512]{3,2,1,0:T(8,128)(2,1)S(1)}, f32[4,9,32,512]{3,2,1,0:T(8,128)S(1)}) custom-call(s32[1]{0:T(128)} %bitcast.refs_0_, bf16[3072,512]{1,0:T(8,128)(2,1)S(1)} %copy-done, bf16[256,3072]{1,0:T(8,128)(2,1)S(1)} %copy-done.1, bf16[256,3072]{1,0:T(8,128)(2,1)} %collective-permute-done.refs_3_, ...), custom_call_target="tpu_custom_call" | custom-call | flops 1 | bytes 1 | tf_op jit(solution)/shard_map/project/pallas_call | solution.py:325
  95.7 6.1 %collective-permute-start.17 = (bf16[4,9,32,512]{3,2,1,0:T(8,128)(2,1)S(1)}, bf16[4,9,32,512]{3,2,1,0:T(8,128)(2,1)S(1)}, u32[]{:S(2)}, u32[]{:S(2)}) collective-permute-start(bf16[4,9,32,512]{3,2,1,0:T(8,128)(2,1)S(1)} %get-tuple-element.46), channel_id=1, source_target_pairs={{0,1},{1,0},{2,3},{3,2},{4,5},{5,4},{6,7},{7,6},{8,9},{9,8},{10,11... | collective-permute-start | bytes 3538952 | tf_op jit(solution)/shard_map/ppermute | solution.py:33
  101.8 2.5 collective-permute-done.17
  104.3 1.9 convert_add_fusion
  106.3 9.3 %collective-permute-done.6.refs_3_.refs_12_ = bf16[256,3072]{1,0:T(8,128)(2,1)} collective-permute-done((bf16[256,3072]{1,0:T(8,128)(2,1)}, bf16[256,3072]{1,0:T(8,128)(2,1)}, u32[]{:S(2)}, u32[]{:S(2)}) %collective-permute-start.6) | collective-permute-done | bytes 1572896 | tf_op jit(solution)/shard_map/ppermute | solution.py:28
  115.6 2.7 %collective-permute-start.18 = (bf16[256,3072]{1,0:T(8,128)(2,1)}, bf16[256,3072]{1,0:T(8,128)(2,1)}, u32[]{:S(2)}, u32[]{:S(2)}) collective-permute-start(bf16[256,3072]{1,0:T(8,128)(2,1)} %collective-permute-done.12.refs_4_.refs_13_), channel_id=1, source_target_pairs={{8,0},{16,8},{24,16},{0,24},{40,32},{48,40},{56,48},{32,56},{72,64... | collective-permute-start | bytes 4718600 | tf_op jit(solution)/shard_map/ppermute | solution.py:28
  118.4 2.4 fusion.9
  120.8 1.2 collective-permute-start.19
  122.3 2.5 collective-permute-start.21
  125.7 2.5 collective-permute-done.19
  128.2 1.3 collective-permute-start.20
  129.5 1.7 fusion.15
  132.0 5.9 %project.4 = (bf16[4,4,32,512]{3,2,1,0:T(8,128)(2,1)S(1)}, f32[4,4,32,512]{3,2,1,0:T(8,128)S(1)}) custom-call(s32[1]{0:T(128)} %bitcast.refs_0_, bf16[3072,512]{1,0:T(8,128)(2,1)S(1)} %copy-done, bf16[256,3072]{1,0:T(8,128)(2,1)} %collective-permute-done.4.refs_2_.refs_11_, bf16[256,3072]{1,0:T(8,128)(2,1)} %collective-permute-done.6.refs_3_.refs_12_, ...), custom_call_target="tpu_custom_call" | custom-call | flops 1 | bytes 1 | tf_op jit(solution)/shard_map/project/pallas_call | solution.py:325
  137.9 8.6 %collective-permute-start.22 = (bf16[4,4,32,512]{3,2,1,0:T(8,128)(2,1)S(1)}, bf16[4,4,32,512]{3,2,1,0:T(8,128)(2,1)S(1)}, u32[]{:S(2)}, u32[]{:S(2)}) collective-permute-start(bf16[4,4,32,512]{3,2,1,0:T(8,128)(2,1)S(1)} %get-tuple-element.53), channel_id=1, source_target_pairs={{0,1},{1,0},{2,3},{3,2},{4,5},{5,4},{6,7},{7,6},{8,9},{9,8},{10,11... | collective-permute-start | bytes 1572872 | tf_op jit(solution)/shard_map/ppermute | solution.py:33
  146.5 1.3 slice_convert_fusion.target_ref.refs_1_
  147.9 1.5 bitcast_add_fusion.refs_2_
  149.6 4.7 %project.5 = (bf16[4,3,32,512]{3,2,1,0:T(8,128)(2,1)S(1)}, f32[4,3,32,512]{3,2,1,0:T(8,128)S(1)}) custom-call(s32[1]{0:T(128)} %bitcast.refs_0_, bf16[3072,512]{1,0:T(8,128)(2,1)S(1)} %copy-done, bf16[256,3072]{1,0:T(8,128)(2,1)} %collective-permute-done.2.refs_2_.refs_15_, bf16[256,3072]{1,0:T(8,128)(2,1)} %collective-permute-done.3.refs_3_.refs_16_, ...), custom_call_target="tpu_custom_call" | custom-call | flops 1 | bytes 1 | tf_op jit(solution)/shard_map/project/pallas_call | solution.py:325
  154.3 4.4 %collective-permute-start.23 = (bf16[4,3,32,512]{3,2,1,0:T(8,128)(2,1)S(1)}, bf16[4,3,32,512]{3,2,1,0:T(8,128)(2,1)S(1)}, u32[]{:S(2)}, u32[]{:S(2)}) collective-permute-start(bf16[4,3,32,512]{3,2,1,0:T(8,128)(2,1)S(1)} %get-tuple-element.64), channel_id=1, source_target_pairs={{0,1},{1,0},{2,3},{3,2},{4,5},{5,4},{6,7},{7,6},{8,9},{9,8},{10,11... | collective-permute-start | bytes 1179656 | tf_op jit(solution)/shard_map/ppermute | solution.py:33
  158.7 1.3 collective-permute-done.23
  160.3 1.3 collective-permute-start.24
  161.6 1.5 collective-permute-start.25
  163.0 1.5 collective-permute-start.26
  164.6 3.8 %collective-permute-done.24 = bf16[7,32,512]{2,1,0:T(8,128)(2,1)S(1)} collective-permute-done((bf16[7,32,512]{2,1,0:T(8,128)(2,1)S(1)}, bf16[7,32,512]{2,1,0:T(8,128)(2,1)S(1)}, u32[]{:S(2)}, u32[]{:S(2)}) %collective-permute-start.24) | collective-permute-done | bytes 229408 | tf_op jit(solution)/shard_map/ppermute | solution.py:33
  168.4 5.9 %collective-permute-done.26 = bf16[7,32,512]{2,1,0:T(8,128)(2,1)S(1)} collective-permute-done((bf16[7,32,512]{2,1,0:T(8,128)(2,1)S(1)}, bf16[7,32,512]{2,1,0:T(8,128)(2,1)S(1)}, u32[]{:S(2)}, u32[]{:S(2)}) %collective-permute-start.26) | collective-permute-done | bytes 229408 | tf_op jit(solution)/shard_map/ppermute | solution.py:33
  174.5 2.0 collective-permute-start.27
  176.5 3.3 %collective-permute-done.27.refs_4_ = f32[16,8,512]{2,1,0:T(8,128)S(1)} collective-permute-done((f32[16,8,512]{2,1,0:T(8,128)S(1)}, f32[16,8,512]{2,1,0:T(8,128)S(1)}, u32[]{:S(2)}, u32[]{:S(2)}) %collective-permute-start.27) | collective-permute-done | bytes 262176 | tf_op jit(solution)/shard_map/ppermute | solution.py:449
  179.7 2.5 %collective-permute-done.28.refs_5_ = f32[16,8,512]{2,1,0:T(8,128)S(1)} collective-permute-done((f32[16,8,512]{2,1,0:T(8,128)S(1)}, f32[16,8,512]{2,1,0:T(8,128)S(1)}, u32[]{:S(2)}, u32[]{:S(2)}) %collective-permute-start.28) | collective-permute-done | bytes 262176 | tf_op jit(solution)/shard_map/ppermute | solution.py:449
  183.1 4.8 %products.1 = f32[24,768]{1,0:T(8,128)S(1)} custom-call(f32[16,48,512]{2,1,0:T(8,128)S(1)} %assemble.1.state_ref.refs_0_, f32[16,48,512]{2,1,0:T(8,128)S(1)} %slice_convert_fusion.target_ref.refs_1_, f32[16,48,1]{2,1,0:T(8,128)S(1)} %slice_convert_fusion.1.keep_ref.refs_2_, f32[3,512]{1,0:T(4,128)S(1)} %copy-done.4), custom_call_target="tpu_custom_call" | custom-call | flops 1 | bytes 1 | tf_op jit(solution)/shard_map/products/pallas_call | solution.py:136
  188.0 1.3 collective-permute-start.31
  189.3 2.1 collective-permute-start.30
  192.8 2.2 collective-permute-done.30
  195.8 2.1 collective-permute-start.32
  197.9 2.1 collective-permute-done.34.refs_8_
  200.5 4.2 %gradients.1 = (bf16[8,32,512]{2,1,0:T(8,128)(2,1)S(1)}, bf16[9,32,512]{2,1,0:T(8,128)(2,1)S(1)}) custom-call(f32[16,48,512]{2,1,0:T(8,128)S(1)} %assemble.1.state_ref.refs_0_, f32[16,48,512]{2,1,0:T(8,128)S(1)} %slice_convert_fusion.target_ref.refs_1_, f32[16,48,1]{2,1,0:T(8,128)S(1)} %slice_convert_fusion.1.keep_ref.refs_2_, ...), custom_call_target="tpu_custom_call" | custom-call | flops 1 | bytes 1 | tf_op jit(solution)/shard_map/gradients/pallas_call | solution.py:274
  204.6 4.3 %collective-permute-start.38 = (bf16[9,32,512]{2,1,0:T(8,128)(2,1)S(1)}, bf16[9,32,512]{2,1,0:T(8,128)(2,1)S(1)}, u32[]{:S(2)}, u32[]{:S(2)}) collective-permute-start(bf16[9,32,512]{2,1,0:T(8,128)(2,1)S(1)} %get-tuple-element.69.refs_19_), channel_id=1, source_target_pairs={{0,6},{1,7},{2,0},{3,1},{4,2},{5,3},{6,4},{7,5},{8,14},{9,15},{10,... | collective-permute-start | bytes 884744 | tf_op jit(solution)/shard_map/ppermute | solution.py:33
  208.9 1.0 collective-permute-start.41
  209.9 1.5 collective-permute-start.35
  211.9 2.6 %collective-permute-done.38.refs_23_ = bf16[9,32,512]{2,1,0:T(8,128)(2,1)S(1)} collective-permute-done((bf16[9,32,512]{2,1,0:T(8,128)(2,1)S(1)}, bf16[9,32,512]{2,1,0:T(8,128)(2,1)S(1)}, u32[]{:S(2)}, u32[]{:S(2)}) %collective-permute-start.38) | collective-permute-done | bytes 294944 | tf_op jit(solution)/shard_map/ppermute | solution.py:33
  214.5 3.4 %collective-permute-start.40 = (bf16[9,32,512]{2,1,0:T(8,128)(2,1)S(1)}, bf16[9,32,512]{2,1,0:T(8,128)(2,1)S(1)}, u32[]{:S(2)}, u32[]{:S(2)}) collective-permute-start(bf16[9,32,512]{2,1,0:T(8,128)(2,1)S(1)} %collective-permute-done.38.refs_23_), channel_id=1, source_target_pairs={{0,6},{1,7},{2,0},{3,1},{4,2},{5,3},{6,4},{7,5},{8,14},{9,15},{10,... | collective-permute-start | bytes 884744 | tf_op jit(solution)/shard_map/ppermute | solution.py:33
  217.9 2.2 collective-permute-done.37.refs_22_
  220.1 2.8 %collective-permute-start.45 = (bf16[8,32,512]{2,1,0:T(8,128)(2,1)S(1)}, bf16[8,32,512]{2,1,0:T(8,128)(2,1)S(1)}, u32[]{:S(2)}, u32[]{:S(2)}) collective-permute-start(bf16[8,32,512]{2,1,0:T(8,128)(2,1)S(1)} %collective-permute-done.37.refs_22_), channel_id=1, source_target_pairs={{0,1},{1,0},{2,3},{3,2},{4,5},{5,4},{6,7},{7,6},{8,9},{9,8},{10,11... | collective-permute-start | bytes 786440 | tf_op jit(solution)/shard_map/ppermute | solution.py:33
  223.0 2.1 collective-permute-done.36.refs_21_
  225.2 1.0 collective-permute-start.44
  226.5 1.6 collective-permute-start.48
  228.1 5.0 %collective-permute-done.39.refs_24_ = bf16[8,32,512]{2,1,0:T(8,128)(2,1)S(1)} collective-permute-done((bf16[8,32,512]{2,1,0:T(8,128)(2,1)S(1)}, bf16[8,32,512]{2,1,0:T(8,128)(2,1)S(1)}, u32[]{:S(2)}, u32[]{:S(2)}) %collective-permute-start.39) | collective-permute-done | bytes 262176 | tf_op jit(solution)/shard_map/ppermute | solution.py:33
  233.6 1.1 collective-permute-done.47.refs_32_
  234.8 18.5 %weight_gradient.1 = (f32[3072,512]{1,0:T(8,128)}, f32[1,128]{1,0:T(1,128)}) custom-call(s32[16]{0:T(128)S(1)} %select_reduce_fusion.refs_0_, s32[8]{0:T(128)S(1)} %stack.112.refs_1_, bf16[256,3072]{1,0:T(8,128)(2,1)S(1)} %copy-done.2, bf16[256,3072]{1,0:T(8,128)(2,1)} %collective-permute-done.refs_3_, bf16[256,3072]{1,0:T(8,128)(2,1)} %collective-permute-done.7.refs_4_, ...), custom_call_target="tpu_custom_call" | custom-call | flops 1 | bytes 1 | tf_op jit(solution)/shard_map/weight_gradient/pallas_call | solution.py:413
  (81 shorter events, 12.3 us)
Async XLA Ops:
  0.6 38.0 %collective-permute-start.7 = (bf16[256,3072]{1,0:T(8,128)(2,1)}, bf16[256,3072]{1,0:T(8,128)(2,1)}, u32[]{:S(2)}, u32[]{:S(2)}) collective-permute-start(bf16[256,3072]{1,0:T(8,128)(2,1)} %refs_2_.3), channel_id=1, source_target_pairs={{8,0},{16,8},{24,16},{0,24},{40,32},{48,40},{56,48},{32,56},{72,64... | collective-permute-start | bytes 4718600 | tf_op jit(solution)/shard_map/ppermute | solution.py:28
  5.3 35.8 %collective-permute-start.14 = (bf16[256,3072]{1,0:T(8,128)(2,1)}, bf16[256,3072]{1,0:T(8,128)(2,1)}, u32[]{:S(2)}, u32[]{:S(2)}) collective-permute-start(bf16[256,3072]{1,0:T(8,128)(2,1)} %refs_2_.3), channel_id=1, source_target_pairs={{32,0},{40,8},{48,16},{56,24},{64,32},{72,40},{80,48},{88,56},{96,... | collective-permute-start | bytes 4718600 | tf_op jit(solution)/shard_map/ppermute | solution.py:28
  8.0 36.5 %collective-permute-start.5 = (bf16[256,3072]{1,0:T(8,128)(2,1)}, bf16[256,3072]{1,0:T(8,128)(2,1)}, u32[]{:S(2)}, u32[]{:S(2)}) collective-permute-start(bf16[256,3072]{1,0:T(8,128)(2,1)} %refs_2_.3), channel_id=1, source_target_pairs={{96,0},{104,8},{112,16},{120,24},{0,32},{8,40},{16,48},{24,56},{32... | collective-permute-start | bytes 4718600 | tf_op jit(solution)/shard_map/ppermute | solution.py:28
  8.0 39.2 %collective-permute-start = (bf16[256,3072]{1,0:T(8,128)(2,1)}, bf16[256,3072]{1,0:T(8,128)(2,1)}, u32[]{:S(2)}, u32[]{:S(2)}) collective-permute-start(bf16[256,3072]{1,0:T(8,128)(2,1)} %refs_2_.3), channel_id=1, source_target_pairs={{24,0},{0,8},{8,16},{16,24},{56,32},{32,40},{40,48},{48,56},{88,64... | collective-permute-start | bytes 4718600 | tf_op jit(solution)/shard_map/ppermute | solution.py:28
  8.7 5.8 %collective-permute-start.9 = (s32[16]{0:T(128)S(1)}, s32[16]{0:T(128)S(1)}, u32[]{:S(2)}, u32[]{:S(2)}) collective-permute-start(s32[16]{0:T(128)S(1)} %slice.37), channel_id=1, source_target_pairs={{1,0},{2,1},{3,2},{4,3},{5,4},{6,5},{7,6},{9,8},{10,9},{11,10},{12... | collective-permute-start | bytes 200 | tf_op jit(solution)/shard_map/ppermute | solution.py:39
  14.6 3.0 %collective-permute-start.10 = (s32[17]{0:T(128)S(1)}, s32[17]{0:T(128)S(1)}, u32[]{:S(2)}, u32[]{:S(2)}) collective-permute-start(s32[17]{0:T(128)S(1)} %slice.38), channel_id=1, source_target_pairs={{0,1},{1,2},{2,3},{3,4},{4,5},{5,6},{6,7},{8,9},{9,10},{10,11},{11... | collective-permute-start | bytes 212 | tf_op jit(solution)/shard_map/ppermute | solution.py:39
  17.6 5.6 %collective-permute-start.8 = (bf16[16,512]{1,0:T(8,128)(2,1)S(1)}, bf16[16,512]{1,0:T(8,128)(2,1)S(1)}, u32[]{:S(2)}, u32[]{:S(2)}) collective-permute-start(bf16[16,512]{1,0:T(8,128)(2,1)S(1)} %slice.36), channel_id=1, source_target_pairs={{1,0},{2,1},{3,2},{4,3},{5,4},{6,5},{7,6},{9,8},{10,9},{11,10},{12... | collective-permute-start | bytes 49160 | tf_op jit(solution)/shard_map/ppermute | solution.py:39
  41.1 36.8 %collective-permute-start.16 = (bf16[256,3072]{1,0:T(8,128)(2,1)}, bf16[256,3072]{1,0:T(8,128)(2,1)}, u32[]{:S(2)}, u32[]{:S(2)}) collective-permute-start(bf16[256,3072]{1,0:T(8,128)(2,1)} %collective-permute-done.14.refs_6_), channel_id=1, source_target_pairs={{24,0},{0,8},{8,16},{16,24},{56,32},{32,40},{40,48},{48,56},{88,64... | collective-permute-start | bytes 4718600 | tf_op jit(solution)/shard_map/ppermute | solution.py:28
  41.1 36.8 %collective-permute-start.11 = (bf16[256,3072]{1,0:T(8,128)(2,1)}, bf16[256,3072]{1,0:T(8,128)(2,1)}, u32[]{:S(2)}, u32[]{:S(2)}) collective-permute-start(bf16[256,3072]{1,0:T(8,128)(2,1)} %collective-permute-done.7.refs_4_), channel_id=1, source_target_pairs={{32,0},{40,8},{48,16},{56,24},{64,32},{72,40},{80,48},{88,56},{96,... | collective-permute-start | bytes 4718600 | tf_op jit(solution)/shard_map/ppermute | solution.py:28
  44.5 36.1 %collective-permute-start.15 = (bf16[256,3072]{1,0:T(8,128)(2,1)}, bf16[256,3072]{1,0:T(8,128)(2,1)}, u32[]{:S(2)}, u32[]{:S(2)}) collective-permute-start(bf16[256,3072]{1,0:T(8,128)(2,1)} %collective-permute-done.5.refs_5_), channel_id=1, source_target_pairs={{8,0},{16,8},{24,16},{0,24},{40,32},{48,40},{56,48},{32,56},{72,64... | collective-permute-start | bytes 4718600 | tf_op jit(solution)/shard_map/ppermute | solution.py:28
  47.2 35.6 %collective-permute-start.1 = (bf16[256,3072]{1,0:T(8,128)(2,1)}, bf16[256,3072]{1,0:T(8,128)(2,1)}, u32[]{:S(2)}, u32[]{:S(2)}) collective-permute-start(bf16[256,3072]{1,0:T(8,128)(2,1)} %collective-permute-done.refs_3_), channel_id=1, source_target_pairs={{96,0},{104,8},{112,16},{120,24},{0,32},{8,40},{16,48},{24,56},{32... | collective-permute-start | bytes 4718600 | tf_op jit(solution)/shard_map/ppermute | solution.py:28
  49.3 33.5 %copy-start = (bf16[3072,512]{1,0:T(8,128)(2,1)S(1)}, bf16[3072,512]{1,0:T(8,128)(2,1)}, u32[]{:S(2)}) copy-start(bf16[3072,512]{1,0:T(8,128)(2,1)} %refs_1_.5) | copy-start | bytes 9437188
  49.4 0.9 copy-start.3
  50.3 32.4 %all-to-all-start = ((bf16[8,2,48,640]{3,2,1,0:T(8,128)(2,1)}), bf16[8,2,48,640]{3,2,1,0:T(8,128)(2,1)}, u32[]{:S(2)}, u32[]{:S(2)}) async-start(bf16[8,2,48,640]{3,2,1,0:T(8,128)(2,1)} %copy-done.3), calls=%async_computation | async-start | bytes 1966080 | tf_op jit(solution)/shard_map/all_to_all | solution.py:503
  57.5 58.1 %collective-permute-start.6 = (bf16[256,3072]{1,0:T(8,128)(2,1)}, bf16[256,3072]{1,0:T(8,128)(2,1)}, u32[]{:S(2)}, u32[]{:S(2)}) collective-permute-start(bf16[256,3072]{1,0:T(8,128)(2,1)} %collective-permute-done.5.refs_5_), channel_id=1, source_target_pairs={{96,0},{104,8},{112,16},{120,24},{0,32},{8,40},{16,48},{24,56},{32... | collective-permute-start | bytes 4718600 | tf_op jit(solution)/shard_map/ppermute | solution.py:28
  77.9 37.7 %collective-permute-start.4 = (bf16[256,3072]{1,0:T(8,128)(2,1)}, bf16[256,3072]{1,0:T(8,128)(2,1)}, u32[]{:S(2)}, u32[]{:S(2)}) collective-permute-start(bf16[256,3072]{1,0:T(8,128)(2,1)} %collective-permute-done.refs_3_), channel_id=1, source_target_pairs={{24,0},{0,8},{8,16},{16,24},{56,32},{32,40},{40,48},{48,56},{88,64... | collective-permute-start | bytes 4718600 | tf_op jit(solution)/shard_map/ppermute | solution.py:28
  77.9 37.7 %collective-permute-start.13 = (bf16[256,3072]{1,0:T(8,128)(2,1)}, bf16[256,3072]{1,0:T(8,128)(2,1)}, u32[]{:S(2)}, u32[]{:S(2)}) collective-permute-start(bf16[256,3072]{1,0:T(8,128)(2,1)} %collective-permute-done.11.refs_9_), channel_id=1, source_target_pairs={{8,0},{16,8},{24,16},{0,24},{40,32},{48,40},{56,48},{32,56},{72,64... | collective-permute-start | bytes 4718600 | tf_op jit(solution)/shard_map/ppermute | solution.py:28
  80.6 35.0 %collective-permute-start.12 = (bf16[256,3072]{1,0:T(8,128)(2,1)}, bf16[256,3072]{1,0:T(8,128)(2,1)}, u32[]{:S(2)}, u32[]{:S(2)}) collective-permute-start(bf16[256,3072]{1,0:T(8,128)(2,1)} %collective-permute-done.11.refs_9_), channel_id=1, source_target_pairs={{32,0},{40,8},{48,16},{56,24},{64,32},{72,40},{80,48},{88,56},{96,... | collective-permute-start | bytes 4718600 | tf_op jit(solution)/shard_map/ppermute | solution.py:28
  82.7 1.4 copy-start.1
  95.7 8.6 %collective-permute-start.17 = (bf16[4,9,32,512]{3,2,1,0:T(8,128)(2,1)S(1)}, bf16[4,9,32,512]{3,2,1,0:T(8,128)(2,1)S(1)}, u32[]{:S(2)}, u32[]{:S(2)}) collective-permute-start(bf16[4,9,32,512]{3,2,1,0:T(8,128)(2,1)S(1)} %get-tuple-element.46), channel_id=1, source_target_pairs={{0,1},{1,0},{2,3},{3,2},{4,5},{5,4},{6,7},{7,6},{8,9},{9,8},{10,11... | collective-permute-start | bytes 3538952 | tf_op jit(solution)/shard_map/ppermute | solution.py:33
  104.3 45.3 %collective-permute-start.3 = (bf16[256,3072]{1,0:T(8,128)(2,1)}, bf16[256,3072]{1,0:T(8,128)(2,1)}, u32[]{:S(2)}, u32[]{:S(2)}) collective-permute-start(bf16[256,3072]{1,0:T(8,128)(2,1)} %collective-permute-done.1.refs_7_), channel_id=1, source_target_pairs={{96,0},{104,8},{112,16},{120,24},{0,32},{8,40},{16,48},{24,56},{32... | collective-permute-start | bytes 4718600 | tf_op jit(solution)/shard_map/ppermute | solution.py:28
  115.6 34.0 %collective-permute-start.2 = (bf16[256,3072]{1,0:T(8,128)(2,1)}, bf16[256,3072]{1,0:T(8,128)(2,1)}, u32[]{:S(2)}, u32[]{:S(2)}) collective-permute-start(bf16[256,3072]{1,0:T(8,128)(2,1)} %collective-permute-done.1.refs_7_), channel_id=1, source_target_pairs={{24,0},{0,8},{8,16},{16,24},{56,32},{32,40},{40,48},{48,56},{88,64... | collective-permute-start | bytes 4718600 | tf_op jit(solution)/shard_map/ppermute | solution.py:28
  115.6 34.0 %collective-permute-start.18 = (bf16[256,3072]{1,0:T(8,128)(2,1)}, bf16[256,3072]{1,0:T(8,128)(2,1)}, u32[]{:S(2)}, u32[]{:S(2)}) collective-permute-start(bf16[256,3072]{1,0:T(8,128)(2,1)} %collective-permute-done.12.refs_4_.refs_13_), channel_id=1, source_target_pairs={{8,0},{16,8},{24,16},{0,24},{40,32},{48,40},{56,48},{32,56},{72,64... | collective-permute-start | bytes 4718600 | tf_op jit(solution)/shard_map/ppermute | solution.py:28
  120.8 7.4 %collective-permute-start.19 = (bf16[9,32,512]{2,1,0:T(8,128)(2,1)}, bf16[9,32,512]{2,1,0:T(8,128)(2,1)}, u32[]{:S(2)}, u32[]{:S(2)}) collective-permute-start(bf16[9,32,512]{2,1,0:T(8,128)(2,1)} %get-tuple-element.72), channel_id=1, source_target_pairs={{0,2},{1,3},{2,4},{3,5},{4,6},{5,7},{6,0},{7,1},{8,10},{9,11},{10,... | collective-permute-start | bytes 884744 | tf_op jit(solution)/shard_map/ppermute | solution.py:33
  122.3 15.6 %collective-permute-start.21 = (bf16[9,32,512]{2,1,0:T(8,128)(2,1)}, bf16[9,32,512]{2,1,0:T(8,128)(2,1)}, u32[]{:S(2)}, u32[]{:S(2)}) collective-permute-start(bf16[9,32,512]{2,1,0:T(8,128)(2,1)} %get-tuple-element.73), channel_id=1, source_target_pairs={{0,4},{1,5},{2,6},{3,7},{4,0},{5,1},{6,2},{7,3},{8,12},{9,13},{10,... | collective-permute-start | bytes 884744 | tf_op jit(solution)/shard_map/ppermute | solution.py:33
  128.2 19.6 %collective-permute-start.20 = (bf16[9,32,512]{2,1,0:T(8,128)(2,1)}, bf16[9,32,512]{2,1,0:T(8,128)(2,1)}, u32[]{:S(2)}, u32[]{:S(2)}) collective-permute-start(bf16[9,32,512]{2,1,0:T(8,128)(2,1)} %get-tuple-element.74), channel_id=1, source_target_pairs={{0,6},{1,7},{2,0},{3,1},{4,2},{5,3},{6,4},{7,5},{8,14},{9,15},{10,... | collective-permute-start | bytes 884744 | tf_op jit(solution)/shard_map/ppermute | solution.py:33
  137.9 11.5 %collective-permute-start.22 = (bf16[4,4,32,512]{3,2,1,0:T(8,128)(2,1)S(1)}, bf16[4,4,32,512]{3,2,1,0:T(8,128)(2,1)S(1)}, u32[]{:S(2)}, u32[]{:S(2)}) collective-permute-start(bf16[4,4,32,512]{3,2,1,0:T(8,128)(2,1)S(1)} %get-tuple-element.53), channel_id=1, source_target_pairs={{0,1},{1,0},{2,3},{3,2},{4,5},{5,4},{6,7},{7,6},{8,9},{9,8},{10,11... | collective-permute-start | bytes 1572872 | tf_op jit(solution)/shard_map/ppermute | solution.py:33
  154.3 5.7 %collective-permute-start.23 = (bf16[4,3,32,512]{3,2,1,0:T(8,128)(2,1)S(1)}, bf16[4,3,32,512]{3,2,1,0:T(8,128)(2,1)S(1)}, u32[]{:S(2)}, u32[]{:S(2)}) collective-permute-start(bf16[4,3,32,512]{3,2,1,0:T(8,128)(2,1)S(1)} %get-tuple-element.64), channel_id=1, source_target_pairs={{0,1},{1,0},{2,3},{3,2},{4,5},{5,4},{6,7},{7,6},{8,9},{9,8},{10,11... | collective-permute-start | bytes 1179656 | tf_op jit(solution)/shard_map/ppermute | solution.py:33
  160.3 8.1 %collective-permute-start.24 = (bf16[7,32,512]{2,1,0:T(8,128)(2,1)S(1)}, bf16[7,32,512]{2,1,0:T(8,128)(2,1)S(1)}, u32[]{:S(2)}, u32[]{:S(2)}) collective-permute-start(bf16[7,32,512]{2,1,0:T(8,128)(2,1)S(1)} %get-tuple-element.75), channel_id=1, source_target_pairs={{0,2},{1,3},{2,4},{3,5},{4,6},{5,7},{6,0},{7,1},{8,10},{9,11},{10,... | collective-permute-start | bytes 688136 | tf_op jit(solution)/shard_map/ppermute | solution.py:33
  161.6 6.8 %collective-permute-start.25 = (bf16[7,32,512]{2,1,0:T(8,128)(2,1)S(1)}, bf16[7,32,512]{2,1,0:T(8,128)(2,1)S(1)}, u32[]{:S(2)}, u32[]{:S(2)}) collective-permute-start(bf16[7,32,512]{2,1,0:T(8,128)(2,1)S(1)} %get-tuple-element.76), channel_id=1, source_target_pairs={{0,6},{1,7},{2,0},{3,1},{4,2},{5,3},{6,4},{7,5},{8,14},{9,15},{10,... | collective-permute-start | bytes 688136 | tf_op jit(solution)/shard_map/ppermute | solution.py:33
  163.0 11.2 %collective-permute-start.26 = (bf16[7,32,512]{2,1,0:T(8,128)(2,1)S(1)}, bf16[7,32,512]{2,1,0:T(8,128)(2,1)S(1)}, u32[]{:S(2)}, u32[]{:S(2)}) collective-permute-start(bf16[7,32,512]{2,1,0:T(8,128)(2,1)S(1)} %get-tuple-element.77), channel_id=1, source_target_pairs={{0,4},{1,5},{2,6},{3,7},{4,0},{5,1},{6,2},{7,3},{8,12},{9,13},{10,... | collective-permute-start | bytes 688136 | tf_op jit(solution)/shard_map/ppermute | solution.py:33
  174.5 5.3 %collective-permute-start.27 = (f32[16,8,512]{2,1,0:T(8,128)S(1)}, f32[16,8,512]{2,1,0:T(8,128)S(1)}, u32[]{:S(2)}, u32[]{:S(2)}) collective-permute-start(f32[16,8,512]{2,1,0:T(8,128)S(1)} %pad_maximum_fusion.1), channel_id=1, source_target_pairs={{7,0},{0,1},{1,2},{2,3},{3,4},{4,5},{5,6},{6,7},{15,8},{8,9},{9,10... | collective-permute-start | bytes 786440 | tf_op jit(solution)/shard_map/ppermute | solution.py:449
  176.4 5.8 %collective-permute-start.28 = (f32[16,8,512]{2,1,0:T(8,128)S(1)}, f32[16,8,512]{2,1,0:T(8,128)S(1)}, u32[]{:S(2)}, u32[]{:S(2)}) collective-permute-start(f32[16,8,512]{2,1,0:T(8,128)S(1)} %pad_maximum_fusion.2), channel_id=1, source_target_pairs={{1,0},{2,1},{3,2},{4,3},{5,4},{6,5},{7,6},{0,7},{9,8},{10,9},{11,1... | collective-permute-start | bytes 786440 | tf_op jit(solution)/shard_map/ppermute | solution.py:449
  182.3 0.8 copy-start.4
  188.0 4.8 %collective-permute-start.31 = (f32[24,768]{1,0:T(8,128)S(1)}, f32[24,768]{1,0:T(8,128)S(1)}, u32[]{:S(2)}, u32[]{:S(2)}) collective-permute-start(f32[24,768]{1,0:T(8,128)S(1)} %products.1), channel_id=1, source_target_pairs={{16,0},{24,8},{0,16},{8,24},{48,32},{56,40},{32,48},{40,56},{80,64... | collective-permute-start | bytes 221192 | tf_op jit(solution)/shard_map/ppermute | solution.py:28
  189.3 5.6 %collective-permute-start.30 = (f32[24,768]{1,0:T(8,128)S(1)}, f32[24,768]{1,0:T(8,128)S(1)}, u32[]{:S(2)}, u32[]{:S(2)}) collective-permute-start(f32[24,768]{1,0:T(8,128)S(1)} %products.1), channel_id=1, source_target_pairs={{24,0},{0,8},{8,16},{16,24},{56,32},{32,40},{40,48},{48,56},{88,64... | collective-permute-start | bytes 221192 | tf_op jit(solution)/shard_map/ppermute | solution.py:28
  191.4 3.7 %collective-permute-start.29 = (f32[24,768]{1,0:T(8,128)S(1)}, f32[24,768]{1,0:T(8,128)S(1)}, u32[]{:S(2)}, u32[]{:S(2)}) collective-permute-start(f32[24,768]{1,0:T(8,128)S(1)} %products.1), channel_id=1, source_target_pairs={{8,0},{16,8},{24,16},{0,24},{40,32},{48,40},{56,48},{32,56},{72,64... | collective-permute-start | bytes 221192 | tf_op jit(solution)/shard_map/ppermute | solution.py:28
  195.1 39.7 %copy-start.2 = (bf16[256,3072]{1,0:T(8,128)(2,1)S(1)}, bf16[256,3072]{1,0:T(8,128)(2,1)}, u32[]{:S(2)}) copy-start(bf16[256,3072]{1,0:T(8,128)(2,1)} %refs_2_.3) | copy-start | bytes 4718596
  195.1 4.9 %collective-permute-start.34 = (f32[24,768]{1,0:T(8,128)S(1)}, f32[24,768]{1,0:T(8,128)S(1)}, u32[]{:S(2)}, u32[]{:S(2)}) collective-permute-start(f32[24,768]{1,0:T(8,128)S(1)} %add_add_fusion.refs_5_), channel_id=1, source_target_pairs={{64,0},{72,8},{80,16},{88,24},{96,32},{104,40},{112,48},{120,56},{... | collective-permute-start | bytes 221192 | tf_op jit(solution)/shard_map/ppermute | solution.py:28
  195.2 5.3 %collective-permute-start.33 = (f32[24,768]{1,0:T(8,128)S(1)}, f32[24,768]{1,0:T(8,128)S(1)}, u32[]{:S(2)}, u32[]{:S(2)}) collective-permute-start(f32[24,768]{1,0:T(8,128)S(1)} %add_add_fusion.refs_5_), channel_id=1, source_target_pairs={{96,0},{104,8},{112,16},{120,24},{0,32},{8,40},{16,48},{24,56},{32... | collective-permute-start | bytes 221192 | tf_op jit(solution)/shard_map/ppermute | solution.py:28
  195.8 4.7 %collective-permute-start.32 = (f32[24,768]{1,0:T(8,128)S(1)}, f32[24,768]{1,0:T(8,128)S(1)}, u32[]{:S(2)}, u32[]{:S(2)}) collective-permute-start(f32[24,768]{1,0:T(8,128)S(1)} %add_add_fusion.refs_5_), channel_id=1, source_target_pairs={{32,0},{40,8},{48,16},{56,24},{64,32},{72,40},{80,48},{88,56},{96,... | collective-permute-start | bytes 221192 | tf_op jit(solution)/shard_map/ppermute | solution.py:28
  204.6 9.9 %collective-permute-start.38 = (bf16[9,32,512]{2,1,0:T(8,128)(2,1)S(1)}, bf16[9,32,512]{2,1,0:T(8,128)(2,1)S(1)}, u32[]{:S(2)}, u32[]{:S(2)}) collective-permute-start(bf16[9,32,512]{2,1,0:T(8,128)(2,1)S(1)} %get-tuple-element.69.refs_19_), channel_id=1, source_target_pairs={{0,6},{1,7},{2,0},{3,1},{4,2},{5,3},{6,4},{7,5},{8,14},{9,15},{10,... | collective-permute-start | bytes 884744 | tf_op jit(solution)/shard_map/ppermute | solution.py:33
  208.9 3.0 %collective-permute-start.41 = (bf16[8,32,512]{2,1,0:T(8,128)(2,1)S(1)}, bf16[8,32,512]{2,1,0:T(8,128)(2,1)S(1)}, u32[]{:S(2)}, u32[]{:S(2)}) collective-permute-start(bf16[8,32,512]{2,1,0:T(8,128)(2,1)S(1)} %get-tuple-element.68.refs_18_), channel_id=1, source_target_pairs={{0,1},{1,0},{2,3},{3,2},{4,5},{5,4},{6,7},{7,6},{8,9},{9,8},{10,11... | collective-permute-start | bytes 786440 | tf_op jit(solution)/shard_map/ppermute | solution.py:33
  209.9 10.3 %collective-permute-start.37 = (bf16[8,32,512]{2,1,0:T(8,128)(2,1)S(1)}, bf16[8,32,512]{2,1,0:T(8,128)(2,1)S(1)}, u32[]{:S(2)}, u32[]{:S(2)}) collective-permute-start(bf16[8,32,512]{2,1,0:T(8,128)(2,1)S(1)} %get-tuple-element.68.refs_18_), channel_id=1, source_target_pairs={{0,6},{1,7},{2,0},{3,1},{4,2},{5,3},{6,4},{7,5},{8,14},{9,15},{10,... | collective-permute-start | bytes 786440 | tf_op jit(solution)/shard_map/ppermute | solution.py:33
  209.9 13.0 %collective-permute-start.35 = (bf16[8,32,512]{2,1,0:T(8,128)(2,1)S(1)}, bf16[8,32,512]{2,1,0:T(8,128)(2,1)S(1)}, u32[]{:S(2)}, u32[]{:S(2)}) collective-permute-start(bf16[8,32,512]{2,1,0:T(8,128)(2,1)S(1)} %get-tuple-element.68.refs_18_), channel_id=1, source_target_pairs={{0,2},{1,3},{2,4},{3,5},{4,6},{5,7},{6,0},{7,1},{8,10},{9,11},{10,... | collective-permute-start | bytes 786440 | tf_op jit(solution)/shard_map/ppermute | solution.py:33
  211.3 11.6 %collective-permute-start.42 = (bf16[9,32,512]{2,1,0:T(8,128)(2,1)S(1)}, bf16[9,32,512]{2,1,0:T(8,128)(2,1)S(1)}, u32[]{:S(2)}, u32[]{:S(2)}) collective-permute-start(bf16[9,32,512]{2,1,0:T(8,128)(2,1)S(1)} %get-tuple-element.69.refs_19_), channel_id=1, source_target_pairs={{0,1},{1,0},{2,3},{3,2},{4,5},{5,4},{6,7},{7,6},{8,9},{9,8},{10,11... | collective-permute-start | bytes 884744 | tf_op jit(solution)/shard_map/ppermute | solution.py:33
  211.9 13.2 %collective-permute-start.36 = (bf16[9,32,512]{2,1,0:T(8,128)(2,1)S(1)}, bf16[9,32,512]{2,1,0:T(8,128)(2,1)S(1)}, u32[]{:S(2)}, u32[]{:S(2)}) collective-permute-start(bf16[9,32,512]{2,1,0:T(8,128)(2,1)S(1)} %get-tuple-element.69.refs_19_), channel_id=1, source_target_pairs={{0,2},{1,3},{2,4},{3,5},{4,6},{5,7},{6,0},{7,1},{8,10},{9,11},{10,... | collective-permute-start | bytes 884744 | tf_op jit(solution)/shard_map/ppermute | solution.py:33
  214.5 11.9 %collective-permute-start.40 = (bf16[9,32,512]{2,1,0:T(8,128)(2,1)S(1)}, bf16[9,32,512]{2,1,0:T(8,128)(2,1)S(1)}, u32[]{:S(2)}, u32[]{:S(2)}) collective-permute-start(bf16[9,32,512]{2,1,0:T(8,128)(2,1)S(1)} %collective-permute-done.38.refs_23_), channel_id=1, source_target_pairs={{0,6},{1,7},{2,0},{3,1},{4,2},{5,3},{6,4},{7,5},{8,14},{9,15},{10,... | collective-permute-start | bytes 884744 | tf_op jit(solution)/shard_map/ppermute | solution.py:33
  220.1 7.9 %collective-permute-start.45 = (bf16[8,32,512]{2,1,0:T(8,128)(2,1)S(1)}, bf16[8,32,512]{2,1,0:T(8,128)(2,1)S(1)}, u32[]{:S(2)}, u32[]{:S(2)}) collective-permute-start(bf16[8,32,512]{2,1,0:T(8,128)(2,1)S(1)} %collective-permute-done.37.refs_22_), channel_id=1, source_target_pairs={{0,1},{1,0},{2,3},{3,2},{4,5},{5,4},{6,7},{7,6},{8,9},{9,8},{10,11... | collective-permute-start | bytes 786440 | tf_op jit(solution)/shard_map/ppermute | solution.py:33
  222.9 10.1 %collective-permute-start.39 = (bf16[8,32,512]{2,1,0:T(8,128)(2,1)S(1)}, bf16[8,32,512]{2,1,0:T(8,128)(2,1)S(1)}, u32[]{:S(2)}, u32[]{:S(2)}) collective-permute-start(bf16[8,32,512]{2,1,0:T(8,128)(2,1)S(1)} %collective-permute-done.35.refs_20_), channel_id=1, source_target_pairs={{0,2},{1,3},{2,4},{3,5},{4,6},{5,7},{6,0},{7,1},{8,10},{9,11},{10,... | collective-permute-start | bytes 786440 | tf_op jit(solution)/shard_map/ppermute | solution.py:33
  222.9 10.7 %collective-permute-start.46 = (bf16[9,32,512]{2,1,0:T(8,128)(2,1)S(1)}, bf16[9,32,512]{2,1,0:T(8,128)(2,1)S(1)}, u32[]{:S(2)}, u32[]{:S(2)}) collective-permute-start(bf16[9,32,512]{2,1,0:T(8,128)(2,1)S(1)} %collective-permute-done.38.refs_23_), channel_id=1, source_target_pairs={{0,1},{1,0},{2,3},{3,2},{4,5},{5,4},{6,7},{7,6},{8,9},{9,8},{10,11... | collective-permute-start | bytes 884744 | tf_op jit(solution)/shard_map/ppermute | solution.py:33
  225.2 8.4 %collective-permute-start.44 = (bf16[9,32,512]{2,1,0:T(8,128)(2,1)S(1)}, bf16[9,32,512]{2,1,0:T(8,128)(2,1)S(1)}, u32[]{:S(2)}, u32[]{:S(2)}) collective-permute-start(bf16[9,32,512]{2,1,0:T(8,128)(2,1)S(1)} %collective-permute-done.36.refs_21_), channel_id=1, source_target_pairs={{0,1},{1,0},{2,3},{3,2},{4,5},{5,4},{6,7},{7,6},{8,9},{9,8},{10,11... | collective-permute-start | bytes 884744 | tf_op jit(solution)/shard_map/ppermute | solution.py:33
  226.5 8.3 %collective-permute-start.48 = (bf16[9,32,512]{2,1,0:T(8,128)(2,1)S(1)}, bf16[9,32,512]{2,1,0:T(8,128)(2,1)S(1)}, u32[]{:S(2)}, u32[]{:S(2)}) collective-permute-start(bf16[9,32,512]{2,1,0:T(8,128)(2,1)S(1)} %collective-permute-done.40.refs_25_), channel_id=1, source_target_pairs={{0,1},{1,0},{2,3},{3,2},{4,5},{5,4},{6,7},{7,6},{8,9},{9,8},{10,11... | collective-permute-start | bytes 884744 | tf_op jit(solution)/shard_map/ppermute | solution.py:33
  228.1 5.5 %collective-permute-start.43 = (bf16[8,32,512]{2,1,0:T(8,128)(2,1)S(1)}, bf16[8,32,512]{2,1,0:T(8,128)(2,1)S(1)}, u32[]{:S(2)}, u32[]{:S(2)}) collective-permute-start(bf16[8,32,512]{2,1,0:T(8,128)(2,1)S(1)} %collective-permute-done.35.refs_20_), channel_id=1, source_target_pairs={{0,1},{1,0},{2,3},{3,2},{4,5},{5,4},{6,7},{7,6},{8,9},{9,8},{10,11... | collective-permute-start | bytes 786440 | tf_op jit(solution)/shard_map/ppermute | solution.py:33
  233.0 1.7 collective-permute-start.47

commit v7 on v6

--- a/solution.py
+++ b/solution.py
@@ -127,7 +127,7 @@
         columns[pl.ds(pl.multiple_of(index * LENGTH, 8), LENGTH), :] = total
         return carry
 
-    lax.fori_loop(0, BLOCKS, block, 0, unroll=2)
+    lax.fori_loop(0, BLOCKS, block, 0, unroll=4)
     out_ref[...] = columns[...].T[:PRODUCTS, :]
 
 

time: 254 us -> 254 us (level)
  no operation moved by 1% of the time
where the time goes in v7:
time: 254 us; the launch traced here: 253 us
  waiting for transfers between devices  94.4 us (37%)
  starting transfers between devices  89.1 us (35%)
  Pallas kernels  50.5 us (20%)
  other arithmetic  10 us (4%)
  local copies, waits for them, and re-layouts  8.04 us (3%)
    ppermute x21, waiting for transfers between devices, from_dp(): return lax.ppermute(block, 'dp', route)  53.4 us
    ppermute x23, starting transfers between devices, along_mp(): return lax.ppermute(block, 'mp', route)  45 us
    ppermute x23, waiting for transfers between devices, along_mp(): return lax.ppermute(block, 'mp', route)  29.4 us
    ppermute x21, starting transfers between devices, from_dp(): return lax.ppermute(block, 'dp', route)  27.9 us
    pallas_call x3, Pallas kernels, project(): pl.pallas_call(lambda *refs: project_kernel(len(rows), blocks, *refs), ou...  22.2 us
    pallas_call x1, Pallas kernels, weight_gradient(): pl.pallas_call(lambda *refs: weight_kernel(len(rows), *refs), out_shape=(...  18.5 us
    ppermute x3, starting transfers between devices, neighbour(): return lax.ppermute(block, 'mp', route)  7.14 us
    all_to_all x1, starting transfers between devices, local(): shares = lax.all_to_all(windows(target, block_rows), 'mp', 0, 0, tiled=True)  7.13 us
  transfers between devices with their start and end apart: 50, of which 25 were waited for; matrix products, arithmetic and copies ran while one was open for 6% of the time, Pallas kernels for 7%

profile of v7, /device:TPU:1, one launch (start us, length us, event | category | flops | bytes accessed | tf_op | source)
XLA Modules:
  0.0 253.3 jit_solution(3904962436746266877)
XLA Ops:
  0.6 4.7 %collective-permute-start.7 = (bf16[256,3072]{1,0:T(8,128)(2,1)}, bf16[256,3072]{1,0:T(8,128)(2,1)}, u32[]{:S(2)}, u32[]{:S(2)}) collective-permute-start(bf16[256,3072]{1,0:T(8,128)(2,1)} %refs_2_.3), channel_id=1, source_target_pairs={{8,0},{16,8},{24,16},{0,24},{40,32},{48,40},{56,48},{32,56},{72,64... | collective-permute-start | bytes 4718600 | tf_op jit(solution)/shard_map/ppermute | solution.py:28
  5.3 2.7 %collective-permute-start.14 = (bf16[256,3072]{1,0:T(8,128)(2,1)}, bf16[256,3072]{1,0:T(8,128)(2,1)}, u32[]{:S(2)}, u32[]{:S(2)}) collective-permute-start(bf16[256,3072]{1,0:T(8,128)(2,1)} %refs_2_.3), channel_id=1, source_target_pairs={{32,0},{40,8},{48,16},{56,24},{64,32},{72,40},{80,48},{88,56},{96,... | collective-permute-start | bytes 4718600 | tf_op jit(solution)/shard_map/ppermute | solution.py:28
  8.7 3.1 %collective-permute-start.9 = (s32[16]{0:T(128)S(1)}, s32[16]{0:T(128)S(1)}, u32[]{:S(2)}, u32[]{:S(2)}) collective-permute-start(s32[16]{0:T(128)S(1)} %slice.37), channel_id=1, source_target_pairs={{1,0},{2,1},{3,2},{4,3},{5,4},{6,5},{7,6},{9,8},{10,9},{11,10},{12... | collective-permute-start | bytes 200 | tf_op jit(solution)/shard_map/ppermute | solution.py:39
  12.6 1.9 collective-permute-done.9
  14.6 1.9 collective-permute-start.10
  17.6 2.1 collective-permute-start.8
  19.7 3.5 %collective-permute-done.8 = bf16[16,512]{1,0:T(8,128)(2,1)S(1)} collective-permute-done((bf16[16,512]{1,0:T(8,128)(2,1)S(1)}, bf16[16,512]{1,0:T(8,128)(2,1)S(1)}, u32[]{:S(2)}, u32[]{:S(2)}) %collective-permute-start.8) | collective-permute-done | bytes 16416 | tf_op jit(solution)/shard_map/ppermute | solution.py:39
  23.1 15.5 %collective-permute-done.7.refs_4_ = bf16[256,3072]{1,0:T(8,128)(2,1)} collective-permute-done((bf16[256,3072]{1,0:T(8,128)(2,1)}, bf16[256,3072]{1,0:T(8,128)(2,1)}, u32[]{:S(2)}, u32[]{:S(2)}) %collective-permute-start.7) | collective-permute-done | bytes 1572896 | tf_op jit(solution)/shard_map/ppermute | solution.py:28
  38.7 2.4 collective-permute-done.14.refs_6_
  41.1 3.4 %collective-permute-start.11 = (bf16[256,3072]{1,0:T(8,128)(2,1)}, bf16[256,3072]{1,0:T(8,128)(2,1)}, u32[]{:S(2)}, u32[]{:S(2)}) collective-permute-start(bf16[256,3072]{1,0:T(8,128)(2,1)} %collective-permute-done.7.refs_4_), channel_id=1, source_target_pairs={{32,0},{40,8},{48,16},{56,24},{64,32},{72,40},{80,48},{88,56},{96,... | collective-permute-start | bytes 4718600 | tf_op jit(solution)/shard_map/ppermute | solution.py:28
  44.5 2.7 %collective-permute-start.15 = (bf16[256,3072]{1,0:T(8,128)(2,1)}, bf16[256,3072]{1,0:T(8,128)(2,1)}, u32[]{:S(2)}, u32[]{:S(2)}) collective-permute-start(bf16[256,3072]{1,0:T(8,128)(2,1)} %collective-permute-done.5.refs_5_), channel_id=1, source_target_pairs={{8,0},{16,8},{24,16},{0,24},{40,32},{48,40},{56,48},{32,56},{72,64... | collective-permute-start | bytes 4718600 | tf_op jit(solution)/shard_map/ppermute | solution.py:28
  48.2 1.1 pad_maximum_fusion.refs_0_
  50.3 7.1 %all-to-all-start = ((bf16[8,2,48,640]{3,2,1,0:T(8,128)(2,1)}), bf16[8,2,48,640]{3,2,1,0:T(8,128)(2,1)}, u32[]{:S(2)}, u32[]{:S(2)}) async-start(bf16[8,2,48,640]{3,2,1,0:T(8,128)(2,1)} %copy-done.3), calls=%async_computation | async-start | bytes 1966080 | tf_op jit(solution)/shard_map/all_to_all | solution.py:503
  57.5 20.5 %collective-permute-done.16.refs_10_ = bf16[256,3072]{1,0:T(8,128)(2,1)} collective-permute-done((bf16[256,3072]{1,0:T(8,128)(2,1)}, bf16[256,3072]{1,0:T(8,128)(2,1)}, u32[]{:S(2)}, u32[]{:S(2)}) %collective-permute-start.16) | collective-permute-done | bytes 1572896 | tf_op jit(solution)/shard_map/ppermute | solution.py:28
  77.9 2.7 %collective-permute-start.13 = (bf16[256,3072]{1,0:T(8,128)(2,1)}, bf16[256,3072]{1,0:T(8,128)(2,1)}, u32[]{:S(2)}, u32[]{:S(2)}) collective-permute-start(bf16[256,3072]{1,0:T(8,128)(2,1)} %collective-permute-done.11.refs_9_), channel_id=1, source_target_pairs={{8,0},{16,8},{24,16},{0,24},{40,32},{48,40},{56,48},{32,56},{72,64... | collective-permute-start | bytes 4718600 | tf_op jit(solution)/shard_map/ppermute | solution.py:28
  80.6 2.1 collective-permute-start.12
  82.7 1.4 copy-done.1
  84.1 11.6 %project.3 = (bf16[4,9,32,512]{3,2,1,0:T(8,128)(2,1)S(1)}, f32[4,9,32,512]{3,2,1,0:T(8,128)S(1)}) custom-call(s32[1]{0:T(128)} %bitcast.refs_0_, bf16[3072,512]{1,0:T(8,128)(2,1)S(1)} %copy-done, bf16[256,3072]{1,0:T(8,128)(2,1)S(1)} %copy-done.1, bf16[256,3072]{1,0:T(8,128)(2,1)} %collective-permute-done.refs_3_, ...), custom_call_target="tpu_custom_call" | custom-call | flops 1 | bytes 1 | tf_op jit(solution)/shard_map/project/pallas_call | solution.py:325
  95.7 6.1 %collective-permute-start.17 = (bf16[4,9,32,512]{3,2,1,0:T(8,128)(2,1)S(1)}, bf16[4,9,32,512]{3,2,1,0:T(8,128)(2,1)S(1)}, u32[]{:S(2)}, u32[]{:S(2)}) collective-permute-start(bf16[4,9,32,512]{3,2,1,0:T(8,128)(2,1)S(1)} %get-tuple-element.46), channel_id=1, source_target_pairs={{0,1},{1,0},{2,3},{3,2},{4,5},{5,4},{6,7},{7,6},{8,9},{9,8},{10,11... | collective-permute-start | bytes 3538952 | tf_op jit(solution)/shard_map/ppermute | solution.py:33
  101.8 2.5 collective-permute-done.17
  104.3 1.9 convert_add_fusion
  106.3 9.3 %collective-permute-done.6.refs_3_.refs_12_ = bf16[256,3072]{1,0:T(8,128)(2,1)} collective-permute-done((bf16[256,3072]{1,0:T(8,128)(2,1)}, bf16[256,3072]{1,0:T(8,128)(2,1)}, u32[]{:S(2)}, u32[]{:S(2)}) %collective-permute-start.6) | collective-permute-done | bytes 1572896 | tf_op jit(solution)/shard_map/ppermute | solution.py:28
  115.6 2.7 %collective-permute-start.18 = (bf16[256,3072]{1,0:T(8,128)(2,1)}, bf16[256,3072]{1,0:T(8,128)(2,1)}, u32[]{:S(2)}, u32[]{:S(2)}) collective-permute-start(bf16[256,3072]{1,0:T(8,128)(2,1)} %collective-permute-done.12.refs_4_.refs_13_), channel_id=1, source_target_pairs={{8,0},{16,8},{24,16},{0,24},{40,32},{48,40},{56,48},{32,56},{72,64... | collective-permute-start | bytes 4718600 | tf_op jit(solution)/shard_map/ppermute | solution.py:28
  118.4 2.4 fusion.9
  120.8 1.2 collective-permute-start.19
  122.3 2.5 collective-permute-start.21
  125.7 2.5 collective-permute-done.19
  128.2 1.3 collective-permute-start.20
  129.5 1.7 fusion.15
  132.0 5.9 %project.4 = (bf16[4,4,32,512]{3,2,1,0:T(8,128)(2,1)S(1)}, f32[4,4,32,512]{3,2,1,0:T(8,128)S(1)}) custom-call(s32[1]{0:T(128)} %bitcast.refs_0_, bf16[3072,512]{1,0:T(8,128)(2,1)S(1)} %copy-done, bf16[256,3072]{1,0:T(8,128)(2,1)} %collective-permute-done.4.refs_2_.refs_11_, bf16[256,3072]{1,0:T(8,128)(2,1)} %collective-permute-done.6.refs_3_.refs_12_, ...), custom_call_target="tpu_custom_call" | custom-call | flops 1 | bytes 1 | tf_op jit(solution)/shard_map/project/pallas_call | solution.py:325
  137.9 8.6 %collective-permute-start.22 = (bf16[4,4,32,512]{3,2,1,0:T(8,128)(2,1)S(1)}, bf16[4,4,32,512]{3,2,1,0:T(8,128)(2,1)S(1)}, u32[]{:S(2)}, u32[]{:S(2)}) collective-permute-start(bf16[4,4,32,512]{3,2,1,0:T(8,128)(2,1)S(1)} %get-tuple-element.53), channel_id=1, source_target_pairs={{0,1},{1,0},{2,3},{3,2},{4,5},{5,4},{6,7},{7,6},{8,9},{9,8},{10,11... | collective-permute-start | bytes 1572872 | tf_op jit(solution)/shard_map/ppermute | solution.py:33
  146.5 1.3 slice_convert_fusion.target_ref.refs_1_
  147.9 1.5 bitcast_add_fusion.refs_2_
  149.6 4.7 %project.5 = (bf16[4,3,32,512]{3,2,1,0:T(8,128)(2,1)S(1)}, f32[4,3,32,512]{3,2,1,0:T(8,128)S(1)}) custom-call(s32[1]{0:T(128)} %bitcast.refs_0_, bf16[3072,512]{1,0:T(8,128)(2,1)S(1)} %copy-done, bf16[256,3072]{1,0:T(8,128)(2,1)} %collective-permute-done.2.refs_2_.refs_15_, bf16[256,3072]{1,0:T(8,128)(2,1)} %collective-permute-done.3.refs_3_.refs_16_, ...), custom_call_target="tpu_custom_call" | custom-call | flops 1 | bytes 1 | tf_op jit(solution)/shard_map/project/pallas_call | solution.py:325
  154.3 4.4 %collective-permute-start.23 = (bf16[4,3,32,512]{3,2,1,0:T(8,128)(2,1)S(1)}, bf16[4,3,32,512]{3,2,1,0:T(8,128)(2,1)S(1)}, u32[]{:S(2)}, u32[]{:S(2)}) collective-permute-start(bf16[4,3,32,512]{3,2,1,0:T(8,128)(2,1)S(1)} %get-tuple-element.64), channel_id=1, source_target_pairs={{0,1},{1,0},{2,3},{3,2},{4,5},{5,4},{6,7},{7,6},{8,9},{9,8},{10,11... | collective-permute-start | bytes 1179656 | tf_op jit(solution)/shard_map/ppermute | solution.py:33
  158.7 1.3 collective-permute-done.23
  160.3 1.3 collective-permute-start.24
  161.6 1.5 collective-permute-start.25
  163.0 1.5 collective-permute-start.26
  164.6 3.8 %collective-permute-done.24 = bf16[7,32,512]{2,1,0:T(8,128)(2,1)S(1)} collective-permute-done((bf16[7,32,512]{2,1,0:T(8,128)(2,1)S(1)}, bf16[7,32,512]{2,1,0:T(8,128)(2,1)S(1)}, u32[]{:S(2)}, u32[]{:S(2)}) %collective-permute-start.24) | collective-permute-done | bytes 229408 | tf_op jit(solution)/shard_map/ppermute | solution.py:33
  168.4 5.9 %collective-permute-done.26 = bf16[7,32,512]{2,1,0:T(8,128)(2,1)S(1)} collective-permute-done((bf16[7,32,512]{2,1,0:T(8,128)(2,1)S(1)}, bf16[7,32,512]{2,1,0:T(8,128)(2,1)S(1)}, u32[]{:S(2)}, u32[]{:S(2)}) %collective-permute-start.26) | collective-permute-done | bytes 229408 | tf_op jit(solution)/shard_map/ppermute | solution.py:33
  174.5 2.0 collective-permute-start.27
  176.5 3.3 %collective-permute-done.27.refs_4_ = f32[16,8,512]{2,1,0:T(8,128)S(1)} collective-permute-done((f32[16,8,512]{2,1,0:T(8,128)S(1)}, f32[16,8,512]{2,1,0:T(8,128)S(1)}, u32[]{:S(2)}, u32[]{:S(2)}) %collective-permute-start.27) | collective-permute-done | bytes 262176 | tf_op jit(solution)/shard_map/ppermute | solution.py:449
  179.7 2.5 %collective-permute-done.28.refs_5_ = f32[16,8,512]{2,1,0:T(8,128)S(1)} collective-permute-done((f32[16,8,512]{2,1,0:T(8,128)S(1)}, f32[16,8,512]{2,1,0:T(8,128)S(1)}, u32[]{:S(2)}, u32[]{:S(2)}) %collective-permute-start.28) | collective-permute-done | bytes 262176 | tf_op jit(solution)/shard_map/ppermute | solution.py:449
  183.1 4.7 %products.1 = f32[24,768]{1,0:T(8,128)S(1)} custom-call(f32[16,48,512]{2,1,0:T(8,128)S(1)} %assemble.1.state_ref.refs_0_, f32[16,48,512]{2,1,0:T(8,128)S(1)} %slice_convert_fusion.target_ref.refs_1_, f32[16,48,1]{2,1,0:T(8,128)S(1)} %slice_convert_fusion.1.keep_ref.refs_2_, f32[3,512]{1,0:T(4,128)S(1)} %copy-done.4), custom_call_target="tpu_custom_call" | custom-call | flops 1 | bytes 1 | tf_op jit(solution)/shard_map/products/pallas_call | solution.py:136
  187.9 1.3 collective-permute-start.31
  189.2 2.1 collective-permute-start.30
  192.6 2.2 collective-permute-done.30
  195.7 2.1 collective-permute-start.32
  197.8 2.1 collective-permute-done.34.refs_8_
  200.3 4.2 %gradients.1 = (bf16[8,32,512]{2,1,0:T(8,128)(2,1)S(1)}, bf16[9,32,512]{2,1,0:T(8,128)(2,1)S(1)}) custom-call(f32[16,48,512]{2,1,0:T(8,128)S(1)} %assemble.1.state_ref.refs_0_, f32[16,48,512]{2,1,0:T(8,128)S(1)} %slice_convert_fusion.target_ref.refs_1_, f32[16,48,1]{2,1,0:T(8,128)S(1)} %slice_convert_fusion.1.keep_ref.refs_2_, ...), custom_call_target="tpu_custom_call" | custom-call | flops 1 | bytes 1 | tf_op jit(solution)/shard_map/gradients/pallas_call | solution.py:274
  204.5 4.3 %collective-permute-start.38 = (bf16[9,32,512]{2,1,0:T(8,128)(2,1)S(1)}, bf16[9,32,512]{2,1,0:T(8,128)(2,1)S(1)}, u32[]{:S(2)}, u32[]{:S(2)}) collective-permute-start(bf16[9,32,512]{2,1,0:T(8,128)(2,1)S(1)} %get-tuple-element.69.refs_19_), channel_id=1, source_target_pairs={{0,6},{1,7},{2,0},{3,1},{4,2},{5,3},{6,4},{7,5},{8,14},{9,15},{10,... | collective-permute-start | bytes 884744 | tf_op jit(solution)/shard_map/ppermute | solution.py:33
  208.8 1.0 collective-permute-start.41
  209.8 1.5 collective-permute-start.35
  211.8 2.6 %collective-permute-done.38.refs_23_ = bf16[9,32,512]{2,1,0:T(8,128)(2,1)S(1)} collective-permute-done((bf16[9,32,512]{2,1,0:T(8,128)(2,1)S(1)}, bf16[9,32,512]{2,1,0:T(8,128)(2,1)S(1)}, u32[]{:S(2)}, u32[]{:S(2)}) %collective-permute-start.38) | collective-permute-done | bytes 294944 | tf_op jit(solution)/shard_map/ppermute | solution.py:33
  214.4 3.4 %collective-permute-start.40 = (bf16[9,32,512]{2,1,0:T(8,128)(2,1)S(1)}, bf16[9,32,512]{2,1,0:T(8,128)(2,1)S(1)}, u32[]{:S(2)}, u32[]{:S(2)}) collective-permute-start(bf16[9,32,512]{2,1,0:T(8,128)(2,1)S(1)} %collective-permute-done.38.refs_23_), channel_id=1, source_target_pairs={{0,6},{1,7},{2,0},{3,1},{4,2},{5,3},{6,4},{7,5},{8,14},{9,15},{10,... | collective-permute-start | bytes 884744 | tf_op jit(solution)/shard_map/ppermute | solution.py:33
  217.8 2.2 collective-permute-done.37.refs_22_
  220.0 2.8 %collective-permute-start.45 = (bf16[8,32,512]{2,1,0:T(8,128)(2,1)S(1)}, bf16[8,32,512]{2,1,0:T(8,128)(2,1)S(1)}, u32[]{:S(2)}, u32[]{:S(2)}) collective-permute-start(bf16[8,32,512]{2,1,0:T(8,128)(2,1)S(1)} %collective-permute-done.37.refs_22_), channel_id=1, source_target_pairs={{0,1},{1,0},{2,3},{3,2},{4,5},{5,4},{6,7},{7,6},{8,9},{9,8},{10,11... | collective-permute-start | bytes 786440 | tf_op jit(solution)/shard_map/ppermute | solution.py:33
  222.9 2.1 collective-permute-done.36.refs_21_
  225.0 1.0 collective-permute-start.44
  226.3 1.6 collective-permute-start.48
  227.9 5.0 %collective-permute-done.39.refs_24_ = bf16[8,32,512]{2,1,0:T(8,128)(2,1)S(1)} collective-permute-done((bf16[8,32,512]{2,1,0:T(8,128)(2,1)S(1)}, bf16[8,32,512]{2,1,0:T(8,128)(2,1)S(1)}, u32[]{:S(2)}, u32[]{:S(2)}) %collective-permute-start.39) | collective-permute-done | bytes 262176 | tf_op jit(solution)/shard_map/ppermute | solution.py:33
  233.5 1.1 collective-permute-done.47.refs_32_
  234.6 18.5 %weight_gradient.1 = (f32[3072,512]{1,0:T(8,128)}, f32[1,128]{1,0:T(1,128)}) custom-call(s32[16]{0:T(128)S(1)} %select_reduce_fusion.refs_0_, s32[8]{0:T(128)S(1)} %stack.112.refs_1_, bf16[256,3072]{1,0:T(8,128)(2,1)S(1)} %copy-done.2, bf16[256,3072]{1,0:T(8,128)(2,1)} %collective-permute-done.refs_3_, bf16[256,3072]{1,0:T(8,128)(2,1)} %collective-permute-done.7.refs_4_, ...), custom_call_target="tpu_custom_call" | custom-call | flops 1 | bytes 1 | tf_op jit(solution)/shard_map/weight_gradient/pallas_call | solution.py:413
  (81 shorter events, 12.3 us)
Async XLA Ops:
  0.6 38.0 %collective-permute-start.7 = (bf16[256,3072]{1,0:T(8,128)(2,1)}, bf16[256,3072]{1,0:T(8,128)(2,1)}, u32[]{:S(2)}, u32[]{:S(2)}) collective-permute-start(bf16[256,3072]{1,0:T(8,128)(2,1)} %refs_2_.3), channel_id=1, source_target_pairs={{8,0},{16,8},{24,16},{0,24},{40,32},{48,40},{56,48},{32,56},{72,64... | collective-permute-start | bytes 4718600 | tf_op jit(solution)/shard_map/ppermute | solution.py:28
  5.3 35.8 %collective-permute-start.14 = (bf16[256,3072]{1,0:T(8,128)(2,1)}, bf16[256,3072]{1,0:T(8,128)(2,1)}, u32[]{:S(2)}, u32[]{:S(2)}) collective-permute-start(bf16[256,3072]{1,0:T(8,128)(2,1)} %refs_2_.3), channel_id=1, source_target_pairs={{32,0},{40,8},{48,16},{56,24},{64,32},{72,40},{80,48},{88,56},{96,... | collective-permute-start | bytes 4718600 | tf_op jit(solution)/shard_map/ppermute | solution.py:28
  8.0 36.5 %collective-permute-start.5 = (bf16[256,3072]{1,0:T(8,128)(2,1)}, bf16[256,3072]{1,0:T(8,128)(2,1)}, u32[]{:S(2)}, u32[]{:S(2)}) collective-permute-start(bf16[256,3072]{1,0:T(8,128)(2,1)} %refs_2_.3), channel_id=1, source_target_pairs={{96,0},{104,8},{112,16},{120,24},{0,32},{8,40},{16,48},{24,56},{32... | collective-permute-start | bytes 4718600 | tf_op jit(solution)/shard_map/ppermute | solution.py:28
  8.0 39.2 %collective-permute-start = (bf16[256,3072]{1,0:T(8,128)(2,1)}, bf16[256,3072]{1,0:T(8,128)(2,1)}, u32[]{:S(2)}, u32[]{:S(2)}) collective-permute-start(bf16[256,3072]{1,0:T(8,128)(2,1)} %refs_2_.3), channel_id=1, source_target_pairs={{24,0},{0,8},{8,16},{16,24},{56,32},{32,40},{40,48},{48,56},{88,64... | collective-permute-start | bytes 4718600 | tf_op jit(solution)/shard_map/ppermute | solution.py:28
  8.7 5.8 %collective-permute-start.9 = (s32[16]{0:T(128)S(1)}, s32[16]{0:T(128)S(1)}, u32[]{:S(2)}, u32[]{:S(2)}) collective-permute-start(s32[16]{0:T(128)S(1)} %slice.37), channel_id=1, source_target_pairs={{1,0},{2,1},{3,2},{4,3},{5,4},{6,5},{7,6},{9,8},{10,9},{11,10},{12... | collective-permute-start | bytes 200 | tf_op jit(solution)/shard_map/ppermute | solution.py:39
  14.6 3.0 %collective-permute-start.10 = (s32[17]{0:T(128)S(1)}, s32[17]{0:T(128)S(1)}, u32[]{:S(2)}, u32[]{:S(2)}) collective-permute-start(s32[17]{0:T(128)S(1)} %slice.38), channel_id=1, source_target_pairs={{0,1},{1,2},{2,3},{3,4},{4,5},{5,6},{6,7},{8,9},{9,10},{10,11},{11... | collective-permute-start | bytes 212 | tf_op jit(solution)/shard_map/ppermute | solution.py:39
  17.6 5.6 %collective-permute-start.8 = (bf16[16,512]{1,0:T(8,128)(2,1)S(1)}, bf16[16,512]{1,0:T(8,128)(2,1)S(1)}, u32[]{:S(2)}, u32[]{:S(2)}) collective-permute-start(bf16[16,512]{1,0:T(8,128)(2,1)S(1)} %slice.36), channel_id=1, source_target_pairs={{1,0},{2,1},{3,2},{4,3},{5,4},{6,5},{7,6},{9,8},{10,9},{11,10},{12... | collective-permute-start | bytes 49160 | tf_op jit(solution)/shard_map/ppermute | solution.py:39
  41.1 36.8 %collective-permute-start.16 = (bf16[256,3072]{1,0:T(8,128)(2,1)}, bf16[256,3072]{1,0:T(8,128)(2,1)}, u32[]{:S(2)}, u32[]{:S(2)}) collective-permute-start(bf16[256,3072]{1,0:T(8,128)(2,1)} %collective-permute-done.14.refs_6_), channel_id=1, source_target_pairs={{24,0},{0,8},{8,16},{16,24},{56,32},{32,40},{40,48},{48,56},{88,64... | collective-permute-start | bytes 4718600 | tf_op jit(solution)/shard_map/ppermute | solution.py:28
  41.1 36.8 %collective-permute-start.11 = (bf16[256,3072]{1,0:T(8,128)(2,1)}, bf16[256,3072]{1,0:T(8,128)(2,1)}, u32[]{:S(2)}, u32[]{:S(2)}) collective-permute-start(bf16[256,3072]{1,0:T(8,128)(2,1)} %collective-permute-done.7.refs_4_), channel_id=1, source_target_pairs={{32,0},{40,8},{48,16},{56,24},{64,32},{72,40},{80,48},{88,56},{96,... | collective-permute-start | bytes 4718600 | tf_op jit(solution)/shard_map/ppermute | solution.py:28
  44.5 36.1 %collective-permute-start.15 = (bf16[256,3072]{1,0:T(8,128)(2,1)}, bf16[256,3072]{1,0:T(8,128)(2,1)}, u32[]{:S(2)}, u32[]{:S(2)}) collective-permute-start(bf16[256,3072]{1,0:T(8,128)(2,1)} %collective-permute-done.5.refs_5_), channel_id=1, source_target_pairs={{8,0},{16,8},{24,16},{0,24},{40,32},{48,40},{56,48},{32,56},{72,64... | collective-permute-start | bytes 4718600 | tf_op jit(solution)/shard_map/ppermute | solution.py:28
  47.2 35.6 %collective-permute-start.1 = (bf16[256,3072]{1,0:T(8,128)(2,1)}, bf16[256,3072]{1,0:T(8,128)(2,1)}, u32[]{:S(2)}, u32[]{:S(2)}) collective-permute-start(bf16[256,3072]{1,0:T(8,128)(2,1)} %collective-permute-done.refs_3_), channel_id=1, source_target_pairs={{96,0},{104,8},{112,16},{120,24},{0,32},{8,40},{16,48},{24,56},{32... | collective-permute-start | bytes 4718600 | tf_op jit(solution)/shard_map/ppermute | solution.py:28
  49.3 33.5 %copy-start = (bf16[3072,512]{1,0:T(8,128)(2,1)S(1)}, bf16[3072,512]{1,0:T(8,128)(2,1)}, u32[]{:S(2)}) copy-start(bf16[3072,512]{1,0:T(8,128)(2,1)} %refs_1_.5) | copy-start | bytes 9437188
  49.4 0.9 copy-start.3
  50.3 32.4 %all-to-all-start = ((bf16[8,2,48,640]{3,2,1,0:T(8,128)(2,1)}), bf16[8,2,48,640]{3,2,1,0:T(8,128)(2,1)}, u32[]{:S(2)}, u32[]{:S(2)}) async-start(bf16[8,2,48,640]{3,2,1,0:T(8,128)(2,1)} %copy-done.3), calls=%async_computation | async-start | bytes 1966080 | tf_op jit(solution)/shard_map/all_to_all | solution.py:503
  57.5 58.1 %collective-permute-start.6 = (bf16[256,3072]{1,0:T(8,128)(2,1)}, bf16[256,3072]{1,0:T(8,128)(2,1)}, u32[]{:S(2)}, u32[]{:S(2)}) collective-permute-start(bf16[256,3072]{1,0:T(8,128)(2,1)} %collective-permute-done.5.refs_5_), channel_id=1, source_target_pairs={{96,0},{104,8},{112,16},{120,24},{0,32},{8,40},{16,48},{24,56},{32... | collective-permute-start | bytes 4718600 | tf_op jit(solution)/shard_map/ppermute | solution.py:28
  77.9 37.7 %collective-permute-start.4 = (bf16[256,3072]{1,0:T(8,128)(2,1)}, bf16[256,3072]{1,0:T(8,128)(2,1)}, u32[]{:S(2)}, u32[]{:S(2)}) collective-permute-start(bf16[256,3072]{1,0:T(8,128)(2,1)} %collective-permute-done.refs_3_), channel_id=1, source_target_pairs={{24,0},{0,8},{8,16},{16,24},{56,32},{32,40},{40,48},{48,56},{88,64... | collective-permute-start | bytes 4718600 | tf_op jit(solution)/shard_map/ppermute | solution.py:28
  77.9 37.7 %collective-permute-start.13 = (bf16[256,3072]{1,0:T(8,128)(2,1)}, bf16[256,3072]{1,0:T(8,128)(2,1)}, u32[]{:S(2)}, u32[]{:S(2)}) collective-permute-start(bf16[256,3072]{1,0:T(8,128)(2,1)} %collective-permute-done.11.refs_9_), channel_id=1, source_target_pairs={{8,0},{16,8},{24,16},{0,24},{40,32},{48,40},{56,48},{32,56},{72,64... | collective-permute-start | bytes 4718600 | tf_op jit(solution)/shard_map/ppermute | solution.py:28
  80.6 35.0 %collective-permute-start.12 = (bf16[256,3072]{1,0:T(8,128)(2,1)}, bf16[256,3072]{1,0:T(8,128)(2,1)}, u32[]{:S(2)}, u32[]{:S(2)}) collective-permute-start(bf16[256,3072]{1,0:T(8,128)(2,1)} %collective-permute-done.11.refs_9_), channel_id=1, source_target_pairs={{32,0},{40,8},{48,16},{56,24},{64,32},{72,40},{80,48},{88,56},{96,... | collective-permute-start | bytes 4718600 | tf_op jit(solution)/shard_map/ppermute | solution.py:28
  82.7 1.4 copy-start.1
  95.7 8.6 %collective-permute-start.17 = (bf16[4,9,32,512]{3,2,1,0:T(8,128)(2,1)S(1)}, bf16[4,9,32,512]{3,2,1,0:T(8,128)(2,1)S(1)}, u32[]{:S(2)}, u32[]{:S(2)}) collective-permute-start(bf16[4,9,32,512]{3,2,1,0:T(8,128)(2,1)S(1)} %get-tuple-element.46), channel_id=1, source_target_pairs={{0,1},{1,0},{2,3},{3,2},{4,5},{5,4},{6,7},{7,6},{8,9},{9,8},{10,11... | collective-permute-start | bytes 3538952 | tf_op jit(solution)/shard_map/ppermute | solution.py:33
  104.3 45.3 %collective-permute-start.3 = (bf16[256,3072]{1,0:T(8,128)(2,1)}, bf16[256,3072]{1,0:T(8,128)(2,1)}, u32[]{:S(2)}, u32[]{:S(2)}) collective-permute-start(bf16[256,3072]{1,0:T(8,128)(2,1)} %collective-permute-done.1.refs_7_), channel_id=1, source_target_pairs={{96,0},{104,8},{112,16},{120,24},{0,32},{8,40},{16,48},{24,56},{32... | collective-permute-start | bytes 4718600 | tf_op jit(solution)/shard_map/ppermute | solution.py:28
  115.6 34.0 %collective-permute-start.2 = (bf16[256,3072]{1,0:T(8,128)(2,1)}, bf16[256,3072]{1,0:T(8,128)(2,1)}, u32[]{:S(2)}, u32[]{:S(2)}) collective-permute-start(bf16[256,3072]{1,0:T(8,128)(2,1)} %collective-permute-done.1.refs_7_), channel_id=1, source_target_pairs={{24,0},{0,8},{8,16},{16,24},{56,32},{32,40},{40,48},{48,56},{88,64... | collective-permute-start | bytes 4718600 | tf_op jit(solution)/shard_map/ppermute | solution.py:28
  115.6 34.0 %collective-permute-start.18 = (bf16[256,3072]{1,0:T(8,128)(2,1)}, bf16[256,3072]{1,0:T(8,128)(2,1)}, u32[]{:S(2)}, u32[]{:S(2)}) collective-permute-start(bf16[256,3072]{1,0:T(8,128)(2,1)} %collective-permute-done.12.refs_4_.refs_13_), channel_id=1, source_target_pairs={{8,0},{16,8},{24,16},{0,24},{40,32},{48,40},{56,48},{32,56},{72,64... | collective-permute-start | bytes 4718600 | tf_op jit(solution)/shard_map/ppermute | solution.py:28
  120.8 7.4 %collective-permute-start.19 = (bf16[9,32,512]{2,1,0:T(8,128)(2,1)}, bf16[9,32,512]{2,1,0:T(8,128)(2,1)}, u32[]{:S(2)}, u32[]{:S(2)}) collective-permute-start(bf16[9,32,512]{2,1,0:T(8,128)(2,1)} %get-tuple-element.72), channel_id=1, source_target_pairs={{0,2},{1,3},{2,4},{3,5},{4,6},{5,7},{6,0},{7,1},{8,10},{9,11},{10,... | collective-permute-start | bytes 884744 | tf_op jit(solution)/shard_map/ppermute | solution.py:33
  122.3 15.6 %collective-permute-start.21 = (bf16[9,32,512]{2,1,0:T(8,128)(2,1)}, bf16[9,32,512]{2,1,0:T(8,128)(2,1)}, u32[]{:S(2)}, u32[]{:S(2)}) collective-permute-start(bf16[9,32,512]{2,1,0:T(8,128)(2,1)} %get-tuple-element.73), channel_id=1, source_target_pairs={{0,4},{1,5},{2,6},{3,7},{4,0},{5,1},{6,2},{7,3},{8,12},{9,13},{10,... | collective-permute-start | bytes 884744 | tf_op jit(solution)/shard_map/ppermute | solution.py:33
  128.2 19.6 %collective-permute-start.20 = (bf16[9,32,512]{2,1,0:T(8,128)(2,1)}, bf16[9,32,512]{2,1,0:T(8,128)(2,1)}, u32[]{:S(2)}, u32[]{:S(2)}) collective-permute-start(bf16[9,32,512]{2,1,0:T(8,128)(2,1)} %get-tuple-element.74), channel_id=1, source_target_pairs={{0,6},{1,7},{2,0},{3,1},{4,2},{5,3},{6,4},{7,5},{8,14},{9,15},{10,... | collective-permute-start | bytes 884744 | tf_op jit(solution)/shard_map/ppermute | solution.py:33
  137.9 11.5 %collective-permute-start.22 = (bf16[4,4,32,512]{3,2,1,0:T(8,128)(2,1)S(1)}, bf16[4,4,32,512]{3,2,1,0:T(8,128)(2,1)S(1)}, u32[]{:S(2)}, u32[]{:S(2)}) collective-permute-start(bf16[4,4,32,512]{3,2,1,0:T(8,128)(2,1)S(1)} %get-tuple-element.53), channel_id=1, source_target_pairs={{0,1},{1,0},{2,3},{3,2},{4,5},{5,4},{6,7},{7,6},{8,9},{9,8},{10,11... | collective-permute-start | bytes 1572872 | tf_op jit(solution)/shard_map/ppermute | solution.py:33
  154.3 5.7 %collective-permute-start.23 = (bf16[4,3,32,512]{3,2,1,0:T(8,128)(2,1)S(1)}, bf16[4,3,32,512]{3,2,1,0:T(8,128)(2,1)S(1)}, u32[]{:S(2)}, u32[]{:S(2)}) collective-permute-start(bf16[4,3,32,512]{3,2,1,0:T(8,128)(2,1)S(1)} %get-tuple-element.64), channel_id=1, source_target_pairs={{0,1},{1,0},{2,3},{3,2},{4,5},{5,4},{6,7},{7,6},{8,9},{9,8},{10,11... | collective-permute-start | bytes 1179656 | tf_op jit(solution)/shard_map/ppermute | solution.py:33
  160.3 8.1 %collective-permute-start.24 = (bf16[7,32,512]{2,1,0:T(8,128)(2,1)S(1)}, bf16[7,32,512]{2,1,0:T(8,128)(2,1)S(1)}, u32[]{:S(2)}, u32[]{:S(2)}) collective-permute-start(bf16[7,32,512]{2,1,0:T(8,128)(2,1)S(1)} %get-tuple-element.75), channel_id=1, source_target_pairs={{0,2},{1,3},{2,4},{3,5},{4,6},{5,7},{6,0},{7,1},{8,10},{9,11},{10,... | collective-permute-start | bytes 688136 | tf_op jit(solution)/shard_map/ppermute | solution.py:33
  161.6 6.8 %collective-permute-start.25 = (bf16[7,32,512]{2,1,0:T(8,128)(2,1)S(1)}, bf16[7,32,512]{2,1,0:T(8,128)(2,1)S(1)}, u32[]{:S(2)}, u32[]{:S(2)}) collective-permute-start(bf16[7,32,512]{2,1,0:T(8,128)(2,1)S(1)} %get-tuple-element.76), channel_id=1, source_target_pairs={{0,6},{1,7},{2,0},{3,1},{4,2},{5,3},{6,4},{7,5},{8,14},{9,15},{10,... | collective-permute-start | bytes 688136 | tf_op jit(solution)/shard_map/ppermute | solution.py:33
  163.0 11.2 %collective-permute-start.26 = (bf16[7,32,512]{2,1,0:T(8,128)(2,1)S(1)}, bf16[7,32,512]{2,1,0:T(8,128)(2,1)S(1)}, u32[]{:S(2)}, u32[]{:S(2)}) collective-permute-start(bf16[7,32,512]{2,1,0:T(8,128)(2,1)S(1)} %get-tuple-element.77), channel_id=1, source_target_pairs={{0,4},{1,5},{2,6},{3,7},{4,0},{5,1},{6,2},{7,3},{8,12},{9,13},{10,... | collective-permute-start | bytes 688136 | tf_op jit(solution)/shard_map/ppermute | solution.py:33
  174.5 5.3 %collective-permute-start.27 = (f32[16,8,512]{2,1,0:T(8,128)S(1)}, f32[16,8,512]{2,1,0:T(8,128)S(1)}, u32[]{:S(2)}, u32[]{:S(2)}) collective-permute-start(f32[16,8,512]{2,1,0:T(8,128)S(1)} %pad_maximum_fusion.1), channel_id=1, source_target_pairs={{7,0},{0,1},{1,2},{2,3},{3,4},{4,5},{5,6},{6,7},{15,8},{8,9},{9,10... | collective-permute-start | bytes 786440 | tf_op jit(solution)/shard_map/ppermute | solution.py:449
  176.4 5.8 %collective-permute-start.28 = (f32[16,8,512]{2,1,0:T(8,128)S(1)}, f32[16,8,512]{2,1,0:T(8,128)S(1)}, u32[]{:S(2)}, u32[]{:S(2)}) collective-permute-start(f32[16,8,512]{2,1,0:T(8,128)S(1)} %pad_maximum_fusion.2), channel_id=1, source_target_pairs={{1,0},{2,1},{3,2},{4,3},{5,4},{6,5},{7,6},{0,7},{9,8},{10,9},{11,1... | collective-permute-start | bytes 786440 | tf_op jit(solution)/shard_map/ppermute | solution.py:449
  182.3 0.8 copy-start.4
  187.9 4.8 %collective-permute-start.31 = (f32[24,768]{1,0:T(8,128)S(1)}, f32[24,768]{1,0:T(8,128)S(1)}, u32[]{:S(2)}, u32[]{:S(2)}) collective-permute-start(f32[24,768]{1,0:T(8,128)S(1)} %products.1), channel_id=1, source_target_pairs={{16,0},{24,8},{0,16},{8,24},{48,32},{56,40},{32,48},{40,56},{80,64... | collective-permute-start | bytes 221192 | tf_op jit(solution)/shard_map/ppermute | solution.py:28
  189.2 5.6 %collective-permute-start.30 = (f32[24,768]{1,0:T(8,128)S(1)}, f32[24,768]{1,0:T(8,128)S(1)}, u32[]{:S(2)}, u32[]{:S(2)}) collective-permute-start(f32[24,768]{1,0:T(8,128)S(1)} %products.1), channel_id=1, source_target_pairs={{24,0},{0,8},{8,16},{16,24},{56,32},{32,40},{40,48},{48,56},{88,64... | collective-permute-start | bytes 221192 | tf_op jit(solution)/shard_map/ppermute | solution.py:28
  191.3 3.7 %collective-permute-start.29 = (f32[24,768]{1,0:T(8,128)S(1)}, f32[24,768]{1,0:T(8,128)S(1)}, u32[]{:S(2)}, u32[]{:S(2)}) collective-permute-start(f32[24,768]{1,0:T(8,128)S(1)} %products.1), channel_id=1, source_target_pairs={{8,0},{16,8},{24,16},{0,24},{40,32},{48,40},{56,48},{32,56},{72,64... | collective-permute-start | bytes 221192 | tf_op jit(solution)/shard_map/ppermute | solution.py:28
  195.0 39.7 %copy-start.2 = (bf16[256,3072]{1,0:T(8,128)(2,1)S(1)}, bf16[256,3072]{1,0:T(8,128)(2,1)}, u32[]{:S(2)}) copy-start(bf16[256,3072]{1,0:T(8,128)(2,1)} %refs_2_.3) | copy-start | bytes 4718596
  195.0 4.9 %collective-permute-start.34 = (f32[24,768]{1,0:T(8,128)S(1)}, f32[24,768]{1,0:T(8,128)S(1)}, u32[]{:S(2)}, u32[]{:S(2)}) collective-permute-start(f32[24,768]{1,0:T(8,128)S(1)} %add_add_fusion.refs_5_), channel_id=1, source_target_pairs={{64,0},{72,8},{80,16},{88,24},{96,32},{104,40},{112,48},{120,56},{... | collective-permute-start | bytes 221192 | tf_op jit(solution)/shard_map/ppermute | solution.py:28
  195.1 5.3 %collective-permute-start.33 = (f32[24,768]{1,0:T(8,128)S(1)}, f32[24,768]{1,0:T(8,128)S(1)}, u32[]{:S(2)}, u32[]{:S(2)}) collective-permute-start(f32[24,768]{1,0:T(8,128)S(1)} %add_add_fusion.refs_5_), channel_id=1, source_target_pairs={{96,0},{104,8},{112,16},{120,24},{0,32},{8,40},{16,48},{24,56},{32... | collective-permute-start | bytes 221192 | tf_op jit(solution)/shard_map/ppermute | solution.py:28
  195.7 4.7 %collective-permute-start.32 = (f32[24,768]{1,0:T(8,128)S(1)}, f32[24,768]{1,0:T(8,128)S(1)}, u32[]{:S(2)}, u32[]{:S(2)}) collective-permute-start(f32[24,768]{1,0:T(8,128)S(1)} %add_add_fusion.refs_5_), channel_id=1, source_target_pairs={{32,0},{40,8},{48,16},{56,24},{64,32},{72,40},{80,48},{88,56},{96,... | collective-permute-start | bytes 221192 | tf_op jit(solution)/shard_map/ppermute | solution.py:28
  204.5 9.9 %collective-permute-start.38 = (bf16[9,32,512]{2,1,0:T(8,128)(2,1)S(1)}, bf16[9,32,512]{2,1,0:T(8,128)(2,1)S(1)}, u32[]{:S(2)}, u32[]{:S(2)}) collective-permute-start(bf16[9,32,512]{2,1,0:T(8,128)(2,1)S(1)} %get-tuple-element.69.refs_19_), channel_id=1, source_target_pairs={{0,6},{1,7},{2,0},{3,1},{4,2},{5,3},{6,4},{7,5},{8,14},{9,15},{10,... | collective-permute-start | bytes 884744 | tf_op jit(solution)/shard_map/ppermute | solution.py:33
  208.8 3.0 %collective-permute-start.41 = (bf16[8,32,512]{2,1,0:T(8,128)(2,1)S(1)}, bf16[8,32,512]{2,1,0:T(8,128)(2,1)S(1)}, u32[]{:S(2)}, u32[]{:S(2)}) collective-permute-start(bf16[8,32,512]{2,1,0:T(8,128)(2,1)S(1)} %get-tuple-element.68.refs_18_), channel_id=1, source_target_pairs={{0,1},{1,0},{2,3},{3,2},{4,5},{5,4},{6,7},{7,6},{8,9},{9,8},{10,11... | collective-permute-start | bytes 786440 | tf_op jit(solution)/shard_map/ppermute | solution.py:33
  209.7 10.3 %collective-permute-start.37 = (bf16[8,32,512]{2,1,0:T(8,128)(2,1)S(1)}, bf16[8,32,512]{2,1,0:T(8,128)(2,1)S(1)}, u32[]{:S(2)}, u32[]{:S(2)}) collective-permute-start(bf16[8,32,512]{2,1,0:T(8,128)(2,1)S(1)} %get-tuple-element.68.refs_18_), channel_id=1, source_target_pairs={{0,6},{1,7},{2,0},{3,1},{4,2},{5,3},{6,4},{7,5},{8,14},{9,15},{10,... | collective-permute-start | bytes 786440 | tf_op jit(solution)/shard_map/ppermute | solution.py:33
  209.8 13.0 %collective-permute-start.35 = (bf16[8,32,512]{2,1,0:T(8,128)(2,1)S(1)}, bf16[8,32,512]{2,1,0:T(8,128)(2,1)S(1)}, u32[]{:S(2)}, u32[]{:S(2)}) collective-permute-start(bf16[8,32,512]{2,1,0:T(8,128)(2,1)S(1)} %get-tuple-element.68.refs_18_), channel_id=1, source_target_pairs={{0,2},{1,3},{2,4},{3,5},{4,6},{5,7},{6,0},{7,1},{8,10},{9,11},{10,... | collective-permute-start | bytes 786440 | tf_op jit(solution)/shard_map/ppermute | solution.py:33
  211.2 11.6 %collective-permute-start.42 = (bf16[9,32,512]{2,1,0:T(8,128)(2,1)S(1)}, bf16[9,32,512]{2,1,0:T(8,128)(2,1)S(1)}, u32[]{:S(2)}, u32[]{:S(2)}) collective-permute-start(bf16[9,32,512]{2,1,0:T(8,128)(2,1)S(1)} %get-tuple-element.69.refs_19_), channel_id=1, source_target_pairs={{0,1},{1,0},{2,3},{3,2},{4,5},{5,4},{6,7},{7,6},{8,9},{9,8},{10,11... | collective-permute-start | bytes 884744 | tf_op jit(solution)/shard_map/ppermute | solution.py:33
  211.8 13.2 %collective-permute-start.36 = (bf16[9,32,512]{2,1,0:T(8,128)(2,1)S(1)}, bf16[9,32,512]{2,1,0:T(8,128)(2,1)S(1)}, u32[]{:S(2)}, u32[]{:S(2)}) collective-permute-start(bf16[9,32,512]{2,1,0:T(8,128)(2,1)S(1)} %get-tuple-element.69.refs_19_), channel_id=1, source_target_pairs={{0,2},{1,3},{2,4},{3,5},{4,6},{5,7},{6,0},{7,1},{8,10},{9,11},{10,... | collective-permute-start | bytes 884744 | tf_op jit(solution)/shard_map/ppermute | solution.py:33
  214.4 11.9 %collective-permute-start.40 = (bf16[9,32,512]{2,1,0:T(8,128)(2,1)S(1)}, bf16[9,32,512]{2,1,0:T(8,128)(2,1)S(1)}, u32[]{:S(2)}, u32[]{:S(2)}) collective-permute-start(bf16[9,32,512]{2,1,0:T(8,128)(2,1)S(1)} %collective-permute-done.38.refs_23_), channel_id=1, source_target_pairs={{0,6},{1,7},{2,0},{3,1},{4,2},{5,3},{6,4},{7,5},{8,14},{9,15},{10,... | collective-permute-start | bytes 884744 | tf_op jit(solution)/shard_map/ppermute | solution.py:33
  220.0 7.9 %collective-permute-start.45 = (bf16[8,32,512]{2,1,0:T(8,128)(2,1)S(1)}, bf16[8,32,512]{2,1,0:T(8,128)(2,1)S(1)}, u32[]{:S(2)}, u32[]{:S(2)}) collective-permute-start(bf16[8,32,512]{2,1,0:T(8,128)(2,1)S(1)} %collective-permute-done.37.refs_22_), channel_id=1, source_target_pairs={{0,1},{1,0},{2,3},{3,2},{4,5},{5,4},{6,7},{7,6},{8,9},{9,8},{10,11... | collective-permute-start | bytes 786440 | tf_op jit(solution)/shard_map/ppermute | solution.py:33
  222.8 10.1 %collective-permute-start.39 = (bf16[8,32,512]{2,1,0:T(8,128)(2,1)S(1)}, bf16[8,32,512]{2,1,0:T(8,128)(2,1)S(1)}, u32[]{:S(2)}, u32[]{:S(2)}) collective-permute-start(bf16[8,32,512]{2,1,0:T(8,128)(2,1)S(1)} %collective-permute-done.35.refs_20_), channel_id=1, source_target_pairs={{0,2},{1,3},{2,4},{3,5},{4,6},{5,7},{6,0},{7,1},{8,10},{9,11},{10,... | collective-permute-start | bytes 786440 | tf_op jit(solution)/shard_map/ppermute | solution.py:33
  222.8 10.7 %collective-permute-start.46 = (bf16[9,32,512]{2,1,0:T(8,128)(2,1)S(1)}, bf16[9,32,512]{2,1,0:T(8,128)(2,1)S(1)}, u32[]{:S(2)}, u32[]{:S(2)}) collective-permute-start(bf16[9,32,512]{2,1,0:T(8,128)(2,1)S(1)} %collective-permute-done.38.refs_23_), channel_id=1, source_target_pairs={{0,1},{1,0},{2,3},{3,2},{4,5},{5,4},{6,7},{7,6},{8,9},{9,8},{10,11... | collective-permute-start | bytes 884744 | tf_op jit(solution)/shard_map/ppermute | solution.py:33
  225.0 8.4 %collective-permute-start.44 = (bf16[9,32,512]{2,1,0:T(8,128)(2,1)S(1)}, bf16[9,32,512]{2,1,0:T(8,128)(2,1)S(1)}, u32[]{:S(2)}, u32[]{:S(2)}) collective-permute-start(bf16[9,32,512]{2,1,0:T(8,128)(2,1)S(1)} %collective-permute-done.36.refs_21_), channel_id=1, source_target_pairs={{0,1},{1,0},{2,3},{3,2},{4,5},{5,4},{6,7},{7,6},{8,9},{9,8},{10,11... | collective-permute-start | bytes 884744 | tf_op jit(solution)/shard_map/ppermute | solution.py:33
  226.3 8.3 %collective-permute-start.48 = (bf16[9,32,512]{2,1,0:T(8,128)(2,1)S(1)}, bf16[9,32,512]{2,1,0:T(8,128)(2,1)S(1)}, u32[]{:S(2)}, u32[]{:S(2)}) collective-permute-start(bf16[9,32,512]{2,1,0:T(8,128)(2,1)S(1)} %collective-permute-done.40.refs_25_), channel_id=1, source_target_pairs={{0,1},{1,0},{2,3},{3,2},{4,5},{5,4},{6,7},{7,6},{8,9},{9,8},{10,11... | collective-permute-start | bytes 884744 | tf_op jit(solution)/shard_map/ppermute | solution.py:33
  227.9 5.5 %collective-permute-start.43 = (bf16[8,32,512]{2,1,0:T(8,128)(2,1)S(1)}, bf16[8,32,512]{2,1,0:T(8,128)(2,1)S(1)}, u32[]{:S(2)}, u32[]{:S(2)}) collective-permute-start(bf16[8,32,512]{2,1,0:T(8,128)(2,1)S(1)} %collective-permute-done.35.refs_20_), channel_id=1, source_target_pairs={{0,1},{1,0},{2,3},{3,2},{4,5},{5,4},{6,7},{7,6},{8,9},{9,8},{10,11... | collective-permute-start | bytes 786440 | tf_op jit(solution)/shard_map/ppermute | solution.py:33
  232.9 1.7 collective-permute-start.47
